TPU v7x, 512 devices: a whole 4x8x8 slice. The times are simulated.
512 devices in a mesh: phase: 2 (over y_lo), lat: 8 (over x, core), lon: 32 (over y_hi, z).
Axes of the slice: x: 4, y: 8 (y_hi: 4, y_lo: 2; y = y_hi * 2 + y_lo), z: 8, core: 2. Of those that a mesh axis runs over, the one named last changes fastest.
Arguments:
- x_in: bfloat16 [2, 2, 48, 384, 512], P('phase', None, 'lat', 'lon'), may hold values from -430 to 430
- out_grad: bfloat16 [2, 2, 48, 384, 512], P('phase', None, 'lat', 'lon'), may hold values from -6 to 6
- w_qkv: bfloat16 [2, 1536, 512], P('phase'), may hold values from -0.25 to 0.25
- w_proj: bfloat16 [2, 512, 512], P('phase'), may hold values from -0.25 to 0.25
- norm_gain: float32 [2, 512], P('phase'), may hold values from 0.25 to 1.75
- bias_table: float32 [2, 8, 759], P('phase'), may hold values from -80 to 165
- lat_labels: int32 [48], P('lat'), may hold values from 0 to 11, never falling along the last dimension, each value on 1 to 8 neighbouring positions
Outputs:
- grad_input: bfloat16 [2, 2, 48, 384, 512], P('phase', None, 'lat', 'lon')
- grad_qkv: float32 [2, 1536, 512], P('phase', 'lat', 'lon')
Inputs may be any that keep to these rules, and one draw needn't show every extreme that they name: `lat_labels`: labels never fall from one latitude row to the next; each label holds 1 to 8 consecutive rows, and one holds 8.
All inputs are finite; a program needn't handle non-finite values.
Results may differ from a plain program's by a relative error of at most 0.028.
Values may be sent and summed in bfloat16 or wider, within the bound.
No kernel may reach another device: no remote copies, remote signals or barrier semaphores. Data moves between devices by JAX's collectives and lax.ppermute only.
A program may use at most 64 MiB of HBM per device.

v0:
```python
import jax
import jax.numpy as jnp
from jax import lax
from jax.sharding import PartitionSpec as P

HEADS = 8
WIN_LEV = 2
WIN_LAT = 6
WIN_LON = 12


EPSILON = 1e-05
MASKED = -1e30


def as_sent(array):

    def short(part):
        return part.astype(jnp.bfloat16) if part.dtype == jnp.float32 else part

    return jax.tree.map(short, array)


def passed_along(array, axis, by):
    devices = lax.axis_size(axis)
    return lax.ppermute(array, axis, [(i, (i + by) % devices) for i in range(devices)])


def from_behind(value, axis, steps):
    count = lax.axis_size(axis)
    first, last = (max(0, -steps), min(count, count - steps))
    return lax.ppermute(value, axis, [(source, source + steps) for source in range(first, last)])


def mixing(formula, left_side, right_side):
    return jnp.einsum(formula, left_side, right_side, preferred_element_type=jnp.float32)


def window_split(grid_field):
    levels, lat_rows, lon_cols, features = grid_field.shape
    grid_field = grid_field.reshape(
        levels // WIN_LEV,
        WIN_LEV,
        lat_rows // WIN_LAT,
        WIN_LAT,
        lon_cols // WIN_LON,
        WIN_LON,
        features,
    )
    grid_field = grid_field.transpose(0, 2, 4, 1, 3, 5, 6)
    return grid_field.reshape(-1, WIN_LEV * WIN_LAT * WIN_LON, features)


def window_merge(blocks, levels, lat_rows, lon_cols):
    features = blocks.shape[-1]
    grid_field = blocks.reshape(
        levels // WIN_LEV,
        lat_rows // WIN_LAT,
        lon_cols // WIN_LON,
        WIN_LEV,
        WIN_LAT,
        WIN_LON,
        features,
    )
    grid_field = grid_field.transpose(0, 3, 1, 4, 2, 5, 6)
    return grid_field.reshape(levels, lat_rows, lon_cols, features)


def make_tags(labels_shifted, levels, lon_cols):
    position = jnp.arange(levels, dtype=jnp.int32)
    region = jnp.where(position < levels - 2, 0, jnp.where(position == levels - 2, 1, 2)).astype(
        jnp.int32
    )
    tag_grid = 3 * labels_shifted[None, :, None] + region[:, None, None]
    tag_grid = jnp.broadcast_to(tag_grid, (levels, labels_shifted.shape[0], lon_cols))
    return window_split(tag_grid[..., None])[..., 0]


def selector(extent):
    offsets = jnp.arange(extent, dtype=jnp.int32)
    target = offsets[:, None] - offsets[None, :] + extent - 1
    return (
        target[:, :, None] == jnp.arange(2 * extent - 1, dtype=jnp.int32)[None, None, :]
    ).astype(jnp.float32)


def window_bias(rel_table):
    head_count = rel_table.shape[0]
    table_grid = rel_table.reshape(head_count, 2 * WIN_LEV - 1, 2 * WIN_LAT - 1, 2 * WIN_LON - 1)
    highest = lax.Precision.HIGHEST
    step_one = jnp.einsum("habc,pqa->hpqbc", table_grid, selector(WIN_LEV), precision=highest)
    step_two = jnp.einsum("hpqbc,rsb->hpqrsc", step_one, selector(WIN_LAT), precision=highest)
    step_three = jnp.einsum("hpqrsc,tuc->hpqrstu", step_two, selector(WIN_LON), precision=highest)
    cell_count = WIN_LEV * WIN_LAT * WIN_LON
    return step_three.transpose(0, 1, 3, 5, 2, 4, 6).reshape(head_count, cell_count, cell_count)


def recompute(blocks, tag_blocks, qkv_weight, gain_vector, attn_bias):
    window_count, cell_count, features = blocks.shape
    head_dim = features // HEADS
    values_wide = blocks.astype(jnp.float32)
    center = jnp.mean(values_wide, axis=-1, keepdims=True)
    spread = jnp.mean(jnp.square(values_wide - center), axis=-1, keepdims=True)
    inv_std = lax.rsqrt(spread + EPSILON)
    normed = (values_wide - center) * inv_std
    scaled_input = (normed * gain_vector).astype(jnp.bfloat16)
    projected = mixing("wnd,ed->wne", scaled_input, qkv_weight).astype(jnp.bfloat16)
    split_heads = projected.reshape(window_count, cell_count, 3, HEADS, head_dim)
    query_heads = split_heads[:, :, 0]
    key_heads = split_heads[:, :, 1]
    value_heads = split_heads[:, :, 2]
    score_scale = head_dim ** (-0.5)
    scores = mixing("wihc,wjhc->whij", query_heads, key_heads) * score_scale + attn_bias[None]
    allowed = tag_blocks[:, None, :, None] == tag_blocks[:, None, None, :]
    scores = jnp.where(allowed, scores, MASKED)
    row_max = jnp.max(scores, axis=-1, keepdims=True)
    weights = jnp.exp(scores - row_max)
    attention = weights / jnp.sum(weights, axis=-1, keepdims=True)
    return (
        scaled_input,
        normed,
        inv_std,
        query_heads,
        key_heads,
        value_heads,
        attention,
        attention.astype(jnp.bfloat16),
    )


def backprop(stored, grad_blocks, qkv_weight, proj_weight, gain_vector):
    scaled_input, normed, inv_std, query_heads, key_heads, value_heads, attention, attention_low = (
        stored
    )
    window_count, cell_count, features = grad_blocks.shape
    head_dim = features // HEADS
    score_scale = head_dim ** (-0.5)
    d_attended = mixing("wne,ed->wnd", grad_blocks, proj_weight).astype(jnp.bfloat16)
    d_heads = d_attended.reshape(window_count, cell_count, HEADS, head_dim)
    d_probs = mixing("wihc,wjhc->whij", d_heads, value_heads)
    d_value = mixing("whij,wihc->wjhc", attention_low, d_heads)
    inner_sum = jnp.sum(attention * d_probs, axis=-1, keepdims=True)
    d_scores = (attention * (d_probs - inner_sum)).astype(jnp.bfloat16)
    d_query = mixing("whij,wjhc->wihc", d_scores, key_heads) * score_scale
    d_key = mixing("whij,wihc->wjhc", d_scores, query_heads) * score_scale
    d_qkv = jnp.stack([d_query, d_key, d_value], axis=2).reshape(
        window_count, cell_count, 3 * features
    )
    d_normed = mixing("wne,ed->wnd", d_qkv.astype(jnp.bfloat16), qkv_weight) * gain_vector
    d_shifted = inv_std * (
        d_normed
        - jnp.mean(d_normed, axis=-1, keepdims=True)
        - normed * jnp.mean(d_normed * normed, axis=-1, keepdims=True)
    )
    return (d_shifted, d_qkv)


def roll_ahead(fields, labels):
    lat_half = WIN_LAT // 2
    lon_half = WIN_LON // 2
    lon_edges = passed_along(
        as_sent(tuple((member[:, :, :lon_half] for member in fields))), "lon", -1
    )
    joined = tuple(
        (
            jnp.concatenate([member[:, :, lon_half:], edge_part], axis=2)
            for member, edge_part in zip(fields, lon_edges)
        )
    )
    outgoing = tuple((member[:, :lat_half] for member in joined))
    if labels is not None:
        outgoing = outgoing + (labels[:lat_half],)
    arrived = jax.tree.map(
        lambda part, own: part.astype(own.dtype),
        passed_along(as_sent(outgoing), "lat", -1),
        outgoing,
    )
    rolled = tuple(
        (
            jnp.roll(
                jnp.concatenate([member[:, lat_half:], incoming], axis=1), -(WIN_LEV // 2), axis=0
            )
            for member, incoming in zip(joined, arrived)
        )
    )
    if labels is None:
        return (rolled, None)
    return (rolled, jnp.concatenate([labels[lat_half:], arrived[-1]]))


def roll_back(grid_field):
    lat_half = WIN_LAT // 2
    lon_half = WIN_LON // 2
    shifted = jnp.roll(grid_field, WIN_LEV // 2, axis=0)
    arrived = passed_along(shifted[:, -lat_half:].astype(jnp.bfloat16), "lat", 1).astype(
        jnp.float32
    )
    shifted = jnp.concatenate([arrived, shifted[:, :-lat_half]], axis=1)
    arrived = passed_along(as_sent(shifted[:, :, -lon_half:]), "lon", 1)
    return jnp.concatenate([arrived, shifted[:, :, :-lon_half]], axis=2)


def pass_down(values_low):
    return from_behind(values_low, "phase", -1)


def weight_grad(grad_low, flat_input):
    partial_sum = lax.psum_scatter(
        lax.dot_general(
            flat_input, grad_low, (((0,), (0,)), ((), ())), preferred_element_type=jnp.float32
        ).astype(jnp.bfloat16),
        "lon",
        scatter_dimension=0,
        tiled=True,
    )
    result_block = (
        lax.psum_scatter(partial_sum, "lat", scatter_dimension=1, tiled=True).astype(jnp.float32).T
    )
    return result_block


def per_device(x_in, out_grad, w_qkv, w_proj, norm_gain, bias_table, lat_labels):
    levels, lat_rows, lon_cols, features = (
        x_in.shape[1],
        x_in.shape[2],
        x_in.shape[3],
        x_in.shape[4],
    )
    qkv_weight = w_qkv[0]
    proj_weight = w_proj[0]
    gain_vector = norm_gain[0]
    attn_bias = window_bias(bias_table[0])
    rolled, labels_shifted = roll_ahead((x_in[0], out_grad[0]), lat_labels)
    tag_blocks = make_tags(labels_shifted, levels, lon_cols)
    stored = recompute(window_split(rolled[0]), tag_blocks, qkv_weight, gain_vector, attn_bias)
    grad_blocks = window_split(rolled[1])
    first_input, first_qkv = backprop(stored, grad_blocks, qkv_weight, proj_weight, gain_vector)
    first_total = out_grad[0].astype(jnp.float32) + roll_back(
        window_merge(first_input, levels, lat_rows, lon_cols)
    )
    passed = pass_down(first_total.astype(jnp.bfloat16))
    passed_rolled, unused = roll_ahead((passed,), None)
    second_input, second_qkv = backprop(
        stored, window_split(passed_rolled[0]), qkv_weight, proj_weight, gain_vector
    )
    grad_field = first_total + (
        passed.astype(jnp.float32)
        + roll_back(window_merge(second_input, levels, lat_rows, lon_cols))
    )
    grad_input = grad_field.astype(jnp.bfloat16)[None]
    grad_low = (first_qkv + second_qkv).astype(jnp.bfloat16).reshape(-1, 3 * features)
    flat_input = stored[0].reshape(-1, features)
    grad_qkv = weight_grad(grad_low, flat_input)[None]
    return (grad_input, grad_qkv)


def solution(mesh):
    in_specs = (
        P("phase", None, "lat", "lon", None),
        P("phase", None, "lat", "lon", None),
        P("phase", None, None),
        P("phase", None, None),
        P("phase", None),
        P("phase", None, None),
        P("lat"),
    )
    out_specs = (P("phase", None, "lat", "lon", None), P("phase", "lat", "lon"))
    return jax.shard_map(
        per_device, mesh=mesh, in_specs=in_specs, out_specs=out_specs, check_vma=False
    )
```

profile of v0, /device:TPU:8, one launch (start us, length us, event | category | flops | bytes accessed | tf_op | source)
XLA Modules:
  0.0 388.3 jit_solution(14413913248556771447)
XLA Ops:
  7.2 1.1 fusion.67
  8.4 13.7 %collective-permute-start = (bf16[2,6,6,512]{3,0,2,1:T(2,128)(2,1)S(1)}, bf16[2,6,6,512]{3,0,2,1:T(2,128)(2,1)S(1)}, u32[]{:S(2)}, u32[]{:S(2)}) collective-permute-start(bf16[2,6,6,512]{3,0,2,1:T(2,128)(2,1)S(1)} %get-tuple-element.19), channel_id=1, source_target_pairs={{0,31},{1,0},{2,1},{3,2},{4,3},{5,4},{6,5},{7,6},{8,7},{9,8},{10,9... | collective-permute-start | bytes 221192 | tf_op jit(solution)/shard_map/ppermute | solution.py:26
  22.1 1.0 fusion.68
  23.1 2.5 collective-permute-start.3
  25.6 0.8 fusion.69
  26.4 1.6 collective-permute-start.2
  28.1 0.9 reshape_squeeze.3
  29.9 5.0 %convolution_bitcast_fusion = f32[8,2,6,12,2,6,12]{6,0,3,5,2,4,1:T(8,128)} fusion(f32[8,2,2,6,6,23,1]{5,4,2,1,0,3,6:T(8,128)S(1)} %convolution_bitcast_fusion.1, s32[12,12]{1,0:T(8,128)S(1)} %subtract_add_fusion), kind=kOutput, calls=%fused_computation.2 | convolution fusion | flops 45788400 | bytes 770112 | tf_op jit(solution)/shard_map/hpqrsc,tuc->hpqrstu/dot_general | solution.py:93
  34.9 13.2 %copy.87 = f32[8,2,6,12,2,6,12]{3,2,1,6,5,4,0:T(8,128)} copy(f32[8,2,6,12,2,6,12]{6,0,3,5,2,4,1:T(8,128)} %convolution_bitcast_fusion) | data formatting | bytes 1327104 | tf_op jit(solution)/shard_map/broadcast_in_dim;reshape | solution.py:113
  48.2 7.5 %reshape.750 = f32[8,144,144]{1,2,0:T(8,128)} reshape(f32[8,2,6,12,2,6,12]{3,2,1,6,5,4,0:T(8,128)} %copy.87) | data formatting | bytes 1327104 | tf_op jit(solution)/shard_map/broadcast_in_dim;reshape | solution.py:113
  56.3 1.2 collective-permute-start.1
  57.8 1.7 collective-permute-done.1
  62.6 0.7 copy-done.13
  63.3 0.7 convolution_convert_fusion.1
  64.2 0.9 copy-done.1
  65.1 1.6 fusion.8
  66.8 1.2 fusion.70
  68.0 2.9 convolution_bitcast_fusion.3
  70.9 1.3 multiply_reduce_fusion.1
  72.4 0.9 copy-done.2
  74.5 0.7 copy-done.7
  75.2 0.6 fusion.61
  75.9 0.7 fusion.65
  76.8 1.1 slice.143
  78.1 5.0 %collective-permute-done.5 = bf16[2,3,12,512]{3,0,2,1:T(2,128)(2,1)S(1)} collective-permute-done((bf16[2,3,12,512]{3,0,2,1:T(2,128)(2,1)S(1)}, bf16[2,3,12,512]{3,0,2,1:T(2,128)(2,1)S(1)}, u32[]{:S(2)}, u32[]{:S(2)}) %collective-permute-start.5) | collective-permute-done | bytes 73760 | tf_op jit(solution)/shard_map/ppermute | solution.py:26
  83.4 3.4 collective-permute-start.6
  86.9 7.0 %collective-permute-done.6 = bf16[2,6,6,512]{3,0,2,1:T(2,128)(2,1)S(1)} collective-permute-done((bf16[2,6,6,512]{3,0,2,1:T(2,128)(2,1)S(1)}, bf16[2,6,6,512]{3,0,2,1:T(2,128)(2,1)S(1)}, u32[]{:S(2)}, u32[]{:S(2)}) %collective-permute-start.6) | collective-permute-done | bytes 73760 | tf_op jit(solution)/shard_map/ppermute | solution.py:26
  94.2 3.8 collective-permute-start.7
  98.0 2.5 collective-permute-done.7
  100.6 1.9 collective-permute-start.8
  102.5 4.3 %collective-permute-done.8 = bf16[2,6,6,512]{3,0,2,1:T(2,128)(2,1)S(1)} collective-permute-done((bf16[2,6,6,512]{3,0,2,1:T(2,128)(2,1)S(1)}, bf16[2,6,6,512]{3,0,2,1:T(2,128)(2,1)S(1)}, u32[]{:S(2)}, u32[]{:S(2)}) %collective-permute-start.8) | collective-permute-done | bytes 73760 | tf_op jit(solution)/shard_map/ppermute | solution.py:26
  107.0 2.0 collective-permute-done.9
  109.7 1.3 convolution_convert_fusion.2
  111.1 2.9 convolution_bitcast_fusion.2
  114.0 1.3 multiply_reduce_fusion
  115.5 0.9 copy-done.3
  118.3 0.6 copy-done.14
  118.9 1.8 convolution_convert_fusion
  120.9 0.6 fusion.60
  122.3 5.0 %collective-permute-done.10 = bf16[2,3,12,512]{3,0,2,1:T(2,128)(2,1)S(1)} collective-permute-done((bf16[2,3,12,512]{3,0,2,1:T(2,128)(2,1)S(1)}, bf16[2,3,12,512]{3,0,2,1:T(2,128)(2,1)S(1)}, u32[]{:S(2)}, u32[]{:S(2)}) %collective-permute-start.10) | collective-permute-done | bytes 73760 | tf_op jit(solution)/shard_map/ppermute | solution.py:26
  127.6 1.9 collective-permute-start.11
  129.6 8.5 %collective-permute-done.11 = bf16[2,6,6,512]{3,0,2,1:T(2,128)(2,1)S(1)} collective-permute-done((bf16[2,6,6,512]{3,0,2,1:T(2,128)(2,1)S(1)}, bf16[2,6,6,512]{3,0,2,1:T(2,128)(2,1)S(1)}, u32[]{:S(2)}, u32[]{:S(2)}) %collective-permute-start.11) | collective-permute-done | bytes 73760 | tf_op jit(solution)/shard_map/ppermute | solution.py:26
  138.1 205.6 %reduce-scatter.5.cloned.1.call-done = bf16[16,1536]{1,0:T(8,128)(2,1)} async-done(((bf16[512,1536]{1,0:T(8,128)(2,1)}), bf16[16,1536]{1,0:T(8,128)(2,1)}) %reduce-scatter.5.cloned.1.call-update) | async-done | bytes 49168 | tf_op jit(solution)/shard_map/reduce_scatter | solution.py:208
  343.7 1.7 copy.88
  345.5 1.0 fusion.45
  346.5 33.4 %reduce-scatter.7.cloned.1.call-done = bf16[192,16]{1,0:T(8,128)(2,1)} async-done(((bf16[1536,16]{1,0:T(8,128)(2,1)}), bf16[192,16]{1,0:T(8,128)(2,1)}) %reduce-scatter.7.cloned.1.call-update) | async-done | bytes 6160
  379.9 0.9 copy.89
  380.8 0.6 convert_bitcast_fusion
  (127 shorter events, 11.8 us)
Async XLA Ops:
  7.2 56.1 %copy-start = (bf16[1,1536,512]{2,1,0:T(8,128)(2,1)S(1)}, bf16[1,1536,512]{2,1,0:T(8,128)(2,1)}, u32[]{:S(2)}) copy-start(bf16[1,1536,512]{2,1,0:T(8,128)(2,1)} %param.9) | copy-start | bytes 4718596
  7.2 336.6 %reduce-scatter.5.cloned.1.call-start = ((), (), s32[]{:S(2)}) async-start(), calls=%async_computation.2 | async-start | bytes 1622016 | tf_op jit(solution)/shard_map/reduce_scatter | solution.py:208
  8.4 47.8 %collective-permute-start = (bf16[2,6,6,512]{3,0,2,1:T(2,128)(2,1)S(1)}, bf16[2,6,6,512]{3,0,2,1:T(2,128)(2,1)S(1)}, u32[]{:S(2)}, u32[]{:S(2)}) collective-permute-start(bf16[2,6,6,512]{3,0,2,1:T(2,128)(2,1)S(1)} %get-tuple-element.19), channel_id=1, source_target_pairs={{0,31},{1,0},{2,1},{3,2},{4,3},{5,4},{6,5},{7,6},{8,7},{9,8},{10,9... | collective-permute-start | bytes 221192 | tf_op jit(solution)/shard_map/ppermute | solution.py:26
  23.1 34.4 %collective-permute-start.3 = (bf16[2,6,6,512]{3,0,2,1:T(2,128)(2,1)S(1)}, bf16[2,6,6,512]{3,0,2,1:T(2,128)(2,1)S(1)}, u32[]{:S(2)}, u32[]{:S(2)}) collective-permute-start(bf16[2,6,6,512]{3,0,2,1:T(2,128)(2,1)S(1)} %get-tuple-element.23), channel_id=1, source_target_pairs={{0,31},{1,0},{2,1},{3,2},{4,3},{5,4},{6,5},{7,6},{8,7},{9,8},{10,9... | collective-permute-start | bytes 221192 | tf_op jit(solution)/shard_map/ppermute | solution.py:26
  26.4 29.3 %collective-permute-start.2 = (s32[3]{0:T(128)S(1)}, s32[3]{0:T(128)S(1)}, u32[]{:S(2)}, u32[]{:S(2)}) collective-permute-start(s32[3]{0:T(128)S(1)} %get-tuple-element.25), channel_id=1, source_target_pairs={{0,224},{32,0},{64,32},{96,64},{128,96},{160,128},{192,160},{224,1... | collective-permute-start | bytes 44 | tf_op jit(solution)/shard_map/ppermute | solution.py:26
  56.3 3.2 collective-permute-start.1
  57.8 3.1 collective-permute-start.4
  60.6 1.0 copy-start.9
  61.2 1.1 copy-start.23
  62.6 0.7 copy-start.13
  64.2 0.9 copy-start.1
  66.7 1.2 copy-start.4
  72.2 1.1 copy-start.2
  73.3 1.0 copy-start.10
  73.7 0.8 copy-start.5
  74.4 0.8 copy-start.7
  76.8 17.2 %copy-start.15 = (bf16[1,2,6,12,512]{4,1,3,2,0:T(2,128)(2,1)S(1)}, bf16[1,2,6,12,512]{4,1,3,2,0:T(2,128)(2,1)}, u32[]{:S(2)}) copy-start(bf16[1,2,6,12,512]{4,1,3,2,0:T(2,128)(2,1)} %param.8) | copy-start | bytes 442372
  78.1 5.0 %collective-permute-start.5 = (bf16[2,3,12,512]{3,0,2,1:T(2,128)(2,1)S(1)}, bf16[2,3,12,512]{3,0,2,1:T(2,128)(2,1)S(1)}, u32[]{:S(2)}, u32[]{:S(2)}) collective-permute-start(bf16[2,3,12,512]{3,0,2,1:T(2,128)(2,1)S(1)} %fusion.43), channel_id=1, source_target_pairs={{0,32},{32,64},{64,96},{96,128},{128,160},{160,192},{192,224},{224... | collective-permute-start | bytes 221192 | tf_op jit(solution)/shard_map/ppermute | solution.py:26
  83.4 10.5 %collective-permute-start.6 = (bf16[2,6,6,512]{3,0,2,1:T(2,128)(2,1)S(1)}, bf16[2,6,6,512]{3,0,2,1:T(2,128)(2,1)S(1)}, u32[]{:S(2)}, u32[]{:S(2)}) collective-permute-start(bf16[2,6,6,512]{3,0,2,1:T(2,128)(2,1)S(1)} %slice.255), channel_id=1, source_target_pairs={{0,1},{1,2},{2,3},{3,4},{4,5},{5,6},{6,7},{7,8},{8,9},{9,10},{10,1... | collective-permute-start | bytes 221192 | tf_op jit(solution)/shard_map/ppermute | solution.py:26
  86.9 7.3 %copy-start.17 = (f32[2,6,6,512]{3,0,2,1:T(2,128)}, f32[2,6,6,512]{3,0,2,1:T(2,128)S(1)}, u32[]{:S(2)}) copy-start(f32[2,6,6,512]{3,0,2,1:T(2,128)S(1)} %slice.184) | copy-start | bytes 442372
  94.0 4.0 %copy-start.19 = (f32[2,6,6,512]{3,0,2,1:T(2,128)}, f32[2,6,6,512]{3,0,2,1:T(2,128)S(1)}, u32[]{:S(2)}) copy-start(f32[2,6,6,512]{3,0,2,1:T(2,128)S(1)} %convert_element_type.192) | copy-start | bytes 442372
  94.2 6.3 %collective-permute-start.7 = (bf16[2,6,12,512]{3,0,2,1:T(2,128)(2,1)S(1)}, bf16[2,6,12,512]{3,0,2,1:T(2,128)(2,1)S(1)}, u32[]{:S(2)}, u32[]{:S(2)}) collective-permute-start(bf16[2,6,12,512]{3,0,2,1:T(2,128)(2,1)S(1)} %fusion.59), channel_id=1, source_target_pairs={{256,0},{257,1},{258,2},{259,3},{260,4},{261,5},{262,6},{263,7},{2... | collective-permute-start | bytes 442376 | tf_op jit(solution)/shard_map/ppermute | solution.py:32
  100.5 8.6 %copy-start.21 = (bf16[2,6,12,512]{3,0,2,1:T(2,128)(2,1)}, bf16[2,6,12,512]{3,0,2,1:T(2,128)(2,1)S(1)}, u32[]{:S(2)}) copy-start(bf16[2,6,12,512]{3,0,2,1:T(2,128)(2,1)S(1)} %collective-permute-done.7) | copy-start | bytes 442372
  100.6 6.2 %collective-permute-start.8 = (bf16[2,6,6,512]{3,0,2,1:T(2,128)(2,1)S(1)}, bf16[2,6,6,512]{3,0,2,1:T(2,128)(2,1)S(1)}, u32[]{:S(2)}, u32[]{:S(2)}) collective-permute-start(bf16[2,6,6,512]{3,0,2,1:T(2,128)(2,1)S(1)} %get-tuple-element.15), channel_id=1, source_target_pairs={{0,31},{1,0},{2,1},{3,2},{4,3},{5,4},{6,5},{7,6},{8,7},{9,8},{10,9... | collective-permute-start | bytes 221192 | tf_op jit(solution)/shard_map/ppermute | solution.py:26
  107.0 2.0 collective-permute-start.9
  115.3 1.1 copy-start.3
  116.4 1.0 copy-start.6
  116.4 1.2 copy-start.8
  116.5 1.4 copy-start.11
  116.5 1.5 copy-start.12
  118.0 0.9 copy-start.14
  120.7 259.2 %reduce-scatter.7.cloned.1.call-start = ((), (), s32[]{:S(2)}) async-start(), calls=%async_computation.3 | async-start | bytes 442368
  122.2 223.3 %copy-start.16 = (bf16[1,2,6,12,512]{4,1,3,2,0:T(2,128)(2,1)S(1)}, bf16[1,2,6,12,512]{4,1,3,2,0:T(2,128)(2,1)}, u32[]{:S(2)}) copy-start(bf16[1,2,6,12,512]{4,1,3,2,0:T(2,128)(2,1)} %param.8) | copy-start | bytes 442372
  122.2 223.3 %copy-start.18 = (f32[2,6,6,512]{3,0,2,1:T(2,128)S(1)}, f32[2,6,6,512]{3,0,2,1:T(2,128)}, u32[]{:S(2)}) copy-start(f32[2,6,6,512]{3,0,2,1:T(2,128)} %copy-done.17) | copy-start | bytes 442372
  122.2 223.3 %copy-start.20 = (f32[2,6,6,512]{3,0,2,1:T(2,128)S(1)}, f32[2,6,6,512]{3,0,2,1:T(2,128)}, u32[]{:S(2)}) copy-start(f32[2,6,6,512]{3,0,2,1:T(2,128)} %copy-done.19) | copy-start | bytes 442372
  122.2 223.3 %copy-start.22 = (bf16[2,6,12,512]{3,0,2,1:T(2,128)(2,1)S(1)}, bf16[2,6,12,512]{3,0,2,1:T(2,128)(2,1)}, u32[]{:S(2)}) copy-start(bf16[2,6,12,512]{3,0,2,1:T(2,128)(2,1)} %copy-done.21) | copy-start | bytes 442372
  122.2 5.1 %collective-permute-start.10 = (bf16[2,3,12,512]{3,0,2,1:T(2,128)(2,1)S(1)}, bf16[2,3,12,512]{3,0,2,1:T(2,128)(2,1)S(1)}, u32[]{:S(2)}, u32[]{:S(2)}) collective-permute-start(bf16[2,3,12,512]{3,0,2,1:T(2,128)(2,1)S(1)} %fusion.44), channel_id=1, source_target_pairs={{0,32},{32,64},{64,96},{96,128},{128,160},{160,192},{192,224},{224... | collective-permute-start | bytes 221192 | tf_op jit(solution)/shard_map/ppermute | solution.py:26
  127.6 10.5 %collective-permute-start.11 = (bf16[2,6,6,512]{3,0,2,1:T(2,128)(2,1)S(1)}, bf16[2,6,6,512]{3,0,2,1:T(2,128)(2,1)S(1)}, u32[]{:S(2)}, u32[]{:S(2)}) collective-permute-start(bf16[2,6,6,512]{3,0,2,1:T(2,128)(2,1)S(1)} %slice.254), channel_id=1, source_target_pairs={{0,1},{1,2},{2,3},{3,4},{4,5},{5,6},{6,7},{7,8},{8,9},{9,10},{10,1... | collective-permute-start | bytes 221192 | tf_op jit(solution)/shard_map/ppermute | solution.py:26
Sparse Core Ops, SparseCore 0:
  120.8 222.8 reduce-scatter.4
  346.5 33.3 reduce-scatter.6
where the time goes:
time: 389 us; the launch traced here: 388 us
  waiting for transfers between devices  275 us (71%)
  local copies, waits for them, and re-layouts  37.4 us (10%)
  starting transfers between devices  30.3 us (8%)
  matrix products  22.2 us (6%)
  between operations  14.8 us (4%)
  other arithmetic  8.38 us (2%)
    reduce_scatter x1, waiting for transfers between devices, weight_grad(): lax.psum_scatter(lax.dot_general(flat_input, grad_low, (((0,), (0,)), (()...  206 us
    ppermute x11, waiting for transfers between devices, passed_along(): lax.ppermute(array, axis, [(i, (i + by) % devices) for i in range(devices)])  33.7 us
    unnamed x3, waiting for transfers between devices  33.5 us
    ppermute x11, starting transfers between devices, passed_along(): lax.ppermute(array, axis, [(i, (i + by) % devices) for i in range(devices)])  26.4 us
    another operation x2, local copies, waits for them, and re-layouts, recompute(): attn_bias[None]  20.8 us
    dot_general x14, matrix products, mixing(): jnp.einsum(formula, left_side, right_side, preferred_element_type=jnp.flo...  14.4 us
    unnamed x50, local copies, waits for them, and re-layouts  8.81 us
  transfers between devices with their start and end apart: 14, of which 10 were waited for; matrix products, arithmetic and copies ran while one was open for 9% of the time, Pallas kernels for 0%

commit v1 on v0

v1 whole, which is shorter than its diff:
```python
import functools

import jax
import jax.numpy as jnp
from jax import lax
from jax.experimental import pallas as pl
from jax.experimental.pallas import tpu as pltpu
from jax.sharding import PartitionSpec as P

F32 = jnp.float32
BF16 = jnp.bfloat16
HEADS = 8
FEATURES = 512
EPSILON = 1e-05
MASKED = -1e30
SCORE_SCALE = 0.125
VMEM_LIMIT = 40 * 1024 * 1024

LEVEL_ROWS = 96
ROWS = 192
PACKED_ROWS = 144


def call(kernel, out_shape, scratch=(), smem_first=0):
    def run(*args):
        specs = [
            pl.BlockSpec(memory_space=pltpu.SMEM if i < smem_first else pltpu.VMEM)
            for i in range(len(args))
        ]
        outs = jax.tree.map(lambda _: pl.BlockSpec(memory_space=pltpu.VMEM), out_shape)
        return pl.pallas_call(
            kernel,
            out_shape=out_shape,
            in_specs=specs,
            out_specs=outs,
            scratch_shapes=list(scratch),
            compiler_params=pltpu.CompilerParams(vmem_limit_bytes=VMEM_LIMIT),
        )(*args)

    return run


def struct(shape, dtype):
    return jax.ShapeDtypeStruct(shape, dtype)


def dot(left, right, dims=((1,), (0,))):
    return lax.dot_general(left, right, (dims, ((), ())), preferred_element_type=F32)


def row_index(shape, dim):
    return lax.broadcasted_iota(jnp.int32, shape, dim)


def cut_kernel(labels, x_ref, g_ref, own, lon, lat, cor):
    row = row_index((8, FEATURES), 0)

    def halves(ref, level, i, fill):
        low = ref[0, level, i, 0:8, :].astype(F32)
        high = ref[0, level, i, 4:12, :].astype(F32)
        return (
            jnp.where(row < 6, low, fill),
            jnp.where(row < 6, pltpu.roll(high, 6, 0), fill),
        )

    for level in range(2):
        for i in range(6):
            label = labels[i].astype(F32)
            x_low, x_high = halves(x_ref, level, i, label)
            g_low, g_high = halves(g_ref, level, i, 0.0)
            low = jnp.concatenate([x_low, g_low], axis=0).astype(BF16)
            high = jnp.concatenate([x_high, g_high], axis=0).astype(BF16)
            if i < 3:
                cor[level, i] = low
                lat[level, i] = high
            else:
                lon[level, i - 3] = low
                own[level, i - 3] = high


def bias_kernel(table, out):
    parts = []
    for h in range(HEADS):
        line = jnp.broadcast_to(table[h : h + 1, :], (8, 256))
        parts.append(pltpu.roll(line, 0, 1, stride=1, stride_axis=0))
        parts.append(pltpu.roll(line, 6, 1, stride=1, stride_axis=0))
    shifted = jnp.concatenate(parts, axis=0)
    source = row_index((256, 256), 0)
    lane = row_index((256, 256), 1)
    column = lane & 7
    target = (lane >> 4) * 23 + ((lane >> 3) & 1) * 6 + column + 11
    picked = jnp.where((source == target) & (column < 6), 1.0, 0.0).astype(BF16)
    first = shifted.astype(BF16)
    rest = shifted - first.astype(F32)
    second = rest.astype(BF16)
    third = (rest - second.astype(F32)).astype(BF16)
    spread = dot(first, picked) + dot(second, picked) + dot(third, picked)
    empty = (row_index((128, 128), 0) & 7) >= 6
    for b in range(6):
        shift = (256 - (5 - b) * 16) % 256
        moved = spread if shift == 0 else pltpu.roll(spread, shift, 1)
        moved = jnp.where(empty, MASKED, moved[:, :128])
        for h in range(HEADS):
            out[h * 96 + b * 16 : h * 96 + b * 16 + 16, :] = moved[h * 16 : h * 16 + 16, :]


def pack_rows(array):
    columns = array.shape[1]
    groups = array.reshape(6, 4, 8, columns)
    row = row_index((8, columns), 0)
    out = []
    for q in range(6):
        last = groups[q, 3]
        for g in range(3):
            out.append(jnp.where(row < 6, groups[q, g], pltpu.roll(last, 6 - 2 * g, 0)))
    return jnp.concatenate(out, axis=0)


def attention_backward(att, d_low, q_ref, k_ref, v_ref, dqkv):
    lane = row_index((LEVEL_ROWS, 128), 1)
    for level in range(2):
        rows = slice(level * LEVEL_ROWS, (level + 1) * LEVEL_ROWS)
        for pair in range(4):
            cols = slice(pair * 128, (pair + 1) * 128)
            probs = att(level, pair)
            probs_low = probs.astype(BF16).reshape(2 * LEVEL_ROWS, LEVEL_ROWS)
            d_out = d_low[rows, cols]
            query = q_ref[rows, cols]
            keys = k_ref[:, rows, cols].reshape(2 * LEVEL_ROWS, 128)
            values = v_ref[:, rows, cols].reshape(2 * LEVEL_ROWS, 128)
            d_probs = dot(values, d_out, ((1,), (1,))).reshape(2, LEVEL_ROWS, LEVEL_ROWS)
            inner = jnp.sum(probs * d_probs, axis=1, keepdims=True)
            d_scores = (probs * (d_probs - inner)).astype(BF16).reshape(2 * LEVEL_ROWS, LEVEL_ROWS)
            d_value = dot(probs_low, d_out)
            d_key = dot(d_scores, query)
            d_query = dot(d_scores, keys, ((0,), (0,)))
            dqkv[rows, pair * 128 : (pair + 1) * 128] = d_query * SCORE_SCALE
            dqkv[rows, 512 + pair * 128 : 512 + (pair + 1) * 128] = (
                jnp.where(lane < 64, d_key[:LEVEL_ROWS], d_key[LEVEL_ROWS:]) * SCORE_SCALE
            )
            dqkv[rows, 1024 + pair * 128 : 1024 + (pair + 1) * 128] = jnp.where(
                lane < 64, d_value[:LEVEL_ROWS], d_value[LEVEL_ROWS:]
            )


def input_gradient(dqkv, w_qkv, gain, normed, inv_std):
    d_normed = dot(dqkv[...].astype(BF16), w_qkv[...]) * gain[...]
    mean_plain = jnp.mean(d_normed, axis=-1, keepdims=True)
    mean_normed = jnp.mean(d_normed * normed, axis=-1, keepdims=True)
    return inv_std * (d_normed - mean_plain - normed * mean_normed)


def first_kernel(
    own, lon, lat, cor, w_qkv, w_proj, gain, bias,
    skip, packed_input, cot, d_first, normed_out, inv_out, q_out, k_out, v_out, att_out,
    dqkv,
):
    tiles_x, tiles_g = [], []
    labels = []
    row = row_index((8, FEATURES), 0)
    for level in range(2):
        for i in range(6):
            left, right = (own, lon) if i < 3 else (lat, cor)
            left, right = left[level, i % 3].astype(F32), right[level, i % 3].astype(F32)
            if level == 0:
                labels.append(left[6:7, :128])
            for tile in (left, right):
                tiles_x.append(jnp.where(row < 6, tile[:8], 0.0))
                tiles_g.append(tile[8:])
    x = jnp.concatenate(tiles_x, axis=0)
    c = jnp.concatenate(tiles_g, axis=0)
    center = jnp.mean(x, axis=-1, keepdims=True)
    moved = x - center
    spread = jnp.mean(jnp.square(moved), axis=-1, keepdims=True)
    inv_std = lax.rsqrt(spread + EPSILON)
    normed = moved * inv_std
    scaled = normed * gain[...]
    packed_input[...] = pack_rows(scaled).astype(BF16)
    projected = dot(scaled.astype(BF16), w_qkv[...], ((1,), (1,)))
    c_low = c.astype(BF16)
    d_first_value = dot(c_low, w_proj[...])
    cot[...] = c_low
    d_first[...] = d_first_value
    normed_out[...] = normed
    inv_out[...] = jnp.broadcast_to(inv_std, (ROWS, 128))
    q_out[...] = projected[:, :512].astype(BF16)
    even = (row_index((ROWS, 512), 1) & 64) == 0
    k = projected[:, 512:1024]
    v = projected[:, 1024:]
    k_out[0] = jnp.where(even, k, 0.0).astype(BF16)
    k_out[1] = jnp.where(even, 0.0, k).astype(BF16)
    v_out[0] = jnp.where(even, v, 0.0).astype(BF16)
    v_out[1] = jnp.where(even, 0.0, v).astype(BF16)

    lane_row = row_index((1, 128), 1) >> 4
    along = labels[0]
    for b in range(1, 6):
        along = jnp.where(lane_row == b, labels[b], along)
    allowed = jnp.concatenate(
        [
            jnp.broadcast_to(jnp.where(labels[b] == along, 0.0, MASKED), (16, 128))
            for b in range(6)
        ],
        axis=0,
    )

    def probabilities(level, pair):
        rows = slice(level * LEVEL_ROWS, (level + 1) * LEVEL_ROWS)
        cols = slice(pair * 128, (pair + 1) * 128)
        added = bias[pair * 192 : (pair + 1) * 192, :].reshape(2, LEVEL_ROWS, 128) + allowed[None]
        keys = k_out[:, rows, cols].reshape(2 * LEVEL_ROWS, 128)
        scores = dot(keys, q_out[rows, cols], ((1,), (1,))).reshape(2, LEVEL_ROWS, LEVEL_ROWS)
        scores = scores * SCORE_SCALE + added[:, :, :LEVEL_ROWS]
        weights = jnp.exp(scores - jnp.max(scores, axis=1, keepdims=True))
        probs = weights * (1.0 / jnp.sum(weights, axis=1, keepdims=True))
        att_out[level, pair] = probs
        return probs

    attention_backward(probabilities, d_first_value.astype(BF16), q_out, k_out, v_out, dqkv)
    skip[...] = (c + input_gradient(dqkv, w_qkv, gain, normed, inv_std)).astype(BF16)


def second_kernel(
    arrived, cot, d_first, normed, inv, q_ref, k_ref, v_ref, att, w_qkv, w_proj, gain,
    blocks, own, lon, lat, cor, dqkv,
):
    c2 = arrived[...]
    d_low = (d_first[...] + dot(c2, w_proj[...])).astype(BF16)
    attention_backward(lambda level, pair: att[level, pair], d_low, q_ref, k_ref, v_ref, dqkv)
    lane = row_index((80, 128), 1)
    for t in range(4):
        whole = [pack_rows(dqkv[:, 384 * t + 128 * j : 384 * t + 128 * (j + 1)]) for j in range(3)]
        blocks[2 * t, :144, :] = whole[0].astype(BF16)
        blocks[2 * t + 1, :144, :] = whole[2].astype(BF16)
        top = whole[1][:80]
        bottom = jnp.concatenate([whole[1][80:], jnp.zeros((16, 128), F32)], axis=0)
        blocks[2 * t, 144:, :] = jnp.where(lane < 64, top, pltpu.roll(bottom, 64, 1)).astype(BF16)
        blocks[2 * t + 1, 144:, :] = jnp.where(lane < 64, pltpu.roll(top, 64, 1), bottom).astype(BF16)
    shifted = input_gradient(dqkv, w_qkv, gain, normed[...], inv[:, 0:1])
    total = cot[...].astype(F32) + (c2.astype(F32) + shifted)
    for i in range(6):
        for half in range(2):
            start = 16 * i + 8 * half
            both = jnp.concatenate(
                [total[start : start + 8], total[96 + start : 96 + start + 8]], axis=0
            )
            target = ((own, lon), (lat, cor))[i // 3][half]
            target[i % 3] = both.astype(BF16)


def product_kernel(blocks, inputs, out):
    whole = jnp.zeros((128, FEATURES), F32)
    upper = jnp.zeros((128, FEATURES), F32)
    lower = jnp.zeros((128, FEATURES), F32)
    for p in range(blocks.shape[0]):
        cells = inputs[p]
        whole += dot(blocks[p, :144], cells, ((0,), (0,)))
        folded = blocks[p, 144:]
        upper += dot(folded, cells[:80], ((0,), (0,)))
        lower += dot(folded[:64], cells[80:], ((0,), (0,)))
    half = upper[:64] + lower[64:]
    whole_t = whole.T
    half_t = jnp.concatenate([half, jnp.zeros((64, FEATURES), F32)], axis=0).T
    bands = out.shape[0]
    width = FEATURES // bands
    lane = row_index((width // 2, 128), 1)
    for band in range(bands):
        out[band, :width, :] = whole_t[band * width : (band + 1) * width].astype(BF16)
        part = half_t[band * width : (band + 1) * width]
        out[band, width:, :] = jnp.where(
            lane < 64, part[: width // 2], pltpu.roll(part[width // 2 :], 64, 1)
        ).astype(BF16)


def sum_kernel(odd, parts, out):
    bands, rows, _ = parts.shape
    width = rows * 2 // 3
    total = parts[0].astype(F32)
    for band in range(1, bands):
        total = total + parts[band].astype(F32)
    whole = total[:width]
    folded = total[width:]
    half = jnp.concatenate([folded, pltpu.roll(folded, 64, 1)], axis=0)
    pad = jnp.zeros((128 - width, 128), F32)
    whole_t = jnp.concatenate([whole, pad], axis=0).T[:, :width]
    half_t = jnp.concatenate([half, pad], axis=0).T[:64, :width]

    @pl.when(odd[0] == 0)
    def _():
        out[0, :128, :] = whole_t
        out[0, 128:, :] = half_t

    @pl.when(odd[0] == 1)
    def _():
        out[0, :64, :] = half_t
        out[0, 64:, :] = whole_t


def join_kernel(own, lon, lat, cor, out):
    row = row_index((8, FEATURES), 0)
    for level in range(2):
        part = slice(level * 8, level * 8 + 8)
        for i in range(6):
            left, right = (cor, lat) if i < 3 else (lon, own)
            left = left[i % 3].astype(F32)[part]
            right = pltpu.roll(right[i % 3].astype(F32)[part], 6, 0)
            out[0, level, i, 0:8, :] = jnp.where(row < 6, left, right).astype(BF16)
            out[0, level, i, 8:12, :] = right[:4].astype(BF16)


def passed(array, lat_by, lon_by):
    lats, lons = lax.axis_size("lat"), lax.axis_size("lon")
    pairs = [
        (a * lons + o, ((a + lat_by) % lats) * lons + (o + lon_by) % lons)
        for a in range(lats)
        for o in range(lons)
    ]
    return lax.ppermute(array, ("lat", "lon"), pairs)


def per_device(x_in, out_grad, w_qkv, w_proj, norm_gain, bias_table, lat_labels):
    lats, lons = lax.axis_size("lat"), lax.axis_size("lon")
    w_qkv, w_proj = w_qkv[0], w_proj[0]
    piece = struct((2, 3, 16, FEATURES), BF16)
    own, lon, lat, cor = call(cut_kernel, (piece,) * 4, smem_first=1)(lat_labels, x_in, out_grad)
    lon = passed(lon, 0, -1)
    lat = passed(lat, -1, 0)
    cor = passed(cor, -1, -1)
    table = jnp.pad(bias_table[0, :, 253:506], ((0, 0), (0, 3)))
    bias = call(bias_kernel, struct((HEADS * LEVEL_ROWS, 128), F32))(table)

    window = struct((ROWS, FEATURES), BF16)
    wide = struct((ROWS, FEATURES), F32)
    scratch = [pltpu.VMEM((ROWS, 3 * FEATURES), F32)]
    skip, packed_input, cot, d_first, normed, inv, q, k, v, att = call(
        first_kernel,
        (
            window,
            struct((PACKED_ROWS, FEATURES), BF16),
            window,
            wide,
            wide,
            struct((ROWS, 128), F32),
            window,
            struct((2, ROWS, FEATURES), BF16),
            struct((2, ROWS, FEATURES), BF16),
            struct((2, 4, 2, LEVEL_ROWS, LEVEL_ROWS), F32),
        ),
        scratch,
    )(own, lon, lat, cor, w_qkv, w_proj, norm_gain, bias)

    inputs = lax.all_gather(packed_input, "lat", axis=0, tiled=False)
    arrived = lax.ppermute(skip, "phase", [(1, 0)])
    back = struct((3, 16, FEATURES), BF16)
    blocks, own, lon, lat, cor = call(
        second_kernel,
        (struct((8, 224, 128), BF16), back, back, back, back),
        scratch,
    )(arrived, cot, d_first, normed, inv, q, k, v, att, w_qkv, w_proj, norm_gain)
    lon = passed(lon, 0, 1)
    lat = passed(lat, 1, 0)
    cor = passed(cor, 1, 1)
    blocks = lax.all_to_all(blocks, "lat", 0, 0, tiled=True)
    slices = call(product_kernel, struct((lons, FEATURES * 3 // 2 // lons, 128), BF16))(
        blocks, inputs
    )
    slices = lax.all_to_all(slices, "lon", 0, 0, tiled=True)
    odd = (lax.axis_index("lat") % 2).astype(jnp.int32).reshape(1)
    grad_qkv = call(sum_kernel, struct((1, 192, FEATURES // lons), F32), smem_first=1)(odd, slices)
    grad_input = call(join_kernel, struct((1, 2, 6, 12, FEATURES), BF16))(own, lon, lat, cor)
    return grad_input, grad_qkv


def solution(mesh):
    in_specs = (
        P("phase", None, "lat", "lon", None),
        P("phase", None, "lat", "lon", None),
        P("phase", None, None),
        P("phase", None, None),
        P("phase", None),
        P("phase", None, None),
        P("lat"),
    )
    out_specs = (P("phase", None, "lat", "lon", None), P("phase", "lat", "lon"))
    return jax.shard_map(
        per_device, mesh=mesh, in_specs=in_specs, out_specs=out_specs, check_vma=False
    )
```

time: 389 us -> 115 us (0.30)
  the two profiles are of different devices: /device:TPU:8 before, /device:TPU:1 now
where the time goes in v1:
time: 115 us; the launch traced here: 114 us
  starting transfers between devices  38.9 us (34%)
  local copies, waits for them, and re-layouts  19.8 us (17%)
  blocking collectives  16.4 us (14%)
  waiting for transfers between devices  15.6 us (14%)
  between operations  14.2 us (12%)
  Pallas kernels  8.98 us (8%)
    ppermute x6, starting transfers between devices, passed(): return lax.ppermute(array, ('lat', 'lon'), pairs)  27.7 us
    unnamed x54, local copies, waits for them, and re-layouts  19 us
    all_to_all x1, blocking collectives, per_device(): blocks = lax.all_to_all(blocks, 'lat', 0, 0, tiled=True)  16.4 us
    ppermute x6, waiting for transfers between devices, passed(): return lax.ppermute(array, ('lat', 'lon'), pairs)  10.3 us
    all_to_all x1, starting transfers between devices, per_device(): slices = lax.all_to_all(slices, 'lon', 0, 0, tiled=True)  9.87 us
    pallas_call x7, Pallas kernels, run(): pl.pallas_call(kernel, out_shape=out_shape, in_specs=specs, out_specs=out...  8.98 us
    ppermute x1, waiting for transfers between devices, per_device(): arrived = lax.ppermute(skip, 'phase', [(1, 0)])  5.32 us
  transfers between devices with their start and end apart: 9, of which 4 were waited for; matrix products, arithmetic and copies ran while one was open for 1% of the time, Pallas kernels for 2%

profile of v1, /device:TPU:1, one launch (start us, length us, event | category | flops | bytes accessed | tf_op | source)
XLA Modules:
  0.0 113.9 jit_solution(289356117715558257)
XLA Ops:
  7.2 0.0 all-gather.3.cloned.1.call-start
  7.2 1.0 copy.10.g_ref
  8.2 0.9 copy.9.x_ref
  9.1 0.0 copy-start.17
  9.2 0.6 copy-done.17
  9.8 0.7 shard_map.86
  10.5 15.2 %collective-permute-start = (bf16[2,3,16,512]{3,2,1,0:T(8,128)(2,1)S(1)}, bf16[2,3,16,512]{3,2,1,0:T(8,128)(2,1)S(1)}, u32[]{:S(2)}, u32[]{:S(2)}) collective-permute-start(bf16[2,3,16,512]{3,2,1,0:T(8,128)(2,1)S(1)} %get-tuple-element.22), channel_id=1, source_target_pairs={{0,31},{1,0},{2,1},{3,2},{4,3},{5,4},{6,5},{7,6},{8,7},{9,8},{10,9... | collective-permute-start | bytes 294920 | tf_op jit(solution)/shard_map/ppermute | solution.py:318
  25.7 1.0 collective-permute-start.1
  26.6 4.0 %collective-permute-start.2 = (bf16[2,3,16,512]{3,2,1,0:T(8,128)(2,1)S(1)}, bf16[2,3,16,512]{3,2,1,0:T(8,128)(2,1)S(1)}, u32[]{:S(2)}, u32[]{:S(2)}) collective-permute-start(bf16[2,3,16,512]{3,2,1,0:T(8,128)(2,1)S(1)} %get-tuple-element.24), channel_id=1, source_target_pairs={{0,255},{1,224},{2,225},{3,226},{4,227},{5,228},{6,229},{7,230},{8... | collective-permute-start | bytes 294920 | tf_op jit(solution)/shard_map/ppermute | solution.py:318
  30.6 0.8 slice_bitcast_fusion
  31.4 0.5 shard_map.87.bias
  31.9 0.0 copy-start.16
  31.9 0.0 collective-permute-done.lon
  31.9 2.0 %collective-permute-done.2.cor = bf16[2,3,16,512]{3,2,1,0:T(8,128)(2,1)S(1)} collective-permute-done((bf16[2,3,16,512]{3,2,1,0:T(8,128)(2,1)S(1)}, bf16[2,3,16,512]{3,2,1,0:T(8,128)(2,1)S(1)}, u32[]{:S(2)}, u32[]{:S(2)}) %collective-permute-start.2) | collective-permute-done | bytes 98336 | tf_op jit(solution)/shard_map/ppermute | solution.py:318
  33.9 1.4 %copy-done = bf16[1,1536,512]{2,1,0:T(8,128)(2,1)S(1)} copy-done((bf16[1,1536,512]{2,1,0:T(8,128)(2,1)S(1)}, bf16[1,1536,512]{2,1,0:T(8,128)(2,1)}, u32[]{:S(2)}) %copy-start) | copy-done | bytes 1572888
  35.3 0.7 copy-done.15
  36.0 3.4 %shard_map.88 = (bf16[192,512]{1,0:T(8,128)(2,1)S(1)}, bf16[144,512]{1,0:T(8,128)(2,1)S(1)}, bf16[192,512]{1,0:T(8,128)(2,1)S(1)}, f32[192,512]{1,0:T(8,128)S(1)...) custom-call(bf16[2,3,16,512]{3,2,1,0:T(8,128)(2,1)S(1)} %get-tuple-e, ...), custom_call_target="tpu_custom_call" | custom-call | tf_op jit(solution)/shard_map/pallas_call | solution.py:31
  39.4 0.7 copy-done.4
  40.2 0.7 copy-done.6
  40.9 0.7 copy-done.8
  41.7 0.7 copy-done.10
  42.3 0.7 copy-done.12
  43.0 0.6 copy-done.13
  43.6 0.7 copy-done.18
  44.3 0.0 all-gather.3.cloned.1.call-update
  44.3 1.3 %collective-permute-start.3 = (bf16[192,512]{1,0:T(8,128)(2,1)}, bf16[192,512]{1,0:T(8,128)(2,1)S(1)}, u32[]{:S(2)}, u32[]{:S(2)}) collective-permute-start(bf16[192,512]{1,0:T(8,128)(2,1)} %copy-done.18), channel_id=1, source_target_pairs={{256,0},{257,1},{258,2},{259,3},{260,4},{261,5},{262,6},{263,7},{2... | collective-permute-start | bytes 589832 | tf_op jit(solution)/shard_map/ppermute | solution.py:353
  45.6 5.3 %collective-permute-done.3.arrived = bf16[192,512]{1,0:T(8,128)(2,1)S(1)} collective-permute-done((bf16[192,512]{1,0:T(8,128)(2,1)}, bf16[192,512]{1,0:T(8,128)(2,1)S(1)}, u32[]{:S(2)}, u32[]{:S(2)}) %collective-permute-start.3) | collective-permute-done | bytes 196640 | tf_op jit(solution)/shard_map/ppermute | solution.py:353
  51.0 1.0 copy-done.5
  52.0 1.0 copy-done.7
  53.0 1.0 copy-done.9
  54.0 0.9 copy-done.11
  54.9 0.9 copy-done.14
  55.8 2.3 %shard_map.89 = (bf16[8,224,128]{2,1,0:T(8,128)(2,1)S(1)}, bf16[3,16,512]{2,1,0:T(8,128)(2,1)S(1)}, bf16[3,16,512]{2,1,0:T(8,128)(2,1)S(1)}, bf16[3,16,512]{2,1,0:T(8,128)(2,1)S(1)}, bf16[3,16,512]{2,1,0:T(8,128)(2,1)S(1)}) custom-call(bf16[192,512]{1,0:T(8,128)(2,1)S(1)} %collective-permute-done.3.arrived, bf16[192,512]{1,0:T(8,128)(2,1)S(1)} %get-tuple-element.26.cot, ...), custom_call_target="tpu_custom_call" | custom-call | tf_op jit(solution)/shard_map/pallas_call | solution.py:31
  58.1 0.6 copy-done.19
  58.7 0.6 copy-done.21
  59.3 0.6 copy-done.23
  60.0 16.4 %all_to_all.10.blocks = bf16[8,224,128]{2,1,0:T(8,128)(2,1)S(1)} all-to-all(bf16[8,224,128]{2,1,0:T(8,128)(2,1)S(1)} %get-tuple-element.38), channel_id=1, replica_groups=mesh['phase'=2,'lat'=8,'lon'=32] {'lat'}, dimensions={0} | all-to-all | bytes 917504 | tf_op jit(solution)/shard_map/all_to_all | solution.py:363
  76.4 1.3 %copy-done.3 = bf16[1152,512]{1,0:T(8,128)(2,1)S(1)} copy-done((bf16[1152,512]{1,0:T(8,128)(2,1)S(1)}, bf16[1152,512]{1,0:T(8,128)(2,1)}, u32[]{:S(2)}) %copy-start.3) | copy-done | bytes 1179672
  77.6 1.9 %shard_map.91 = bf16[32,24,128]{2,1,0:T(8,128)(2,1)} custom-call(bf16[8,224,128]{2,1,0:T(8,128)(2,1)S(1)} %all_to_all.10.blocks, bf16[8,144,512]{2,1,0:T(8,128)(2,1)S(1)} %bitcast.10), custom_call_target="tpu_custom_call" | custom-call | tf_op jit(solution)/shard_map/pallas_call | solution.py:31
  79.5 9.9 %all-to-all-start.1 = ((bf16[32,24,128]{2,1,0:T(8,128)(2,1)}), bf16[32,24,128]{2,1,0:T(8,128)(2,1)S(1)}, u32[]{:S(2)}, u32[]{:S(2)}) async-start(bf16[32,24,128]{2,1,0:T(8,128)(2,1)} %shard_map.91), calls=%async_computation.1 | async-start | bytes 393216 | tf_op jit(solution)/shard_map/all_to_all | solution.py:367
  89.4 3.1 %collective-permute-start.4 = (bf16[3,16,512]{2,1,0:T(8,128)(2,1)S(1)}, bf16[3,16,512]{2,1,0:T(8,128)(2,1)S(1)}, u32[]{:S(2)}, u32[]{:S(2)}) collective-permute-start(bf16[3,16,512]{2,1,0:T(8,128)(2,1)S(1)} %copy-done.24), channel_id=1, source_target_pairs={{0,1},{1,2},{2,3},{3,4},{4,5},{5,6},{6,7},{7,8},{8,9},{9,10},{10,1... | collective-permute-start | bytes 147464 | tf_op jit(solution)/shard_map/ppermute | solution.py:318
  92.5 1.6 %collective-permute-start.5 = (bf16[3,16,512]{2,1,0:T(8,128)(2,1)S(1)}, bf16[3,16,512]{2,1,0:T(8,128)(2,1)S(1)}, u32[]{:S(2)}, u32[]{:S(2)}) collective-permute-start(bf16[3,16,512]{2,1,0:T(8,128)(2,1)S(1)} %copy-done.22), channel_id=1, source_target_pairs={{0,32},{1,33},{2,34},{3,35},{4,36},{5,37},{6,38},{7,39},{8,40},{9,... | collective-permute-start | bytes 147464 | tf_op jit(solution)/shard_map/ppermute | solution.py:318
  94.1 2.8 %collective-permute-start.6 = (bf16[3,16,512]{2,1,0:T(8,128)(2,1)S(1)}, bf16[3,16,512]{2,1,0:T(8,128)(2,1)S(1)}, u32[]{:S(2)}, u32[]{:S(2)}) collective-permute-start(bf16[3,16,512]{2,1,0:T(8,128)(2,1)S(1)} %copy-done.20), channel_id=1, source_target_pairs={{0,33},{1,34},{2,35},{3,36},{4,37},{5,38},{6,39},{7,40},{8,41},{9,... | collective-permute-start | bytes 147464 | tf_op jit(solution)/shard_map/ppermute | solution.py:318
  97.0 4.1 %collective-permute-done.4.lon = bf16[3,16,512]{2,1,0:T(8,128)(2,1)S(1)} collective-permute-done((bf16[3,16,512]{2,1,0:T(8,128)(2,1)S(1)}, bf16[3,16,512]{2,1,0:T(8,128)(2,1)S(1)}, u32[]{:S(2)}, u32[]{:S(2)}) %collective-permute-start.4) | collective-permute-done | bytes 49184 | tf_op jit(solution)/shard_map/ppermute | solution.py:318
  101.0 4.3 %collective-permute-done.6.cor = bf16[3,16,512]{2,1,0:T(8,128)(2,1)S(1)} collective-permute-done((bf16[3,16,512]{2,1,0:T(8,128)(2,1)S(1)}, bf16[3,16,512]{2,1,0:T(8,128)(2,1)S(1)}, u32[]{:S(2)}, u32[]{:S(2)}) %collective-permute-start.6) | collective-permute-done | bytes 49184 | tf_op jit(solution)/shard_map/ppermute | solution.py:318
  105.3 0.8 copy.11
  106.1 0.2 shard_map.92
  106.3 0.7 copy.12
  (35 shorter events, 0.1 us)
Async XLA Ops:
  7.2 26.7 %copy-start.2 = (bf16[1,512,512]{2,1,0:T(8,128)(2,1)S(1)}, bf16[1,512,512]{2,1,0:T(8,128)(2,1)}, u32[]{:S(2)}) copy-start(bf16[1,512,512]{2,1,0:T(8,128)(2,1)} %param.10) | copy-start | bytes 1572868
  7.2 69.2 %all-gather.3.cloned.1.call-start = ((), (), s32[]{:S(2)}) async-start(), calls=%async_computation.2 | async-start | bytes 1327104 | tf_op jit(solution)/shard_map/all_gather | solution.py:352
  9.1 0.7 copy-start.17
  10.5 21.4 %collective-permute-start = (bf16[2,3,16,512]{3,2,1,0:T(8,128)(2,1)S(1)}, bf16[2,3,16,512]{3,2,1,0:T(8,128)(2,1)S(1)}, u32[]{:S(2)}, u32[]{:S(2)}) collective-permute-start(bf16[2,3,16,512]{3,2,1,0:T(8,128)(2,1)S(1)} %get-tuple-element.22), channel_id=1, source_target_pairs={{0,31},{1,0},{2,1},{3,2},{4,3},{5,4},{6,5},{7,6},{8,7},{9,8},{10,9... | collective-permute-start | bytes 294920 | tf_op jit(solution)/shard_map/ppermute | solution.py:318
  25.7 6.2 %collective-permute-start.1 = (bf16[2,3,16,512]{3,2,1,0:T(8,128)(2,1)S(1)}, bf16[2,3,16,512]{3,2,1,0:T(8,128)(2,1)S(1)}, u32[]{:S(2)}, u32[]{:S(2)}) collective-permute-start(bf16[2,3,16,512]{3,2,1,0:T(8,128)(2,1)S(1)} %get-tuple-element.23), channel_id=1, source_target_pairs={{0,224},{1,225},{2,226},{3,227},{4,228},{5,229},{6,230},{7,231},{8... | collective-permute-start | bytes 294920 | tf_op jit(solution)/shard_map/ppermute | solution.py:318
  26.6 7.2 %collective-permute-start.2 = (bf16[2,3,16,512]{3,2,1,0:T(8,128)(2,1)S(1)}, bf16[2,3,16,512]{3,2,1,0:T(8,128)(2,1)S(1)}, u32[]{:S(2)}, u32[]{:S(2)}) collective-permute-start(bf16[2,3,16,512]{3,2,1,0:T(8,128)(2,1)S(1)} %get-tuple-element.24), channel_id=1, source_target_pairs={{0,255},{1,224},{2,225},{3,226},{4,227},{5,228},{6,229},{7,230},{8... | collective-permute-start | bytes 294920 | tf_op jit(solution)/shard_map/ppermute | solution.py:318
  31.9 19.1 %copy-start.16 = (f32[1,512]{1,0:T(1,128)S(1)}, f32[1,512]{1,0:T(1,128)}, u32[]{:S(2)}) copy-start(f32[1,512]{1,0:T(1,128)} %gain.3) | copy-start | bytes 6148
  33.9 1.4 %copy-start = (bf16[1,1536,512]{2,1,0:T(8,128)(2,1)S(1)}, bf16[1,1536,512]{2,1,0:T(8,128)(2,1)}, u32[]{:S(2)}) copy-start(bf16[1,1536,512]{2,1,0:T(8,128)(2,1)} %param.9) | copy-start | bytes 4718596
  35.3 0.7 copy-start.15
  36.0 15.0 %copy-start.1 = (bf16[1,1536,512]{2,1,0:T(8,128)(2,1)S(1)}, bf16[1,1536,512]{2,1,0:T(8,128)(2,1)}, u32[]{:S(2)}) copy-start(bf16[1,1536,512]{2,1,0:T(8,128)(2,1)} %param.9) | copy-start | bytes 4718596
  39.4 0.7 copy-start.4
  40.2 0.7 copy-start.6
  40.9 0.7 copy-start.8
  41.7 0.7 copy-start.10
  42.3 0.7 copy-start.12
  43.0 0.6 copy-start.13
  43.6 0.7 copy-start.18
  44.3 6.6 %collective-permute-start.3 = (bf16[192,512]{1,0:T(8,128)(2,1)}, bf16[192,512]{1,0:T(8,128)(2,1)S(1)}, u32[]{:S(2)}, u32[]{:S(2)}) collective-permute-start(bf16[192,512]{1,0:T(8,128)(2,1)} %copy-done.18), channel_id=1, source_target_pairs={{256,0},{257,1},{258,2},{259,3},{260,4},{261,5},{262,6},{263,7},{2... | collective-permute-start | bytes 589832 | tf_op jit(solution)/shard_map/ppermute | solution.py:353
  51.0 1.0 copy-start.5
  52.0 1.0 copy-start.7
  53.0 1.0 copy-start.9
  54.0 0.9 copy-start.11
  54.9 0.9 copy-start.14
  58.1 0.6 copy-start.19
  58.7 0.6 copy-start.21
  59.3 0.6 copy-start.23
  60.0 29.4 %copy-start.24 = (bf16[3,16,512]{2,1,0:T(8,128)(2,1)S(1)}, bf16[3,16,512]{2,1,0:T(8,128)(2,1)}, u32[]{:S(2)}) copy-start(bf16[3,16,512]{2,1,0:T(8,128)(2,1)} %copy-done.23) | copy-start | bytes 147460
  60.0 32.6 %copy-start.22 = (bf16[3,16,512]{2,1,0:T(8,128)(2,1)S(1)}, bf16[3,16,512]{2,1,0:T(8,128)(2,1)}, u32[]{:S(2)}) copy-start(bf16[3,16,512]{2,1,0:T(8,128)(2,1)} %copy-done.21) | copy-start | bytes 147460
  60.0 34.1 %copy-start.20 = (bf16[3,16,512]{2,1,0:T(8,128)(2,1)S(1)}, bf16[3,16,512]{2,1,0:T(8,128)(2,1)}, u32[]{:S(2)}) copy-start(bf16[3,16,512]{2,1,0:T(8,128)(2,1)} %copy-done.19) | copy-start | bytes 147460
  76.4 1.3 %copy-start.3 = (bf16[1152,512]{1,0:T(8,128)(2,1)S(1)}, bf16[1152,512]{1,0:T(8,128)(2,1)}, u32[]{:S(2)}) copy-start(bf16[1152,512]{1,0:T(8,128)(2,1)} %all-gather.3.cloned.1.call-done) | copy-start | bytes 3538948
  79.5 26.7 %all-to-all-start.1 = ((bf16[32,24,128]{2,1,0:T(8,128)(2,1)}), bf16[32,24,128]{2,1,0:T(8,128)(2,1)S(1)}, u32[]{:S(2)}, u32[]{:S(2)}) async-start(bf16[32,24,128]{2,1,0:T(8,128)(2,1)} %shard_map.91), calls=%async_computation.1 | async-start | bytes 393216 | tf_op jit(solution)/shard_map/all_to_all | solution.py:367
  89.4 11.6 %collective-permute-start.4 = (bf16[3,16,512]{2,1,0:T(8,128)(2,1)S(1)}, bf16[3,16,512]{2,1,0:T(8,128)(2,1)S(1)}, u32[]{:S(2)}, u32[]{:S(2)}) collective-permute-start(bf16[3,16,512]{2,1,0:T(8,128)(2,1)S(1)} %copy-done.24), channel_id=1, source_target_pairs={{0,1},{1,2},{2,3},{3,4},{4,5},{5,6},{6,7},{7,8},{8,9},{9,10},{10,1... | collective-permute-start | bytes 147464 | tf_op jit(solution)/shard_map/ppermute | solution.py:318
  92.5 8.5 %collective-permute-start.5 = (bf16[3,16,512]{2,1,0:T(8,128)(2,1)S(1)}, bf16[3,16,512]{2,1,0:T(8,128)(2,1)S(1)}, u32[]{:S(2)}, u32[]{:S(2)}) collective-permute-start(bf16[3,16,512]{2,1,0:T(8,128)(2,1)S(1)} %copy-done.22), channel_id=1, source_target_pairs={{0,32},{1,33},{2,34},{3,35},{4,36},{5,37},{6,38},{7,39},{8,40},{9,... | collective-permute-start | bytes 147464 | tf_op jit(solution)/shard_map/ppermute | solution.py:318
  94.1 11.2 %collective-permute-start.6 = (bf16[3,16,512]{2,1,0:T(8,128)(2,1)S(1)}, bf16[3,16,512]{2,1,0:T(8,128)(2,1)S(1)}, u32[]{:S(2)}, u32[]{:S(2)}) collective-permute-start(bf16[3,16,512]{2,1,0:T(8,128)(2,1)S(1)} %copy-done.20), channel_id=1, source_target_pairs={{0,33},{1,34},{2,35},{3,36},{4,37},{5,38},{6,39},{7,40},{8,41},{9,... | collective-permute-start | bytes 147464 | tf_op jit(solution)/shard_map/ppermute | solution.py:318
Sparse Core Ops, SparseCore 0:
  44.5 27.5 all-gather.2

commit v2 on v1

--- a/solution.py
+++ b/solution.py
@@ -14,20 +14,25 @@
 EPSILON = 1e-05
 MASKED = -1e30
 SCORE_SCALE = 0.125
-VMEM_LIMIT = 40 * 1024 * 1024
+VMEM_LIMIT = 16 * 1024 * 1024
 
 LEVEL_ROWS = 96
 ROWS = 192
 PACKED_ROWS = 144
 
 
-def call(kernel, out_shape, scratch=(), smem_first=0):
+def call(kernel, out_shape, scratch=(), places=(), out_places=()):
     def run(*args):
+        places_of = dict(places)
         specs = [
-            pl.BlockSpec(memory_space=pltpu.SMEM if i < smem_first else pltpu.VMEM)
-            for i in range(len(args))
+            pl.BlockSpec(memory_space=places_of.get(i, pltpu.VMEM)) for i in range(len(args))
         ]
-        outs = jax.tree.map(lambda _: pl.BlockSpec(memory_space=pltpu.VMEM), out_shape)
+        outs_of = dict(out_places)
+        outs = [
+            pl.BlockSpec(memory_space=outs_of.get(i, pltpu.VMEM))
+            for i in range(len(jax.tree.leaves(out_shape)))
+        ]
+        outs = tuple(outs) if isinstance(out_shape, tuple) else outs[0]
         return pl.pallas_call(
             kernel,
             out_shape=out_shape,
@@ -52,7 +57,10 @@
     return lax.broadcasted_iota(jnp.int32, shape, dim)
 
 
-def cut_kernel(labels, x_ref, g_ref, own, lon, lat, cor):
+def cut_kernel(labels_ref, x_ref, g_ref, own, lon, lat, cor, labels, sem):
+    fetch = pltpu.make_async_copy(labels_ref, labels, sem)
+    fetch.start()
+    fetch.wait()
     row = row_index((8, FEATURES), 0)
 
     def halves(ref, level, i, fill):
@@ -116,7 +124,15 @@
     return jnp.concatenate(out, axis=0)
 
 
-def attention_backward(att, d_low, q_ref, k_ref, v_ref, dqkv):
+def per_head(pair):
+    even = row_index(pair.shape, 1) < 64
+    wide = pair.astype(F32)
+    return jnp.concatenate(
+        [jnp.where(even, wide, 0.0).astype(BF16), jnp.where(even, 0.0, wide).astype(BF16)], axis=0
+    )
+
+
+def attention_backward(att, d_low, projected, dqkv):
     lane = row_index((LEVEL_ROWS, 128), 1)
     for level in range(2):
         rows = slice(level * LEVEL_ROWS, (level + 1) * LEVEL_ROWS)
@@ -125,9 +141,9 @@
             probs = att(level, pair)
             probs_low = probs.astype(BF16).reshape(2 * LEVEL_ROWS, LEVEL_ROWS)
             d_out = d_low[rows, cols]
-            query = q_ref[rows, cols]
-            keys = k_ref[:, rows, cols].reshape(2 * LEVEL_ROWS, 128)
-            values = v_ref[:, rows, cols].reshape(2 * LEVEL_ROWS, 128)
+            query = projected[rows, cols]
+            keys = per_head(projected[rows, 512 + pair * 128 : 512 + (pair + 1) * 128])
+            values = per_head(projected[rows, 1024 + pair * 128 : 1024 + (pair + 1) * 128])
             d_probs = dot(values, d_out, ((1,), (1,))).reshape(2, LEVEL_ROWS, LEVEL_ROWS)
             inner = jnp.sum(probs * d_probs, axis=1, keepdims=True)
             d_scores = (probs * (d_probs - inner)).astype(BF16).reshape(2 * LEVEL_ROWS, LEVEL_ROWS)
@@ -152,8 +168,8 @@
 
 def first_kernel(
     own, lon, lat, cor, w_qkv, w_proj, gain, bias,
-    skip, packed_input, cot, d_first, normed_out, inv_out, q_out, k_out, v_out, att_out,
-    dqkv,
+    skip, inputs_out, cot, normed_out, inv_out, projected_out, att_out,
+    dqkv, packed, sems,
 ):
     tiles_x, tiles_g = [], []
     labels = []
@@ -175,22 +191,20 @@
     inv_std = lax.rsqrt(spread + EPSILON)
     normed = moved * inv_std
     scaled = normed * gain[...]
-    packed_input[...] = pack_rows(scaled).astype(BF16)
+    packed[...] = pack_rows(scaled).astype(BF16)
+    copies = [
+        pltpu.make_async_copy(packed, inputs_out.at[p], sems.at[p])
+        for p in range(inputs_out.shape[0])
+    ]
+    for copy in copies:
+        copy.start()
     projected = dot(scaled.astype(BF16), w_qkv[...], ((1,), (1,)))
     c_low = c.astype(BF16)
     d_first_value = dot(c_low, w_proj[...])
     cot[...] = c_low
-    d_first[...] = d_first_value
     normed_out[...] = normed
     inv_out[...] = jnp.broadcast_to(inv_std, (ROWS, 128))
-    q_out[...] = projected[:, :512].astype(BF16)
-    even = (row_index((ROWS, 512), 1) & 64) == 0
-    k = projected[:, 512:1024]
-    v = projected[:, 1024:]
-    k_out[0] = jnp.where(even, k, 0.0).astype(BF16)
-    k_out[1] = jnp.where(even, 0.0, k).astype(BF16)
-    v_out[0] = jnp.where(even, v, 0.0).astype(BF16)
-    v_out[1] = jnp.where(even, 0.0, v).astype(BF16)
+    projected_out[...] = projected.astype(BF16)
 
     lane_row = row_index((1, 128), 1) >> 4
     along = labels[0]
@@ -208,25 +222,27 @@
         rows = slice(level * LEVEL_ROWS, (level + 1) * LEVEL_ROWS)
         cols = slice(pair * 128, (pair + 1) * 128)
         added = bias[pair * 192 : (pair + 1) * 192, :].reshape(2, LEVEL_ROWS, 128) + allowed[None]
-        keys = k_out[:, rows, cols].reshape(2 * LEVEL_ROWS, 128)
-        scores = dot(keys, q_out[rows, cols], ((1,), (1,))).reshape(2, LEVEL_ROWS, LEVEL_ROWS)
+        keys = per_head(projected_out[rows, 512 + pair * 128 : 512 + (pair + 1) * 128])
+        scores = dot(keys, projected_out[rows, cols], ((1,), (1,))).reshape(2, LEVEL_ROWS, LEVEL_ROWS)
         scores = scores * SCORE_SCALE + added[:, :, :LEVEL_ROWS]
         weights = jnp.exp(scores - jnp.max(scores, axis=1, keepdims=True))
         probs = weights * (1.0 / jnp.sum(weights, axis=1, keepdims=True))
         att_out[level, pair] = probs
         return probs
 
-    attention_backward(probabilities, d_first_value.astype(BF16), q_out, k_out, v_out, dqkv)
+    attention_backward(probabilities, d_first_value.astype(BF16), projected_out, dqkv)
     skip[...] = (c + input_gradient(dqkv, w_qkv, gain, normed, inv_std)).astype(BF16)
+    for copy in copies:
+        copy.wait()
 
 
 def second_kernel(
-    arrived, cot, d_first, normed, inv, q_ref, k_ref, v_ref, att, w_qkv, w_proj, gain,
-    blocks, own, lon, lat, cor, dqkv,
+    arrived, cot, projected, att, w_proj,
+    blocks, low, dqkv,
 ):
-    c2 = arrived[...]
-    d_low = (d_first[...] + dot(c2, w_proj[...])).astype(BF16)
-    attention_backward(lambda level, pair: att[level, pair], d_low, q_ref, k_ref, v_ref, dqkv)
+    d_low = (dot(cot[...], w_proj[...]) + dot(arrived[...], w_proj[...])).astype(BF16)
+    attention_backward(lambda level, pair: att[level, pair], d_low, projected, dqkv)
+    low[...] = dqkv[...].astype(BF16)
     lane = row_index((80, 128), 1)
     for t in range(4):
         whole = [pack_rows(dqkv[:, 384 * t + 128 * j : 384 * t + 128 * (j + 1)]) for j in range(3)]
@@ -236,8 +252,11 @@
         bottom = jnp.concatenate([whole[1][80:], jnp.zeros((16, 128), F32)], axis=0)
         blocks[2 * t, 144:, :] = jnp.where(lane < 64, top, pltpu.roll(bottom, 64, 1)).astype(BF16)
         blocks[2 * t + 1, 144:, :] = jnp.where(lane < 64, pltpu.roll(top, 64, 1), bottom).astype(BF16)
-    shifted = input_gradient(dqkv, w_qkv, gain, normed[...], inv[:, 0:1])
-    total = cot[...].astype(F32) + (c2.astype(F32) + shifted)
+
+
+def third_kernel(arrived, cot, low, normed, inv, w_qkv, gain, own, lon, lat, cor):
+    shifted = input_gradient(low, w_qkv, gain, normed[...], inv[:, 0:1])
+    total = cot[...].astype(F32) + (arrived[...].astype(F32) + shifted)
     for i in range(6):
         for half in range(2):
             start = 16 * i + 8 * half
@@ -281,19 +300,17 @@
     whole = total[:width]
     folded = total[width:]
     half = jnp.concatenate([folded, pltpu.roll(folded, 64, 1)], axis=0)
-    pad = jnp.zeros((128 - width, 128), F32)
-    whole_t = jnp.concatenate([whole, pad], axis=0).T[:, :width]
-    half_t = jnp.concatenate([half, pad], axis=0).T[:64, :width]
+    half = half[:, :64]
 
     @pl.when(odd[0] == 0)
     def _():
-        out[0, :128, :] = whole_t
-        out[0, 128:, :] = half_t
+        out[0, :, :128] = whole
+        out[0, :, 128:] = half
 
     @pl.when(odd[0] == 1)
     def _():
-        out[0, :64, :] = half_t
-        out[0, 64:, :] = whole_t
+        out[0, :, :64] = half
+        out[0, :, 64:] = whole
 
 
 def join_kernel(own, lon, lat, cor, out):
@@ -322,7 +339,12 @@
     lats, lons = lax.axis_size("lat"), lax.axis_size("lon")
     w_qkv, w_proj = w_qkv[0], w_proj[0]
     piece = struct((2, 3, 16, FEATURES), BF16)
-    own, lon, lat, cor = call(cut_kernel, (piece,) * 4, smem_first=1)(lat_labels, x_in, out_grad)
+    own, lon, lat, cor = call(
+        cut_kernel,
+        (piece,) * 4,
+        [pltpu.SMEM(lat_labels.shape, jnp.int32), pltpu.SemaphoreType.DMA],
+        places={0: pl.ANY},
+    )(lat_labels, x_in, out_grad)
     lon = passed(lon, 0, -1)
     lat = passed(lat, -1, 0)
     cor = passed(cor, -1, -1)
@@ -330,45 +352,48 @@
     bias = call(bias_kernel, struct((HEADS * LEVEL_ROWS, 128), F32))(table)
 
     window = struct((ROWS, FEATURES), BF16)
-    wide = struct((ROWS, FEATURES), F32)
     scratch = [pltpu.VMEM((ROWS, 3 * FEATURES), F32)]
-    skip, packed_input, cot, d_first, normed, inv, q, k, v, att = call(
+    skip, inputs, cot, normed, inv, projected, att = call(
         first_kernel,
         (
             window,
-            struct((PACKED_ROWS, FEATURES), BF16),
+            struct((lats, PACKED_ROWS, FEATURES), BF16),
             window,
-            wide,
-            wide,
+            struct((ROWS, FEATURES), F32),
             struct((ROWS, 128), F32),
-            window,
-            struct((2, ROWS, FEATURES), BF16),
-            struct((2, ROWS, FEATURES), BF16),
+            struct((ROWS, 3 * FEATURES), BF16),
             struct((2, 4, 2, LEVEL_ROWS, LEVEL_ROWS), F32),
         ),
+        scratch
+        + [pltpu.VMEM((PACKED_ROWS, FEATURES), BF16), pltpu.SemaphoreType.DMA((lats,))],
+        out_places={1: pl.ANY},
+    )(own, lon, lat, cor, w_qkv, w_proj, norm_gain, bias)
+
+    arrived = lax.ppermute(skip, "phase", [(1, 0)])
+    inputs = lax.all_to_all(inputs, "lat", 0, 0, tiled=True)
+    back = struct((3, 16, FEATURES), BF16)
+    blocks, low = call(
+        second_kernel,
+        (struct((8, 224, 128), BF16), struct((ROWS, 3 * FEATURES), BF16)),
         scratch,
-    )(own, lon, lat, cor, w_qkv, w_proj, norm_gain, bias)
-
-    inputs = lax.all_gather(packed_input, "lat", axis=0, tiled=False)
-    arrived = lax.ppermute(skip, "phase", [(1, 0)])
-    back = struct((3, 16, FEATURES), BF16)
-    blocks, own, lon, lat, cor = call(
-        second_kernel,
-        (struct((8, 224, 128), BF16), back, back, back, back),
-        scratch,
-    )(arrived, cot, d_first, normed, inv, q, k, v, att, w_qkv, w_proj, norm_gain)
+    )(arrived, cot, projected, att, w_proj)
+    blocks = lax.all_to_all(blocks, "lat", 0, 0, tiled=True)
+    own, lon, lat, cor = call(third_kernel, (back,) * 4)(
+        arrived, cot, low, normed, inv, w_qkv, norm_gain
+    )
     lon = passed(lon, 0, 1)
     lat = passed(lat, 1, 0)
     cor = passed(cor, 1, 1)
-    blocks = lax.all_to_all(blocks, "lat", 0, 0, tiled=True)
     slices = call(product_kernel, struct((lons, FEATURES * 3 // 2 // lons, 128), BF16))(
         blocks, inputs
     )
     slices = lax.all_to_all(slices, "lon", 0, 0, tiled=True)
     odd = (lax.axis_index("lat") % 2).astype(jnp.int32).reshape(1)
-    grad_qkv = call(sum_kernel, struct((1, 192, FEATURES // lons), F32), smem_first=1)(odd, slices)
+    grad_qkv = call(
+        sum_kernel, struct((1, FEATURES // lons, 192), F32), places={0: pltpu.SMEM}
+    )(odd, slices)
     grad_input = call(join_kernel, struct((1, 2, 6, 12, FEATURES), BF16))(own, lon, lat, cor)
-    return grad_input, grad_qkv
+    return grad_input, grad_qkv.transpose(0, 2, 1)
 
 
 def solution(mesh):

time: 115 us -> 107 us (0.930)
  blocking collectives: 16.4 us -> 36.2 us
  local copies, waits for them, and re-layouts: 19.8 us -> 5.6 us
  between operations: 14.2 us -> 0.8 us
  Pallas kernels: 8.98 us -> 11.5 us
    all_to_all x0 -> x1, blocking collectives: none -> 20 us  [per_device(): inputs = lax.all_to_all(inputs, 'lat', 0, 0, tiled=True)]
    unnamed x54 -> x13, local copies, waits for them, and re-layouts: 19 us -> 4.81 us
    pallas_call x7 -> x8, Pallas kernels: 8.98 us -> 11.5 us  [run(): pl.pallas_call(kernel, out_shape=out_shape, in_specs=specs, out_specs=out...]
  transfers between devices with their start and end apart: 9 -> 8, of which waited for: 4 -> 4; matrix products, arithmetic and copies ran while one was open for 1% -> 2% of each run, Pallas kernels for 2% -> 1%
where the time goes in v2:
time: 107 us
  starting transfers between devices  38.2 us (36%)
  blocking collectives  36.2 us (34%)
  waiting for transfers between devices  14.5 us (14%)
  Pallas kernels  11.5 us (11%)
  local copies, waits for them, and re-layouts  5.6 us (5%)
    ppermute x6, starting transfers between devices, passed(): return lax.ppermute(array, ('lat', 'lon'), pairs)  28 us
    all_to_all x1, blocking collectives, per_device(): inputs = lax.all_to_all(inputs, 'lat', 0, 0, tiled=True)  20 us
    all_to_all x1, blocking collectives, per_device(): blocks = lax.all_to_all(blocks, 'lat', 0, 0, tiled=True)  16.2 us
    pallas_call x8, Pallas kernels, run(): pl.pallas_call(kernel, out_shape=out_shape, in_specs=specs, out_specs=out...  11.5 us
    ppermute x6, waiting for transfers between devices, passed(): return lax.ppermute(array, ('lat', 'lon'), pairs)  9.43 us
    all_to_all x1, starting transfers between devices, per_device(): slices = lax.all_to_all(slices, 'lon', 0, 0, tiled=True)  8.89 us
    ppermute x1, waiting for transfers between devices, per_device(): arrived = lax.ppermute(skip, 'phase', [(1, 0)])  5.11 us
    unnamed x13, local copies, waits for them, and re-layouts  4.81 us
  transfers between devices with their start and end apart: 8, of which 4 were waited for; matrix products, arithmetic and copies ran while one was open for 2% of the time, Pallas kernels for 1%

profile of v2, /device:TPU:1, one launch (start us, length us, event | category | flops | bytes accessed | tf_op | source)
XLA Modules:
  0.0 106.8 jit_solution(7850390201729134664)
XLA Ops:
  0.6 0.0 copy-start.2
  0.6 0.0 copy-start.3
  0.7 1.0 copy.10.g_ref
  1.6 0.9 copy.9.x_ref
  2.6 0.0 copy-start.4
  2.6 0.6 copy-done.4
  3.2 0.7 shard_map.86
  3.9 15.2 %collective-permute-start = (bf16[2,3,16,512]{3,2,1,0:T(8,128)(2,1)S(1)}, bf16[2,3,16,512]{3,2,1,0:T(8,128)(2,1)S(1)}, u32[]{:S(2)}, u32[]{:S(2)}) collective-permute-start(bf16[2,3,16,512]{3,2,1,0:T(8,128)(2,1)S(1)} %get-tuple-element.20), channel_id=1, source_target_pairs={{0,31},{1,0},{2,1},{3,2},{4,3},{5,4},{6,5},{7,6},{8,7},{9,8},{10,9... | collective-permute-start | bytes 294920 | tf_op jit(solution)/shard_map/ppermute | solution.py:335
  19.1 1.0 collective-permute-start.1
  20.1 4.0 %collective-permute-start.2 = (bf16[2,3,16,512]{3,2,1,0:T(8,128)(2,1)S(1)}, bf16[2,3,16,512]{3,2,1,0:T(8,128)(2,1)S(1)}, u32[]{:S(2)}, u32[]{:S(2)}) collective-permute-start(bf16[2,3,16,512]{3,2,1,0:T(8,128)(2,1)S(1)} %get-tuple-element.22), channel_id=1, source_target_pairs={{0,255},{1,224},{2,225},{3,226},{4,227},{5,228},{6,229},{7,230},{8... | collective-permute-start | bytes 294920 | tf_op jit(solution)/shard_map/ppermute | solution.py:335
  24.1 0.8 slice_bitcast_fusion
  24.9 0.5 shard_map.87.bias
  25.4 0.0 collective-permute-done.lon
  25.4 0.0 collective-permute-done.1.lat
  25.4 2.0 %collective-permute-done.2.cor = bf16[2,3,16,512]{3,2,1,0:T(8,128)(2,1)S(1)} collective-permute-done((bf16[2,3,16,512]{3,2,1,0:T(8,128)(2,1)S(1)}, bf16[2,3,16,512]{3,2,1,0:T(8,128)(2,1)S(1)}, u32[]{:S(2)}, u32[]{:S(2)}) %collective-permute-start.2) | collective-permute-done | bytes 98336 | tf_op jit(solution)/shard_map/ppermute | solution.py:335
  27.3 0.0 copy-done.2
  27.3 0.0 copy-done.3
  27.3 0.0 copy-start
  27.3 1.4 %copy-done = bf16[1,1536,512]{2,1,0:T(8,128)(2,1)S(1)} copy-done((bf16[1,1536,512]{2,1,0:T(8,128)(2,1)S(1)}, bf16[1,1536,512]{2,1,0:T(8,128)(2,1)}, u32[]{:S(2)}) %copy-start) | copy-done | bytes 1572888
  28.8 5.1 %shard_map.88 = (bf16[192,512]{1,0:T(8,128)(2,1)S(1)}, bf16[8,144,512]{2,1,0:T(8,128)(2,1)S(1)}, bf16[192,512]{1,0:T(8,128)(2,1)S(1)}, f32[192,512]{1,0:T(8,128)...) custom-call(bf16[2,3,16,512]{3,2,1,0:T(8,128)(2,1)S(1)} %get-tuple-element.19.own, ...), custom_call_target="tpu_custom_call" | custom-call | tf_op jit(solution)/shard_map/pallas_call | solution.py:36
  33.9 1.3 %collective-permute-start.3 = (bf16[192,512]{1,0:T(8,128)(2,1)S(1)}, bf16[192,512]{1,0:T(8,128)(2,1)S(1)}, u32[]{:S(2)}, u32[]{:S(2)}) collective-permute-start(bf16[192,512]{1,0:T(8,128)(2,1)S(1)} %get-tuple-element.23), channel_id=1, source_target_pairs={{256,0},{257,1},{258,2},{259,3},{260,4},{261,5},{262,6},{263,7},{2... | collective-permute-start | bytes 589832 | tf_op jit(solution)/shard_map/ppermute | solution.py:372
  35.2 5.1 %collective-permute-done.3.arrived = bf16[192,512]{1,0:T(8,128)(2,1)S(1)} collective-permute-done((bf16[192,512]{1,0:T(8,128)(2,1)S(1)}, bf16[192,512]{1,0:T(8,128)(2,1)S(1)}, u32[]{:S(2)}, u32[]{:S(2)}) %collective-permute-start.3) | collective-permute-done | bytes 196640 | tf_op jit(solution)/shard_map/ppermute | solution.py:372
  40.3 1.9 %shard_map.89 = (bf16[8,224,128]{2,1,0:T(8,128)(2,1)S(1)}, bf16[192,1536]{1,0:T(8,128)(2,1)S(1)}) custom-call(bf16[192,512]{1,0:T(8,128)(2,1)S(1)} %collective-permute-done.3.arrived, bf16[192,512]{1,0:T(8,128)(2,1)S(1)} %get-tuple-element.24.cot, bf16[192,1536]{1,0:T(8,128)(2,1)S(1)} %get-tuple-element.25.projected, ...), custom_call_target="tpu_custom_call" | custom-call | tf_op jit(solution)/shard_map/pallas_call | solution.py:36
  42.2 16.2 %all_to_all.15.blocks = bf16[8,224,128]{2,1,0:T(8,128)(2,1)S(1)} all-to-all(bf16[8,224,128]{2,1,0:T(8,128)(2,1)S(1)} %get-tuple-element.34), channel_id=1, replica_groups=mesh['phase'=2,'lat'=8,'lon'=32] {'lat'}, dimensions={0} | all-to-all | bytes 917504 | tf_op jit(solution)/shard_map/all_to_all | solution.py:380
  58.5 20.0 %all_to_all.16.inputs = bf16[8,144,512]{2,1,0:T(8,128)(2,1)S(1)} all-to-all(bf16[8,144,512]{2,1,0:T(8,128)(2,1)S(1)} %get-tuple-element.35), channel_id=1, replica_groups=mesh['phase'=2,'lat'=8,'lon'=32] {'lat'}, dimensions={0} | all-to-all | bytes 2359296 | tf_op jit(solution)/shard_map/all_to_all | solution.py:373
  78.4 0.0 copy-start.1
  78.4 1.9 %shard_map.92 = bf16[32,24,128]{2,1,0:T(8,128)(2,1)} custom-call(bf16[8,224,128]{2,1,0:T(8,128)(2,1)S(1)} %all_to_all.15.blocks, bf16[8,144,512]{2,1,0:T(8,128)(2,1)S(1)} %all_to_all.16.inputs), custom_call_target="tpu_custom_call" | custom-call | tf_op jit(solution)/shard_map/pallas_call | solution.py:36
  80.3 8.9 %all-to-all-start.2 = ((bf16[32,24,128]{2,1,0:T(8,128)(2,1)}), bf16[32,24,128]{2,1,0:T(8,128)(2,1)S(1)}, u32[]{:S(2)}, u32[]{:S(2)}) async-start(bf16[32,24,128]{2,1,0:T(8,128)(2,1)} %shard_map.92), calls=%async_computation.2 | async-start | bytes 393216 | tf_op jit(solution)/shard_map/all_to_all | solution.py:390
  89.2 0.0 copy-done.1
  89.2 0.6 shard_map.90
  89.9 3.1 %collective-permute-start.4 = (bf16[3,16,512]{2,1,0:T(8,128)(2,1)S(1)}, bf16[3,16,512]{2,1,0:T(8,128)(2,1)S(1)}, u32[]{:S(2)}, u32[]{:S(2)}) collective-permute-start(bf16[3,16,512]{2,1,0:T(8,128)(2,1)S(1)} %get-tuple-element.31), channel_id=1, source_target_pairs={{0,1},{1,2},{2,3},{3,4},{4,5},{5,6},{6,7},{7,8},{8,9},{9,10},{10,1... | collective-permute-start | bytes 147464 | tf_op jit(solution)/shard_map/ppermute | solution.py:335
  93.0 1.9 %collective-permute-start.5 = (bf16[3,16,512]{2,1,0:T(8,128)(2,1)S(1)}, bf16[3,16,512]{2,1,0:T(8,128)(2,1)S(1)}, u32[]{:S(2)}, u32[]{:S(2)}) collective-permute-start(bf16[3,16,512]{2,1,0:T(8,128)(2,1)S(1)} %get-tuple-element.32), channel_id=1, source_target_pairs={{0,32},{1,33},{2,34},{3,35},{4,36},{5,37},{6,38},{7,39},{8,40},{9,... | collective-permute-start | bytes 147464 | tf_op jit(solution)/shard_map/ppermute | solution.py:335
  94.9 2.8 %collective-permute-start.6 = (bf16[3,16,512]{2,1,0:T(8,128)(2,1)S(1)}, bf16[3,16,512]{2,1,0:T(8,128)(2,1)S(1)}, u32[]{:S(2)}, u32[]{:S(2)}) collective-permute-start(bf16[3,16,512]{2,1,0:T(8,128)(2,1)S(1)} %get-tuple-element.33), channel_id=1, source_target_pairs={{0,33},{1,34},{2,35},{3,36},{4,37},{5,38},{6,39},{7,40},{8,41},{9,... | collective-permute-start | bytes 147464 | tf_op jit(solution)/shard_map/ppermute | solution.py:335
  97.7 2.5 %collective-permute-done.4.lon = bf16[3,16,512]{2,1,0:T(8,128)(2,1)S(1)} collective-permute-done((bf16[3,16,512]{2,1,0:T(8,128)(2,1)S(1)}, bf16[3,16,512]{2,1,0:T(8,128)(2,1)S(1)}, u32[]{:S(2)}, u32[]{:S(2)}) %collective-permute-start.4) | collective-permute-done | bytes 49184 | tf_op jit(solution)/shard_map/ppermute | solution.py:335
  100.3 0.0 collective-permute-done.5.lat
  100.3 4.9 %collective-permute-done.6.cor = bf16[3,16,512]{2,1,0:T(8,128)(2,1)S(1)} collective-permute-done((bf16[3,16,512]{2,1,0:T(8,128)(2,1)S(1)}, bf16[3,16,512]{2,1,0:T(8,128)(2,1)S(1)}, u32[]{:S(2)}, u32[]{:S(2)}) %collective-permute-start.6) | collective-permute-done | bytes 49184 | tf_op jit(solution)/shard_map/ppermute | solution.py:335
  105.2 0.8 copy.11
  106.0 0.0 all-to-all-done.2.parts
  106.0 0.8 shard_map.93
  (2 shorter events, 0.0 us)
Async XLA Ops:
  0.6 26.7 %copy-start.2 = (bf16[1,512,512]{2,1,0:T(8,128)(2,1)S(1)}, bf16[1,512,512]{2,1,0:T(8,128)(2,1)}, u32[]{:S(2)}) copy-start(bf16[1,512,512]{2,1,0:T(8,128)(2,1)} %param.10) | copy-start | bytes 1572868
  0.6 26.7 %copy-start.3 = (f32[1,512]{1,0:T(1,128)S(1)}, f32[1,512]{1,0:T(1,128)}, u32[]{:S(2)}) copy-start(f32[1,512]{1,0:T(1,128)} %gain.3) | copy-start | bytes 6148
  2.6 0.7 copy-start.4
  3.9 21.4 %collective-permute-start = (bf16[2,3,16,512]{3,2,1,0:T(8,128)(2,1)S(1)}, bf16[2,3,16,512]{3,2,1,0:T(8,128)(2,1)S(1)}, u32[]{:S(2)}, u32[]{:S(2)}) collective-permute-start(bf16[2,3,16,512]{3,2,1,0:T(8,128)(2,1)S(1)} %get-tuple-element.20), channel_id=1, source_target_pairs={{0,31},{1,0},{2,1},{3,2},{4,3},{5,4},{6,5},{7,6},{8,7},{9,8},{10,9... | collective-permute-start | bytes 294920 | tf_op jit(solution)/shard_map/ppermute | solution.py:335
  19.1 6.2 %collective-permute-start.1 = (bf16[2,3,16,512]{3,2,1,0:T(8,128)(2,1)S(1)}, bf16[2,3,16,512]{3,2,1,0:T(8,128)(2,1)S(1)}, u32[]{:S(2)}, u32[]{:S(2)}) collective-permute-start(bf16[2,3,16,512]{3,2,1,0:T(8,128)(2,1)S(1)} %get-tuple-element.21), channel_id=1, source_target_pairs={{0,224},{1,225},{2,226},{3,227},{4,228},{5,229},{6,230},{7,231},{8... | collective-permute-start | bytes 294920 | tf_op jit(solution)/shard_map/ppermute | solution.py:335
  20.1 7.2 %collective-permute-start.2 = (bf16[2,3,16,512]{3,2,1,0:T(8,128)(2,1)S(1)}, bf16[2,3,16,512]{3,2,1,0:T(8,128)(2,1)S(1)}, u32[]{:S(2)}, u32[]{:S(2)}) collective-permute-start(bf16[2,3,16,512]{3,2,1,0:T(8,128)(2,1)S(1)} %get-tuple-element.22), channel_id=1, source_target_pairs={{0,255},{1,224},{2,225},{3,226},{4,227},{5,228},{6,229},{7,230},{8... | collective-permute-start | bytes 294920 | tf_op jit(solution)/shard_map/ppermute | solution.py:335
  27.3 1.4 %copy-start = (bf16[1,1536,512]{2,1,0:T(8,128)(2,1)S(1)}, bf16[1,1536,512]{2,1,0:T(8,128)(2,1)}, u32[]{:S(2)}) copy-start(bf16[1,1536,512]{2,1,0:T(8,128)(2,1)} %param.9) | copy-start | bytes 4718596
  33.9 6.4 %collective-permute-start.3 = (bf16[192,512]{1,0:T(8,128)(2,1)S(1)}, bf16[192,512]{1,0:T(8,128)(2,1)S(1)}, u32[]{:S(2)}, u32[]{:S(2)}) collective-permute-start(bf16[192,512]{1,0:T(8,128)(2,1)S(1)} %get-tuple-element.23), channel_id=1, source_target_pairs={{256,0},{257,1},{258,2},{259,3},{260,4},{261,5},{262,6},{263,7},{2... | collective-permute-start | bytes 589832 | tf_op jit(solution)/shard_map/ppermute | solution.py:372
  78.4 10.8 %copy-start.1 = (bf16[1,1536,512]{2,1,0:T(8,128)(2,1)S(1)}, bf16[1,1536,512]{2,1,0:T(8,128)(2,1)}, u32[]{:S(2)}) copy-start(bf16[1,1536,512]{2,1,0:T(8,128)(2,1)} %param.9) | copy-start | bytes 4718596
  80.3 25.7 %all-to-all-start.2 = ((bf16[32,24,128]{2,1,0:T(8,128)(2,1)}), bf16[32,24,128]{2,1,0:T(8,128)(2,1)S(1)}, u32[]{:S(2)}, u32[]{:S(2)}) async-start(bf16[32,24,128]{2,1,0:T(8,128)(2,1)} %shard_map.92), calls=%async_computation.2 | async-start | bytes 393216 | tf_op jit(solution)/shard_map/all_to_all | solution.py:390
  89.9 10.4 %collective-permute-start.4 = (bf16[3,16,512]{2,1,0:T(8,128)(2,1)S(1)}, bf16[3,16,512]{2,1,0:T(8,128)(2,1)S(1)}, u32[]{:S(2)}, u32[]{:S(2)}) collective-permute-start(bf16[3,16,512]{2,1,0:T(8,128)(2,1)S(1)} %get-tuple-element.31), channel_id=1, source_target_pairs={{0,1},{1,2},{2,3},{3,4},{4,5},{5,6},{6,7},{7,8},{8,9},{9,10},{10,1... | collective-permute-start | bytes 147464 | tf_op jit(solution)/shard_map/ppermute | solution.py:335
  93.0 7.3 %collective-permute-start.5 = (bf16[3,16,512]{2,1,0:T(8,128)(2,1)S(1)}, bf16[3,16,512]{2,1,0:T(8,128)(2,1)S(1)}, u32[]{:S(2)}, u32[]{:S(2)}) collective-permute-start(bf16[3,16,512]{2,1,0:T(8,128)(2,1)S(1)} %get-tuple-element.32), channel_id=1, source_target_pairs={{0,32},{1,33},{2,34},{3,35},{4,36},{5,37},{6,38},{7,39},{8,40},{9,... | collective-permute-start | bytes 147464 | tf_op jit(solution)/shard_map/ppermute | solution.py:335
  94.9 10.3 %collective-permute-start.6 = (bf16[3,16,512]{2,1,0:T(8,128)(2,1)S(1)}, bf16[3,16,512]{2,1,0:T(8,128)(2,1)S(1)}, u32[]{:S(2)}, u32[]{:S(2)}) collective-permute-start(bf16[3,16,512]{2,1,0:T(8,128)(2,1)S(1)} %get-tuple-element.33), channel_id=1, source_target_pairs={{0,33},{1,34},{2,35},{3,36},{4,37},{5,38},{6,39},{7,40},{8,41},{9,... | collective-permute-start | bytes 147464 | tf_op jit(solution)/shard_map/ppermute | solution.py:335

commit v3 on v2

--- a/solution.py
+++ b/solution.py
@@ -14,14 +14,14 @@
 EPSILON = 1e-05
 MASKED = -1e30
 SCORE_SCALE = 0.125
-VMEM_LIMIT = 16 * 1024 * 1024
+VMEM_LIMIT = 8 * 1024 * 1024
 
 LEVEL_ROWS = 96
 ROWS = 192
 PACKED_ROWS = 144
 
 
-def call(kernel, out_shape, scratch=(), places=(), out_places=()):
+def call(kernel, out_shape, scratch=(), places=(), out_places=(), cost=None):
     def run(*args):
         places_of = dict(places)
         specs = [
@@ -39,6 +39,7 @@
             in_specs=specs,
             out_specs=outs,
             scratch_shapes=list(scratch),
+            cost_estimate=cost,
             compiler_params=pltpu.CompilerParams(vmem_limit_bytes=VMEM_LIMIT),
         )(*args)
 
@@ -166,10 +167,18 @@
     return inv_std * (d_normed - mean_plain - normed * mean_normed)
 
 
+def normalised(x):
+    center = jnp.mean(x, axis=-1, keepdims=True)
+    moved = x - center
+    spread = jnp.mean(jnp.square(moved), axis=-1, keepdims=True)
+    inv_std = lax.rsqrt(spread + EPSILON)
+    return moved * inv_std, inv_std
+
+
 def first_kernel(
     own, lon, lat, cor, w_qkv, w_proj, gain, bias,
-    skip, inputs_out, cot, normed_out, inv_out, projected_out, att_out,
-    dqkv, packed, sems,
+    skip, packed, fields, projected_out, att_out,
+    dqkv,
 ):
     tiles_x, tiles_g = [], []
     labels = []
@@ -185,25 +194,14 @@
                 tiles_g.append(tile[8:])
     x = jnp.concatenate(tiles_x, axis=0)
     c = jnp.concatenate(tiles_g, axis=0)
-    center = jnp.mean(x, axis=-1, keepdims=True)
-    moved = x - center
-    spread = jnp.mean(jnp.square(moved), axis=-1, keepdims=True)
-    inv_std = lax.rsqrt(spread + EPSILON)
-    normed = moved * inv_std
+    normed, inv_std = normalised(x)
     scaled = normed * gain[...]
     packed[...] = pack_rows(scaled).astype(BF16)
-    copies = [
-        pltpu.make_async_copy(packed, inputs_out.at[p], sems.at[p])
-        for p in range(inputs_out.shape[0])
-    ]
-    for copy in copies:
-        copy.start()
     projected = dot(scaled.astype(BF16), w_qkv[...], ((1,), (1,)))
     c_low = c.astype(BF16)
     d_first_value = dot(c_low, w_proj[...])
-    cot[...] = c_low
-    normed_out[...] = normed
-    inv_out[...] = jnp.broadcast_to(inv_std, (ROWS, 128))
+    fields[0] = x.astype(BF16)
+    fields[1] = c_low
     projected_out[...] = projected.astype(BF16)
 
     lane_row = row_index((1, 128), 1) >> 4
@@ -227,36 +225,57 @@
         scores = scores * SCORE_SCALE + added[:, :, :LEVEL_ROWS]
         weights = jnp.exp(scores - jnp.max(scores, axis=1, keepdims=True))
         probs = weights * (1.0 / jnp.sum(weights, axis=1, keepdims=True))
-        att_out[level, pair] = probs
+        att_out[level, pair] = probs.astype(BF16)
         return probs
 
     attention_backward(probabilities, d_first_value.astype(BF16), projected_out, dqkv)
     skip[...] = (c + input_gradient(dqkv, w_qkv, gain, normed, inv_std)).astype(BF16)
-    for copy in copies:
-        copy.wait()
 
 
 def second_kernel(
-    arrived, cot, projected, att, w_proj,
-    blocks, low, dqkv,
+    core, arrived, fields, projected, att, w_proj, w_qkv, gain,
+    kept, sent, own, lon, lat, cor, dqkv,
 ):
-    d_low = (dot(cot[...], w_proj[...]) + dot(arrived[...], w_proj[...])).astype(BF16)
-    attention_backward(lambda level, pair: att[level, pair], d_low, projected, dqkv)
-    low[...] = dqkv[...].astype(BF16)
-    lane = row_index((80, 128), 1)
+    d_low = (dot(fields[1], w_proj[...]) + dot(arrived[...], w_proj[...])).astype(BF16)
+    attention_backward(lambda level, pair: att[level, pair].astype(F32), d_low, projected, dqkv)
+    lane = row_index((PACKED_ROWS, 128), 1)
+    halves = []
     for t in range(4):
-        whole = [pack_rows(dqkv[:, 384 * t + 128 * j : 384 * t + 128 * (j + 1)]) for j in range(3)]
-        blocks[2 * t, :144, :] = whole[0].astype(BF16)
-        blocks[2 * t + 1, :144, :] = whole[2].astype(BF16)
-        top = whole[1][:80]
-        bottom = jnp.concatenate([whole[1][80:], jnp.zeros((16, 128), F32)], axis=0)
-        blocks[2 * t, 144:, :] = jnp.where(lane < 64, top, pltpu.roll(bottom, 64, 1)).astype(BF16)
-        blocks[2 * t + 1, 144:, :] = jnp.where(lane < 64, pltpu.roll(top, 64, 1), bottom).astype(BF16)
-
-
-def third_kernel(arrived, cot, low, normed, inv, w_qkv, gain, own, lon, lat, cor):
-    shifted = input_gradient(low, w_qkv, gain, normed[...], inv[:, 0:1])
-    total = cot[...].astype(F32) + (arrived[...].astype(F32) + shifted)
+        first, middle, last = (
+            pack_rows(dqkv[:, 384 * t + 128 * j : 384 * t + 128 * (j + 1)]) for j in range(3)
+        )
+        halves.append(middle)
+        cols = slice(128 * t, 128 * (t + 1))
+
+        @pl.when(core[0] == 0)
+        def _():
+            kept[:, cols] = first.astype(BF16)
+            sent[:, cols] = last.astype(BF16)
+
+        @pl.when(core[0] == 1)
+        def _():
+            kept[:, cols] = last.astype(BF16)
+            sent[:, cols] = first.astype(BF16)
+
+    for t in range(2):
+        left, right = halves[2 * t], halves[2 * t + 1]
+        first = jnp.where(lane < 64, left, pltpu.roll(right, 64, 1)).astype(BF16)
+        last = jnp.where(lane < 64, pltpu.roll(left, 64, 1), right).astype(BF16)
+        cols = slice(512 + 128 * t, 512 + 128 * (t + 1))
+
+        @pl.when(core[0] == 0)
+        def _():
+            kept[:, cols] = first
+            sent[:, cols] = last
+
+        @pl.when(core[0] == 1)
+        def _():
+            kept[:, cols] = last
+            sent[:, cols] = first
+
+    normed, inv_std = normalised(fields[0].astype(F32))
+    shifted = input_gradient(dqkv, w_qkv, gain, normed, inv_std)
+    total = fields[1].astype(F32) + (arrived[...].astype(F32) + shifted)
     for i in range(6):
         for half in range(2):
             start = 16 * i + 8 * half
@@ -267,28 +286,31 @@
             target[i % 3] = both.astype(BF16)
 
 
-def product_kernel(blocks, inputs, out):
-    whole = jnp.zeros((128, FEATURES), F32)
-    upper = jnp.zeros((128, FEATURES), F32)
-    lower = jnp.zeros((128, FEATURES), F32)
-    for p in range(blocks.shape[0]):
-        cells = inputs[p]
-        whole += dot(blocks[p, :144], cells, ((0,), (0,)))
-        folded = blocks[p, 144:]
-        upper += dot(folded, cells[:80], ((0,), (0,)))
-        lower += dot(folded[:64], cells[80:], ((0,), (0,)))
-    half = upper[:64] + lower[64:]
-    whole_t = whole.T
-    half_t = jnp.concatenate([half, jnp.zeros((64, FEATURES), F32)], axis=0).T
-    bands = out.shape[0]
+def product_kernel(kept, got, inputs, other_inputs, out):
+    product = dot(inputs[...], kept[...], ((0,), (0,)))
+    product = product + dot(other_inputs[...], got[...], ((0,), (0,)))
+    bands = out.shape[1]
     width = FEATURES // bands
-    lane = row_index((width // 2, 128), 1)
-    for band in range(bands):
-        out[band, :width, :] = whole_t[band * width : (band + 1) * width].astype(BF16)
-        part = half_t[band * width : (band + 1) * width]
-        out[band, width:, :] = jnp.where(
-            lane < 64, part[: width // 2], pltpu.roll(part[width // 2 :], 64, 1)
-        ).astype(BF16)
+    lane = row_index((bands, width // 2, 128), 2)
+    for t in range(4):
+        whole = product[:, 128 * t : 128 * (t + 1)].reshape(bands, width, 128)
+        out[t, :, :width, :] = whole.astype(BF16)
+        start = 512 + 128 * (t // 2)
+        half = product[:, start : start + 128].reshape(bands, width, 128)
+        top, bottom = half[:, : width // 2], half[:, width // 2 :]
+        if t % 2 == 0:
+            folded = jnp.where(lane < 64, top, pltpu.roll(bottom, 64, 2))
+        else:
+            folded = jnp.where(lane < 64, pltpu.roll(top, 64, 2), bottom)
+        out[t, :, width:, :] = folded.astype(BF16)
+
+
+def chips_kernel(products, own, lon, lat, cor, out, joined):
+    total = products[0].astype(F32)
+    for t in range(1, products.shape[0]):
+        total = total + products[t].astype(F32)
+    out[...] = total.astype(BF16)
+    join(own, lon, lat, cor, joined)
 
 
 def sum_kernel(odd, parts, out):
@@ -313,7 +335,7 @@
         out[0, :, 64:] = whole
 
 
-def join_kernel(own, lon, lat, cor, out):
+def join(own, lon, lat, cor, out):
     row = row_index((8, FEATURES), 0)
     for level in range(2):
         part = slice(level * 8, level * 8 + 8)
@@ -333,6 +355,10 @@
         for o in range(lons)
     ]
     return lax.ppermute(array, ("lat", "lon"), pairs)
+
+
+def other_core(array):
+    return lax.ppermute(array, "lat", [(a, a ^ 1) for a in range(lax.axis_size("lat"))])
 
 
 def per_device(x_in, out_grad, w_qkv, w_proj, norm_gain, bias_table, lat_labels):
@@ -349,50 +375,55 @@
     lat = passed(lat, -1, 0)
     cor = passed(cor, -1, -1)
     table = jnp.pad(bias_table[0, :, 253:506], ((0, 0), (0, 3)))
-    bias = call(bias_kernel, struct((HEADS * LEVEL_ROWS, 128), F32))(table)
+    bias = call(
+        bias_kernel,
+        struct((HEADS * LEVEL_ROWS, 128), F32),
+        cost=pl.CostEstimate(flops=4_000_000_000, bytes_accessed=20_000_000, transcendentals=0),
+    )(table)
 
     window = struct((ROWS, FEATURES), BF16)
     scratch = [pltpu.VMEM((ROWS, 3 * FEATURES), F32)]
-    skip, inputs, cot, normed, inv, projected, att = call(
+    skip, packed, fields, projected, att = call(
         first_kernel,
         (
             window,
-            struct((lats, PACKED_ROWS, FEATURES), BF16),
-            window,
-            struct((ROWS, FEATURES), F32),
-            struct((ROWS, 128), F32),
+            struct((PACKED_ROWS, FEATURES), BF16),
+            struct((2, ROWS, FEATURES), BF16),
             struct((ROWS, 3 * FEATURES), BF16),
-            struct((2, 4, 2, LEVEL_ROWS, LEVEL_ROWS), F32),
+            struct((2, 4, 2, LEVEL_ROWS, LEVEL_ROWS), BF16),
         ),
-        scratch
-        + [pltpu.VMEM((PACKED_ROWS, FEATURES), BF16), pltpu.SemaphoreType.DMA((lats,))],
-        out_places={1: pl.ANY},
+        scratch,
     )(own, lon, lat, cor, w_qkv, w_proj, norm_gain, bias)
 
+    core = (lax.axis_index("lat") % 2).astype(jnp.int32).reshape(1)
     arrived = lax.ppermute(skip, "phase", [(1, 0)])
-    inputs = lax.all_to_all(inputs, "lat", 0, 0, tiled=True)
+    other_packed = other_core(packed)
     back = struct((3, 16, FEATURES), BF16)
-    blocks, low = call(
+    half = struct((PACKED_ROWS, 768), BF16)
+    kept, sent, own, lon, lat, cor = call(
         second_kernel,
-        (struct((8, 224, 128), BF16), struct((ROWS, 3 * FEATURES), BF16)),
+        (half, half, back, back, back, back),
         scratch,
-    )(arrived, cot, projected, att, w_proj)
-    blocks = lax.all_to_all(blocks, "lat", 0, 0, tiled=True)
-    own, lon, lat, cor = call(third_kernel, (back,) * 4)(
-        arrived, cot, low, normed, inv, w_qkv, norm_gain
-    )
+        places={0: pltpu.SMEM},
+    )(core, arrived, fields, projected, att, w_proj, w_qkv, norm_gain)
+    got = other_core(sent)
     lon = passed(lon, 0, 1)
     lat = passed(lat, 1, 0)
     cor = passed(cor, 1, 1)
-    slices = call(product_kernel, struct((lons, FEATURES * 3 // 2 // lons, 128), BF16))(
-        blocks, inputs
+    rows = FEATURES * 3 // 2 // lons
+    products = call(product_kernel, struct((lats // 2, lons, rows, 128), BF16))(
+        kept, got, packed, other_packed
     )
+    chips = [[2 * x + c for x in range(lats // 2)] for c in range(2)]
+    products = lax.all_to_all(products, "lat", 0, 0, tiled=True, axis_index_groups=chips)
+    slices, grad_input = call(
+        chips_kernel,
+        (struct((lons, rows, 128), BF16), struct((1, 2, 6, 12, FEATURES), BF16)),
+    )(products, own, lon, lat, cor)
     slices = lax.all_to_all(slices, "lon", 0, 0, tiled=True)
-    odd = (lax.axis_index("lat") % 2).astype(jnp.int32).reshape(1)
     grad_qkv = call(
         sum_kernel, struct((1, FEATURES // lons, 192), F32), places={0: pltpu.SMEM}
-    )(odd, slices)
-    grad_input = call(join_kernel, struct((1, 2, 6, 12, FEATURES), BF16))(own, lon, lat, cor)
+    )(core, slices)
     return grad_input, grad_qkv.transpose(0, 2, 1)
 
 

time: 107 us -> 94.8 us (0.89)
  the two profiles are of different devices: /device:TPU:1 before, /device:TPU:64 now
where the time goes in v3:
time: 94.8 us; the launch traced here: 94.2 us
  starting transfers between devices  43.5 us (46%)
  waiting for transfers between devices  30.9 us (33%)
  Pallas kernels  12.2 us (13%)
  local copies, waits for them, and re-layouts  6.74 us (7%)
    ppermute x6, starting transfers between devices, passed(): return lax.ppermute(array, ('lat', 'lon'), pairs)  22.7 us
    pallas_call x7, Pallas kernels, run(): pl.pallas_call(kernel, out_shape=out_shape, in_specs=specs, out_specs=out...  12.2 us
    all_to_all x1, starting transfers between devices, per_device(): slices = lax.all_to_all(slices, 'lon', 0, 0, tiled=True)  11.6 us
    all_to_all x1, waiting for transfers between devices, per_device(): slices = lax.all_to_all(slices, 'lon', 0, 0, tiled=True)  11.4 us
    ppermute x6, waiting for transfers between devices, passed(): return lax.ppermute(array, ('lat', 'lon'), pairs)  9.05 us
    ppermute x1, waiting for transfers between devices, per_device(): arrived = lax.ppermute(skip, 'phase', [(1, 0)])  7.42 us
    unnamed x27, local copies, waits for them, and re-layouts  5.95 us
    ppermute x2, starting transfers between devices, other_core(): lax.ppermute(array, 'lat', [(a, a ^ 1) for a in range(lax.axis_size('lat'...  4.45 us
  transfers between devices with their start and end apart: 11, of which 7 were waited for; matrix products, arithmetic and copies ran while one was open for 2% of the time, Pallas kernels for 1%

profile of v3, /device:TPU:64, one launch (start us, length us, event | category | flops | bytes accessed | tf_op | source)
XLA Modules:
  0.0 94.2 jit_solution(17594923803330243498)
XLA Ops:
  0.6 0.9 copy.9.x_ref
  1.6 0.9 copy.10.g_ref
  2.5 0.0 copy-start.5
  2.5 0.6 copy-done.5
  3.2 0.7 shard_map.86
  3.9 6.9 %collective-permute-start = (bf16[2,3,16,512]{3,2,1,0:T(8,128)(2,1)S(1)}, bf16[2,3,16,512]{3,2,1,0:T(8,128)(2,1)S(1)}, u32[]{:S(2)}, u32[]{:S(2)}) collective-permute-start(bf16[2,3,16,512]{3,2,1,0:T(8,128)(2,1)S(1)} %get-tuple-element.20), channel_id=1, source_target_pairs={{0,31},{1,0},{2,1},{3,2},{4,3},{5,4},{6,5},{7,6},{8,7},{9,8},{10,9... | collective-permute-start | bytes 294920 | tf_op jit(solution)/shard_map/ppermute | solution.py:357
  10.8 0.0 collective-permute-start.1
  10.8 11.5 %collective-permute-start.2 = (bf16[2,3,16,512]{3,2,1,0:T(8,128)(2,1)S(1)}, bf16[2,3,16,512]{3,2,1,0:T(8,128)(2,1)S(1)}, u32[]{:S(2)}, u32[]{:S(2)}) collective-permute-start(bf16[2,3,16,512]{3,2,1,0:T(8,128)(2,1)S(1)} %get-tuple-element.22), channel_id=1, source_target_pairs={{0,255},{1,224},{2,225},{3,226},{4,227},{5,228},{6,229},{7,230},{8... | collective-permute-start | bytes 294920 | tf_op jit(solution)/shard_map/ppermute | solution.py:357
  22.4 0.8 slice_bitcast_fusion
  23.2 0.0 copy-start.4
  23.2 0.5 shard_map.87.bias
  23.7 0.0 collective-permute-done.lon
  23.7 0.0 collective-permute-done.1.lat
  23.7 0.9 collective-permute-done.2.cor
  24.6 0.0 copy-done
  24.6 0.1 copy-done.1
  24.7 0.0 copy-done.4
  24.7 4.1 %shard_map.88 = (bf16[192,512]{1,0:T(8,128)(2,1)}, bf16[144,512]{1,0:T(8,128)(2,1)S(1)}, bf16[2,192,512]{2,1,0:T(8,128)(2,1)S(1)}, bf16[192,1536]{1,0:T(8,128)(2,1)S(1)}, bf16[2,4,2,96,96]{4,3,2,1,0:T(8,128)(2,1)S(1)}) custom-call(bf16[2,3,16,512]{3,2,1,0:T(8,128)(2,1)S(1)} %get-tuple-element.19.own, bf16[2,3,16,512]{3,2,1,0:T(8,128)(2,1)S(1)} %collective-permute-done.lon, ...), custom_call_target="tpu_custom_call" | custom-call | tf_op jit(solution)/shard_map/pallas_call | solution.py:36
  28.8 0.7 copy-done.2
  29.5 1.3 %collective-permute-start.3 = (bf16[192,512]{1,0:T(8,128)(2,1)}, bf16[192,512]{1,0:T(8,128)(2,1)}, u32[]{:S(2)}, u32[]{:S(2)}) collective-permute-start(bf16[192,512]{1,0:T(8,128)(2,1)} %get-tuple-element.23), channel_id=1, source_target_pairs={{256,0},{257,1},{258,2},{259,3},{260,4},{261,5},{262,6},{263,7},{2... | collective-permute-start | bytes 589832 | tf_op jit(solution)/shard_map/ppermute | solution.py:399
  30.8 7.4 %collective-permute-done.3.arrived = bf16[192,512]{1,0:T(8,128)(2,1)} collective-permute-done((bf16[192,512]{1,0:T(8,128)(2,1)}, bf16[192,512]{1,0:T(8,128)(2,1)}, u32[]{:S(2)}, u32[]{:S(2)}) %collective-permute-start.3) | collective-permute-done | bytes 196640 | tf_op jit(solution)/shard_map/ppermute | solution.py:399
  38.2 3.8 %shard_map.89 = (bf16[144,768]{1,0:T(8,128)(2,1)S(1)}, bf16[144,768]{1,0:T(8,128)(2,1)S(1)}, bf16[3,16,512]{2,1,0:T(8,128)(2,1)S(1)}, bf16[3,16,512]{2,1,0:T(8,1...) custom-call(s32[1]{0:T(128)} %bitcast.core.odd, ...), custom_call_target="tpu_custom_call" | custom-call | tf_op jit(solution)/shard_map/pallas_call | solution.py:36
  42.0 0.0 copy-start.6
  42.1 0.6 copy-done.6
  42.7 0.6 copy-done.8
  43.3 0.6 copy-done.10
  43.9 2.0 %collective-permute-start.4 = (bf16[144,768]{1,0:T(8,128)(2,1)S(1)}, bf16[144,768]{1,0:T(8,128)(2,1)S(1)}, u32[]{:S(2)}, u32[]{:S(2)}) collective-permute-start(bf16[144,768]{1,0:T(8,128)(2,1)S(1)} %get-tuple-element.28), channel_id=1, source_target_pairs={{0,32},{32,0},{64,96},{96,64},{128,160},{160,128},{192,224},{224,1... | collective-permute-start | bytes 663560 | tf_op jit(solution)/shard_map/ppermute | solution.py:361
  45.9 0.0 copy-done.3
  45.9 2.4 %collective-permute-start.5 = (bf16[144,512]{1,0:T(8,128)(2,1)S(1)}, bf16[144,512]{1,0:T(8,128)(2,1)S(1)}, u32[]{:S(2)}, u32[]{:S(2)}) collective-permute-start(bf16[144,512]{1,0:T(8,128)(2,1)S(1)} %copy-done.3), channel_id=1, source_target_pairs={{0,32},{32,0},{64,96},{96,64},{128,160},{160,128},{192,224},{224,1... | collective-permute-start | bytes 442376 | tf_op jit(solution)/shard_map/ppermute | solution.py:361
  48.4 1.0 %collective-permute-done.5.other_inputs = bf16[144,512]{1,0:T(8,128)(2,1)S(1)} collective-permute-done((bf16[144,512]{1,0:T(8,128)(2,1)S(1)}, bf16[144,512]{1,0:T(8,128)(2,1)S(1)}, u32[]{:S(2)}, u32[]{:S(2)}) %collective-permute-start.5) | collective-permute-done | bytes 147488 | tf_op jit(solution)/shard_map/ppermute | solution.py:361
  49.3 0.0 collective-permute-done.4.got
  49.3 1.6 %shard_map.90 = bf16[4,32,24,128]{3,2,1,0:T(8,128)(2,1)} custom-call(bf16[144,768]{1,0:T(8,128)(2,1)S(1)} %get-tuple-element.27.kept, bf16[144,768]{1,0:T(8,128)(2,1)S(1)} %collective-permute-done.4.got, bf16[144,512]{1,0:T(8,128)(2,1)S(1)} %copy-done.3, bf16[144,512]{1,0:T(8,128)(2,1)S(1)} %collective-permute-done.5.other_inputs), custom_call_target="tpu_custom_call" | custom-call | tf_op jit(solution)/shard_map/pallas_call | solution.py:36
  50.9 3.5 %all-to-all-start = ((bf16[4,32,24,128]{3,2,1,0:T(8,128)(2,1)}), bf16[4,32,24,128]{3,2,1,0:T(8,128)(2,1)S(1)}, u32[]{:S(2)}, u32[]{:S(2)}) async-start(bf16[4,32,24,128]{3,2,1,0:T(8,128)(2,1)} %shard_map.90), calls=%async_computation | async-start | bytes 1572864 | tf_op jit(solution)/shard_map/all_to_all | solution.py:418
  54.4 0.0 copy-done.11
  54.4 1.9 %collective-permute-start.6 = (bf16[3,16,512]{2,1,0:T(8,128)(2,1)S(1)}, bf16[3,16,512]{2,1,0:T(8,128)(2,1)S(1)}, u32[]{:S(2)}, u32[]{:S(2)}) collective-permute-start(bf16[3,16,512]{2,1,0:T(8,128)(2,1)S(1)} %copy-done.11), channel_id=1, source_target_pairs={{0,1},{1,2},{2,3},{3,4},{4,5},{5,6},{6,7},{7,8},{8,9},{9,10},{10,1... | collective-permute-start | bytes 147464 | tf_op jit(solution)/shard_map/ppermute | solution.py:357
  56.4 0.0 copy-done.9
  56.4 0.4 collective-permute-start.7
  56.8 0.0 copy-done.7
  56.8 1.9 %collective-permute-start.8 = (bf16[3,16,512]{2,1,0:T(8,128)(2,1)S(1)}, bf16[3,16,512]{2,1,0:T(8,128)(2,1)S(1)}, u32[]{:S(2)}, u32[]{:S(2)}) collective-permute-start(bf16[3,16,512]{2,1,0:T(8,128)(2,1)S(1)} %copy-done.7), channel_id=1, source_target_pairs={{0,33},{1,34},{2,35},{3,36},{4,37},{5,38},{6,39},{7,40},{8,41},{9,... | collective-permute-start | bytes 147464 | tf_op jit(solution)/shard_map/ppermute | solution.py:357
  58.7 2.7 %collective-permute-done.6.lon = bf16[3,16,512]{2,1,0:T(8,128)(2,1)S(1)} collective-permute-done((bf16[3,16,512]{2,1,0:T(8,128)(2,1)S(1)}, bf16[3,16,512]{2,1,0:T(8,128)(2,1)S(1)}, u32[]{:S(2)}, u32[]{:S(2)}) %collective-permute-start.6) | collective-permute-done | bytes 49184 | tf_op jit(solution)/shard_map/ppermute | solution.py:357
  61.3 5.5 %collective-permute-done.7.lat = bf16[3,16,512]{2,1,0:T(8,128)(2,1)S(1)} collective-permute-done((bf16[3,16,512]{2,1,0:T(8,128)(2,1)S(1)}, bf16[3,16,512]{2,1,0:T(8,128)(2,1)S(1)}, u32[]{:S(2)}, u32[]{:S(2)}) %collective-permute-start.7) | collective-permute-done | bytes 49184 | tf_op jit(solution)/shard_map/ppermute | solution.py:357
  66.8 0.0 collective-permute-done.8.cor
  66.8 2.0 %all-to-all-done.products = bf16[4,32,24,128]{3,2,1,0:T(8,128)(2,1)S(1)} async-done(((bf16[4,32,24,128]{3,2,1,0:T(8,128)(2,1)}), bf16[4,32,24,128]{3,2,1,0:T(8,128)(2,1)S(1)}, u32[]{:S(2)}, u32[]{:S(2)}) %all-to-all-start) | async-done | bytes 786464 | tf_op jit(solution)/shard_map/all_to_all | solution.py:418
  68.9 0.8 shard_map.91
  69.6 11.6 %all-to-all-start.1 = ((bf16[32,24,128]{2,1,0:T(8,128)(2,1)}), bf16[32,24,128]{2,1,0:T(8,128)(2,1)S(1)}, u32[]{:S(2)}, u32[]{:S(2)}) async-start(bf16[32,24,128]{2,1,0:T(8,128)(2,1)} %get-tuple-element.35), calls=%async_computation.1 | async-start | bytes 393216 | tf_op jit(solution)/shard_map/all_to_all | solution.py:423
  81.2 0.8 copy.11
  82.1 11.4 %all-to-all-done.1.parts = bf16[32,24,128]{2,1,0:T(8,128)(2,1)S(1)} async-done(((bf16[32,24,128]{2,1,0:T(8,128)(2,1)}), bf16[32,24,128]{2,1,0:T(8,128)(2,1)S(1)}, u32[]{:S(2)}, u32[]{:S(2)}) %all-to-all-start.1) | async-done | bytes 196640 | tf_op jit(solution)/shard_map/all_to_all | solution.py:423
  93.5 0.7 shard_map.92
  (10 shorter events, 0.0 us)
Async XLA Ops:
  2.5 0.7 copy-start.5
  3.9 19.8 %collective-permute-start = (bf16[2,3,16,512]{3,2,1,0:T(8,128)(2,1)S(1)}, bf16[2,3,16,512]{3,2,1,0:T(8,128)(2,1)S(1)}, u32[]{:S(2)}, u32[]{:S(2)}) collective-permute-start(bf16[2,3,16,512]{3,2,1,0:T(8,128)(2,1)S(1)} %get-tuple-element.20), channel_id=1, source_target_pairs={{0,31},{1,0},{2,1},{3,2},{4,3},{5,4},{6,5},{7,6},{8,7},{9,8},{10,9... | collective-permute-start | bytes 294920 | tf_op jit(solution)/shard_map/ppermute | solution.py:357
  10.8 12.9 %collective-permute-start.1 = (bf16[2,3,16,512]{3,2,1,0:T(8,128)(2,1)S(1)}, bf16[2,3,16,512]{3,2,1,0:T(8,128)(2,1)S(1)}, u32[]{:S(2)}, u32[]{:S(2)}) collective-permute-start(bf16[2,3,16,512]{3,2,1,0:T(8,128)(2,1)S(1)} %get-tuple-element.21), channel_id=1, source_target_pairs={{0,224},{1,225},{2,226},{3,227},{4,228},{5,229},{6,230},{7,231},{8... | collective-permute-start | bytes 294920 | tf_op jit(solution)/shard_map/ppermute | solution.py:357
  10.8 13.8 %collective-permute-start.2 = (bf16[2,3,16,512]{3,2,1,0:T(8,128)(2,1)S(1)}, bf16[2,3,16,512]{3,2,1,0:T(8,128)(2,1)S(1)}, u32[]{:S(2)}, u32[]{:S(2)}) collective-permute-start(bf16[2,3,16,512]{3,2,1,0:T(8,128)(2,1)S(1)} %get-tuple-element.22), channel_id=1, source_target_pairs={{0,255},{1,224},{2,225},{3,226},{4,227},{5,228},{6,229},{7,230},{8... | collective-permute-start | bytes 294920 | tf_op jit(solution)/shard_map/ppermute | solution.py:357
  23.2 1.4 %copy-start = (bf16[1,1536,512]{2,1,0:T(8,128)(2,1)S(1)}, bf16[1,1536,512]{2,1,0:T(8,128)(2,1)}, u32[]{:S(2)}) copy-start(bf16[1,1536,512]{2,1,0:T(8,128)(2,1)} %param.9) | copy-start | bytes 4718596
  23.2 1.5 %copy-start.1 = (bf16[1,512,512]{2,1,0:T(8,128)(2,1)S(1)}, bf16[1,512,512]{2,1,0:T(8,128)(2,1)}, u32[]{:S(2)}) copy-start(bf16[1,512,512]{2,1,0:T(8,128)(2,1)} %param.10) | copy-start | bytes 1572868
  23.2 1.5 %copy-start.4 = (f32[1,512]{1,0:T(1,128)S(1)}, f32[1,512]{1,0:T(1,128)}, u32[]{:S(2)}) copy-start(f32[1,512]{1,0:T(1,128)} %gain.3) | copy-start | bytes 6148
  28.8 0.7 copy-start.2
  29.5 8.7 %collective-permute-start.3 = (bf16[192,512]{1,0:T(8,128)(2,1)}, bf16[192,512]{1,0:T(8,128)(2,1)}, u32[]{:S(2)}, u32[]{:S(2)}) collective-permute-start(bf16[192,512]{1,0:T(8,128)(2,1)} %get-tuple-element.23), channel_id=1, source_target_pairs={{256,0},{257,1},{258,2},{259,3},{260,4},{261,5},{262,6},{263,7},{2... | collective-permute-start | bytes 589832 | tf_op jit(solution)/shard_map/ppermute | solution.py:399
  38.2 7.7 %copy-start.3 = (bf16[144,512]{1,0:T(8,128)(2,1)S(1)}, bf16[144,512]{1,0:T(8,128)(2,1)}, u32[]{:S(2)}) copy-start(bf16[144,512]{1,0:T(8,128)(2,1)} %copy-done.2) | copy-start | bytes 442372
  42.0 0.6 copy-start.6
  42.7 0.6 copy-start.8
  43.3 0.6 copy-start.10
  43.9 10.6 %copy-start.11 = (bf16[3,16,512]{2,1,0:T(8,128)(2,1)S(1)}, bf16[3,16,512]{2,1,0:T(8,128)(2,1)}, u32[]{:S(2)}) copy-start(bf16[3,16,512]{2,1,0:T(8,128)(2,1)} %copy-done.10) | copy-start | bytes 147460
  43.9 12.5 %copy-start.9 = (bf16[3,16,512]{2,1,0:T(8,128)(2,1)S(1)}, bf16[3,16,512]{2,1,0:T(8,128)(2,1)}, u32[]{:S(2)}) copy-start(bf16[3,16,512]{2,1,0:T(8,128)(2,1)} %copy-done.8) | copy-start | bytes 147460
  43.9 12.9 %copy-start.7 = (bf16[3,16,512]{2,1,0:T(8,128)(2,1)S(1)}, bf16[3,16,512]{2,1,0:T(8,128)(2,1)}, u32[]{:S(2)}) copy-start(bf16[3,16,512]{2,1,0:T(8,128)(2,1)} %copy-done.6) | copy-start | bytes 147460
  43.9 5.5 %collective-permute-start.4 = (bf16[144,768]{1,0:T(8,128)(2,1)S(1)}, bf16[144,768]{1,0:T(8,128)(2,1)S(1)}, u32[]{:S(2)}, u32[]{:S(2)}) collective-permute-start(bf16[144,768]{1,0:T(8,128)(2,1)S(1)} %get-tuple-element.28), channel_id=1, source_target_pairs={{0,32},{32,0},{64,96},{96,64},{128,160},{160,128},{192,224},{224,1... | collective-permute-start | bytes 663560 | tf_op jit(solution)/shard_map/ppermute | solution.py:361
  45.9 3.4 %collective-permute-start.5 = (bf16[144,512]{1,0:T(8,128)(2,1)S(1)}, bf16[144,512]{1,0:T(8,128)(2,1)S(1)}, u32[]{:S(2)}, u32[]{:S(2)}) collective-permute-start(bf16[144,512]{1,0:T(8,128)(2,1)S(1)} %copy-done.3), channel_id=1, source_target_pairs={{0,32},{32,0},{64,96},{96,64},{128,160},{160,128},{192,224},{224,1... | collective-permute-start | bytes 442376 | tf_op jit(solution)/shard_map/ppermute | solution.py:361
  50.9 17.9 %all-to-all-start = ((bf16[4,32,24,128]{3,2,1,0:T(8,128)(2,1)}), bf16[4,32,24,128]{3,2,1,0:T(8,128)(2,1)S(1)}, u32[]{:S(2)}, u32[]{:S(2)}) async-start(bf16[4,32,24,128]{3,2,1,0:T(8,128)(2,1)} %shard_map.90), calls=%async_computation | async-start | bytes 1572864 | tf_op jit(solution)/shard_map/all_to_all | solution.py:418
  54.4 6.9 %collective-permute-start.6 = (bf16[3,16,512]{2,1,0:T(8,128)(2,1)S(1)}, bf16[3,16,512]{2,1,0:T(8,128)(2,1)S(1)}, u32[]{:S(2)}, u32[]{:S(2)}) collective-permute-start(bf16[3,16,512]{2,1,0:T(8,128)(2,1)S(1)} %copy-done.11), channel_id=1, source_target_pairs={{0,1},{1,2},{2,3},{3,4},{4,5},{5,6},{6,7},{7,8},{8,9},{9,10},{10,1... | collective-permute-start | bytes 147464 | tf_op jit(solution)/shard_map/ppermute | solution.py:357
  56.4 10.5 %collective-permute-start.7 = (bf16[3,16,512]{2,1,0:T(8,128)(2,1)S(1)}, bf16[3,16,512]{2,1,0:T(8,128)(2,1)S(1)}, u32[]{:S(2)}, u32[]{:S(2)}) collective-permute-start(bf16[3,16,512]{2,1,0:T(8,128)(2,1)S(1)} %copy-done.9), channel_id=1, source_target_pairs={{0,32},{1,33},{2,34},{3,35},{4,36},{5,37},{6,38},{7,39},{8,40},{9,... | collective-permute-start | bytes 147464 | tf_op jit(solution)/shard_map/ppermute | solution.py:357
  56.8 10.1 %collective-permute-start.8 = (bf16[3,16,512]{2,1,0:T(8,128)(2,1)S(1)}, bf16[3,16,512]{2,1,0:T(8,128)(2,1)S(1)}, u32[]{:S(2)}, u32[]{:S(2)}) collective-permute-start(bf16[3,16,512]{2,1,0:T(8,128)(2,1)S(1)} %copy-done.7), channel_id=1, source_target_pairs={{0,33},{1,34},{2,35},{3,36},{4,37},{5,38},{6,39},{7,40},{8,41},{9,... | collective-permute-start | bytes 147464 | tf_op jit(solution)/shard_map/ppermute | solution.py:357
  69.6 23.8 %all-to-all-start.1 = ((bf16[32,24,128]{2,1,0:T(8,128)(2,1)}), bf16[32,24,128]{2,1,0:T(8,128)(2,1)S(1)}, u32[]{:S(2)}, u32[]{:S(2)}) async-start(bf16[32,24,128]{2,1,0:T(8,128)(2,1)} %get-tuple-element.35), calls=%async_computation.1 | async-start | bytes 393216 | tf_op jit(solution)/shard_map/all_to_all | solution.py:423

commit v4 on v3

--- a/solution.py
+++ b/solution.py
@@ -122,6 +122,21 @@
         last = groups[q, 3]
         for g in range(3):
             out.append(jnp.where(row < 6, groups[q, g], pltpu.roll(last, 6 - 2 * g, 0)))
+    return jnp.concatenate(out, axis=0)
+
+
+def unpack_rows(array):
+    columns = array.shape[1]
+    groups = array.reshape(6, 3, 8, columns)
+    row = row_index((8, columns), 0)
+    out = []
+    for q in range(6):
+        for g in range(3):
+            out.append(jnp.where(row < 6, groups[q, g], 0.0))
+        last = jnp.where(row < 2, pltpu.roll(groups[q, 0], 2, 0), 0.0)
+        last = jnp.where((row >= 2) & (row < 4), pltpu.roll(groups[q, 1], 4, 0), last)
+        last = jnp.where((row >= 4) & (row < 6), pltpu.roll(groups[q, 2], 6, 0), last)
+        out.append(last)
     return jnp.concatenate(out, axis=0)
 
 
@@ -229,66 +244,55 @@
         return probs
 
     attention_backward(probabilities, d_first_value.astype(BF16), projected_out, dqkv)
-    skip[...] = (c + input_gradient(dqkv, w_qkv, gain, normed, inv_std)).astype(BF16)
+    skip[...] = pack_rows(c + input_gradient(dqkv, w_qkv, gain, normed, inv_std)).astype(BF16)
 
 
 def second_kernel(
     core, arrived, fields, projected, att, w_proj, w_qkv, gain,
-    kept, sent, own, lon, lat, cor, dqkv,
+    kept, sent, near, far, dqkv,
 ):
-    d_low = (dot(fields[1], w_proj[...]) + dot(arrived[...], w_proj[...])).astype(BF16)
+    c2 = unpack_rows(arrived[...].astype(F32))
+    d_low = (dot(fields[1], w_proj[...]) + dot(c2.astype(BF16), w_proj[...])).astype(BF16)
     attention_backward(lambda level, pair: att[level, pair].astype(F32), d_low, projected, dqkv)
     lane = row_index((PACKED_ROWS, 128), 1)
+    is_first = core[0] == 0
     halves = []
+
+    def share(cols, first, last):
+        kept[:, cols] = jnp.where(is_first, first, last).astype(BF16)
+        sent[:, cols] = jnp.where(is_first, last, first).astype(BF16)
+
     for t in range(4):
         first, middle, last = (
             pack_rows(dqkv[:, 384 * t + 128 * j : 384 * t + 128 * (j + 1)]) for j in range(3)
         )
         halves.append(middle)
-        cols = slice(128 * t, 128 * (t + 1))
-
-        @pl.when(core[0] == 0)
-        def _():
-            kept[:, cols] = first.astype(BF16)
-            sent[:, cols] = last.astype(BF16)
-
-        @pl.when(core[0] == 1)
-        def _():
-            kept[:, cols] = last.astype(BF16)
-            sent[:, cols] = first.astype(BF16)
-
+        share(slice(128 * t, 128 * (t + 1)), first, last)
     for t in range(2):
         left, right = halves[2 * t], halves[2 * t + 1]
-        first = jnp.where(lane < 64, left, pltpu.roll(right, 64, 1)).astype(BF16)
-        last = jnp.where(lane < 64, pltpu.roll(left, 64, 1), right).astype(BF16)
-        cols = slice(512 + 128 * t, 512 + 128 * (t + 1))
-
-        @pl.when(core[0] == 0)
-        def _():
-            kept[:, cols] = first
-            sent[:, cols] = last
-
-        @pl.when(core[0] == 1)
-        def _():
-            kept[:, cols] = last
-            sent[:, cols] = first
+        first = jnp.where(lane < 64, left, pltpu.roll(right, 64, 1))
+        last = jnp.where(lane < 64, pltpu.roll(left, 64, 1), right)
+        share(slice(512 + 128 * t, 512 + 128 * (t + 1)), first, last)
 
     normed, inv_std = normalised(fields[0].astype(F32))
     shifted = input_gradient(dqkv, w_qkv, gain, normed, inv_std)
-    total = fields[1].astype(F32) + (arrived[...].astype(F32) + shifted)
+    total = fields[1].astype(F32) + (c2 + shifted)
     for i in range(6):
-        for half in range(2):
+        for half, target in ((0, near), (1, far)):
             start = 16 * i + 8 * half
             both = jnp.concatenate(
                 [total[start : start + 8], total[96 + start : 96 + start + 8]], axis=0
             )
-            target = ((own, lon), (lat, cor))[i // 3][half]
-            target[i % 3] = both.astype(BF16)
-
-
-def product_kernel(kept, got, inputs, other_inputs, out):
-    product = dot(inputs[...], kept[...], ((0,), (0,)))
-    product = product + dot(other_inputs[...], got[...], ((0,), (0,)))
+            target[i] = both.astype(BF16)
+
+
+def turn_kernel(inputs, other_inputs, out):
+    out[0] = inputs[...].astype(F32).T.astype(BF16)
+    out[1] = other_inputs[...].astype(F32).T.astype(BF16)
+
+
+def product_kernel(kept, got, inputs, out):
+    product = dot(inputs[0], kept[...]) + dot(inputs[1], got[...])
     bands = out.shape[1]
     width = FEATURES // bands
     lane = row_index((bands, width // 2, 128), 2)
@@ -305,12 +309,10 @@
         out[t, :, width:, :] = folded.astype(BF16)
 
 
-def chips_kernel(products, own, lon, lat, cor, out, joined):
-    total = products[0].astype(F32)
-    for t in range(1, products.shape[0]):
-        total = total + products[t].astype(F32)
-    out[...] = total.astype(BF16)
-    join(own, lon, lat, cor, joined)
+def upward_kernel(near, left, out):
+    for i in range(3):
+        out[0, i] = left[3 + i]
+        out[1, i] = near[3 + i]
 
 
 def sum_kernel(odd, parts, out):
@@ -335,16 +337,16 @@
         out[0, :, 64:] = whole
 
 
-def join(own, lon, lat, cor, out):
+def join_kernel(near, left, arrived, out):
     row = row_index((8, FEATURES), 0)
     for level in range(2):
         part = slice(level * 8, level * 8 + 8)
         for i in range(6):
-            left, right = (cor, lat) if i < 3 else (lon, own)
-            left = left[i % 3].astype(F32)[part]
-            right = pltpu.roll(right[i % 3].astype(F32)[part], 6, 0)
-            out[0, level, i, 0:8, :] = jnp.where(row < 6, left, right).astype(BF16)
-            out[0, level, i, 8:12, :] = right[:4].astype(BF16)
+            low, high = (arrived[0, i], arrived[1, i]) if i < 3 else (left[i - 3], near[i - 3])
+            low = low.astype(F32)[part]
+            high = pltpu.roll(high.astype(F32)[part], 6, 0)
+            out[0, level, i, 0:8, :] = jnp.where(row < 6, low, high).astype(BF16)
+            out[0, level, i, 8:12, :] = high[:4].astype(BF16)
 
 
 def passed(array, lat_by, lon_by):
@@ -381,12 +383,11 @@
         cost=pl.CostEstimate(flops=4_000_000_000, bytes_accessed=20_000_000, transcendentals=0),
     )(table)
 
-    window = struct((ROWS, FEATURES), BF16)
     scratch = [pltpu.VMEM((ROWS, 3 * FEATURES), F32)]
     skip, packed, fields, projected, att = call(
         first_kernel,
         (
-            window,
+            struct((PACKED_ROWS, FEATURES), BF16),
             struct((PACKED_ROWS, FEATURES), BF16),
             struct((2, ROWS, FEATURES), BF16),
             struct((ROWS, 3 * FEATURES), BF16),
@@ -397,30 +398,38 @@
 
     core = (lax.axis_index("lat") % 2).astype(jnp.int32).reshape(1)
     arrived = lax.ppermute(skip, "phase", [(1, 0)])
-    other_packed = other_core(packed)
-    back = struct((3, 16, FEATURES), BF16)
+    turned = call(turn_kernel, struct((2, FEATURES, PACKED_ROWS), BF16))(
+        packed, other_core(packed)
+    )
+    arrived, turned = lax.optimization_barrier((arrived, turned))
+    back = struct((6, 16, FEATURES), BF16)
     half = struct((PACKED_ROWS, 768), BF16)
-    kept, sent, own, lon, lat, cor = call(
+    kept, sent, near, far = call(
         second_kernel,
-        (half, half, back, back, back, back),
+        (half, half, back, back),
         scratch,
         places={0: pltpu.SMEM},
     )(core, arrived, fields, projected, att, w_proj, w_qkv, norm_gain)
     got = other_core(sent)
-    lon = passed(lon, 0, 1)
-    lat = passed(lat, 1, 0)
-    cor = passed(cor, 1, 1)
+    left = passed(far, 0, 1)
     rows = FEATURES * 3 // 2 // lons
     products = call(product_kernel, struct((lats // 2, lons, rows, 128), BF16))(
-        kept, got, packed, other_packed
-    )
-    chips = [[2 * x + c for x in range(lats // 2)] for c in range(2)]
-    products = lax.all_to_all(products, "lat", 0, 0, tiled=True, axis_index_groups=chips)
-    slices, grad_input = call(
-        chips_kernel,
-        (struct((lons, rows, 128), BF16), struct((1, 2, 6, 12, FEATURES), BF16)),
-    )(products, own, lon, lat, cor)
-    slices = lax.all_to_all(slices, "lon", 0, 0, tiled=True)
+        kept, got, turned
+    )
+    upward = call(upward_kernel, struct((2, 3, 16, FEATURES), BF16))(near, left)
+    above = passed(upward, 1, 0)
+    grad_input = call(join_kernel, struct((1, 2, 6, 12, FEATURES), BF16))(near, left, above)
+    same_core = [
+        [(2 * x + c) * lons + o for x in range(lats // 2) for o in range(lons)] for c in range(2)
+    ]
+    slices = lax.all_to_all(
+        products.reshape(lats // 2 * lons, rows, 128),
+        ("lat", "lon"),
+        0,
+        0,
+        tiled=True,
+        axis_index_groups=same_core,
+    )
     grad_qkv = call(
         sum_kernel, struct((1, FEATURES // lons, 192), F32), places={0: pltpu.SMEM}
     )(core, slices)

time: 94.8 us -> 97.2 us (1.025)
  the two profiles are of different devices: /device:TPU:64 before, /device:TPU:6 now
where the time goes in v4:
time: 97.2 us; the launch traced here: 96.7 us
  waiting for transfers between devices  40.1 us (41%)
  starting transfers between devices  39.5 us (41%)
  Pallas kernels  12.1 us (12%)
  local copies, waits for them, and re-layouts  4.16 us (4%)
    ppermute x5, waiting for transfers between devices, passed(): return lax.ppermute(array, ('lat', 'lon'), pairs)  33 us
    ppermute x5, starting transfers between devices, passed(): return lax.ppermute(array, ('lat', 'lon'), pairs)  20.9 us
    all_to_all x1, starting transfers between devices, per_device(): lax.all_to_all(products.reshape(lats // 2 * lons, rows, 128), ('lat', 'lo...  13.2 us
    pallas_call x9, Pallas kernels, run(): pl.pallas_call(kernel, out_shape=out_shape, in_specs=specs, out_specs=out...  12.1 us
    ppermute x1, waiting for transfers between devices, per_device(): arrived = lax.ppermute(skip, 'phase', [(1, 0)])  5.59 us
    ppermute x2, starting transfers between devices, other_core(): lax.ppermute(array, 'lat', [(a, a ^ 1) for a in range(lax.axis_size('lat'...  4.08 us
    unnamed x19, local copies, waits for them, and re-layouts  3.37 us
  transfers between devices with their start and end apart: 9, of which 7 were waited for; matrix products, arithmetic and copies ran while one was open for 2% of the time, Pallas kernels for 2%

profile of v4, /device:TPU:6, one launch (start us, length us, event | category | flops | bytes accessed | tf_op | source)
XLA Modules:
  0.0 96.7 jit_solution(2807837128268704060)
XLA Ops:
  0.6 0.9 copy.9.x_ref
  1.6 0.9 copy.10.g_ref
  2.5 0.0 copy-start.5
  2.5 0.6 copy-done.5
  3.2 0.7 shard_map.86
  3.9 14.6 %collective-permute-start = (bf16[2,3,16,512]{3,2,1,0:T(8,128)(2,1)S(1)}, bf16[2,3,16,512]{3,2,1,0:T(8,128)(2,1)S(1)}, u32[]{:S(2)}, u32[]{:S(2)}) collective-permute-start(bf16[2,3,16,512]{3,2,1,0:T(8,128)(2,1)S(1)} %get-tuple-element.18), channel_id=1, source_target_pairs={{0,31},{1,0},{2,1},{3,2},{4,3},{5,4},{6,5},{7,6},{8,7},{9,8},{10,9... | collective-permute-start | bytes 294920 | tf_op jit(solution)/shard_map/ppermute | solution.py:359
  18.5 0.0 collective-permute-start.1
  18.5 2.8 %collective-permute-start.2 = (bf16[2,3,16,512]{3,2,1,0:T(8,128)(2,1)S(1)}, bf16[2,3,16,512]{3,2,1,0:T(8,128)(2,1)S(1)}, u32[]{:S(2)}, u32[]{:S(2)}) collective-permute-start(bf16[2,3,16,512]{3,2,1,0:T(8,128)(2,1)S(1)} %get-tuple-element.20), channel_id=1, source_target_pairs={{0,255},{1,224},{2,225},{3,226},{4,227},{5,228},{6,229},{7,230},{8... | collective-permute-start | bytes 294920 | tf_op jit(solution)/shard_map/ppermute | solution.py:359
  21.4 0.8 slice_bitcast_fusion
  22.1 0.0 copy-start
  22.1 0.0 copy-start.1
  22.1 0.0 copy-start.4
  22.2 0.5 shard_map.87.bias
  22.6 1.3 %collective-permute-done.lon = bf16[2,3,16,512]{3,2,1,0:T(8,128)(2,1)S(1)} collective-permute-done((bf16[2,3,16,512]{3,2,1,0:T(8,128)(2,1)S(1)}, bf16[2,3,16,512]{3,2,1,0:T(8,128)(2,1)S(1)}, u32[]{:S(2)}, u32[]{:S(2)}) %collective-permute-start) | collective-permute-done | bytes 98336 | tf_op jit(solution)/shard_map/ppermute | solution.py:359
  24.0 0.0 collective-permute-done.1.lat
  24.0 2.9 %collective-permute-done.2.cor = bf16[2,3,16,512]{3,2,1,0:T(8,128)(2,1)S(1)} collective-permute-done((bf16[2,3,16,512]{3,2,1,0:T(8,128)(2,1)S(1)}, bf16[2,3,16,512]{3,2,1,0:T(8,128)(2,1)S(1)}, u32[]{:S(2)}, u32[]{:S(2)}) %collective-permute-start.2) | collective-permute-done | bytes 98336 | tf_op jit(solution)/shard_map/ppermute | solution.py:359
  26.9 0.0 copy-done
  26.9 0.0 copy-done.1
  26.9 0.0 copy-done.4
  26.9 4.1 %shard_map.88 = (bf16[144,512]{1,0:T(8,128)(2,1)}, bf16[144,512]{1,0:T(8,128)(2,1)}, bf16[2,192,512]{2,1,0:T(8,128)(2,1)S(1)}, bf16[192,1536]{1,0:T(8,128)(2,1)S(1)}, bf16[2,4,2,96,96]{4,3,2,1,0:T(8,128)(2,1)S(1)}) custom-call(bf16[2,3,16,512]{3,2,1,0:T(8,128)(2,1)S(1)} %get-tuple-element.17.own, bf16[2,3,16,512]{3,2,1,0:T(8,128)(2,1)S(1)} %collective-permute-done.lon, ...), custom_call_target="tpu_custom_call" | custom-call | tf_op jit(solution)/shard_map/pallas_call | solution.py:36
  31.0 2.2 %collective-permute-start.4 = (bf16[144,512]{1,0:T(8,128)(2,1)}, bf16[144,512]{1,0:T(8,128)(2,1)}, u32[]{:S(2)}, u32[]{:S(2)}) collective-permute-start(bf16[144,512]{1,0:T(8,128)(2,1)} %get-tuple-element.22.inputs), channel_id=1, source_target_pairs={{0,32},{32,0},{64,96},{96,64},{128,160},{160,128},{192,224},{224,1... | collective-permute-start | bytes 442376 | tf_op jit(solution)/shard_map/ppermute | solution.py:363
  33.2 1.3 %collective-permute-start.3 = (bf16[144,512]{1,0:T(8,128)(2,1)}, bf16[144,512]{1,0:T(8,128)(2,1)}, u32[]{:S(2)}, u32[]{:S(2)}) collective-permute-start(bf16[144,512]{1,0:T(8,128)(2,1)} %get-tuple-element.21), channel_id=1, source_target_pairs={{256,0},{257,1},{258,2},{259,3},{260,4},{261,5},{262,6},{263,7},{2... | collective-permute-start | bytes 442376 | tf_op jit(solution)/shard_map/ppermute | solution.py:400
  34.5 0.1 collective-permute-done.4.other_inputs
  34.6 1.2 %shard_map.89.inputs = bf16[2,512,144]{2,1,0:T(8,128)(2,1)S(1)} custom-call(bf16[144,512]{1,0:T(8,128)(2,1)} %get-tuple-element.22.inputs, bf16[144,512]{1,0:T(8,128)(2,1)} %collective-permute-done.4.other_inputs), custom_call_target="tpu_custom_call" | custom-call | tf_op jit(solution)/shard_map/pallas_call | solution.py:36
  35.8 5.6 %collective-permute-done.3.arrived = bf16[144,512]{1,0:T(8,128)(2,1)} collective-permute-done((bf16[144,512]{1,0:T(8,128)(2,1)}, bf16[144,512]{1,0:T(8,128)(2,1)}, u32[]{:S(2)}, u32[]{:S(2)}) %collective-permute-start.3) | collective-permute-done | bytes 147488 | tf_op jit(solution)/shard_map/ppermute | solution.py:400
  41.4 3.3 %shard_map.90 = (bf16[144,768]{1,0:T(8,128)(2,1)S(1)}, bf16[144,768]{1,0:T(8,128)(2,1)S(1)}, bf16[6,16,512]{2,1,0:T(8,128)(2,1)S(1)}, bf16[6,16,512]{2,1,0:T(8,128)(2,1)S(1)}) custom-call(s32[1]{0:T(128)} %bitcast.core.odd, bf16[144,512]{1,0:T(8,128)(2,1)} %collective-permute-done.3.arrived, bf16[2,192,512]{2,1,0:T(8,128)(2,1)S(1)} %get-tuple-element.24.fields, ...), custom_call_target="tpu_custom_call" | custom-call | tf_op jit(solution)/shard_map/pallas_call | solution.py:36
  44.7 0.0 copy-start.2
  44.7 0.0 copy-start.6
  44.7 1.9 %collective-permute-start.7 = (bf16[144,768]{1,0:T(8,128)(2,1)S(1)}, bf16[144,768]{1,0:T(8,128)(2,1)S(1)}, u32[]{:S(2)}, u32[]{:S(2)}) collective-permute-start(bf16[144,768]{1,0:T(8,128)(2,1)S(1)} %get-tuple-element.30), channel_id=1, source_target_pairs={{0,32},{32,0},{64,96},{96,64},{128,160},{160,128},{192,224},{224,1... | collective-permute-start | bytes 663560 | tf_op jit(solution)/shard_map/ppermute | solution.py:363
  46.7 1.4 %collective-permute-done.7.got = bf16[144,768]{1,0:T(8,128)(2,1)S(1)} collective-permute-done((bf16[144,768]{1,0:T(8,128)(2,1)S(1)}, bf16[144,768]{1,0:T(8,128)(2,1)S(1)}, u32[]{:S(2)}, u32[]{:S(2)}) %collective-permute-start.7) | collective-permute-done | bytes 221216 | tf_op jit(solution)/shard_map/ppermute | solution.py:363
  48.1 1.5 %shard_map.93 = bf16[4,32,24,128]{3,2,1,0:T(8,128)(2,1)} custom-call(bf16[144,768]{1,0:T(8,128)(2,1)S(1)} %get-tuple-element.29.kept, bf16[144,768]{1,0:T(8,128)(2,1)S(1)} %collective-permute-done.7.got, bf16[2,512,144]{2,1,0:T(8,128)(2,1)S(1)} %shard_map.89.inputs), custom_call_target="tpu_custom_call" | custom-call | tf_op jit(solution)/shard_map/pallas_call | solution.py:36
  49.6 0.0 copy-done.2
  49.6 0.0 copy-done.6
  49.6 0.0 copy-start.7
  49.6 0.0 copy-start.3
  49.6 13.2 %all-to-all-start = ((bf16[128,24,128]{2,1,0:T(8,128)(2,1)}), bf16[128,24,128]{2,1,0:T(8,128)(2,1)S(1)}, u32[]{:S(2)}, u32[]{:S(2)}) async-start(bf16[128,24,128]{2,1,0:T(8,128)(2,1)} %bitcast.4), calls=%async_computation | async-start | bytes 1572864 | tf_op jit(solution)/shard_map/all_to_all | solution.py:425
  62.9 0.0 copy-done.7
  62.9 3.4 %collective-permute-start.5 = (bf16[6,16,512]{2,1,0:T(8,128)(2,1)S(1)}, bf16[6,16,512]{2,1,0:T(8,128)(2,1)S(1)}, u32[]{:S(2)}, u32[]{:S(2)}) collective-permute-start(bf16[6,16,512]{2,1,0:T(8,128)(2,1)S(1)} %copy-done.7), channel_id=1, source_target_pairs={{0,1},{1,2},{2,3},{3,4},{4,5},{5,6},{6,7},{7,8},{8,9},{9,10},{10,1... | collective-permute-start | bytes 294920 | tf_op jit(solution)/shard_map/ppermute | solution.py:359
  66.3 24.7 %collective-permute-done.5.left = bf16[6,16,512]{2,1,0:T(8,128)(2,1)S(1)} collective-permute-done((bf16[6,16,512]{2,1,0:T(8,128)(2,1)S(1)}, bf16[6,16,512]{2,1,0:T(8,128)(2,1)S(1)}, u32[]{:S(2)}, u32[]{:S(2)}) %collective-permute-start.5) | collective-permute-done | bytes 98336 | tf_op jit(solution)/shard_map/ppermute | solution.py:359
  91.0 0.0 copy-done.3
  91.0 0.0 collective-permute-start.6
  91.0 4.0 %collective-permute-done.6.arrived = bf16[2,3,16,512]{3,2,1,0:T(8,128)(2,1)S(1)} collective-permute-done((bf16[2,3,16,512]{3,2,1,0:T(8,128)(2,1)S(1)}, bf16[2,3,16,512]{3,2,1,0:T(8,128)(2,1)S(1)}, u32[]{:S(2)}, u32[]{:S(2)}) %collective-permute-start.6) | collective-permute-done | bytes 98336 | tf_op jit(solution)/shard_map/ppermute | solution.py:359
  95.1 0.8 copy.11
  95.9 0.0 all-to-all-done.parts
  95.9 0.8 shard_map.94
  (3 shorter events, 0.1 us)
Async XLA Ops:
  2.5 0.7 copy-start.5
  3.9 20.1 %collective-permute-start = (bf16[2,3,16,512]{3,2,1,0:T(8,128)(2,1)S(1)}, bf16[2,3,16,512]{3,2,1,0:T(8,128)(2,1)S(1)}, u32[]{:S(2)}, u32[]{:S(2)}) collective-permute-start(bf16[2,3,16,512]{3,2,1,0:T(8,128)(2,1)S(1)} %get-tuple-element.18), channel_id=1, source_target_pairs={{0,31},{1,0},{2,1},{3,2},{4,3},{5,4},{6,5},{7,6},{8,7},{9,8},{10,9... | collective-permute-start | bytes 294920 | tf_op jit(solution)/shard_map/ppermute | solution.py:359
  18.5 5.5 %collective-permute-start.1 = (bf16[2,3,16,512]{3,2,1,0:T(8,128)(2,1)S(1)}, bf16[2,3,16,512]{3,2,1,0:T(8,128)(2,1)S(1)}, u32[]{:S(2)}, u32[]{:S(2)}) collective-permute-start(bf16[2,3,16,512]{3,2,1,0:T(8,128)(2,1)S(1)} %get-tuple-element.19), channel_id=1, source_target_pairs={{0,224},{1,225},{2,226},{3,227},{4,228},{5,229},{6,230},{7,231},{8... | collective-permute-start | bytes 294920 | tf_op jit(solution)/shard_map/ppermute | solution.py:359
  18.5 8.4 %collective-permute-start.2 = (bf16[2,3,16,512]{3,2,1,0:T(8,128)(2,1)S(1)}, bf16[2,3,16,512]{3,2,1,0:T(8,128)(2,1)S(1)}, u32[]{:S(2)}, u32[]{:S(2)}) collective-permute-start(bf16[2,3,16,512]{3,2,1,0:T(8,128)(2,1)S(1)} %get-tuple-element.20), channel_id=1, source_target_pairs={{0,255},{1,224},{2,225},{3,226},{4,227},{5,228},{6,229},{7,230},{8... | collective-permute-start | bytes 294920 | tf_op jit(solution)/shard_map/ppermute | solution.py:359
  22.1 4.7 %copy-start = (bf16[1,1536,512]{2,1,0:T(8,128)(2,1)S(1)}, bf16[1,1536,512]{2,1,0:T(8,128)(2,1)}, u32[]{:S(2)}) copy-start(bf16[1,1536,512]{2,1,0:T(8,128)(2,1)} %param.9) | copy-start | bytes 4718596
  22.1 4.7 %copy-start.1 = (bf16[1,512,512]{2,1,0:T(8,128)(2,1)S(1)}, bf16[1,512,512]{2,1,0:T(8,128)(2,1)}, u32[]{:S(2)}) copy-start(bf16[1,512,512]{2,1,0:T(8,128)(2,1)} %param.10) | copy-start | bytes 1572868
  22.1 4.7 %copy-start.4 = (f32[1,512]{1,0:T(1,128)S(1)}, f32[1,512]{1,0:T(1,128)}, u32[]{:S(2)}) copy-start(f32[1,512]{1,0:T(1,128)} %gain.3) | copy-start | bytes 6148
  31.0 3.6 %collective-permute-start.4 = (bf16[144,512]{1,0:T(8,128)(2,1)}, bf16[144,512]{1,0:T(8,128)(2,1)}, u32[]{:S(2)}, u32[]{:S(2)}) collective-permute-start(bf16[144,512]{1,0:T(8,128)(2,1)} %get-tuple-element.22.inputs), channel_id=1, source_target_pairs={{0,32},{32,0},{64,96},{96,64},{128,160},{160,128},{192,224},{224,1... | collective-permute-start | bytes 442376 | tf_op jit(solution)/shard_map/ppermute | solution.py:363
  33.2 8.2 %collective-permute-start.3 = (bf16[144,512]{1,0:T(8,128)(2,1)}, bf16[144,512]{1,0:T(8,128)(2,1)}, u32[]{:S(2)}, u32[]{:S(2)}) collective-permute-start(bf16[144,512]{1,0:T(8,128)(2,1)} %get-tuple-element.21), channel_id=1, source_target_pairs={{256,0},{257,1},{258,2},{259,3},{260,4},{261,5},{262,6},{263,7},{2... | collective-permute-start | bytes 442376 | tf_op jit(solution)/shard_map/ppermute | solution.py:400
  44.7 4.9 %copy-start.2 = (bf16[6,16,512]{2,1,0:T(8,128)(2,1)}, bf16[6,16,512]{2,1,0:T(8,128)(2,1)S(1)}, u32[]{:S(2)}) copy-start(bf16[6,16,512]{2,1,0:T(8,128)(2,1)S(1)} %get-tuple-element.27.near) | copy-start | bytes 294916
  44.7 4.9 %copy-start.6 = (bf16[6,16,512]{2,1,0:T(8,128)(2,1)}, bf16[6,16,512]{2,1,0:T(8,128)(2,1)S(1)}, u32[]{:S(2)}) copy-start(bf16[6,16,512]{2,1,0:T(8,128)(2,1)S(1)} %get-tuple-element.28) | copy-start | bytes 294916
  44.7 3.4 %collective-permute-start.7 = (bf16[144,768]{1,0:T(8,128)(2,1)S(1)}, bf16[144,768]{1,0:T(8,128)(2,1)S(1)}, u32[]{:S(2)}, u32[]{:S(2)}) collective-permute-start(bf16[144,768]{1,0:T(8,128)(2,1)S(1)} %get-tuple-element.30), channel_id=1, source_target_pairs={{0,32},{32,0},{64,96},{96,64},{128,160},{160,128},{192,224},{224,1... | collective-permute-start | bytes 663560 | tf_op jit(solution)/shard_map/ppermute | solution.py:363
  49.6 13.3 %copy-start.7 = (bf16[6,16,512]{2,1,0:T(8,128)(2,1)S(1)}, bf16[6,16,512]{2,1,0:T(8,128)(2,1)}, u32[]{:S(2)}) copy-start(bf16[6,16,512]{2,1,0:T(8,128)(2,1)} %copy-done.6) | copy-start | bytes 294916
  49.6 41.4 %copy-start.3 = (bf16[6,16,512]{2,1,0:T(8,128)(2,1)S(1)}, bf16[6,16,512]{2,1,0:T(8,128)(2,1)}, u32[]{:S(2)}) copy-start(bf16[6,16,512]{2,1,0:T(8,128)(2,1)} %copy-done.2) | copy-start | bytes 294916
  49.6 46.3 %all-to-all-start = ((bf16[128,24,128]{2,1,0:T(8,128)(2,1)}), bf16[128,24,128]{2,1,0:T(8,128)(2,1)S(1)}, u32[]{:S(2)}, u32[]{:S(2)}) async-start(bf16[128,24,128]{2,1,0:T(8,128)(2,1)} %bitcast.4), calls=%async_computation | async-start | bytes 1572864 | tf_op jit(solution)/shard_map/all_to_all | solution.py:425
  62.9 28.1 %collective-permute-start.5 = (bf16[6,16,512]{2,1,0:T(8,128)(2,1)S(1)}, bf16[6,16,512]{2,1,0:T(8,128)(2,1)S(1)}, u32[]{:S(2)}, u32[]{:S(2)}) collective-permute-start(bf16[6,16,512]{2,1,0:T(8,128)(2,1)S(1)} %copy-done.7), channel_id=1, source_target_pairs={{0,1},{1,2},{2,3},{3,4},{4,5},{5,6},{6,7},{7,8},{8,9},{9,10},{10,1... | collective-permute-start | bytes 294920 | tf_op jit(solution)/shard_map/ppermute | solution.py:359
  91.0 4.1 %collective-permute-start.6 = (bf16[2,3,16,512]{3,2,1,0:T(8,128)(2,1)S(1)}, bf16[2,3,16,512]{3,2,1,0:T(8,128)(2,1)S(1)}, u32[]{:S(2)}, u32[]{:S(2)}) collective-permute-start(bf16[2,3,16,512]{3,2,1,0:T(8,128)(2,1)S(1)} %shard_map.91), channel_id=1, source_target_pairs={{0,32},{1,33},{2,34},{3,35},{4,36},{5,37},{6,38},{7,39},{8,40},{9,... | collective-permute-start | bytes 294920 | tf_op jit(solution)/shard_map/ppermute | solution.py:359

commit v5 on v4

--- a/solution.py
+++ b/solution.py
@@ -309,10 +309,14 @@
         out[t, :, width:, :] = folded.astype(BF16)
 
 
-def upward_kernel(near, left, out):
+def chips_kernel(products, near, left, out, upward):
+    total = products[0].astype(F32)
+    for t in range(1, products.shape[0]):
+        total = total + products[t].astype(F32)
+    out[...] = total.astype(BF16)
     for i in range(3):
-        out[0, i] = left[3 + i]
-        out[1, i] = near[3 + i]
+        upward[0, i] = left[3 + i]
+        upward[1, i] = near[3 + i]
 
 
 def sum_kernel(odd, parts, out):
@@ -416,20 +420,15 @@
     products = call(product_kernel, struct((lats // 2, lons, rows, 128), BF16))(
         kept, got, turned
     )
-    upward = call(upward_kernel, struct((2, 3, 16, FEATURES), BF16))(near, left)
+    chips = [[2 * x + c for x in range(lats // 2)] for c in range(2)]
+    products = lax.all_to_all(products, "lat", 0, 0, tiled=True, axis_index_groups=chips)
+    slices, upward = call(
+        chips_kernel,
+        (struct((lons, rows, 128), BF16), struct((2, 3, 16, FEATURES), BF16)),
+    )(products, near, left)
     above = passed(upward, 1, 0)
     grad_input = call(join_kernel, struct((1, 2, 6, 12, FEATURES), BF16))(near, left, above)
-    same_core = [
-        [(2 * x + c) * lons + o for x in range(lats // 2) for o in range(lons)] for c in range(2)
-    ]
-    slices = lax.all_to_all(
-        products.reshape(lats // 2 * lons, rows, 128),
-        ("lat", "lon"),
-        0,
-        0,
-        tiled=True,
-        axis_index_groups=same_core,
-    )
+    slices = lax.all_to_all(slices, "lon", 0, 0, tiled=True)
     grad_qkv = call(
         sum_kernel, struct((1, FEATURES // lons, 192), F32), places={0: pltpu.SMEM}
     )(core, slices)

time: 97.2 us -> 90.3 us (0.929)
  the two profiles are of different devices: /device:TPU:6 before, /device:TPU:2 now
where the time goes in v5:
time: 90.3 us; the launch traced here: 89.8 us
  starting transfers between devices  37.1 us (41%)
  waiting for transfers between devices  33.6 us (37%)
  Pallas kernels  12.8 us (14%)
  local copies, waits for them, and re-layouts  5.42 us (6%)
    ppermute x5, starting transfers between devices, passed(): return lax.ppermute(array, ('lat', 'lon'), pairs)  19.1 us
    ppermute x5, waiting for transfers between devices, passed(): return lax.ppermute(array, ('lat', 'lon'), pairs)  18.3 us
    pallas_call x9, Pallas kernels, run(): pl.pallas_call(kernel, out_shape=out_shape, in_specs=specs, out_specs=out...  12.8 us
    all_to_all x1, starting transfers between devices, per_device(): slices = lax.all_to_all(slices, 'lon', 0, 0, tiled=True)  8.11 us
    all_to_all x1, waiting for transfers between devices, per_device(): slices = lax.all_to_all(slices, 'lon', 0, 0, tiled=True)  7.91 us
    ppermute x1, waiting for transfers between devices, per_device(): arrived = lax.ppermute(skip, 'phase', [(1, 0)])  5.59 us
    all_to_all x1, starting transfers between devices, per_device(): lax.all_to_all(products, 'lat', 0, 0, tiled=True, axis_index_groups=chips)  4.82 us
    unnamed x19, local copies, waits for them, and re-layouts  4.63 us
  transfers between devices with their start and end apart: 10, of which 8 were waited for; matrix products, arithmetic and copies ran while one was open for 2% of the time, Pallas kernels for 2%

profile of v5, /device:TPU:2, one launch (start us, length us, event | category | flops | bytes accessed | tf_op | source)
XLA Modules:
  0.0 89.8 jit_solution(5319192270523171098)
XLA Ops:
  0.6 0.9 %copy.9.x_ref = bf16[1,2,6,12,512]{4,3,2,1,0:T(8,128)(2,1)S(1)} copy(bf16[1,2,6,12,512]{4,1,3,2,0:T(2,128)(2,1)} %param.7) | data formatting | bytes 294912 | tf_op args[0]
  1.6 0.9 %copy.10.g_ref = bf16[1,2,6,12,512]{4,3,2,1,0:T(8,128)(2,1)S(1)} copy(bf16[1,2,6,12,512]{4,1,3,2,0:T(2,128)(2,1)} %param.8) | data formatting | bytes 294912 | tf_op args[1]
  2.5 0.0 copy-start.5
  2.5 0.6 copy-done.5
  3.2 0.7 shard_map.86
  3.9 14.6 %collective-permute-start = (bf16[2,3,16,512]{3,2,1,0:T(8,128)(2,1)S(1)}, bf16[2,3,16,512]{3,2,1,0:T(8,128)(2,1)S(1)}, u32[]{:S(2)}, u32[]{:S(2)}) collective-permute-start(bf16[2,3,16,512]{3,2,1,0:T(8,128)(2,1)S(1)} %get-tuple-element.20), channel_id=1, source_target_pairs={{0,31},{1,0},{2,1},{3,2},{4,3},{5,4},{6,5},{7,6},{8,7},{9,8},{10,9... | collective-permute-start | bytes 294920 | tf_op jit(solution)/shard_map/ppermute | solution.py:363
  18.5 0.0 collective-permute-start.1
  18.5 2.5 %collective-permute-start.2 = (bf16[2,3,16,512]{3,2,1,0:T(8,128)(2,1)S(1)}, bf16[2,3,16,512]{3,2,1,0:T(8,128)(2,1)S(1)}, u32[]{:S(2)}, u32[]{:S(2)}) collective-permute-start(bf16[2,3,16,512]{3,2,1,0:T(8,128)(2,1)S(1)} %get-tuple-element.22), channel_id=1, source_target_pairs={{0,255},{1,224},{2,225},{3,226},{4,227},{5,228},{6,229},{7,230},{8... | collective-permute-start | bytes 294920 | tf_op jit(solution)/shard_map/ppermute | solution.py:363
  21.1 0.8 slice_bitcast_fusion
  21.8 0.0 copy-start
  21.9 0.0 copy-start.1
  21.9 0.0 copy-start.4
  21.9 0.5 shard_map.87.bias
  22.3 1.6 %collective-permute-done.lon = bf16[2,3,16,512]{3,2,1,0:T(8,128)(2,1)S(1)} collective-permute-done((bf16[2,3,16,512]{3,2,1,0:T(8,128)(2,1)S(1)}, bf16[2,3,16,512]{3,2,1,0:T(8,128)(2,1)S(1)}, u32[]{:S(2)}, u32[]{:S(2)}) %collective-permute-start) | collective-permute-done | bytes 98336 | tf_op jit(solution)/shard_map/ppermute | solution.py:363
  24.0 0.0 collective-permute-done.1.lat
  24.0 2.9 %collective-permute-done.2.cor = bf16[2,3,16,512]{3,2,1,0:T(8,128)(2,1)S(1)} collective-permute-done((bf16[2,3,16,512]{3,2,1,0:T(8,128)(2,1)S(1)}, bf16[2,3,16,512]{3,2,1,0:T(8,128)(2,1)S(1)}, u32[]{:S(2)}, u32[]{:S(2)}) %collective-permute-start.2) | collective-permute-done | bytes 98336 | tf_op jit(solution)/shard_map/ppermute | solution.py:363
  26.9 0.0 copy-done
  26.9 0.0 copy-done.1
  26.9 0.0 copy-done.4
  26.9 4.1 %shard_map.88 = (bf16[144,512]{1,0:T(8,128)(2,1)}, bf16[144,512]{1,0:T(8,128)(2,1)}, bf16[2,192,512]{2,1,0:T(8,128)(2,1)S(1)}, bf16[192,1536]{1,0:T(8,128)(2,1)S(1)}, bf16[2,4,2,96,96]{4,3,2,1,0:T(8,128)(2,1)S(1)}) custom-call(bf16[2,3,16,512]{3,2,1,0:T(8,128)(2,1)S(1)} %get-tuple-element.19.own, bf16[2,3,16,512]{3,2,1,0:T(8,128)(2,1)S(1)} %collective-permute-done.lon, ...), custom_call_target="tpu_custom_call" | custom-call | tf_op jit(solution)/shard_map/pallas_call | solution.py:36
  31.0 1.9 %collective-permute-start.4 = (bf16[144,512]{1,0:T(8,128)(2,1)}, bf16[144,512]{1,0:T(8,128)(2,1)}, u32[]{:S(2)}, u32[]{:S(2)}) collective-permute-start(bf16[144,512]{1,0:T(8,128)(2,1)} %get-tuple-element.24.inputs), channel_id=1, source_target_pairs={{0,32},{32,0},{64,96},{96,64},{128,160},{160,128},{192,224},{224,1... | collective-permute-start | bytes 442376 | tf_op jit(solution)/shard_map/ppermute | solution.py:367
  33.0 1.3 %collective-permute-start.3 = (bf16[144,512]{1,0:T(8,128)(2,1)}, bf16[144,512]{1,0:T(8,128)(2,1)}, u32[]{:S(2)}, u32[]{:S(2)}) collective-permute-start(bf16[144,512]{1,0:T(8,128)(2,1)} %get-tuple-element.23), channel_id=1, source_target_pairs={{256,0},{257,1},{258,2},{259,3},{260,4},{261,5},{262,6},{263,7},{2... | collective-permute-start | bytes 442376 | tf_op jit(solution)/shard_map/ppermute | solution.py:404
  34.3 0.4 collective-permute-done.4.other_inputs
  34.6 1.2 %shard_map.89.inputs = bf16[2,512,144]{2,1,0:T(8,128)(2,1)S(1)} custom-call(bf16[144,512]{1,0:T(8,128)(2,1)} %get-tuple-element.24.inputs, bf16[144,512]{1,0:T(8,128)(2,1)} %collective-permute-done.4.other_inputs), custom_call_target="tpu_custom_call" | custom-call | tf_op jit(solution)/shard_map/pallas_call | solution.py:36
  35.8 5.6 %collective-permute-done.3.arrived = bf16[144,512]{1,0:T(8,128)(2,1)} collective-permute-done((bf16[144,512]{1,0:T(8,128)(2,1)}, bf16[144,512]{1,0:T(8,128)(2,1)}, u32[]{:S(2)}, u32[]{:S(2)}) %collective-permute-start.3) | collective-permute-done | bytes 147488 | tf_op jit(solution)/shard_map/ppermute | solution.py:404
  41.4 3.3 %shard_map.90 = (bf16[144,768]{1,0:T(8,128)(2,1)S(1)}, bf16[144,768]{1,0:T(8,128)(2,1)S(1)}, bf16[6,16,512]{2,1,0:T(8,128)(2,1)S(1)}, bf16[6,16,512]{2,1,0:T(8,128)(2,1)S(1)}) custom-call(s32[1]{0:T(128)} %bitcast.core.odd, bf16[144,512]{1,0:T(8,128)(2,1)} %collective-permute-done.3.arrived, bf16[2,192,512]{2,1,0:T(8,128)(2,1)S(1)} %get-tuple-element.26.fields, ...), custom_call_target="tpu_custom_call" | custom-call | tf_op jit(solution)/shard_map/pallas_call | solution.py:36
  44.7 0.0 copy-start.2
  44.7 0.6 copy-done.2
  45.4 0.0 copy-start.6
  45.4 0.6 copy-done.6
  46.0 1.9 %collective-permute-start.6 = (bf16[144,768]{1,0:T(8,128)(2,1)S(1)}, bf16[144,768]{1,0:T(8,128)(2,1)S(1)}, u32[]{:S(2)}, u32[]{:S(2)}) collective-permute-start(bf16[144,768]{1,0:T(8,128)(2,1)S(1)} %get-tuple-element.32), channel_id=1, source_target_pairs={{0,32},{32,0},{64,96},{96,64},{128,160},{160,128},{192,224},{224,1... | collective-permute-start | bytes 663560 | tf_op jit(solution)/shard_map/ppermute | solution.py:367
  47.9 1.4 %collective-permute-done.6.got = bf16[144,768]{1,0:T(8,128)(2,1)S(1)} collective-permute-done((bf16[144,768]{1,0:T(8,128)(2,1)S(1)}, bf16[144,768]{1,0:T(8,128)(2,1)S(1)}, u32[]{:S(2)}, u32[]{:S(2)}) %collective-permute-start.6) | collective-permute-done | bytes 221216 | tf_op jit(solution)/shard_map/ppermute | solution.py:367
  49.4 0.0 copy-start.7
  49.4 0.0 copy-start.3
  49.4 1.5 %shard_map.91 = bf16[4,32,24,128]{3,2,1,0:T(8,128)(2,1)} custom-call(bf16[144,768]{1,0:T(8,128)(2,1)S(1)} %get-tuple-element.31.kept, bf16[144,768]{1,0:T(8,128)(2,1)S(1)} %collective-permute-done.6.got, bf16[2,512,144]{2,1,0:T(8,128)(2,1)S(1)} %shard_map.89.inputs), custom_call_target="tpu_custom_call" | custom-call | tf_op jit(solution)/shard_map/pallas_call | solution.py:36
  50.9 4.8 %all-to-all-start = ((bf16[4,32,24,128]{3,2,1,0:T(8,128)(2,1)}), bf16[4,32,24,128]{3,2,1,0:T(8,128)(2,1)S(1)}, u32[]{:S(2)}, u32[]{:S(2)}) async-start(bf16[4,32,24,128]{3,2,1,0:T(8,128)(2,1)} %shard_map.91), calls=%async_computation | async-start | bytes 1572864 | tf_op jit(solution)/shard_map/all_to_all | solution.py:424
  55.7 0.0 copy-done.7
  55.7 1.9 %collective-permute-start.5 = (bf16[6,16,512]{2,1,0:T(8,128)(2,1)S(1)}, bf16[6,16,512]{2,1,0:T(8,128)(2,1)S(1)}, u32[]{:S(2)}, u32[]{:S(2)}) collective-permute-start(bf16[6,16,512]{2,1,0:T(8,128)(2,1)S(1)} %copy-done.7), channel_id=1, source_target_pairs={{0,1},{1,2},{2,3},{3,4},{4,5},{5,6},{6,7},{7,8},{8,9},{9,10},{10,1... | collective-permute-start | bytes 294920 | tf_op jit(solution)/shard_map/ppermute | solution.py:363
  57.6 9.8 %collective-permute-done.5.left = bf16[6,16,512]{2,1,0:T(8,128)(2,1)S(1)} collective-permute-done((bf16[6,16,512]{2,1,0:T(8,128)(2,1)S(1)}, bf16[6,16,512]{2,1,0:T(8,128)(2,1)S(1)}, u32[]{:S(2)}, u32[]{:S(2)}) %collective-permute-start.5) | collective-permute-done | bytes 98336 | tf_op jit(solution)/shard_map/ppermute | solution.py:363
  67.4 0.0 all-to-all-done.products
  67.4 0.0 copy-done.3
  67.4 0.8 shard_map.92
  68.2 8.1 %all-to-all-start.1 = ((bf16[32,24,128]{2,1,0:T(8,128)(2,1)}), bf16[32,24,128]{2,1,0:T(8,128)(2,1)S(1)}, u32[]{:S(2)}, u32[]{:S(2)}) async-start(bf16[32,24,128]{2,1,0:T(8,128)(2,1)} %get-tuple-element.35), calls=%async_computation.1 | async-start | bytes 393216 | tf_op jit(solution)/shard_map/all_to_all | solution.py:431
  76.3 0.0 collective-permute-start.7
  76.3 4.0 %collective-permute-done.7.arrived = bf16[2,3,16,512]{3,2,1,0:T(8,128)(2,1)S(1)} collective-permute-done((bf16[2,3,16,512]{3,2,1,0:T(8,128)(2,1)S(1)}, bf16[2,3,16,512]{3,2,1,0:T(8,128)(2,1)S(1)}, u32[]{:S(2)}, u32[]{:S(2)}) %collective-permute-start.7) | collective-permute-done | bytes 98336 | tf_op jit(solution)/shard_map/ppermute | solution.py:363
  80.4 0.8 copy.11
  81.2 7.9 %all-to-all-done.1.parts = bf16[32,24,128]{2,1,0:T(8,128)(2,1)S(1)} async-done(((bf16[32,24,128]{2,1,0:T(8,128)(2,1)}), bf16[32,24,128]{2,1,0:T(8,128)(2,1)S(1)}, u32[]{:S(2)}, u32[]{:S(2)}) %all-to-all-start.1) | async-done | bytes 196640 | tf_op jit(solution)/shard_map/all_to_all | solution.py:431
  89.1 0.7 shard_map.94
  (2 shorter events, 0.0 us)
Async XLA Ops:
  2.5 0.7 copy-start.5
  3.9 20.1 %collective-permute-start = (bf16[2,3,16,512]{3,2,1,0:T(8,128)(2,1)S(1)}, bf16[2,3,16,512]{3,2,1,0:T(8,128)(2,1)S(1)}, u32[]{:S(2)}, u32[]{:S(2)}) collective-permute-start(bf16[2,3,16,512]{3,2,1,0:T(8,128)(2,1)S(1)} %get-tuple-element.20), channel_id=1, source_target_pairs={{0,31},{1,0},{2,1},{3,2},{4,3},{5,4},{6,5},{7,6},{8,7},{9,8},{10,9... | collective-permute-start | bytes 294920 | tf_op jit(solution)/shard_map/ppermute | solution.py:363
  18.5 5.5 %collective-permute-start.1 = (bf16[2,3,16,512]{3,2,1,0:T(8,128)(2,1)S(1)}, bf16[2,3,16,512]{3,2,1,0:T(8,128)(2,1)S(1)}, u32[]{:S(2)}, u32[]{:S(2)}) collective-permute-start(bf16[2,3,16,512]{3,2,1,0:T(8,128)(2,1)S(1)} %get-tuple-element.21), channel_id=1, source_target_pairs={{0,224},{1,225},{2,226},{3,227},{4,228},{5,229},{6,230},{7,231},{8... | collective-permute-start | bytes 294920 | tf_op jit(solution)/shard_map/ppermute | solution.py:363
  18.5 8.4 %collective-permute-start.2 = (bf16[2,3,16,512]{3,2,1,0:T(8,128)(2,1)S(1)}, bf16[2,3,16,512]{3,2,1,0:T(8,128)(2,1)S(1)}, u32[]{:S(2)}, u32[]{:S(2)}) collective-permute-start(bf16[2,3,16,512]{3,2,1,0:T(8,128)(2,1)S(1)} %get-tuple-element.22), channel_id=1, source_target_pairs={{0,255},{1,224},{2,225},{3,226},{4,227},{5,228},{6,229},{7,230},{8... | collective-permute-start | bytes 294920 | tf_op jit(solution)/shard_map/ppermute | solution.py:363
  21.8 5.0 %copy-start = (bf16[1,1536,512]{2,1,0:T(8,128)(2,1)S(1)}, bf16[1,1536,512]{2,1,0:T(8,128)(2,1)}, u32[]{:S(2)}) copy-start(bf16[1,1536,512]{2,1,0:T(8,128)(2,1)} %param.9) | copy-start | bytes 4718596
  21.9 5.0 %copy-start.1 = (bf16[1,512,512]{2,1,0:T(8,128)(2,1)S(1)}, bf16[1,512,512]{2,1,0:T(8,128)(2,1)}, u32[]{:S(2)}) copy-start(bf16[1,512,512]{2,1,0:T(8,128)(2,1)} %param.10) | copy-start | bytes 1572868
  21.9 5.0 %copy-start.4 = (f32[1,512]{1,0:T(1,128)S(1)}, f32[1,512]{1,0:T(1,128)}, u32[]{:S(2)}) copy-start(f32[1,512]{1,0:T(1,128)} %gain.3) | copy-start | bytes 6148
  31.0 3.6 %collective-permute-start.4 = (bf16[144,512]{1,0:T(8,128)(2,1)}, bf16[144,512]{1,0:T(8,128)(2,1)}, u32[]{:S(2)}, u32[]{:S(2)}) collective-permute-start(bf16[144,512]{1,0:T(8,128)(2,1)} %get-tuple-element.24.inputs), channel_id=1, source_target_pairs={{0,32},{32,0},{64,96},{96,64},{128,160},{160,128},{192,224},{224,1... | collective-permute-start | bytes 442376 | tf_op jit(solution)/shard_map/ppermute | solution.py:367
  33.0 8.5 %collective-permute-start.3 = (bf16[144,512]{1,0:T(8,128)(2,1)}, bf16[144,512]{1,0:T(8,128)(2,1)}, u32[]{:S(2)}, u32[]{:S(2)}) collective-permute-start(bf16[144,512]{1,0:T(8,128)(2,1)} %get-tuple-element.23), channel_id=1, source_target_pairs={{256,0},{257,1},{258,2},{259,3},{260,4},{261,5},{262,6},{263,7},{2... | collective-permute-start | bytes 442376 | tf_op jit(solution)/shard_map/ppermute | solution.py:404
  44.7 0.6 copy-start.2
  45.4 0.6 copy-start.6
  46.0 3.4 %collective-permute-start.6 = (bf16[144,768]{1,0:T(8,128)(2,1)S(1)}, bf16[144,768]{1,0:T(8,128)(2,1)S(1)}, u32[]{:S(2)}, u32[]{:S(2)}) collective-permute-start(bf16[144,768]{1,0:T(8,128)(2,1)S(1)} %get-tuple-element.32), channel_id=1, source_target_pairs={{0,32},{32,0},{64,96},{96,64},{128,160},{160,128},{192,224},{224,1... | collective-permute-start | bytes 663560 | tf_op jit(solution)/shard_map/ppermute | solution.py:367
  49.4 6.4 %copy-start.7 = (bf16[6,16,512]{2,1,0:T(8,128)(2,1)S(1)}, bf16[6,16,512]{2,1,0:T(8,128)(2,1)}, u32[]{:S(2)}) copy-start(bf16[6,16,512]{2,1,0:T(8,128)(2,1)} %copy-done.6) | copy-start | bytes 294916
  49.4 18.0 %copy-start.3 = (bf16[6,16,512]{2,1,0:T(8,128)(2,1)S(1)}, bf16[6,16,512]{2,1,0:T(8,128)(2,1)}, u32[]{:S(2)}) copy-start(bf16[6,16,512]{2,1,0:T(8,128)(2,1)} %copy-done.2) | copy-start | bytes 294916
  50.9 16.5 %all-to-all-start = ((bf16[4,32,24,128]{3,2,1,0:T(8,128)(2,1)}), bf16[4,32,24,128]{3,2,1,0:T(8,128)(2,1)S(1)}, u32[]{:S(2)}, u32[]{:S(2)}) async-start(bf16[4,32,24,128]{3,2,1,0:T(8,128)(2,1)} %shard_map.91), calls=%async_computation | async-start | bytes 1572864 | tf_op jit(solution)/shard_map/all_to_all | solution.py:424
  55.7 11.7 %collective-permute-start.5 = (bf16[6,16,512]{2,1,0:T(8,128)(2,1)S(1)}, bf16[6,16,512]{2,1,0:T(8,128)(2,1)S(1)}, u32[]{:S(2)}, u32[]{:S(2)}) collective-permute-start(bf16[6,16,512]{2,1,0:T(8,128)(2,1)S(1)} %copy-done.7), channel_id=1, source_target_pairs={{0,1},{1,2},{2,3},{3,4},{4,5},{5,6},{6,7},{7,8},{8,9},{9,10},{10,1... | collective-permute-start | bytes 294920 | tf_op jit(solution)/shard_map/ppermute | solution.py:363
  68.2 20.9 %all-to-all-start.1 = ((bf16[32,24,128]{2,1,0:T(8,128)(2,1)}), bf16[32,24,128]{2,1,0:T(8,128)(2,1)S(1)}, u32[]{:S(2)}, u32[]{:S(2)}) async-start(bf16[32,24,128]{2,1,0:T(8,128)(2,1)} %get-tuple-element.35), calls=%async_computation.1 | async-start | bytes 393216 | tf_op jit(solution)/shard_map/all_to_all | solution.py:431
  76.3 4.1 %collective-permute-start.7 = (bf16[2,3,16,512]{3,2,1,0:T(8,128)(2,1)S(1)}, bf16[2,3,16,512]{3,2,1,0:T(8,128)(2,1)S(1)}, u32[]{:S(2)}, u32[]{:S(2)}) collective-permute-start(bf16[2,3,16,512]{3,2,1,0:T(8,128)(2,1)S(1)} %get-tuple-element.34), channel_id=1, source_target_pairs={{0,32},{1,33},{2,34},{3,35},{4,36},{5,37},{6,38},{7,39},{8,40},{9,... | collective-permute-start | bytes 294920 | tf_op jit(solution)/shard_map/ppermute | solution.py:363

commit v6 on v5

--- a/solution.py
+++ b/solution.py
@@ -14,14 +14,13 @@
 EPSILON = 1e-05
 MASKED = -1e30
 SCORE_SCALE = 0.125
-VMEM_LIMIT = 8 * 1024 * 1024
+MIB = 1024 * 1024
 
 LEVEL_ROWS = 96
 ROWS = 192
-PACKED_ROWS = 144
-
-
-def call(kernel, out_shape, scratch=(), places=(), out_places=(), cost=None):
+
+
+def call(kernel, out_shape, scratch=(), places=(), out_places=(), cost=None, limit=50 * MIB):
     def run(*args):
         places_of = dict(places)
         specs = [
@@ -40,7 +39,7 @@
             out_specs=outs,
             scratch_shapes=list(scratch),
             cost_estimate=cost,
-            compiler_params=pltpu.CompilerParams(vmem_limit_bytes=VMEM_LIMIT),
+            compiler_params=pltpu.CompilerParams(vmem_limit_bytes=limit),
         )(*args)
 
     return run
@@ -58,25 +57,33 @@
     return lax.broadcasted_iota(jnp.int32, shape, dim)
 
 
-def cut_kernel(labels_ref, x_ref, g_ref, own, lon, lat, cor, labels, sem):
+def cut_kernel(labels_ref, x_ref, g_ref, own, lon, lat, cor, labels, x_rows, g_rows, sem, sems):
     fetch = pltpu.make_async_copy(labels_ref, labels, sem)
     fetch.start()
-    fetch.wait()
+    fetches = []
+    for i in range(6):
+        fetches.append(pltpu.make_async_copy(x_ref.at[i], x_rows.at[i], sems.at[0, i]))
+        fetches.append(pltpu.make_async_copy(g_ref.at[i], g_rows.at[i], sems.at[1, i]))
+    for copy in fetches:
+        copy.start()
     row = row_index((8, FEATURES), 0)
 
-    def halves(ref, level, i, fill):
-        low = ref[0, level, i, 0:8, :].astype(F32)
-        high = ref[0, level, i, 4:12, :].astype(F32)
+    def halves(field, level, fill):
+        low, high = field[0:8, level, :], field[4:12, level, :]
         return (
             jnp.where(row < 6, low, fill),
             jnp.where(row < 6, pltpu.roll(high, 6, 0), fill),
         )
 
-    for level in range(2):
-        for i in range(6):
-            label = labels[i].astype(F32)
-            x_low, x_high = halves(x_ref, level, i, label)
-            g_low, g_high = halves(g_ref, level, i, 0.0)
+    fetch.wait()
+    for i in range(6):
+        label = labels[i].astype(F32)
+        fetches[2 * i].wait()
+        fetches[2 * i + 1].wait()
+        x, g = x_rows[i].astype(F32), g_rows[i].astype(F32)
+        for level in range(2):
+            x_low, x_high = halves(x, level, label)
+            g_low, g_high = halves(g, level, 0.0)
             low = jnp.concatenate([x_low, g_low], axis=0).astype(BF16)
             high = jnp.concatenate([x_high, g_high], axis=0).astype(BF16)
             if i < 3:
@@ -113,33 +120,6 @@
             out[h * 96 + b * 16 : h * 96 + b * 16 + 16, :] = moved[h * 16 : h * 16 + 16, :]
 
 
-def pack_rows(array):
-    columns = array.shape[1]
-    groups = array.reshape(6, 4, 8, columns)
-    row = row_index((8, columns), 0)
-    out = []
-    for q in range(6):
-        last = groups[q, 3]
-        for g in range(3):
-            out.append(jnp.where(row < 6, groups[q, g], pltpu.roll(last, 6 - 2 * g, 0)))
-    return jnp.concatenate(out, axis=0)
-
-
-def unpack_rows(array):
-    columns = array.shape[1]
-    groups = array.reshape(6, 3, 8, columns)
-    row = row_index((8, columns), 0)
-    out = []
-    for q in range(6):
-        for g in range(3):
-            out.append(jnp.where(row < 6, groups[q, g], 0.0))
-        last = jnp.where(row < 2, pltpu.roll(groups[q, 0], 2, 0), 0.0)
-        last = jnp.where((row >= 2) & (row < 4), pltpu.roll(groups[q, 1], 4, 0), last)
-        last = jnp.where((row >= 4) & (row < 6), pltpu.roll(groups[q, 2], 6, 0), last)
-        out.append(last)
-    return jnp.concatenate(out, axis=0)
-
-
 def per_head(pair):
     even = row_index(pair.shape, 1) < 64
     wide = pair.astype(F32)
@@ -166,17 +146,17 @@
             d_value = dot(probs_low, d_out)
             d_key = dot(d_scores, query)
             d_query = dot(d_scores, keys, ((0,), (0,)))
-            dqkv[rows, pair * 128 : (pair + 1) * 128] = d_query * SCORE_SCALE
+            dqkv[rows, pair * 128 : (pair + 1) * 128] = (d_query * SCORE_SCALE).astype(BF16)
             dqkv[rows, 512 + pair * 128 : 512 + (pair + 1) * 128] = (
                 jnp.where(lane < 64, d_key[:LEVEL_ROWS], d_key[LEVEL_ROWS:]) * SCORE_SCALE
-            )
+            ).astype(BF16)
             dqkv[rows, 1024 + pair * 128 : 1024 + (pair + 1) * 128] = jnp.where(
                 lane < 64, d_value[:LEVEL_ROWS], d_value[LEVEL_ROWS:]
-            )
+            ).astype(BF16)
 
 
 def input_gradient(dqkv, w_qkv, gain, normed, inv_std):
-    d_normed = dot(dqkv[...].astype(BF16), w_qkv[...]) * gain[...]
+    d_normed = dot(dqkv[...], w_qkv[...]) * gain[...]
     mean_plain = jnp.mean(d_normed, axis=-1, keepdims=True)
     mean_normed = jnp.mean(d_normed * normed, axis=-1, keepdims=True)
     return inv_std * (d_normed - mean_plain - normed * mean_normed)
@@ -191,10 +171,12 @@
 
 
 def first_kernel(
-    own, lon, lat, cor, w_qkv, w_proj, gain, bias,
-    skip, packed, fields, projected_out, att_out,
-    dqkv,
+    own, lon, lat, cor, w_qkv_ref, w_proj, gain, bias,
+    skip, inputs, fields, projected_out, att_out,
+    dqkv, w_qkv, sem,
 ):
+    fetch = pltpu.make_async_copy(w_qkv_ref, w_qkv, sem)
+    fetch.start()
     tiles_x, tiles_g = [], []
     labels = []
     row = row_index((8, FEATURES), 0)
@@ -211,8 +193,9 @@
     c = jnp.concatenate(tiles_g, axis=0)
     normed, inv_std = normalised(x)
     scaled = normed * gain[...]
-    packed[...] = pack_rows(scaled).astype(BF16)
-    projected = dot(scaled.astype(BF16), w_qkv[...], ((1,), (1,)))
+    inputs[...] = scaled.astype(BF16)
+    fetch.wait()
+    projected = dot(inputs[...], w_qkv[...], ((1,), (1,)))
     c_low = c.astype(BF16)
     d_first_value = dot(c_low, w_proj[...])
     fields[0] = x.astype(BF16)
@@ -244,17 +227,18 @@
         return probs
 
     attention_backward(probabilities, d_first_value.astype(BF16), projected_out, dqkv)
-    skip[...] = pack_rows(c + input_gradient(dqkv, w_qkv, gain, normed, inv_std)).astype(BF16)
+    skip[...] = (c + input_gradient(dqkv, w_qkv, gain, normed, inv_std)).astype(BF16)
 
 
 def second_kernel(
-    core, arrived, fields, projected, att, w_proj, w_qkv, gain,
-    kept, sent, near, far, dqkv,
+    core, arrived, inputs, fields, projected, att, w_proj, w_qkv_ref, gain,
+    kept, sent, near, far, dqkv, w_qkv, sem,
 ):
-    c2 = unpack_rows(arrived[...].astype(F32))
-    d_low = (dot(fields[1], w_proj[...]) + dot(c2.astype(BF16), w_proj[...])).astype(BF16)
+    fetch = pltpu.make_async_copy(w_qkv_ref, w_qkv, sem)
+    fetch.start()
+    d_low = (dot(fields[1], w_proj[...]) + dot(arrived[...], w_proj[...])).astype(BF16)
     attention_backward(lambda level, pair: att[level, pair].astype(F32), d_low, projected, dqkv)
-    lane = row_index((PACKED_ROWS, 128), 1)
+    lane = row_index((ROWS, 128), 1)
     is_first = core[0] == 0
     halves = []
 
@@ -264,7 +248,7 @@
 
     for t in range(4):
         first, middle, last = (
-            pack_rows(dqkv[:, 384 * t + 128 * j : 384 * t + 128 * (j + 1)]) for j in range(3)
+            dqkv[:, 384 * t + 128 * j : 384 * t + 128 * (j + 1)].astype(F32) for j in range(3)
         )
         halves.append(middle)
         share(slice(128 * t, 128 * (t + 1)), first, last)
@@ -273,10 +257,12 @@
         first = jnp.where(lane < 64, left, pltpu.roll(right, 64, 1))
         last = jnp.where(lane < 64, pltpu.roll(left, 64, 1), right)
         share(slice(512 + 128 * t, 512 + 128 * (t + 1)), first, last)
+    sent[:, 768:] = inputs[...]
 
     normed, inv_std = normalised(fields[0].astype(F32))
+    fetch.wait()
     shifted = input_gradient(dqkv, w_qkv, gain, normed, inv_std)
-    total = fields[1].astype(F32) + (c2 + shifted)
+    total = fields[1].astype(F32) + (arrived[...].astype(F32) + shifted)
     for i in range(6):
         for half, target in ((0, near), (1, far)):
             start = 16 * i + 8 * half
@@ -286,13 +272,9 @@
             target[i] = both.astype(BF16)
 
 
-def turn_kernel(inputs, other_inputs, out):
-    out[0] = inputs[...].astype(F32).T.astype(BF16)
-    out[1] = other_inputs[...].astype(F32).T.astype(BF16)
-
-
-def product_kernel(kept, got, inputs, out):
-    product = dot(inputs[0], kept[...]) + dot(inputs[1], got[...])
+def product_kernel(kept, inputs, got, out):
+    product = dot(inputs[...], kept[...], ((0,), (0,)))
+    product = product + dot(got[:, 768:], got[:, :768], ((0,), (0,)))
     bands = out.shape[1]
     width = FEATURES // bands
     lane = row_index((bands, width // 2, 128), 2)
@@ -374,9 +356,16 @@
     own, lon, lat, cor = call(
         cut_kernel,
         (piece,) * 4,
-        [pltpu.SMEM(lat_labels.shape, jnp.int32), pltpu.SemaphoreType.DMA],
-        places={0: pl.ANY},
-    )(lat_labels, x_in, out_grad)
+        [
+            pltpu.SMEM(lat_labels.shape, jnp.int32),
+            pltpu.VMEM((6, 12, 2, FEATURES), BF16),
+            pltpu.VMEM((6, 12, 2, FEATURES), BF16),
+            pltpu.SemaphoreType.DMA,
+            pltpu.SemaphoreType.DMA((2, 6)),
+        ],
+        places={0: pl.ANY, 1: pl.ANY, 2: pl.ANY},
+        limit=58 * MIB,
+    )(lat_labels, x_in[0].transpose(1, 2, 0, 3), out_grad[0].transpose(1, 2, 0, 3))
     lon = passed(lon, 0, -1)
     lat = passed(lat, -1, 0)
     cor = passed(cor, -1, -1)
@@ -387,38 +376,40 @@
         cost=pl.CostEstimate(flops=4_000_000_000, bytes_accessed=20_000_000, transcendentals=0),
     )(table)
 
-    scratch = [pltpu.VMEM((ROWS, 3 * FEATURES), F32)]
-    skip, packed, fields, projected, att = call(
+    scratch = [
+        pltpu.VMEM((ROWS, 3 * FEATURES), BF16),
+        pltpu.VMEM(w_qkv.shape, BF16),
+        pltpu.SemaphoreType.DMA,
+    ]
+    skip, inputs, fields, projected, att = call(
         first_kernel,
         (
-            struct((PACKED_ROWS, FEATURES), BF16),
-            struct((PACKED_ROWS, FEATURES), BF16),
+            struct((ROWS, FEATURES), BF16),
+            struct((ROWS, FEATURES), BF16),
             struct((2, ROWS, FEATURES), BF16),
             struct((ROWS, 3 * FEATURES), BF16),
             struct((2, 4, 2, LEVEL_ROWS, LEVEL_ROWS), BF16),
         ),
         scratch,
+        places={4: pl.ANY},
     )(own, lon, lat, cor, w_qkv, w_proj, norm_gain, bias)
 
     core = (lax.axis_index("lat") % 2).astype(jnp.int32).reshape(1)
     arrived = lax.ppermute(skip, "phase", [(1, 0)])
-    turned = call(turn_kernel, struct((2, FEATURES, PACKED_ROWS), BF16))(
-        packed, other_core(packed)
-    )
-    arrived, turned = lax.optimization_barrier((arrived, turned))
     back = struct((6, 16, FEATURES), BF16)
-    half = struct((PACKED_ROWS, 768), BF16)
+    half = struct((ROWS, 768), BF16)
+    half_and_inputs = struct((ROWS, 768 + FEATURES), BF16)
     kept, sent, near, far = call(
         second_kernel,
-        (half, half, back, back),
+        (half, half_and_inputs, back, back),
         scratch,
-        places={0: pltpu.SMEM},
-    )(core, arrived, fields, projected, att, w_proj, w_qkv, norm_gain)
+        places={0: pltpu.SMEM, 7: pl.ANY},
+    )(core, arrived, inputs, fields, projected, att, w_proj, w_qkv, norm_gain)
     got = other_core(sent)
     left = passed(far, 0, 1)
     rows = FEATURES * 3 // 2 // lons
     products = call(product_kernel, struct((lats // 2, lons, rows, 128), BF16))(
-        kept, got, turned
+        kept, inputs, got
     )
     chips = [[2 * x + c for x in range(lats // 2)] for c in range(2)]
     products = lax.all_to_all(products, "lat", 0, 0, tiled=True, axis_index_groups=chips)

time: 90.3 us -> 87.2 us (0.966)
  local copies, waits for them, and re-layouts: 5.42 us -> 1.62 us
  waiting for transfers between devices: 33.6 us -> 36 us
  starting transfers between devices: 37.1 us -> 35.4 us
    unnamed x19 -> x7, local copies, waits for them, and re-layouts: 4.63 us -> 0.83 us
    ppermute x2 -> x1, starting transfers between devices: 3.82 us -> 1.92 us  [other_core(): lax.ppermute(array, 'lat', [(a, a ^ 1) for a in range(lax.axis_size('lat'...]
    ppermute x1, waiting for transfers between devices: 5.59 us -> 7.12 us  [per_device(): arrived = lax.ppermute(skip, 'phase', [(1, 0)])]
    pallas_call x9 -> x8, Pallas kernels: 12.8 us -> 12.9 us  [run(): pl.pallas_call(kernel, out_shape=out_shape, in_specs=specs, out_specs=out...]
    ppermute x2 -> x1, waiting for transfers between devices: 1.81 us -> 1.83 us  [other_core(): lax.ppermute(array, 'lat', [(a, a ^ 1) for a in range(lax.axis_size('lat'...]
  transfers between devices with their start and end apart: 10 -> 9, of which waited for: 8 -> 7; matrix products, arithmetic and copies ran while one was open for 2% -> 2% of each run, Pallas kernels for 2% -> 1%
where the time goes in v6:
time: 87.2 us; the launch traced here: 86.7 us
  waiting for transfers between devices  36 us (41%)
  starting transfers between devices  35.4 us (41%)
  Pallas kernels  12.9 us (15%)
  local copies, waits for them, and re-layouts  1.62 us (2%)
    ppermute x5, waiting for transfers between devices, passed(): return lax.ppermute(array, ('lat', 'lon'), pairs)  19.2 us
    ppermute x5, starting transfers between devices, passed(): return lax.ppermute(array, ('lat', 'lon'), pairs)  19.1 us
    pallas_call x8, Pallas kernels, run(): pl.pallas_call(kernel, out_shape=out_shape, in_specs=specs, out_specs=out...  12.9 us
    all_to_all x1, starting transfers between devices, per_device(): slices = lax.all_to_all(slices, 'lon', 0, 0, tiled=True)  8.11 us
    all_to_all x1, waiting for transfers between devices, per_device(): slices = lax.all_to_all(slices, 'lon', 0, 0, tiled=True)  7.91 us
    ppermute x1, waiting for transfers between devices, per_device(): arrived = lax.ppermute(skip, 'phase', [(1, 0)])  7.12 us
    all_to_all x1, starting transfers between devices, per_device(): lax.all_to_all(products, 'lat', 0, 0, tiled=True, axis_index_groups=chips)  4.99 us
    ppermute x1, starting transfers between devices, other_core(): lax.ppermute(array, 'lat', [(a, a ^ 1) for a in range(lax.axis_size('lat'...  1.92 us
  transfers between devices with their start and end apart: 9, of which 7 were waited for; matrix products, arithmetic and copies ran while one was open for 2% of the time, Pallas kernels for 1%

profile of v6, /device:TPU:2, one launch (start us, length us, event | category | flops | bytes accessed | tf_op | source)
XLA Modules:
  0.0 86.7 jit_solution(8297588135425352118)
XLA Ops:
  0.6 1.9 %shard_map.86 = (bf16[2,3,16,512]{3,2,1,0:T(8,128)(2,1)}, bf16[2,3,16,512]{3,2,1,0:T(8,128)(2,1)}, bf16[2,3,16,512]{3,2,1,0:T(8,128)(2,1)}, bf16[2,3,16,512]{3,2,1,0:T(8,128)(2,1)}) custom-call(s32[6]{0:T(128)} %labels_ref.1, bf16[6,12,2,512]{3,2,1,0:T(2,128)(2,1)} %bitcast.16, bf16[6,12,2,512]{3,2,1,0:T(2,128)(2,1)} %bitcast.17), custom_call_target="tpu_custom_call" | custom-call | tf_op jit(solution)/shard_map/pallas_call | solution.py:35
  2.5 14.6 %collective-permute-start = (bf16[2,3,16,512]{3,2,1,0:T(8,128)(2,1)}, bf16[2,3,16,512]{3,2,1,0:T(8,128)(2,1)S(1)}, u32[]{:S(2)}, u32[]{:S(2)}) collective-permute-start(bf16[2,3,16,512]{3,2,1,0:T(8,128)(2,1)} %get-tuple-element.18), channel_id=1, source_target_pairs={{0,31},{1,0},{2,1},{3,2},{4,3},{5,4},{6,5},{7,6},{8,7},{9,8},{10,9... | collective-permute-start | bytes 294920 | tf_op jit(solution)/shard_map/ppermute | solution.py:345
  17.2 0.0 collective-permute-start.1
  17.2 2.5 %collective-permute-start.2 = (bf16[2,3,16,512]{3,2,1,0:T(8,128)(2,1)}, bf16[2,3,16,512]{3,2,1,0:T(8,128)(2,1)S(1)}, u32[]{:S(2)}, u32[]{:S(2)}) collective-permute-start(bf16[2,3,16,512]{3,2,1,0:T(8,128)(2,1)} %get-tuple-element.20), channel_id=1, source_target_pairs={{0,255},{1,224},{2,225},{3,226},{4,227},{5,228},{6,229},{7,230},{8... | collective-permute-start | bytes 294920 | tf_op jit(solution)/shard_map/ppermute | solution.py:345
  19.7 0.8 slice_bitcast_fusion
  20.5 0.0 copy-start
  20.5 0.0 copy-start.1
  20.5 0.0 copy-start.2
  20.5 0.5 shard_map.87.bias
  21.0 1.9 %collective-permute-done.lon = bf16[2,3,16,512]{3,2,1,0:T(8,128)(2,1)S(1)} collective-permute-done((bf16[2,3,16,512]{3,2,1,0:T(8,128)(2,1)}, bf16[2,3,16,512]{3,2,1,0:T(8,128)(2,1)S(1)}, u32[]{:S(2)}, u32[]{:S(2)}) %collective-permute-start) | collective-permute-done | bytes 98336 | tf_op jit(solution)/shard_map/ppermute | solution.py:345
  23.0 0.0 collective-permute-done.1.lat
  23.0 2.9 %collective-permute-done.2.cor = bf16[2,3,16,512]{3,2,1,0:T(8,128)(2,1)S(1)} collective-permute-done((bf16[2,3,16,512]{3,2,1,0:T(8,128)(2,1)}, bf16[2,3,16,512]{3,2,1,0:T(8,128)(2,1)S(1)}, u32[]{:S(2)}, u32[]{:S(2)}) %collective-permute-start.2) | collective-permute-done | bytes 98336 | tf_op jit(solution)/shard_map/ppermute | solution.py:345
  25.9 0.0 copy-done
  25.9 0.0 copy-done.1
  25.9 0.0 copy-done.2
  25.9 4.8 %shard_map.88 = (bf16[192,512]{1,0:T(8,128)(2,1)S(1)}, bf16[192,512]{1,0:T(8,128)(2,1)S(1)}, bf16[2,192,512]{2,1,0:T(8,128)(2,1)S(1)}, bf16[192,1536]{1,0:T(8,128)(2,1)S(1)}, bf16[2,4,2,96,96]{4,3,2,1,0:T(8,128)(2,1)S(1)}) custom-call(bf16[2,3,16,512]{3,2,1,0:T(8,128)(2,1)S(1)} %copy-done.1, bf16[2,3,16,512]{3,2,1,0:T(8,128)(2,1)S(1)} %collective-permute-done.lon, ...), custom_call_target="tpu_custom_call" | custom-call | tf_op jit(solution)/shard_map/pallas_call | solution.py:35
  30.7 1.3 %collective-permute-start.3 = (bf16[192,512]{1,0:T(8,128)(2,1)S(1)}, bf16[192,512]{1,0:T(8,128)(2,1)S(1)}, u32[]{:S(2)}, u32[]{:S(2)}) collective-permute-start(bf16[192,512]{1,0:T(8,128)(2,1)S(1)} %get-tuple-element.21), channel_id=1, source_target_pairs={{256,0},{257,1},{258,2},{259,3},{260,4},{261,5},{262,6},{263,7},{2... | collective-permute-start | bytes 589832 | tf_op jit(solution)/shard_map/ppermute | solution.py:398
  32.0 7.1 %collective-permute-done.3.arrived = bf16[192,512]{1,0:T(8,128)(2,1)S(1)} collective-permute-done((bf16[192,512]{1,0:T(8,128)(2,1)S(1)}, bf16[192,512]{1,0:T(8,128)(2,1)S(1)}, u32[]{:S(2)}, u32[]{:S(2)}) %collective-permute-start.3) | collective-permute-done | bytes 196640 | tf_op jit(solution)/shard_map/ppermute | solution.py:398
  39.1 2.7 %shard_map.89 = (bf16[192,768]{1,0:T(8,128)(2,1)S(1)}, bf16[192,1280]{1,0:T(8,128)(2,1)S(1)}, bf16[6,16,512]{2,1,0:T(8,128)(2,1)S(1)}, bf16[6,16,512]{2,1,0:T(8,128)(2,1)S(1)}) custom-call(s32[1]{0:T(128)} %bitcast.core.odd, bf16[192,512]{1,0:T(8,128)(2,1)S(1)} %collective-permute-done.3.arrived, bf16[192,512]{1,0:T(8,128)(2,1)S(1)} %get-tuple-element.22.inputs, ...), custom_call_target="tpu_custom_call" | custom-call | tf_op jit(solution)/shard_map/pallas_call | solution.py:35
  41.8 1.9 %collective-permute-start.5 = (bf16[192,1280]{1,0:T(8,128)(2,1)S(1)}, bf16[192,1280]{1,0:T(8,128)(2,1)S(1)}, u32[]{:S(2)}, u32[]{:S(2)}) collective-permute-start(bf16[192,1280]{1,0:T(8,128)(2,1)S(1)} %get-tuple-element.29), channel_id=1, source_target_pairs={{0,32},{32,0},{64,96},{96,64},{128,160},{160,128},{192,224},{224,1... | collective-permute-start | bytes 1474568 | tf_op jit(solution)/shard_map/ppermute | solution.py:349
  43.7 1.8 %collective-permute-done.5.got = bf16[192,1280]{1,0:T(8,128)(2,1)S(1)} collective-permute-done((bf16[192,1280]{1,0:T(8,128)(2,1)S(1)}, bf16[192,1280]{1,0:T(8,128)(2,1)S(1)}, u32[]{:S(2)}, u32[]{:S(2)}) %collective-permute-start.5) | collective-permute-done | bytes 491552 | tf_op jit(solution)/shard_map/ppermute | solution.py:349
  45.5 1.6 %shard_map.90 = bf16[4,32,24,128]{3,2,1,0:T(8,128)(2,1)} custom-call(bf16[192,768]{1,0:T(8,128)(2,1)S(1)} %get-tuple-element.28.kept, bf16[192,512]{1,0:T(8,128)(2,1)S(1)} %get-tuple-element.22.inputs, bf16[192,1280]{1,0:T(8,128)(2,1)S(1)} %collective-permute-done.5.got), custom_call_target="tpu_custom_call" | custom-call | tf_op jit(solution)/shard_map/pallas_call | solution.py:35
  47.1 5.0 %all-to-all-start = ((bf16[4,32,24,128]{3,2,1,0:T(8,128)(2,1)}), bf16[4,32,24,128]{3,2,1,0:T(8,128)(2,1)S(1)}, u32[]{:S(2)}, u32[]{:S(2)}) async-start(bf16[4,32,24,128]{3,2,1,0:T(8,128)(2,1)} %shard_map.90), calls=%async_computation | async-start | bytes 1572864 | tf_op jit(solution)/shard_map/all_to_all | solution.py:415
  52.1 1.9 %collective-permute-start.4 = (bf16[6,16,512]{2,1,0:T(8,128)(2,1)S(1)}, bf16[6,16,512]{2,1,0:T(8,128)(2,1)S(1)}, u32[]{:S(2)}, u32[]{:S(2)}) collective-permute-start(bf16[6,16,512]{2,1,0:T(8,128)(2,1)S(1)} %get-tuple-element.27), channel_id=1, source_target_pairs={{0,1},{1,2},{2,3},{3,4},{4,5},{5,6},{6,7},{7,8},{8,9},{9,10},{10,1... | collective-permute-start | bytes 294920 | tf_op jit(solution)/shard_map/ppermute | solution.py:345
  54.0 10.3 %collective-permute-done.4.left = bf16[6,16,512]{2,1,0:T(8,128)(2,1)S(1)} collective-permute-done((bf16[6,16,512]{2,1,0:T(8,128)(2,1)S(1)}, bf16[6,16,512]{2,1,0:T(8,128)(2,1)S(1)}, u32[]{:S(2)}, u32[]{:S(2)}) %collective-permute-start.4) | collective-permute-done | bytes 98336 | tf_op jit(solution)/shard_map/ppermute | solution.py:345
  64.3 0.0 all-to-all-done.products
  64.3 0.8 shard_map.91
  65.1 8.1 %all-to-all-start.1 = ((bf16[32,24,128]{2,1,0:T(8,128)(2,1)}), bf16[32,24,128]{2,1,0:T(8,128)(2,1)S(1)}, u32[]{:S(2)}, u32[]{:S(2)}) async-start(bf16[32,24,128]{2,1,0:T(8,128)(2,1)} %get-tuple-element.31), calls=%async_computation.1 | async-start | bytes 393216 | tf_op jit(solution)/shard_map/all_to_all | solution.py:422
  73.2 0.0 collective-permute-start.6
  73.2 4.0 %collective-permute-done.6.arrived = bf16[2,3,16,512]{3,2,1,0:T(8,128)(2,1)S(1)} collective-permute-done((bf16[2,3,16,512]{3,2,1,0:T(8,128)(2,1)S(1)}, bf16[2,3,16,512]{3,2,1,0:T(8,128)(2,1)S(1)}, u32[]{:S(2)}, u32[]{:S(2)}) %collective-permute-start.6) | collective-permute-done | bytes 98336 | tf_op jit(solution)/shard_map/ppermute | solution.py:345
  77.3 0.8 copy.9
  78.1 7.9 %all-to-all-done.1.parts = bf16[32,24,128]{2,1,0:T(8,128)(2,1)S(1)} async-done(((bf16[32,24,128]{2,1,0:T(8,128)(2,1)}), bf16[32,24,128]{2,1,0:T(8,128)(2,1)S(1)}, u32[]{:S(2)}, u32[]{:S(2)}) %all-to-all-start.1) | async-done | bytes 196640 | tf_op jit(solution)/shard_map/all_to_all | solution.py:422
  86.0 0.7 shard_map.93
  (2 shorter events, 0.0 us)
Async XLA Ops:
  2.5 20.4 %collective-permute-start = (bf16[2,3,16,512]{3,2,1,0:T(8,128)(2,1)}, bf16[2,3,16,512]{3,2,1,0:T(8,128)(2,1)S(1)}, u32[]{:S(2)}, u32[]{:S(2)}) collective-permute-start(bf16[2,3,16,512]{3,2,1,0:T(8,128)(2,1)} %get-tuple-element.18), channel_id=1, source_target_pairs={{0,31},{1,0},{2,1},{3,2},{4,3},{5,4},{6,5},{7,6},{8,7},{9,8},{10,9... | collective-permute-start | bytes 294920 | tf_op jit(solution)/shard_map/ppermute | solution.py:345
  17.2 5.8 %collective-permute-start.1 = (bf16[2,3,16,512]{3,2,1,0:T(8,128)(2,1)}, bf16[2,3,16,512]{3,2,1,0:T(8,128)(2,1)S(1)}, u32[]{:S(2)}, u32[]{:S(2)}) collective-permute-start(bf16[2,3,16,512]{3,2,1,0:T(8,128)(2,1)} %get-tuple-element.19), channel_id=1, source_target_pairs={{0,224},{1,225},{2,226},{3,227},{4,228},{5,229},{6,230},{7,231},{8... | collective-permute-start | bytes 294920 | tf_op jit(solution)/shard_map/ppermute | solution.py:345
  17.2 8.7 %collective-permute-start.2 = (bf16[2,3,16,512]{3,2,1,0:T(8,128)(2,1)}, bf16[2,3,16,512]{3,2,1,0:T(8,128)(2,1)S(1)}, u32[]{:S(2)}, u32[]{:S(2)}) collective-permute-start(bf16[2,3,16,512]{3,2,1,0:T(8,128)(2,1)} %get-tuple-element.20), channel_id=1, source_target_pairs={{0,255},{1,224},{2,225},{3,226},{4,227},{5,228},{6,229},{7,230},{8... | collective-permute-start | bytes 294920 | tf_op jit(solution)/shard_map/ppermute | solution.py:345
  20.5 5.4 %copy-start = (bf16[1,512,512]{2,1,0:T(8,128)(2,1)S(1)}, bf16[1,512,512]{2,1,0:T(8,128)(2,1)}, u32[]{:S(2)}) copy-start(bf16[1,512,512]{2,1,0:T(8,128)(2,1)} %param.10) | copy-start | bytes 1572868
  20.5 5.4 %copy-start.1 = (bf16[2,3,16,512]{3,2,1,0:T(8,128)(2,1)S(1)}, bf16[2,3,16,512]{3,2,1,0:T(8,128)(2,1)}, u32[]{:S(2)}) copy-start(bf16[2,3,16,512]{3,2,1,0:T(8,128)(2,1)} %get-tuple-element.17.own) | copy-start | bytes 294916
  20.5 5.4 %copy-start.2 = (f32[1,512]{1,0:T(1,128)S(1)}, f32[1,512]{1,0:T(1,128)}, u32[]{:S(2)}) copy-start(f32[1,512]{1,0:T(1,128)} %gain.3) | copy-start | bytes 6148
  30.7 8.4 %collective-permute-start.3 = (bf16[192,512]{1,0:T(8,128)(2,1)S(1)}, bf16[192,512]{1,0:T(8,128)(2,1)S(1)}, u32[]{:S(2)}, u32[]{:S(2)}) collective-permute-start(bf16[192,512]{1,0:T(8,128)(2,1)S(1)} %get-tuple-element.21), channel_id=1, source_target_pairs={{256,0},{257,1},{258,2},{259,3},{260,4},{261,5},{262,6},{263,7},{2... | collective-permute-start | bytes 589832 | tf_op jit(solution)/shard_map/ppermute | solution.py:398
  41.8 3.8 %collective-permute-start.5 = (bf16[192,1280]{1,0:T(8,128)(2,1)S(1)}, bf16[192,1280]{1,0:T(8,128)(2,1)S(1)}, u32[]{:S(2)}, u32[]{:S(2)}) collective-permute-start(bf16[192,1280]{1,0:T(8,128)(2,1)S(1)} %get-tuple-element.29), channel_id=1, source_target_pairs={{0,32},{32,0},{64,96},{96,64},{128,160},{160,128},{192,224},{224,1... | collective-permute-start | bytes 1474568 | tf_op jit(solution)/shard_map/ppermute | solution.py:349
  47.1 17.2 %all-to-all-start = ((bf16[4,32,24,128]{3,2,1,0:T(8,128)(2,1)}), bf16[4,32,24,128]{3,2,1,0:T(8,128)(2,1)S(1)}, u32[]{:S(2)}, u32[]{:S(2)}) async-start(bf16[4,32,24,128]{3,2,1,0:T(8,128)(2,1)} %shard_map.90), calls=%async_computation | async-start | bytes 1572864 | tf_op jit(solution)/shard_map/all_to_all | solution.py:415
  52.1 12.2 %collective-permute-start.4 = (bf16[6,16,512]{2,1,0:T(8,128)(2,1)S(1)}, bf16[6,16,512]{2,1,0:T(8,128)(2,1)S(1)}, u32[]{:S(2)}, u32[]{:S(2)}) collective-permute-start(bf16[6,16,512]{2,1,0:T(8,128)(2,1)S(1)} %get-tuple-element.27), channel_id=1, source_target_pairs={{0,1},{1,2},{2,3},{3,4},{4,5},{5,6},{6,7},{7,8},{8,9},{9,10},{10,1... | collective-permute-start | bytes 294920 | tf_op jit(solution)/shard_map/ppermute | solution.py:345
  65.1 20.9 %all-to-all-start.1 = ((bf16[32,24,128]{2,1,0:T(8,128)(2,1)}), bf16[32,24,128]{2,1,0:T(8,128)(2,1)S(1)}, u32[]{:S(2)}, u32[]{:S(2)}) async-start(bf16[32,24,128]{2,1,0:T(8,128)(2,1)} %get-tuple-element.31), calls=%async_computation.1 | async-start | bytes 393216 | tf_op jit(solution)/shard_map/all_to_all | solution.py:422
  73.2 4.1 %collective-permute-start.6 = (bf16[2,3,16,512]{3,2,1,0:T(8,128)(2,1)S(1)}, bf16[2,3,16,512]{3,2,1,0:T(8,128)(2,1)S(1)}, u32[]{:S(2)}, u32[]{:S(2)}) collective-permute-start(bf16[2,3,16,512]{3,2,1,0:T(8,128)(2,1)S(1)} %get-tuple-element.30), channel_id=1, source_target_pairs={{0,32},{1,33},{2,34},{3,35},{4,36},{5,37},{6,38},{7,39},{8,40},{9,... | collective-permute-start | bytes 294920 | tf_op jit(solution)/shard_map/ppermute | solution.py:345

commit v7 on v6

--- a/solution.py
+++ b/solution.py
@@ -18,6 +18,7 @@
 
 LEVEL_ROWS = 96
 ROWS = 192
+PACKED_ROWS = 144
 
 
 def call(kernel, out_shape, scratch=(), places=(), out_places=(), cost=None, limit=50 * MIB):
@@ -118,6 +119,18 @@
         moved = jnp.where(empty, MASKED, moved[:, :128])
         for h in range(HEADS):
             out[h * 96 + b * 16 : h * 96 + b * 16 + 16, :] = moved[h * 16 : h * 16 + 16, :]
+
+
+def pack_rows(array):
+    columns = array.shape[1]
+    groups = array.reshape(6, 4, 8, columns)
+    row = row_index((8, columns), 0)
+    out = []
+    for q in range(6):
+        last = groups[q, 3]
+        for g in range(3):
+            out.append(jnp.where(row < 6, groups[q, g], pltpu.roll(last, 6 - 2 * g, 0)))
+    return jnp.concatenate(out, axis=0)
 
 
 def per_head(pair):
@@ -193,9 +206,11 @@
     c = jnp.concatenate(tiles_g, axis=0)
     normed, inv_std = normalised(x)
     scaled = normed * gain[...]
-    inputs[...] = scaled.astype(BF16)
+    packed = pack_rows(scaled).astype(BF16)
+    for p in range(inputs.shape[0]):
+        inputs[p] = packed
     fetch.wait()
-    projected = dot(inputs[...], w_qkv[...], ((1,), (1,)))
+    projected = dot(scaled.astype(BF16), w_qkv[...], ((1,), (1,)))
     c_low = c.astype(BF16)
     d_first_value = dot(c_low, w_proj[...])
     fields[0] = x.astype(BF16)
@@ -231,34 +246,27 @@
 
 
 def second_kernel(
-    core, arrived, inputs, fields, projected, att, w_proj, w_qkv_ref, gain,
-    kept, sent, near, far, dqkv, w_qkv, sem,
+    arrived, fields, projected, att, w_proj, w_qkv_ref, gain,
+    blocks, near, far, dqkv, w_qkv, sem,
 ):
     fetch = pltpu.make_async_copy(w_qkv_ref, w_qkv, sem)
     fetch.start()
     d_low = (dot(fields[1], w_proj[...]) + dot(arrived[...], w_proj[...])).astype(BF16)
     attention_backward(lambda level, pair: att[level, pair].astype(F32), d_low, projected, dqkv)
-    lane = row_index((ROWS, 128), 1)
-    is_first = core[0] == 0
-    halves = []
-
-    def share(cols, first, last):
-        kept[:, cols] = jnp.where(is_first, first, last).astype(BF16)
-        sent[:, cols] = jnp.where(is_first, last, first).astype(BF16)
-
+    lane = row_index((80, 128), 1)
     for t in range(4):
-        first, middle, last = (
-            dqkv[:, 384 * t + 128 * j : 384 * t + 128 * (j + 1)].astype(F32) for j in range(3)
+        whole = [
+            pack_rows(dqkv[:, 384 * t + 128 * j : 384 * t + 128 * (j + 1)].astype(F32))
+            for j in range(3)
+        ]
+        blocks[2 * t, :144, :] = whole[0].astype(BF16)
+        blocks[2 * t + 1, :144, :] = whole[2].astype(BF16)
+        top = whole[1][:80]
+        bottom = jnp.concatenate([whole[1][80:], jnp.zeros((16, 128), F32)], axis=0)
+        blocks[2 * t, 144:, :] = jnp.where(lane < 64, top, pltpu.roll(bottom, 64, 1)).astype(BF16)
+        blocks[2 * t + 1, 144:, :] = jnp.where(lane < 64, pltpu.roll(top, 64, 1), bottom).astype(
+            BF16
         )
-        halves.append(middle)
-        share(slice(128 * t, 128 * (t + 1)), first, last)
-    for t in range(2):
-        left, right = halves[2 * t], halves[2 * t + 1]
-        first = jnp.where(lane < 64, left, pltpu.roll(right, 64, 1))
-        last = jnp.where(lane < 64, pltpu.roll(left, 64, 1), right)
-        share(slice(512 + 128 * t, 512 + 128 * (t + 1)), first, last)
-    sent[:, 768:] = inputs[...]
-
     normed, inv_std = normalised(fields[0].astype(F32))
     fetch.wait()
     shifted = input_gradient(dqkv, w_qkv, gain, normed, inv_std)
@@ -272,30 +280,28 @@
             target[i] = both.astype(BF16)
 
 
-def product_kernel(kept, inputs, got, out):
-    product = dot(inputs[...], kept[...], ((0,), (0,)))
-    product = product + dot(got[:, 768:], got[:, :768], ((0,), (0,)))
-    bands = out.shape[1]
+def product_kernel(core, blocks, inputs, other_inputs, near, left, out, upward):
+    whole = jnp.zeros((128, FEATURES), F32)
+    upper = jnp.zeros((128, FEATURES), F32)
+    lower = jnp.zeros((128, FEATURES), F32)
+    for x in range(inputs.shape[0]):
+        for cells, place in ((inputs, 2 * x + core[0]), (other_inputs, 2 * x + 1 - core[0])):
+            whole += dot(blocks[place, :144, :], cells[x], ((0,), (0,)))
+            folded = blocks[place, 144:, :]
+            upper += dot(folded, cells[x, :80, :], ((0,), (0,)))
+            lower += dot(folded[:64], cells[x, 80:, :], ((0,), (0,)))
+    half = upper[:64] + lower[64:]
+    whole_t = whole.T
+    half_t = jnp.concatenate([half, jnp.zeros((64, FEATURES), F32)], axis=0).T
+    bands = out.shape[0]
     width = FEATURES // bands
-    lane = row_index((bands, width // 2, 128), 2)
-    for t in range(4):
-        whole = product[:, 128 * t : 128 * (t + 1)].reshape(bands, width, 128)
-        out[t, :, :width, :] = whole.astype(BF16)
-        start = 512 + 128 * (t // 2)
-        half = product[:, start : start + 128].reshape(bands, width, 128)
-        top, bottom = half[:, : width // 2], half[:, width // 2 :]
-        if t % 2 == 0:
-            folded = jnp.where(lane < 64, top, pltpu.roll(bottom, 64, 2))
-        else:
-            folded = jnp.where(lane < 64, pltpu.roll(top, 64, 2), bottom)
-        out[t, :, width:, :] = folded.astype(BF16)
-
-
-def chips_kernel(products, near, left, out, upward):
-    total = products[0].astype(F32)
-    for t in range(1, products.shape[0]):
-        total = total + products[t].astype(F32)
-    out[...] = total.astype(BF16)
+    lane = row_index((width // 2, 128), 1)
+    for band in range(bands):
+        out[band, :width, :] = whole_t[band * width : (band + 1) * width].astype(BF16)
+        part = half_t[band * width : (band + 1) * width]
+        out[band, width:, :] = jnp.where(
+            lane < 64, part[: width // 2], pltpu.roll(part[width // 2 :], 64, 1)
+        ).astype(BF16)
     for i in range(3):
         upward[0, i] = left[3 + i]
         upward[1, i] = near[3 + i]
@@ -385,7 +391,7 @@
         first_kernel,
         (
             struct((ROWS, FEATURES), BF16),
-            struct((ROWS, FEATURES), BF16),
+            struct((lats // 2, PACKED_ROWS, FEATURES), BF16),
             struct((2, ROWS, FEATURES), BF16),
             struct((ROWS, 3 * FEATURES), BF16),
             struct((2, 4, 2, LEVEL_ROWS, LEVEL_ROWS), BF16),
@@ -395,28 +401,27 @@
     )(own, lon, lat, cor, w_qkv, w_proj, norm_gain, bias)
 
     core = (lax.axis_index("lat") % 2).astype(jnp.int32).reshape(1)
+    same_core = [[2 * x + c for x in range(lats // 2)] for c in range(2)]
     arrived = lax.ppermute(skip, "phase", [(1, 0)])
+    inputs = lax.all_to_all(inputs, "lat", 0, 0, tiled=True, axis_index_groups=same_core)
     back = struct((6, 16, FEATURES), BF16)
-    half = struct((ROWS, 768), BF16)
-    half_and_inputs = struct((ROWS, 768 + FEATURES), BF16)
-    kept, sent, near, far = call(
+    blocks, near, far = call(
         second_kernel,
-        (half, half_and_inputs, back, back),
+        (struct((lats, 224, 128), BF16), back, back),
         scratch,
-        places={0: pltpu.SMEM, 7: pl.ANY},
-    )(core, arrived, inputs, fields, projected, att, w_proj, w_qkv, norm_gain)
-    got = other_core(sent)
+        places={5: pl.ANY},
+        cost=pl.CostEstimate(flops=4_000_000_000, bytes_accessed=20_000_000, transcendentals=0),
+    )(arrived, fields, projected, att, w_proj, w_qkv, norm_gain)
+    blocks = lax.all_to_all(blocks, "lat", 0, 0, tiled=True)
+    inputs, near = lax.optimization_barrier((inputs, near))
+    other_inputs = other_core(inputs)
     left = passed(far, 0, 1)
     rows = FEATURES * 3 // 2 // lons
-    products = call(product_kernel, struct((lats // 2, lons, rows, 128), BF16))(
-        kept, inputs, got
-    )
-    chips = [[2 * x + c for x in range(lats // 2)] for c in range(2)]
-    products = lax.all_to_all(products, "lat", 0, 0, tiled=True, axis_index_groups=chips)
     slices, upward = call(
-        chips_kernel,
+        product_kernel,
         (struct((lons, rows, 128), BF16), struct((2, 3, 16, FEATURES), BF16)),
-    )(products, near, left)
+        places={0: pltpu.SMEM},
+    )(core, blocks, inputs, other_inputs, near, left)
     above = passed(upward, 1, 0)
     grad_input = call(join_kernel, struct((1, 2, 6, 12, FEATURES), BF16))(near, left, above)
     slices = lax.all_to_all(slices, "lon", 0, 0, tiled=True)

time: 87.2 us -> 87.9 us (level)
  the two profiles are of different devices: /device:TPU:2 before, /device:TPU:8 now
where the time goes in v7:
time: 87.9 us; the launch traced here: 87.3 us
  starting transfers between devices  39.1 us (44%)
  waiting for transfers between devices  33.1 us (38%)
  Pallas kernels  12.6 us (14%)
  local copies, waits for them, and re-layouts  1.62 us (2%)
    ppermute x5, starting transfers between devices, passed(): return lax.ppermute(array, ('lat', 'lon'), pairs)  20.4 us
    ppermute x5, waiting for transfers between devices, passed(): return lax.ppermute(array, ('lat', 'lon'), pairs)  18.9 us
    pallas_call x7, Pallas kernels, run(): pl.pallas_call(kernel, out_shape=out_shape, in_specs=specs, out_specs=out...  12.6 us
    all_to_all x1, waiting for transfers between devices, per_device(): slices = lax.all_to_all(slices, 'lon', 0, 0, tiled=True)  7.12 us
    all_to_all x1, waiting for transfers between devices, per_device(): lax.all_to_all(inputs, 'lat', 0, 0, tiled=True, axis_index_groups=same_core)  7.09 us
    all_to_all x1, starting transfers between devices, per_device(): slices = lax.all_to_all(slices, 'lon', 0, 0, tiled=True)  5.18 us
    ppermute x1, starting transfers between devices, per_device(): arrived = lax.ppermute(skip, 'phase', [(1, 0)])  4.54 us
    all_to_all x1, starting transfers between devices, per_device(): lax.all_to_all(inputs, 'lat', 0, 0, tiled=True, axis_index_groups=same_core)  3.57 us
  transfers between devices with their start and end apart: 10, of which 5 were waited for; matrix products, arithmetic and copies ran while one was open for 2% of the time, Pallas kernels for 4%

profile of v7, /device:TPU:8, one launch (start us, length us, event | category | flops | bytes accessed | tf_op | source)
XLA Modules:
  0.0 87.3 jit_solution(9457735952913569428)
XLA Ops:
  0.6 1.9 %shard_map.86 = (bf16[2,3,16,512]{3,2,1,0:T(8,128)(2,1)}, bf16[2,3,16,512]{3,2,1,0:T(8,128)(2,1)}, bf16[2,3,16,512]{3,2,1,0:T(8,128)(2,1)}, bf16[2,3,16,512]{3,2,1,0:T(8,128)(2,1)}) custom-call(s32[6]{0:T(128)} %labels_ref.1, bf16[6,12,2,512]{3,2,1,0:T(2,128)(2,1)} %bitcast.16, bf16[6,12,2,512]{3,2,1,0:T(2,128)(2,1)} %bitcast.17), custom_call_target="tpu_custom_call" | custom-call | tf_op jit(solution)/shard_map/pallas_call | solution.py:36
  2.5 13.7 %collective-permute-start = (bf16[2,3,16,512]{3,2,1,0:T(8,128)(2,1)}, bf16[2,3,16,512]{3,2,1,0:T(8,128)(2,1)S(1)}, u32[]{:S(2)}, u32[]{:S(2)}) collective-permute-start(bf16[2,3,16,512]{3,2,1,0:T(8,128)(2,1)} %get-tuple-element.19), channel_id=1, source_target_pairs={{0,31},{1,0},{2,1},{3,2},{4,3},{5,4},{6,5},{7,6},{8,7},{9,8},{10,9... | collective-permute-start | bytes 294920 | tf_op jit(solution)/shard_map/ppermute | solution.py:351
  16.3 1.9 %collective-permute-start.1 = (bf16[2,3,16,512]{3,2,1,0:T(8,128)(2,1)}, bf16[2,3,16,512]{3,2,1,0:T(8,128)(2,1)S(1)}, u32[]{:S(2)}, u32[]{:S(2)}) collective-permute-start(bf16[2,3,16,512]{3,2,1,0:T(8,128)(2,1)} %get-tuple-element.20), channel_id=1, source_target_pairs={{0,224},{1,225},{2,226},{3,227},{4,228},{5,229},{6,230},{7,231},{8... | collective-permute-start | bytes 294920 | tf_op jit(solution)/shard_map/ppermute | solution.py:351
  18.2 2.8 %collective-permute-start.2 = (bf16[2,3,16,512]{3,2,1,0:T(8,128)(2,1)}, bf16[2,3,16,512]{3,2,1,0:T(8,128)(2,1)S(1)}, u32[]{:S(2)}, u32[]{:S(2)}) collective-permute-start(bf16[2,3,16,512]{3,2,1,0:T(8,128)(2,1)} %get-tuple-element.21), channel_id=1, source_target_pairs={{0,255},{1,224},{2,225},{3,226},{4,227},{5,228},{6,229},{7,230},{8... | collective-permute-start | bytes 294920 | tf_op jit(solution)/shard_map/ppermute | solution.py:351
  21.1 0.8 slice_bitcast_fusion
  21.8 0.0 copy-start
  21.9 0.0 copy-start.1
  21.9 0.0 copy-start.2
  21.9 0.5 shard_map.87.bias
  22.3 0.0 collective-permute-done.lon
  22.4 0.0 collective-permute-done.1.lat
  22.4 2.1 %collective-permute-done.2.cor = bf16[2,3,16,512]{3,2,1,0:T(8,128)(2,1)S(1)} collective-permute-done((bf16[2,3,16,512]{3,2,1,0:T(8,128)(2,1)}, bf16[2,3,16,512]{3,2,1,0:T(8,128)(2,1)S(1)}, u32[]{:S(2)}, u32[]{:S(2)}) %collective-permute-start.2) | collective-permute-done | bytes 98336 | tf_op jit(solution)/shard_map/ppermute | solution.py:351
  24.4 0.0 copy-done
  24.4 0.0 copy-done.1
  24.4 0.0 copy-done.2
  24.4 4.8 %shard_map.88 = (bf16[192,512]{1,0:T(8,128)(2,1)S(1)}, bf16[4,144,512]{2,1,0:T(8,128)(2,1)}, bf16[2,192,512]{2,1,0:T(8,128)(2,1)S(1)}, bf16[192,1536]{1,0:T(8,128)(2,1)S(1)}, bf16[2,4,2,96,96]{4,3,2,1,0:T(8,128)(2,1)S(1)}) custom-call(bf16[2,3,16,512]{3,2,1,0:T(8,128)(2,1)S(1)} %copy-done.1, bf16[2,3,16,512]{3,2,1,0:T(8,128)(2,1)S(1)} %collective-permute-done.lon, ...), custom_call_target="tpu_custom_call" | custom-call | tf_op jit(solution)/shard_map/pallas_call | solution.py:36
  29.2 4.5 %collective-permute-start.3 = (bf16[192,512]{1,0:T(8,128)(2,1)S(1)}, bf16[192,512]{1,0:T(8,128)(2,1)S(1)}, u32[]{:S(2)}, u32[]{:S(2)}) collective-permute-start(bf16[192,512]{1,0:T(8,128)(2,1)S(1)} %get-tuple-element.23), channel_id=1, source_target_pairs={{256,0},{257,1},{258,2},{259,3},{260,4},{261,5},{262,6},{263,7},{2... | collective-permute-start | bytes 589832 | tf_op jit(solution)/shard_map/ppermute | solution.py:405
  33.8 3.6 %all-to-all-start = ((bf16[4,144,512]{2,1,0:T(8,128)(2,1)}), bf16[4,144,512]{2,1,0:T(8,128)(2,1)S(1)}, u32[]{:S(2)}, u32[]{:S(2)}) async-start(bf16[4,144,512]{2,1,0:T(8,128)(2,1)} %get-tuple-element.22), calls=%async_computation | async-start | bytes 1179648 | tf_op jit(solution)/shard_map/all_to_all | solution.py:406
  37.4 0.0 collective-permute-done.3.arrived
  37.4 2.8 %shard_map.89 = (bf16[8,224,128]{2,1,0:T(8,128)(2,1)}, bf16[6,16,512]{2,1,0:T(8,128)(2,1)S(1)}, bf16[6,16,512]{2,1,0:T(8,128)(2,1)S(1)}) custom-call(bf16[192,512]{1,0:T(8,128)(2,1)S(1)} %collective-permute-done.3.arrived, bf16[2,192,512]{2,1,0:T(8,128)(2,1)S(1)} %get-tuple-element.24.fields, bf16[192,1536]{1,0:T(8,128)(2,1)S(1)} %get-tuple-element.25.projected, ...), custom_call_target="tpu_custom_call" | custom-call | flops 4000000000 | bytes 20000000 | tf_op jit(solution)/shard_map/pallas_call | solution.py:36
  40.2 7.1 %all-to-all-done.inputs = bf16[4,144,512]{2,1,0:T(8,128)(2,1)S(1)} async-done(((bf16[4,144,512]{2,1,0:T(8,128)(2,1)}), bf16[4,144,512]{2,1,0:T(8,128)(2,1)S(1)}, u32[]{:S(2)}, u32[]{:S(2)}) %all-to-all-start) | async-done | bytes 589856 | tf_op jit(solution)/shard_map/all_to_all | solution.py:406
  47.3 1.9 %collective-permute-start.5 = (bf16[4,144,512]{2,1,0:T(8,128)(2,1)S(1)}, bf16[4,144,512]{2,1,0:T(8,128)(2,1)S(1)}, u32[]{:S(2)}, u32[]{:S(2)}) collective-permute-start(bf16[4,144,512]{2,1,0:T(8,128)(2,1)S(1)} %all-to-all-done.inputs), channel_id=1, source_target_pairs={{0,32},{32,0},{64,96},{96,64},{128,160},{160,128},{192,224},{224,1... | collective-permute-start | bytes 1769480 | tf_op jit(solution)/shard_map/ppermute | solution.py:355
  49.2 3.5 %all-to-all-start.1 = ((bf16[8,224,128]{2,1,0:T(8,128)(2,1)}), bf16[8,224,128]{2,1,0:T(8,128)(2,1)S(1)}, u32[]{:S(2)}, u32[]{:S(2)}) async-start(bf16[8,224,128]{2,1,0:T(8,128)(2,1)} %get-tuple-element.30), calls=%async_computation.1 | async-start | bytes 917504 | tf_op jit(solution)/shard_map/all_to_all | solution.py:415
  52.7 1.9 %collective-permute-start.4 = (bf16[6,16,512]{2,1,0:T(8,128)(2,1)S(1)}, bf16[6,16,512]{2,1,0:T(8,128)(2,1)S(1)}, u32[]{:S(2)}, u32[]{:S(2)}) collective-permute-start(bf16[6,16,512]{2,1,0:T(8,128)(2,1)S(1)} %get-tuple-element.29), channel_id=1, source_target_pairs={{0,1},{1,2},{2,3},{3,4},{4,5},{5,6},{6,7},{7,8},{8,9},{9,10},{10,1... | collective-permute-start | bytes 294920 | tf_op jit(solution)/shard_map/ppermute | solution.py:351
  54.7 11.6 %collective-permute-done.4.left = bf16[6,16,512]{2,1,0:T(8,128)(2,1)S(1)} collective-permute-done((bf16[6,16,512]{2,1,0:T(8,128)(2,1)S(1)}, bf16[6,16,512]{2,1,0:T(8,128)(2,1)S(1)}, u32[]{:S(2)}, u32[]{:S(2)}) %collective-permute-start.4) | collective-permute-done | bytes 98336 | tf_op jit(solution)/shard_map/ppermute | solution.py:351
  66.3 0.0 all-to-all-done.1.blocks
  66.3 0.0 collective-permute-done.5.other_inputs
  66.3 1.9 %shard_map.90 = (bf16[32,24,128]{2,1,0:T(8,128)(2,1)}, bf16[2,3,16,512]{3,2,1,0:T(8,128)(2,1)S(1)}) custom-call(s32[1]{0:T(128)} %bitcast.7.core.odd, bf16[8,224,128]{2,1,0:T(8,128)(2,1)S(1)} %all-to-all-done.1.blocks, bf16[4,144,512]{2,1,0:T(8,128)(2,1)S(1)} %all-to-all-done.inputs, bf16[4,144,512]{2,1,0:T(8,128)(2,1)S(1)} %collective-permute-done.5.other_inputs, ...), custom_call_target="tpu_custom_call" | custom-call | tf_op jit(solution)/shard_map/pallas_call | solution.py:36
  68.1 5.2 %all-to-all-start.2 = ((bf16[32,24,128]{2,1,0:T(8,128)(2,1)}), bf16[32,24,128]{2,1,0:T(8,128)(2,1)S(1)}, u32[]{:S(2)}, u32[]{:S(2)}) async-start(bf16[32,24,128]{2,1,0:T(8,128)(2,1)} %get-tuple-element.33), calls=%async_computation.2 | async-start | bytes 393216 | tf_op jit(solution)/shard_map/all_to_all | solution.py:427
  73.3 0.0 collective-permute-start.6
  73.4 5.2 %collective-permute-done.6.arrived = bf16[2,3,16,512]{3,2,1,0:T(8,128)(2,1)S(1)} collective-permute-done((bf16[2,3,16,512]{3,2,1,0:T(8,128)(2,1)S(1)}, bf16[2,3,16,512]{3,2,1,0:T(8,128)(2,1)S(1)}, u32[]{:S(2)}, u32[]{:S(2)}) %collective-permute-start.6) | collective-permute-done | bytes 98336 | tf_op jit(solution)/shard_map/ppermute | solution.py:351
  78.6 0.8 copy.9
  79.5 7.1 %all-to-all-done.2.parts = bf16[32,24,128]{2,1,0:T(8,128)(2,1)S(1)} async-done(((bf16[32,24,128]{2,1,0:T(8,128)(2,1)}), bf16[32,24,128]{2,1,0:T(8,128)(2,1)S(1)}, u32[]{:S(2)}, u32[]{:S(2)}) %all-to-all-start.2) | async-done | bytes 196640 | tf_op jit(solution)/shard_map/all_to_all | solution.py:427
  86.6 0.7 shard_map.92
  (2 shorter events, 0.0 us)
Async XLA Ops:
  2.5 19.8 %collective-permute-start = (bf16[2,3,16,512]{3,2,1,0:T(8,128)(2,1)}, bf16[2,3,16,512]{3,2,1,0:T(8,128)(2,1)S(1)}, u32[]{:S(2)}, u32[]{:S(2)}) collective-permute-start(bf16[2,3,16,512]{3,2,1,0:T(8,128)(2,1)} %get-tuple-element.19), channel_id=1, source_target_pairs={{0,31},{1,0},{2,1},{3,2},{4,3},{5,4},{6,5},{7,6},{8,7},{9,8},{10,9... | collective-permute-start | bytes 294920 | tf_op jit(solution)/shard_map/ppermute | solution.py:351
  16.3 6.1 %collective-permute-start.1 = (bf16[2,3,16,512]{3,2,1,0:T(8,128)(2,1)}, bf16[2,3,16,512]{3,2,1,0:T(8,128)(2,1)S(1)}, u32[]{:S(2)}, u32[]{:S(2)}) collective-permute-start(bf16[2,3,16,512]{3,2,1,0:T(8,128)(2,1)} %get-tuple-element.20), channel_id=1, source_target_pairs={{0,224},{1,225},{2,226},{3,227},{4,228},{5,229},{6,230},{7,231},{8... | collective-permute-start | bytes 294920 | tf_op jit(solution)/shard_map/ppermute | solution.py:351
  18.2 6.2 %collective-permute-start.2 = (bf16[2,3,16,512]{3,2,1,0:T(8,128)(2,1)}, bf16[2,3,16,512]{3,2,1,0:T(8,128)(2,1)S(1)}, u32[]{:S(2)}, u32[]{:S(2)}) collective-permute-start(bf16[2,3,16,512]{3,2,1,0:T(8,128)(2,1)} %get-tuple-element.21), channel_id=1, source_target_pairs={{0,255},{1,224},{2,225},{3,226},{4,227},{5,228},{6,229},{7,230},{8... | collective-permute-start | bytes 294920 | tf_op jit(solution)/shard_map/ppermute | solution.py:351
  21.8 2.6 %copy-start = (bf16[1,512,512]{2,1,0:T(8,128)(2,1)S(1)}, bf16[1,512,512]{2,1,0:T(8,128)(2,1)}, u32[]{:S(2)}) copy-start(bf16[1,512,512]{2,1,0:T(8,128)(2,1)} %param.10) | copy-start | bytes 1572868
  21.9 2.6 %copy-start.1 = (bf16[2,3,16,512]{3,2,1,0:T(8,128)(2,1)S(1)}, bf16[2,3,16,512]{3,2,1,0:T(8,128)(2,1)}, u32[]{:S(2)}) copy-start(bf16[2,3,16,512]{3,2,1,0:T(8,128)(2,1)} %get-tuple-element.18.own) | copy-start | bytes 294916
  21.9 2.6 %copy-start.2 = (f32[1,512]{1,0:T(1,128)S(1)}, f32[1,512]{1,0:T(1,128)}, u32[]{:S(2)}) copy-start(f32[1,512]{1,0:T(1,128)} %gain.3) | copy-start | bytes 6148
  29.2 8.1 %collective-permute-start.3 = (bf16[192,512]{1,0:T(8,128)(2,1)S(1)}, bf16[192,512]{1,0:T(8,128)(2,1)S(1)}, u32[]{:S(2)}, u32[]{:S(2)}) collective-permute-start(bf16[192,512]{1,0:T(8,128)(2,1)S(1)} %get-tuple-element.23), channel_id=1, source_target_pairs={{256,0},{257,1},{258,2},{259,3},{260,4},{261,5},{262,6},{263,7},{2... | collective-permute-start | bytes 589832 | tf_op jit(solution)/shard_map/ppermute | solution.py:405
  33.8 13.5 %all-to-all-start = ((bf16[4,144,512]{2,1,0:T(8,128)(2,1)}), bf16[4,144,512]{2,1,0:T(8,128)(2,1)S(1)}, u32[]{:S(2)}, u32[]{:S(2)}) async-start(bf16[4,144,512]{2,1,0:T(8,128)(2,1)} %get-tuple-element.22), calls=%async_computation | async-start | bytes 1179648 | tf_op jit(solution)/shard_map/all_to_all | solution.py:406
  47.3 19.0 %collective-permute-start.5 = (bf16[4,144,512]{2,1,0:T(8,128)(2,1)S(1)}, bf16[4,144,512]{2,1,0:T(8,128)(2,1)S(1)}, u32[]{:S(2)}, u32[]{:S(2)}) collective-permute-start(bf16[4,144,512]{2,1,0:T(8,128)(2,1)S(1)} %all-to-all-done.inputs), channel_id=1, source_target_pairs={{0,32},{32,0},{64,96},{96,64},{128,160},{160,128},{192,224},{224,1... | collective-permute-start | bytes 1769480 | tf_op jit(solution)/shard_map/ppermute | solution.py:355
  49.2 17.1 %all-to-all-start.1 = ((bf16[8,224,128]{2,1,0:T(8,128)(2,1)}), bf16[8,224,128]{2,1,0:T(8,128)(2,1)S(1)}, u32[]{:S(2)}, u32[]{:S(2)}) async-start(bf16[8,224,128]{2,1,0:T(8,128)(2,1)} %get-tuple-element.30), calls=%async_computation.1 | async-start | bytes 917504 | tf_op jit(solution)/shard_map/all_to_all | solution.py:415
  52.7 13.6 %collective-permute-start.4 = (bf16[6,16,512]{2,1,0:T(8,128)(2,1)S(1)}, bf16[6,16,512]{2,1,0:T(8,128)(2,1)S(1)}, u32[]{:S(2)}, u32[]{:S(2)}) collective-permute-start(bf16[6,16,512]{2,1,0:T(8,128)(2,1)S(1)} %get-tuple-element.29), channel_id=1, source_target_pairs={{0,1},{1,2},{2,3},{3,4},{4,5},{5,6},{6,7},{7,8},{8,9},{9,10},{10,1... | collective-permute-start | bytes 294920 | tf_op jit(solution)/shard_map/ppermute | solution.py:351
  68.1 18.4 %all-to-all-start.2 = ((bf16[32,24,128]{2,1,0:T(8,128)(2,1)}), bf16[32,24,128]{2,1,0:T(8,128)(2,1)S(1)}, u32[]{:S(2)}, u32[]{:S(2)}) async-start(bf16[32,24,128]{2,1,0:T(8,128)(2,1)} %get-tuple-element.33), calls=%async_computation.2 | async-start | bytes 393216 | tf_op jit(solution)/shard_map/all_to_all | solution.py:427
  73.3 5.3 %collective-permute-start.6 = (bf16[2,3,16,512]{3,2,1,0:T(8,128)(2,1)S(1)}, bf16[2,3,16,512]{3,2,1,0:T(8,128)(2,1)S(1)}, u32[]{:S(2)}, u32[]{:S(2)}) collective-permute-start(bf16[2,3,16,512]{3,2,1,0:T(8,128)(2,1)S(1)} %get-tuple-element.32), channel_id=1, source_target_pairs={{0,32},{1,33},{2,34},{3,35},{4,36},{5,37},{6,38},{7,39},{8,40},{9,... | collective-permute-start | bytes 294920 | tf_op jit(solution)/shard_map/ppermute | solution.py:351

commit v8 on v7

--- a/solution.py
+++ b/solution.py
@@ -207,8 +207,7 @@
     normed, inv_std = normalised(x)
     scaled = normed * gain[...]
     packed = pack_rows(scaled).astype(BF16)
-    for p in range(inputs.shape[0]):
-        inputs[p] = packed
+    inputs[...] = packed
     fetch.wait()
     projected = dot(scaled.astype(BF16), w_qkv[...], ((1,), (1,)))
     c_low = c.astype(BF16)
@@ -247,7 +246,7 @@
 
 def second_kernel(
     arrived, fields, projected, att, w_proj, w_qkv_ref, gain,
-    blocks, near, far, dqkv, w_qkv, sem,
+    blocks, kept, up, dqkv, w_qkv, sem,
 ):
     fetch = pltpu.make_async_copy(w_qkv_ref, w_qkv, sem)
     fetch.start()
@@ -272,24 +271,35 @@
     shifted = input_gradient(dqkv, w_qkv, gain, normed, inv_std)
     total = fields[1].astype(F32) + (arrived[...].astype(F32) + shifted)
     for i in range(6):
-        for half, target in ((0, near), (1, far)):
+        for half in range(2):
             start = 16 * i + 8 * half
             both = jnp.concatenate(
                 [total[start : start + 8], total[96 + start : 96 + start + 8]], axis=0
             )
-            target[i] = both.astype(BF16)
-
-
-def product_kernel(core, blocks, inputs, other_inputs, near, left, out, upward):
+            (kept, up)[i // 3][half, i % 3] = both.astype(BF16)
+
+
+def stack_kernel(a, b, c, d, kept, low, high):
+    low[0], low[1], high[0], high[1] = a[...], b[...], c[...], d[...]
+
+
+def product_kernel(
+    lat_index, blocks, low, high, other_low, other_high, kept, above, out, sideways
+):
     whole = jnp.zeros((128, FEATURES), F32)
     upper = jnp.zeros((128, FEATURES), F32)
     lower = jnp.zeros((128, FEATURES), F32)
-    for x in range(inputs.shape[0]):
-        for cells, place in ((inputs, 2 * x + core[0]), (other_inputs, 2 * x + 1 - core[0])):
-            whole += dot(blocks[place, :144, :], cells[x], ((0,), (0,)))
+    lats = blocks.shape[0]
+    for x in range(lats // 2):
+        inputs, other_inputs = (low, other_low) if x < 2 else (high, other_high)
+        first = lat_index[0] + 2 * x
+        first = jnp.where(first >= lats, first - lats, first)
+        second = first + 1 - 2 * lax.rem(lat_index[0], 2)
+        for cells, place in ((inputs, first), (other_inputs, second)):
+            whole += dot(blocks[place, :144, :], cells[x % 2], ((0,), (0,)))
             folded = blocks[place, 144:, :]
-            upper += dot(folded, cells[x, :80, :], ((0,), (0,)))
-            lower += dot(folded[:64], cells[x, 80:, :], ((0,), (0,)))
+            upper += dot(folded, cells[x % 2, :80, :], ((0,), (0,)))
+            lower += dot(folded[:64], cells[x % 2, 80:, :], ((0,), (0,)))
     half = upper[:64] + lower[64:]
     whole_t = whole.T
     half_t = jnp.concatenate([half, jnp.zeros((64, FEATURES), F32)], axis=0).T
@@ -303,11 +313,11 @@
             lane < 64, part[: width // 2], pltpu.roll(part[width // 2 :], 64, 1)
         ).astype(BF16)
     for i in range(3):
-        upward[0, i] = left[3 + i]
-        upward[1, i] = near[3 + i]
-
-
-def sum_kernel(odd, parts, out):
+        sideways[i] = above[1, i]
+        sideways[3 + i] = kept[1, i]
+
+
+def sum_kernel(lat_index, parts, out):
     bands, rows, _ = parts.shape
     width = rows * 2 // 3
     total = parts[0].astype(F32)
@@ -318,23 +328,23 @@
     half = jnp.concatenate([folded, pltpu.roll(folded, 64, 1)], axis=0)
     half = half[:, :64]
 
-    @pl.when(odd[0] == 0)
+    @pl.when(lax.rem(lat_index[0], 2) == 0)
     def _():
         out[0, :, :128] = whole
         out[0, :, 128:] = half
 
-    @pl.when(odd[0] == 1)
+    @pl.when(lax.rem(lat_index[0], 2) == 1)
     def _():
         out[0, :, :64] = half
         out[0, :, 64:] = whole
 
 
-def join_kernel(near, left, arrived, out):
+def join_kernel(kept, above, left, out):
     row = row_index((8, FEATURES), 0)
     for level in range(2):
         part = slice(level * 8, level * 8 + 8)
         for i in range(6):
-            low, high = (arrived[0, i], arrived[1, i]) if i < 3 else (left[i - 3], near[i - 3])
+            low, high = left[i], above[0, i] if i < 3 else kept[0, i - 3]
             low = low.astype(F32)[part]
             high = pltpu.roll(high.astype(F32)[part], 6, 0)
             out[0, level, i, 0:8, :] = jnp.where(row < 6, low, high).astype(BF16)
@@ -391,7 +401,7 @@
         first_kernel,
         (
             struct((ROWS, FEATURES), BF16),
-            struct((lats // 2, PACKED_ROWS, FEATURES), BF16),
+            struct((PACKED_ROWS, FEATURES), BF16),
             struct((2, ROWS, FEATURES), BF16),
             struct((ROWS, 3 * FEATURES), BF16),
             struct((2, 4, 2, LEVEL_ROWS, LEVEL_ROWS), BF16),
@@ -400,12 +410,11 @@
         places={4: pl.ANY},
     )(own, lon, lat, cor, w_qkv, w_proj, norm_gain, bias)
 
-    core = (lax.axis_index("lat") % 2).astype(jnp.int32).reshape(1)
-    same_core = [[2 * x + c for x in range(lats // 2)] for c in range(2)]
+    lat_index = lax.axis_index("lat").astype(jnp.int32).reshape(1)
     arrived = lax.ppermute(skip, "phase", [(1, 0)])
-    inputs = lax.all_to_all(inputs, "lat", 0, 0, tiled=True, axis_index_groups=same_core)
-    back = struct((6, 16, FEATURES), BF16)
-    blocks, near, far = call(
+    along = [inputs] + [passed(inputs, -2 * x, 0) for x in range(1, lats // 2)]
+    back = struct((2, 3, 16, FEATURES), BF16)
+    blocks, kept, up = call(
         second_kernel,
         (struct((lats, 224, 128), BF16), back, back),
         scratch,
@@ -413,21 +422,22 @@
         cost=pl.CostEstimate(flops=4_000_000_000, bytes_accessed=20_000_000, transcendentals=0),
     )(arrived, fields, projected, att, w_proj, w_qkv, norm_gain)
     blocks = lax.all_to_all(blocks, "lat", 0, 0, tiled=True)
-    inputs, near = lax.optimization_barrier((inputs, near))
-    other_inputs = other_core(inputs)
-    left = passed(far, 0, 1)
+    two = struct((2, PACKED_ROWS, FEATURES), BF16)
+    low, high = call(stack_kernel, (two, two), places={4: pl.ANY})(*along, kept)
+    other_low, other_high = other_core(low), other_core(high)
+    above = passed(up, 1, 0)
     rows = FEATURES * 3 // 2 // lons
-    slices, upward = call(
+    slices, sideways = call(
         product_kernel,
-        (struct((lons, rows, 128), BF16), struct((2, 3, 16, FEATURES), BF16)),
+        (struct((lons, rows, 128), BF16), struct((6, 16, FEATURES), BF16)),
         places={0: pltpu.SMEM},
-    )(core, blocks, inputs, other_inputs, near, left)
-    above = passed(upward, 1, 0)
-    grad_input = call(join_kernel, struct((1, 2, 6, 12, FEATURES), BF16))(near, left, above)
+    )(lat_index, blocks, low, high, other_low, other_high, kept, above)
+    left = passed(sideways, 0, 1)
+    grad_input = call(join_kernel, struct((1, 2, 6, 12, FEATURES), BF16))(kept, above, left)
     slices = lax.all_to_all(slices, "lon", 0, 0, tiled=True)
     grad_qkv = call(
         sum_kernel, struct((1, FEATURES // lons, 192), F32), places={0: pltpu.SMEM}
-    )(core, slices)
+    )(lat_index, slices)
     return grad_input, grad_qkv.transpose(0, 2, 1)
 
 

time: 87.9 us -> 85.8 us (0.976)
  waiting for transfers between devices: 33.1 us -> 17.1 us
  starting transfers between devices: 39.1 us -> 53 us
    ppermute x5 -> x8, starting transfers between devices: 20.4 us -> 32.1 us  [passed(): return lax.ppermute(array, ('lat', 'lon'), pairs)]
    all_to_all x1, waiting for transfers between devices: 7.12 us -> 0.01 us  [per_device(): slices = lax.all_to_all(slices, 'lon', 0, 0, tiled=True)]
    all_to_all x1 -> x0, waiting for transfers between devices: 7.09 us -> none  [per_device(): lax.all_to_all(inputs, 'lat', 0, 0, tiled=True, axis_index_groups=same_core)]
    all_to_all x1 -> x0, starting transfers between devices: 3.57 us -> none  [per_device(): lax.all_to_all(inputs, 'lat', 0, 0, tiled=True, axis_index_groups=same_core)]
    all_to_all x1, starting transfers between devices: 5.18 us -> 8.28 us  [per_device(): slices = lax.all_to_all(slices, 'lon', 0, 0, tiled=True)]
    ppermute x1 -> x2, starting transfers between devices: 1.91 us -> 4.33 us  [other_core(): lax.ppermute(array, 'lat', [(a, a ^ 1) for a in range(lax.axis_size('lat'...]
    ppermute x5 -> x8, waiting for transfers between devices: 18.9 us -> 17.1 us  [passed(): return lax.ppermute(array, ('lat', 'lon'), pairs)]
    pallas_call x7 -> x8, Pallas kernels: 12.6 us -> 12.6 us  [run(): pl.pallas_call(kernel, out_shape=out_shape, in_specs=specs, out_specs=out...]
  transfers between devices with their start and end apart: 10 -> 13, of which waited for: 5 -> 3; matrix products, arithmetic and copies ran while one was open for 2% -> 2% of each run, Pallas kernels for 4% -> 4%
where the time goes in v8:
time: 85.8 us; the launch traced here: 85.2 us
  starting transfers between devices  53 us (62%)
  waiting for transfers between devices  17.1 us (20%)
  Pallas kernels  12.6 us (15%)
  local copies, waits for them, and re-layouts  1.62 us (2%)
    ppermute x8, starting transfers between devices, passed(): return lax.ppermute(array, ('lat', 'lon'), pairs)  32.1 us
    ppermute x8, waiting for transfers between devices, passed(): return lax.ppermute(array, ('lat', 'lon'), pairs)  17.1 us
    pallas_call x8, Pallas kernels, run(): pl.pallas_call(kernel, out_shape=out_shape, in_specs=specs, out_specs=out...  12.6 us
    all_to_all x1, starting transfers between devices, per_device(): slices = lax.all_to_all(slices, 'lon', 0, 0, tiled=True)  8.28 us
    ppermute x1, starting transfers between devices, per_device(): arrived = lax.ppermute(skip, 'phase', [(1, 0)])  4.54 us
    ppermute x2, starting transfers between devices, other_core(): lax.ppermute(array, 'lat', [(a, a ^ 1) for a in range(lax.axis_size('lat'...  4.33 us
    all_to_all x1, starting transfers between devices, per_device(): blocks = lax.all_to_all(blocks, 'lat', 0, 0, tiled=True)  3.74 us
  transfers between devices with their start and end apart: 13, of which 3 were waited for; matrix products, arithmetic and copies ran while one was open for 2% of the time, Pallas kernels for 4%

profile of v8, /device:TPU:8, one launch (start us, length us, event | category | flops | bytes accessed | tf_op | source)
XLA Modules:
  0.0 85.2 jit_solution(12870200396316433818)
XLA Ops:
  0.6 1.9 %shard_map.86 = (bf16[2,3,16,512]{3,2,1,0:T(8,128)(2,1)}, bf16[2,3,16,512]{3,2,1,0:T(8,128)(2,1)}, bf16[2,3,16,512]{3,2,1,0:T(8,128)(2,1)}, bf16[2,3,16,512]{3,2,1,0:T(8,128)(2,1)}) custom-call(s32[6]{0:T(128)} %labels_ref.1, bf16[6,12,2,512]{3,2,1,0:T(2,128)(2,1)} %bitcast.16, bf16[6,12,2,512]{3,2,1,0:T(2,128)(2,1)} %bitcast.17), custom_call_target="tpu_custom_call" | custom-call | tf_op jit(solution)/shard_map/pallas_call | solution.py:36
  2.5 13.7 %collective-permute-start = (bf16[2,3,16,512]{3,2,1,0:T(8,128)(2,1)}, bf16[2,3,16,512]{3,2,1,0:T(8,128)(2,1)S(1)}, u32[]{:S(2)}, u32[]{:S(2)}) collective-permute-start(bf16[2,3,16,512]{3,2,1,0:T(8,128)(2,1)} %get-tuple-element.19), channel_id=1, source_target_pairs={{0,31},{1,0},{2,1},{3,2},{4,3},{5,4},{6,5},{7,6},{8,7},{9,8},{10,9... | collective-permute-start | bytes 294920 | tf_op jit(solution)/shard_map/ppermute | solution.py:361
  16.3 1.9 %collective-permute-start.1 = (bf16[2,3,16,512]{3,2,1,0:T(8,128)(2,1)}, bf16[2,3,16,512]{3,2,1,0:T(8,128)(2,1)S(1)}, u32[]{:S(2)}, u32[]{:S(2)}) collective-permute-start(bf16[2,3,16,512]{3,2,1,0:T(8,128)(2,1)} %get-tuple-element.20), channel_id=1, source_target_pairs={{0,224},{1,225},{2,226},{3,227},{4,228},{5,229},{6,230},{7,231},{8... | collective-permute-start | bytes 294920 | tf_op jit(solution)/shard_map/ppermute | solution.py:361
  18.2 2.8 %collective-permute-start.2 = (bf16[2,3,16,512]{3,2,1,0:T(8,128)(2,1)}, bf16[2,3,16,512]{3,2,1,0:T(8,128)(2,1)S(1)}, u32[]{:S(2)}, u32[]{:S(2)}) collective-permute-start(bf16[2,3,16,512]{3,2,1,0:T(8,128)(2,1)} %get-tuple-element.21), channel_id=1, source_target_pairs={{0,255},{1,224},{2,225},{3,226},{4,227},{5,228},{6,229},{7,230},{8... | collective-permute-start | bytes 294920 | tf_op jit(solution)/shard_map/ppermute | solution.py:361
  21.1 0.8 slice_bitcast_fusion
  21.8 0.0 copy-start
  21.9 0.0 copy-start.1
  21.9 0.0 copy-start.2
  21.9 0.5 shard_map.87.bias
  22.3 0.0 collective-permute-done.lon
  22.4 0.0 collective-permute-done.1.lat
  22.4 2.1 %collective-permute-done.2.cor = bf16[2,3,16,512]{3,2,1,0:T(8,128)(2,1)S(1)} collective-permute-done((bf16[2,3,16,512]{3,2,1,0:T(8,128)(2,1)}, bf16[2,3,16,512]{3,2,1,0:T(8,128)(2,1)S(1)}, u32[]{:S(2)}, u32[]{:S(2)}) %collective-permute-start.2) | collective-permute-done | bytes 98336 | tf_op jit(solution)/shard_map/ppermute | solution.py:361
  24.4 0.0 copy-done
  24.4 0.0 copy-done.1
  24.4 0.0 copy-done.2
  24.4 4.8 %shard_map.88 = (bf16[192,512]{1,0:T(8,128)(2,1)S(1)}, bf16[144,512]{1,0:T(8,128)(2,1)S(1)}, bf16[2,192,512]{2,1,0:T(8,128)(2,1)S(1)}, bf16[192,1536]{1,0:T(8,128)(2,1)S(1)}, bf16[2,4,2,96,96]{4,3,2,1,0:T(8,128)(2,1)S(1)}) custom-call(bf16[2,3,16,512]{3,2,1,0:T(8,128)(2,1)S(1)} %copy-done.1, bf16[2,3,16,512]{3,2,1,0:T(8,128)(2,1)S(1)} %collective-permute-done.lon, ...), custom_call_target="tpu_custom_call" | custom-call | tf_op jit(solution)/shard_map/pallas_call | solution.py:36
  29.2 4.5 %collective-permute-start.3 = (bf16[192,512]{1,0:T(8,128)(2,1)S(1)}, bf16[192,512]{1,0:T(8,128)(2,1)S(1)}, u32[]{:S(2)}, u32[]{:S(2)}) collective-permute-start(bf16[192,512]{1,0:T(8,128)(2,1)S(1)} %get-tuple-element.22), channel_id=1, source_target_pairs={{256,0},{257,1},{258,2},{259,3},{260,4},{261,5},{262,6},{263,7},{2... | collective-permute-start | bytes 589832 | tf_op jit(solution)/shard_map/ppermute | solution.py:414
  33.8 3.9 %collective-permute-start.5 = (bf16[144,512]{1,0:T(8,128)(2,1)S(1)}, bf16[144,512]{1,0:T(8,128)(2,1)S(1)}, u32[]{:S(2)}, u32[]{:S(2)}) collective-permute-start(bf16[144,512]{1,0:T(8,128)(2,1)S(1)} %get-tuple-element.29.a), channel_id=1, source_target_pairs={{0,192},{1,193},{2,194},{3,195},{4,196},{5,197},{6,198},{7,199},{8... | collective-permute-start | bytes 442376 | tf_op jit(solution)/shard_map/ppermute | solution.py:361
  37.7 2.7 %collective-permute-start.6 = (bf16[144,512]{1,0:T(8,128)(2,1)S(1)}, bf16[144,512]{1,0:T(8,128)(2,1)S(1)}, u32[]{:S(2)}, u32[]{:S(2)}) collective-permute-start(bf16[144,512]{1,0:T(8,128)(2,1)S(1)} %get-tuple-element.29.a), channel_id=1, source_target_pairs={{0,128},{1,129},{2,130},{3,131},{4,132},{5,133},{6,134},{7,135},{8... | collective-permute-start | bytes 442376 | tf_op jit(solution)/shard_map/ppermute | solution.py:361
  40.4 2.8 %collective-permute-start.7 = (bf16[144,512]{1,0:T(8,128)(2,1)S(1)}, bf16[144,512]{1,0:T(8,128)(2,1)S(1)}, u32[]{:S(2)}, u32[]{:S(2)}) collective-permute-start(bf16[144,512]{1,0:T(8,128)(2,1)S(1)} %get-tuple-element.29.a), channel_id=1, source_target_pairs={{0,64},{1,65},{2,66},{3,67},{4,68},{5,69},{6,70},{7,71},{8,72},{9,... | collective-permute-start | bytes 442376 | tf_op jit(solution)/shard_map/ppermute | solution.py:361
  43.2 0.0 collective-permute-done.3.arrived
  43.2 2.8 %shard_map.89 = (bf16[8,224,128]{2,1,0:T(8,128)(2,1)}, bf16[2,3,16,512]{3,2,1,0:T(8,128)(2,1)S(1)}, bf16[2,3,16,512]{3,2,1,0:T(8,128)(2,1)S(1)}) custom-call(bf16[192,512]{1,0:T(8,128)(2,1)S(1)} %collective-permute-done.3.arrived, bf16[2,192,512]{2,1,0:T(8,128)(2,1)S(1)} %get-tuple-element.23.fields, bf16[192,1536]{1,0:T(8,128)(2,1)S(1)} %get-tuple-element.24.projected, ...), custom_call_target="tpu_custom_call" | custom-call | flops 4000000000 | bytes 20000000 | tf_op jit(solution)/shard_map/pallas_call | solution.py:36
  46.1 3.7 %all-to-all-start = ((bf16[8,224,128]{2,1,0:T(8,128)(2,1)}), bf16[8,224,128]{2,1,0:T(8,128)(2,1)S(1)}, u32[]{:S(2)}, u32[]{:S(2)}) async-start(bf16[8,224,128]{2,1,0:T(8,128)(2,1)} %get-tuple-element.28), calls=%async_computation | async-start | bytes 917504 | tf_op jit(solution)/shard_map/all_to_all | solution.py:424
  49.8 0.0 collective-permute-done.5.b
  49.8 0.0 collective-permute-done.6.c
  49.8 0.0 collective-permute-done.7.d
  49.9 2.4 %collective-permute-start.8 = (bf16[2,144,512]{2,1,0:T(8,128)(2,1)S(1)}, bf16[2,144,512]{2,1,0:T(8,128)(2,1)S(1)}, u32[]{:S(2)}, u32[]{:S(2)}) collective-permute-start(bf16[2,144,512]{2,1,0:T(8,128)(2,1)S(1)} %get-tuple-element.30.low), channel_id=1, source_target_pairs={{0,32},{32,0},{64,96},{96,64},{128,160},{160,128},{192,224},{224,1... | collective-permute-start | bytes 884744 | tf_op jit(solution)/shard_map/ppermute | solution.py:365
  52.3 1.9 %collective-permute-start.9 = (bf16[2,144,512]{2,1,0:T(8,128)(2,1)S(1)}, bf16[2,144,512]{2,1,0:T(8,128)(2,1)S(1)}, u32[]{:S(2)}, u32[]{:S(2)}) collective-permute-start(bf16[2,144,512]{2,1,0:T(8,128)(2,1)S(1)} %get-tuple-element.31.high), channel_id=1, source_target_pairs={{0,32},{32,0},{64,96},{96,64},{128,160},{160,128},{192,224},{224,1... | collective-permute-start | bytes 884744 | tf_op jit(solution)/shard_map/ppermute | solution.py:365
  54.2 0.5 collective-permute-start.4
  54.8 5.8 %collective-permute-done.4.above = bf16[2,3,16,512]{3,2,1,0:T(8,128)(2,1)S(1)} collective-permute-done((bf16[2,3,16,512]{3,2,1,0:T(8,128)(2,1)S(1)}, bf16[2,3,16,512]{3,2,1,0:T(8,128)(2,1)S(1)}, u32[]{:S(2)}, u32[]{:S(2)}) %collective-permute-start.4) | collective-permute-done | bytes 98336 | tf_op jit(solution)/shard_map/ppermute | solution.py:361
  60.5 0.0 collective-permute-done.8.other_low
  60.5 0.0 collective-permute-done.9.other_high
  60.5 0.0 all-to-all-done.blocks
  60.5 1.9 %shard_map.91 = (bf16[32,24,128]{2,1,0:T(8,128)(2,1)}, bf16[6,16,512]{2,1,0:T(8,128)(2,1)S(1)}) custom-call(s32[1]{0:T(128)} %bitcast.7.lat_index, bf16[8,224,128]{2,1,0:T(8,128)(2,1)S(1)} %all-to-all-done.blocks, bf16[2,144,512]{2,1,0:T(8,128)(2,1)S(1)} %get-tuple-element.30.low, bf16[2,144,512]{2,1,0:T(8,128)(2,1)S(1)} %get-tuple-element.31.high, ...), custom_call_target="tpu_custom_call" | custom-call | tf_op jit(solution)/shard_map/pallas_call | solution.py:36
  62.4 8.3 %all-to-all-start.1 = ((bf16[32,24,128]{2,1,0:T(8,128)(2,1)}), bf16[32,24,128]{2,1,0:T(8,128)(2,1)S(1)}, u32[]{:S(2)}, u32[]{:S(2)}) async-start(bf16[32,24,128]{2,1,0:T(8,128)(2,1)} %get-tuple-element.33), calls=%async_computation.1 | async-start | bytes 393216 | tf_op jit(solution)/shard_map/all_to_all | solution.py:437
  70.7 3.7 %collective-permute-start.10 = (bf16[6,16,512]{2,1,0:T(8,128)(2,1)S(1)}, bf16[6,16,512]{2,1,0:T(8,128)(2,1)S(1)}, u32[]{:S(2)}, u32[]{:S(2)}) collective-permute-start(bf16[6,16,512]{2,1,0:T(8,128)(2,1)S(1)} %get-tuple-element.32), channel_id=1, source_target_pairs={{0,1},{1,2},{2,3},{3,4},{4,5},{5,6},{6,7},{7,8},{8,9},{9,10},{10,1... | collective-permute-start | bytes 294920 | tf_op jit(solution)/shard_map/ppermute | solution.py:361
  74.4 9.2 %collective-permute-done.10.left = bf16[6,16,512]{2,1,0:T(8,128)(2,1)S(1)} collective-permute-done((bf16[6,16,512]{2,1,0:T(8,128)(2,1)S(1)}, bf16[6,16,512]{2,1,0:T(8,128)(2,1)S(1)}, u32[]{:S(2)}, u32[]{:S(2)}) %collective-permute-start.10) | collective-permute-done | bytes 98336 | tf_op jit(solution)/shard_map/ppermute | solution.py:361
  83.7 0.8 copy.9
  84.5 0.0 all-to-all-done.1.parts
  84.5 0.7 shard_map.93
  (3 shorter events, 0.1 us)
Async XLA Ops:
  2.5 19.8 %collective-permute-start = (bf16[2,3,16,512]{3,2,1,0:T(8,128)(2,1)}, bf16[2,3,16,512]{3,2,1,0:T(8,128)(2,1)S(1)}, u32[]{:S(2)}, u32[]{:S(2)}) collective-permute-start(bf16[2,3,16,512]{3,2,1,0:T(8,128)(2,1)} %get-tuple-element.19), channel_id=1, source_target_pairs={{0,31},{1,0},{2,1},{3,2},{4,3},{5,4},{6,5},{7,6},{8,7},{9,8},{10,9... | collective-permute-start | bytes 294920 | tf_op jit(solution)/shard_map/ppermute | solution.py:361
  16.3 6.1 %collective-permute-start.1 = (bf16[2,3,16,512]{3,2,1,0:T(8,128)(2,1)}, bf16[2,3,16,512]{3,2,1,0:T(8,128)(2,1)S(1)}, u32[]{:S(2)}, u32[]{:S(2)}) collective-permute-start(bf16[2,3,16,512]{3,2,1,0:T(8,128)(2,1)} %get-tuple-element.20), channel_id=1, source_target_pairs={{0,224},{1,225},{2,226},{3,227},{4,228},{5,229},{6,230},{7,231},{8... | collective-permute-start | bytes 294920 | tf_op jit(solution)/shard_map/ppermute | solution.py:361
  18.2 6.2 %collective-permute-start.2 = (bf16[2,3,16,512]{3,2,1,0:T(8,128)(2,1)}, bf16[2,3,16,512]{3,2,1,0:T(8,128)(2,1)S(1)}, u32[]{:S(2)}, u32[]{:S(2)}) collective-permute-start(bf16[2,3,16,512]{3,2,1,0:T(8,128)(2,1)} %get-tuple-element.21), channel_id=1, source_target_pairs={{0,255},{1,224},{2,225},{3,226},{4,227},{5,228},{6,229},{7,230},{8... | collective-permute-start | bytes 294920 | tf_op jit(solution)/shard_map/ppermute | solution.py:361
  21.8 2.6 %copy-start = (bf16[1,512,512]{2,1,0:T(8,128)(2,1)S(1)}, bf16[1,512,512]{2,1,0:T(8,128)(2,1)}, u32[]{:S(2)}) copy-start(bf16[1,512,512]{2,1,0:T(8,128)(2,1)} %param.10) | copy-start | bytes 1572868
  21.9 2.6 %copy-start.1 = (bf16[2,3,16,512]{3,2,1,0:T(8,128)(2,1)S(1)}, bf16[2,3,16,512]{3,2,1,0:T(8,128)(2,1)}, u32[]{:S(2)}) copy-start(bf16[2,3,16,512]{3,2,1,0:T(8,128)(2,1)} %get-tuple-element.18.own) | copy-start | bytes 294916
  21.9 2.6 %copy-start.2 = (f32[1,512]{1,0:T(1,128)S(1)}, f32[1,512]{1,0:T(1,128)}, u32[]{:S(2)}) copy-start(f32[1,512]{1,0:T(1,128)} %gain.3) | copy-start | bytes 6148
  29.2 14.0 %collective-permute-start.3 = (bf16[192,512]{1,0:T(8,128)(2,1)S(1)}, bf16[192,512]{1,0:T(8,128)(2,1)S(1)}, u32[]{:S(2)}, u32[]{:S(2)}) collective-permute-start(bf16[192,512]{1,0:T(8,128)(2,1)S(1)} %get-tuple-element.22), channel_id=1, source_target_pairs={{256,0},{257,1},{258,2},{259,3},{260,4},{261,5},{262,6},{263,7},{2... | collective-permute-start | bytes 589832 | tf_op jit(solution)/shard_map/ppermute | solution.py:414
  33.8 16.1 %collective-permute-start.5 = (bf16[144,512]{1,0:T(8,128)(2,1)S(1)}, bf16[144,512]{1,0:T(8,128)(2,1)S(1)}, u32[]{:S(2)}, u32[]{:S(2)}) collective-permute-start(bf16[144,512]{1,0:T(8,128)(2,1)S(1)} %get-tuple-element.29.a), channel_id=1, source_target_pairs={{0,192},{1,193},{2,194},{3,195},{4,196},{5,197},{6,198},{7,199},{8... | collective-permute-start | bytes 442376 | tf_op jit(solution)/shard_map/ppermute | solution.py:361
  37.7 12.1 %collective-permute-start.6 = (bf16[144,512]{1,0:T(8,128)(2,1)S(1)}, bf16[144,512]{1,0:T(8,128)(2,1)S(1)}, u32[]{:S(2)}, u32[]{:S(2)}) collective-permute-start(bf16[144,512]{1,0:T(8,128)(2,1)S(1)} %get-tuple-element.29.a), channel_id=1, source_target_pairs={{0,128},{1,129},{2,130},{3,131},{4,132},{5,133},{6,134},{7,135},{8... | collective-permute-start | bytes 442376 | tf_op jit(solution)/shard_map/ppermute | solution.py:361
  40.4 9.4 %collective-permute-start.7 = (bf16[144,512]{1,0:T(8,128)(2,1)S(1)}, bf16[144,512]{1,0:T(8,128)(2,1)S(1)}, u32[]{:S(2)}, u32[]{:S(2)}) collective-permute-start(bf16[144,512]{1,0:T(8,128)(2,1)S(1)} %get-tuple-element.29.a), channel_id=1, source_target_pairs={{0,64},{1,65},{2,66},{3,67},{4,68},{5,69},{6,70},{7,71},{8,72},{9,... | collective-permute-start | bytes 442376 | tf_op jit(solution)/shard_map/ppermute | solution.py:361
  46.1 14.5 %all-to-all-start = ((bf16[8,224,128]{2,1,0:T(8,128)(2,1)}), bf16[8,224,128]{2,1,0:T(8,128)(2,1)S(1)}, u32[]{:S(2)}, u32[]{:S(2)}) async-start(bf16[8,224,128]{2,1,0:T(8,128)(2,1)} %get-tuple-element.28), calls=%async_computation | async-start | bytes 917504 | tf_op jit(solution)/shard_map/all_to_all | solution.py:424
  49.9 10.6 %collective-permute-start.8 = (bf16[2,144,512]{2,1,0:T(8,128)(2,1)S(1)}, bf16[2,144,512]{2,1,0:T(8,128)(2,1)S(1)}, u32[]{:S(2)}, u32[]{:S(2)}) collective-permute-start(bf16[2,144,512]{2,1,0:T(8,128)(2,1)S(1)} %get-tuple-element.30.low), channel_id=1, source_target_pairs={{0,32},{32,0},{64,96},{96,64},{128,160},{160,128},{192,224},{224,1... | collective-permute-start | bytes 884744 | tf_op jit(solution)/shard_map/ppermute | solution.py:365
  52.3 8.2 %collective-permute-start.9 = (bf16[2,144,512]{2,1,0:T(8,128)(2,1)S(1)}, bf16[2,144,512]{2,1,0:T(8,128)(2,1)S(1)}, u32[]{:S(2)}, u32[]{:S(2)}) collective-permute-start(bf16[2,144,512]{2,1,0:T(8,128)(2,1)S(1)} %get-tuple-element.31.high), channel_id=1, source_target_pairs={{0,32},{32,0},{64,96},{96,64},{128,160},{160,128},{192,224},{224,1... | collective-permute-start | bytes 884744 | tf_op jit(solution)/shard_map/ppermute | solution.py:365
  54.2 6.3 %collective-permute-start.4 = (bf16[2,3,16,512]{3,2,1,0:T(8,128)(2,1)S(1)}, bf16[2,3,16,512]{3,2,1,0:T(8,128)(2,1)S(1)}, u32[]{:S(2)}, u32[]{:S(2)}) collective-permute-start(bf16[2,3,16,512]{3,2,1,0:T(8,128)(2,1)S(1)} %get-tuple-element.27), channel_id=1, source_target_pairs={{0,32},{1,33},{2,34},{3,35},{4,36},{5,37},{6,38},{7,39},{8,40},{9,... | collective-permute-start | bytes 294920 | tf_op jit(solution)/shard_map/ppermute | solution.py:361
  62.4 22.1 %all-to-all-start.1 = ((bf16[32,24,128]{2,1,0:T(8,128)(2,1)}), bf16[32,24,128]{2,1,0:T(8,128)(2,1)S(1)}, u32[]{:S(2)}, u32[]{:S(2)}) async-start(bf16[32,24,128]{2,1,0:T(8,128)(2,1)} %get-tuple-element.33), calls=%async_computation.1 | async-start | bytes 393216 | tf_op jit(solution)/shard_map/all_to_all | solution.py:437
  70.7 12.9 %collective-permute-start.10 = (bf16[6,16,512]{2,1,0:T(8,128)(2,1)S(1)}, bf16[6,16,512]{2,1,0:T(8,128)(2,1)S(1)}, u32[]{:S(2)}, u32[]{:S(2)}) collective-permute-start(bf16[6,16,512]{2,1,0:T(8,128)(2,1)S(1)} %get-tuple-element.32), channel_id=1, source_target_pairs={{0,1},{1,2},{2,3},{3,4},{4,5},{5,6},{6,7},{7,8},{8,9},{9,10},{10,1... | collective-permute-start | bytes 294920 | tf_op jit(solution)/shard_map/ppermute | solution.py:361

commit v9 on v8

--- a/solution.py
+++ b/solution.py
@@ -58,6 +58,20 @@
     return lax.broadcasted_iota(jnp.int32, shape, dim)
 
 
+def pack(tiles):
+    row = row_index(tiles[3].shape, 0)
+    return [jnp.where(row < 6, tiles[g], pltpu.roll(tiles[3], 6 - 2 * g, 0)) for g in range(3)]
+
+
+def unpack(rows):
+    tiles = [rows[8 * g : 8 * g + 8] for g in range(3)]
+    row = row_index(tiles[0].shape, 0)
+    last = jnp.where(row < 2, pltpu.roll(tiles[0], 2, 0), 0.0)
+    last = jnp.where((row >= 2) & (row < 4), pltpu.roll(tiles[1], 4, 0), last)
+    last = jnp.where((row >= 4) & (row < 6), pltpu.roll(tiles[2], 6, 0), last)
+    return [jnp.where(row < 6, tile, 0.0) for tile in tiles] + [last]
+
+
 def cut_kernel(labels_ref, x_ref, g_ref, own, lon, lat, cor, labels, x_rows, g_rows, sem, sems):
     fetch = pltpu.make_async_copy(labels_ref, labels, sem)
     fetch.start()
@@ -69,30 +83,22 @@
         copy.start()
     row = row_index((8, FEATURES), 0)
 
-    def halves(field, level, fill):
-        low, high = field[0:8, level, :], field[4:12, level, :]
-        return (
-            jnp.where(row < 6, low, fill),
-            jnp.where(row < 6, pltpu.roll(high, 6, 0), fill),
-        )
-
     fetch.wait()
+    parts = {}
+    marks = [jnp.zeros((8, FEATURES), F32)] * 2
     for i in range(6):
-        label = labels[i].astype(F32)
         fetches[2 * i].wait()
         fetches[2 * i + 1].wait()
-        x, g = x_rows[i].astype(F32), g_rows[i].astype(F32)
-        for level in range(2):
-            x_low, x_high = halves(x, level, label)
-            g_low, g_high = halves(g, level, 0.0)
-            low = jnp.concatenate([x_low, g_low], axis=0).astype(BF16)
-            high = jnp.concatenate([x_high, g_high], axis=0).astype(BF16)
-            if i < 3:
-                cor[level, i] = low
-                lat[level, i] = high
-            else:
-                lon[level, i - 3] = low
-                own[level, i - 3] = high
+        fields = x_rows[i].astype(F32), g_rows[i].astype(F32)
+        low = [field[0:8, level, :] for field in fields for level in range(2)]
+        high = [pltpu.roll(field[4:12, level, :], 6, 0) for field in fields for level in range(2)]
+        parts.setdefault((i // 3, 0), []).extend(pack(low))
+        parts.setdefault((i // 3, 1), []).extend(pack(high))
+        marks[i // 3] = jnp.where(row == i % 3, labels[i].astype(F32), marks[i // 3])
+    cor[...] = jnp.concatenate(parts[0, 0] + [marks[0]], axis=0).astype(BF16)
+    lat[...] = jnp.concatenate(parts[0, 1], axis=0).astype(BF16)
+    lon[...] = jnp.concatenate(parts[1, 0], axis=0).astype(BF16)
+    own[...] = jnp.concatenate(parts[1, 1] + [marks[1]], axis=0).astype(BF16)
 
 
 def bias_kernel(table, out):
@@ -186,35 +192,41 @@
 def first_kernel(
     own, lon, lat, cor, w_qkv_ref, w_proj, gain, bias,
     skip, inputs, fields, projected_out, att_out,
-    dqkv, w_qkv, sem,
+    dqkv, w_qkv, sems,
 ):
-    fetch = pltpu.make_async_copy(w_qkv_ref, w_qkv, sem)
-    fetch.start()
-    tiles_x, tiles_g = [], []
+    thirds = [slice(FEATURES * j, FEATURES * (j + 1)) for j in range(3)]
+    fetches = [
+        pltpu.make_async_copy(w_qkv_ref.at[third], w_qkv.at[third], sems.at[j])
+        for j, third in enumerate(thirds)
+    ]
+    for copy in fetches:
+        copy.start()
     labels = []
-    row = row_index((8, FEATURES), 0)
-    for level in range(2):
-        for i in range(6):
-            left, right = (own, lon) if i < 3 else (lat, cor)
-            left, right = left[level, i % 3].astype(F32), right[level, i % 3].astype(F32)
-            if level == 0:
-                labels.append(left[6:7, :128])
-            for tile in (left, right):
-                tiles_x.append(jnp.where(row < 6, tile[:8], 0.0))
-                tiles_g.append(tile[8:])
+    tiles = {}
+    for upper, (left, right) in enumerate(((own, lon), (lat, cor))):
+        left, right = left[...].astype(F32), right[...].astype(F32)
+        marked = right if upper else left
+        labels.extend(marked[72 + i : 73 + i, :128] for i in range(3))
+        for i in range(3):
+            for half, piece in ((0, left), (1, right)):
+                found = unpack(piece[24 * i : 24 * i + 24])
+                for k in range(4):
+                    tiles[k // 2, k % 2, 3 * upper + i, half] = found[k]
+    order = [(level, i, half) for level in range(2) for i in range(6) for half in range(2)]
+    tiles_x, tiles_g = ([tiles[(field,) + place] for place in order] for field in range(2))
     x = jnp.concatenate(tiles_x, axis=0)
     c = jnp.concatenate(tiles_g, axis=0)
     normed, inv_std = normalised(x)
     scaled = normed * gain[...]
-    packed = pack_rows(scaled).astype(BF16)
-    inputs[...] = packed
-    fetch.wait()
-    projected = dot(scaled.astype(BF16), w_qkv[...], ((1,), (1,)))
+    inputs[...] = pack_rows(scaled).astype(BF16)
     c_low = c.astype(BF16)
-    d_first_value = dot(c_low, w_proj[...])
+    d_low = dot(c_low, w_proj[...]).astype(BF16)
     fields[0] = x.astype(BF16)
     fields[1] = c_low
-    projected_out[...] = projected.astype(BF16)
+    scaled_low = scaled.astype(BF16)
+    for copy, third in zip(fetches, thirds):
+        copy.wait()
+        projected_out[:, third] = dot(scaled_low, w_qkv[third, :], ((1,), (1,))).astype(BF16)
 
     lane_row = row_index((1, 128), 1) >> 4
     along = labels[0]
@@ -240,7 +252,7 @@
         att_out[level, pair] = probs.astype(BF16)
         return probs
 
-    attention_backward(probabilities, d_first_value.astype(BF16), projected_out, dqkv)
+    attention_backward(probabilities, d_low, projected_out, dqkv)
     skip[...] = (c + input_gradient(dqkv, w_qkv, gain, normed, inv_std)).astype(BF16)
 
 
@@ -270,13 +282,12 @@
     fetch.wait()
     shifted = input_gradient(dqkv, w_qkv, gain, normed, inv_std)
     total = fields[1].astype(F32) + (arrived[...].astype(F32) + shifted)
-    for i in range(6):
-        for half in range(2):
-            start = 16 * i + 8 * half
-            both = jnp.concatenate(
-                [total[start : start + 8], total[96 + start : 96 + start + 8]], axis=0
-            )
-            (kept, up)[i // 3][half, i % 3] = both.astype(BF16)
+    for target, first in ((kept, 0), (up, 3)):
+        parts = []
+        for i in range(first, first + 3):
+            starts = [96 * level + 16 * i + 8 * half for half in range(2) for level in range(2)]
+            parts.extend(pack([total[start : start + 8] for start in starts]))
+        target[...] = jnp.concatenate(parts, axis=0).astype(BF16)
 
 
 def stack_kernel(a, b, c, d, kept, low, high):
@@ -312,9 +323,13 @@
         out[band, width:, :] = jnp.where(
             lane < 64, part[: width // 2], pltpu.roll(part[width // 2 :], 64, 1)
         ).astype(BF16)
-    for i in range(3):
-        sideways[i] = above[1, i]
-        sideways[3 + i] = kept[1, i]
+    tiles = []
+    for part in (above, kept):
+        part = part[...].astype(F32)
+        for i in range(3):
+            tiles.extend(unpack(part[24 * i : 24 * i + 24])[2:])
+    packed = pack(tiles[:4]) + pack(tiles[4:8]) + pack(tiles[8:])
+    sideways[...] = jnp.concatenate(packed, axis=0).astype(BF16)
 
 
 def sum_kernel(lat_index, parts, out):
@@ -341,14 +356,19 @@
 
 def join_kernel(kept, above, left, out):
     row = row_index((8, FEATURES), 0)
-    for level in range(2):
-        part = slice(level * 8, level * 8 + 8)
-        for i in range(6):
-            low, high = left[i], above[0, i] if i < 3 else kept[0, i - 3]
-            low = low.astype(F32)[part]
-            high = pltpu.roll(high.astype(F32)[part], 6, 0)
-            out[0, level, i, 0:8, :] = jnp.where(row < 6, low, high).astype(BF16)
-            out[0, level, i, 8:12, :] = high[:4].astype(BF16)
+    low, high = [], []
+    side = left[...].astype(F32)
+    for g in range(3):
+        low.extend(unpack(side[24 * g : 24 * g + 24]))
+    for part in (above, kept):
+        part = part[...].astype(F32)
+        for i in range(3):
+            high.extend(unpack(part[24 * i : 24 * i + 24])[:2])
+    for i in range(6):
+        for level in range(2):
+            moved = pltpu.roll(high[2 * i + level], 6, 0)
+            out[0, level, i, 0:8, :] = jnp.where(row < 6, low[2 * i + level], moved).astype(BF16)
+            out[0, level, i, 8:12, :] = moved[:4].astype(BF16)
 
 
 def passed(array, lat_by, lon_by):
@@ -368,10 +388,11 @@
 def per_device(x_in, out_grad, w_qkv, w_proj, norm_gain, bias_table, lat_labels):
     lats, lons = lax.axis_size("lat"), lax.axis_size("lon")
     w_qkv, w_proj = w_qkv[0], w_proj[0]
-    piece = struct((2, 3, 16, FEATURES), BF16)
+    part = struct((72, FEATURES), BF16)
+    marked = struct((80, FEATURES), BF16)
     own, lon, lat, cor = call(
         cut_kernel,
-        (piece,) * 4,
+        (marked, part, part, marked),
         [
             pltpu.SMEM(lat_labels.shape, jnp.int32),
             pltpu.VMEM((6, 12, 2, FEATURES), BF16),
@@ -406,17 +427,16 @@
             struct((ROWS, 3 * FEATURES), BF16),
             struct((2, 4, 2, LEVEL_ROWS, LEVEL_ROWS), BF16),
         ),
-        scratch,
+        scratch[:2] + [pltpu.SemaphoreType.DMA((3,))],
         places={4: pl.ANY},
     )(own, lon, lat, cor, w_qkv, w_proj, norm_gain, bias)
 
     lat_index = lax.axis_index("lat").astype(jnp.int32).reshape(1)
     arrived = lax.ppermute(skip, "phase", [(1, 0)])
     along = [inputs] + [passed(inputs, -2 * x, 0) for x in range(1, lats // 2)]
-    back = struct((2, 3, 16, FEATURES), BF16)
     blocks, kept, up = call(
         second_kernel,
-        (struct((lats, 224, 128), BF16), back, back),
+        (struct((lats, 224, 128), BF16), part, part),
         scratch,
         places={5: pl.ANY},
         cost=pl.CostEstimate(flops=4_000_000_000, bytes_accessed=20_000_000, transcendentals=0),
@@ -429,7 +449,7 @@
     rows = FEATURES * 3 // 2 // lons
     slices, sideways = call(
         product_kernel,
-        (struct((lons, rows, 128), BF16), struct((6, 16, FEATURES), BF16)),
+        (struct((lons, rows, 128), BF16), part),
         places={0: pltpu.SMEM},
     )(lat_index, blocks, low, high, other_low, other_high, kept, above)
     left = passed(sideways, 0, 1)

time: 85.8 us -> 83.7 us (0.976)
  starting transfers between devices: 53 us -> 52 us
  waiting for transfers between devices: 17.1 us -> 16.2 us
    ppermute x1, starting transfers between devices: 4.54 us -> 3.55 us  [per_device(): arrived = lax.ppermute(skip, 'phase', [(1, 0)])]
    ppermute x8, waiting for transfers between devices: 17.1 us -> 16.2 us  [passed(): return lax.ppermute(array, ('lat', 'lon'), pairs)]
where the time goes in v9:
time: 83.7 us; the launch traced here: 83.1 us
  starting transfers between devices  52 us (62%)
  waiting for transfers between devices  16.2 us (19%)
  Pallas kernels  12.4 us (15%)
  local copies, waits for them, and re-layouts  1.61 us (2%)
    ppermute x8, starting transfers between devices, passed(): return lax.ppermute(array, ('lat', 'lon'), pairs)  31.7 us
    ppermute x8, waiting for transfers between devices, passed(): return lax.ppermute(array, ('lat', 'lon'), pairs)  16.2 us
    pallas_call x8, Pallas kernels, run(): pl.pallas_call(kernel, out_shape=out_shape, in_specs=specs, out_specs=out...  12.4 us
    all_to_all x1, starting transfers between devices, per_device(): slices = lax.all_to_all(slices, 'lon', 0, 0, tiled=True)  8.33 us
    ppermute x2, starting transfers between devices, other_core(): lax.ppermute(array, 'lat', [(a, a ^ 1) for a in range(lax.axis_size('lat'...  4.33 us
    all_to_all x1, starting transfers between devices, per_device(): blocks = lax.all_to_all(blocks, 'lat', 0, 0, tiled=True)  4.07 us
    ppermute x1, starting transfers between devices, per_device(): arrived = lax.ppermute(skip, 'phase', [(1, 0)])  3.55 us
  transfers between devices with their start and end apart: 13, of which 3 were waited for; matrix products, arithmetic and copies ran while one was open for 2% of the time, Pallas kernels for 4%

profile of v9, /device:TPU:8, one launch (start us, length us, event | category | flops | bytes accessed | tf_op | source)
XLA Modules:
  0.0 83.1 jit_solution(13603859338993035686)
XLA Ops:
  0.6 1.9 %shard_map.86 = (bf16[80,512]{1,0:T(8,128)(2,1)}, bf16[72,512]{1,0:T(8,128)(2,1)}, bf16[72,512]{1,0:T(8,128)(2,1)}, bf16[80,512]{1,0:T(8,128)(2,1)}) custom-call(s32[6]{0:T(128)} %labels_ref.1, bf16[6,12,2,512]{3,2,1,0:T(2,128)(2,1)} %bitcast.16, bf16[6,12,2,512]{3,2,1,0:T(2,128)(2,1)} %bitcast.17), custom_call_target="tpu_custom_call" | custom-call | tf_op jit(solution)/shard_map/pallas_call | solution.py:36
  2.5 15.4 %collective-permute-start.2 = (bf16[80,512]{1,0:T(8,128)(2,1)}, bf16[80,512]{1,0:T(8,128)(2,1)S(1)}, u32[]{:S(2)}, u32[]{:S(2)}) collective-permute-start(bf16[80,512]{1,0:T(8,128)(2,1)} %get-tuple-element.21), channel_id=1, source_target_pairs={{0,255},{1,224},{2,225},{3,226},{4,227},{5,228},{6,229},{7,230},{8... | collective-permute-start | bytes 245768 | tf_op jit(solution)/shard_map/ppermute | solution.py:381
  17.9 2.5 %collective-permute-start = (bf16[72,512]{1,0:T(8,128)(2,1)}, bf16[72,512]{1,0:T(8,128)(2,1)S(1)}, u32[]{:S(2)}, u32[]{:S(2)}) collective-permute-start(bf16[72,512]{1,0:T(8,128)(2,1)} %get-tuple-element.19), channel_id=1, source_target_pairs={{0,31},{1,0},{2,1},{3,2},{4,3},{5,4},{6,5},{7,6},{8,7},{9,8},{10,9... | collective-permute-start | bytes 221192 | tf_op jit(solution)/shard_map/ppermute | solution.py:381
  20.4 0.6 collective-permute-start.1
  20.9 0.8 slice_bitcast_fusion
  21.7 0.0 copy-start
  21.7 0.0 copy-start.1
  21.7 0.0 copy-start.2
  21.8 0.5 shard_map.87.bias
  22.2 2.1 %collective-permute-done.lon = bf16[72,512]{1,0:T(8,128)(2,1)S(1)} collective-permute-done((bf16[72,512]{1,0:T(8,128)(2,1)}, bf16[72,512]{1,0:T(8,128)(2,1)S(1)}, u32[]{:S(2)}, u32[]{:S(2)}) %collective-permute-start) | collective-permute-done | bytes 73760 | tf_op jit(solution)/shard_map/ppermute | solution.py:381
  24.3 0.0 collective-permute-done.1.lat
  24.3 0.0 collective-permute-done.2.cor
  24.3 0.0 copy-done
  24.4 0.0 copy-done.1
  24.4 0.0 copy-done.2
  24.4 4.6 %shard_map.88 = (bf16[192,512]{1,0:T(8,128)(2,1)S(1)}, bf16[144,512]{1,0:T(8,128)(2,1)S(1)}, bf16[2,192,512]{2,1,0:T(8,128)(2,1)S(1)}, bf16[192,1536]{1,0:T(8,128)(2,1)S(1)}, bf16[2,4,2,96,96]{4,3,2,1,0:T(8,128)(2,1)S(1)}) custom-call(bf16[80,512]{1,0:T(8,128)(2,1)S(1)} %copy-done.1, bf16[72,512]{1,0:T(8,128)(2,1)S(1)} %collective-permute-done.lon, ...), custom_call_target="tpu_custom_call" | custom-call | tf_op jit(solution)/shard_map/pallas_call | solution.py:36
  29.0 3.6 %collective-permute-start.3 = (bf16[192,512]{1,0:T(8,128)(2,1)S(1)}, bf16[192,512]{1,0:T(8,128)(2,1)S(1)}, u32[]{:S(2)}, u32[]{:S(2)}) collective-permute-start(bf16[192,512]{1,0:T(8,128)(2,1)S(1)} %get-tuple-element.22), channel_id=1, source_target_pairs={{256,0},{257,1},{258,2},{259,3},{260,4},{261,5},{262,6},{263,7},{2... | collective-permute-start | bytes 589832 | tf_op jit(solution)/shard_map/ppermute | solution.py:435
  32.5 3.8 %collective-permute-start.5 = (bf16[144,512]{1,0:T(8,128)(2,1)S(1)}, bf16[144,512]{1,0:T(8,128)(2,1)S(1)}, u32[]{:S(2)}, u32[]{:S(2)}) collective-permute-start(bf16[144,512]{1,0:T(8,128)(2,1)S(1)} %get-tuple-element.29.a), channel_id=1, source_target_pairs={{0,192},{1,193},{2,194},{3,195},{4,196},{5,197},{6,198},{7,199},{8... | collective-permute-start | bytes 442376 | tf_op jit(solution)/shard_map/ppermute | solution.py:381
  36.3 2.5 %collective-permute-start.6 = (bf16[144,512]{1,0:T(8,128)(2,1)S(1)}, bf16[144,512]{1,0:T(8,128)(2,1)S(1)}, u32[]{:S(2)}, u32[]{:S(2)}) collective-permute-start(bf16[144,512]{1,0:T(8,128)(2,1)S(1)} %get-tuple-element.29.a), channel_id=1, source_target_pairs={{0,128},{1,129},{2,130},{3,131},{4,132},{5,133},{6,134},{7,135},{8... | collective-permute-start | bytes 442376 | tf_op jit(solution)/shard_map/ppermute | solution.py:381
  38.8 2.8 %collective-permute-start.7 = (bf16[144,512]{1,0:T(8,128)(2,1)S(1)}, bf16[144,512]{1,0:T(8,128)(2,1)S(1)}, u32[]{:S(2)}, u32[]{:S(2)}) collective-permute-start(bf16[144,512]{1,0:T(8,128)(2,1)S(1)} %get-tuple-element.29.a), channel_id=1, source_target_pairs={{0,64},{1,65},{2,66},{3,67},{4,68},{5,69},{6,70},{7,71},{8,72},{9,... | collective-permute-start | bytes 442376 | tf_op jit(solution)/shard_map/ppermute | solution.py:381
  41.6 0.0 collective-permute-done.3.arrived
  41.6 2.8 %shard_map.89 = (bf16[8,224,128]{2,1,0:T(8,128)(2,1)}, bf16[72,512]{1,0:T(8,128)(2,1)S(1)}, bf16[72,512]{1,0:T(8,128)(2,1)S(1)}) custom-call(bf16[192,512]{1,0:T(8,128)(2,1)S(1)} %collective-permute-done.3.arrived, bf16[2,192,512]{2,1,0:T(8,128)(2,1)S(1)} %get-tuple-element.23.fields, bf16[192,1536]{1,0:T(8,128)(2,1)S(1)} %get-tuple-element.24.projected, ...), custom_call_target="tpu_custom_call" | custom-call | flops 4000000000 | bytes 20000000 | tf_op jit(solution)/shard_map/pallas_call | solution.py:36
  44.5 4.1 %all-to-all-start = ((bf16[8,224,128]{2,1,0:T(8,128)(2,1)}), bf16[8,224,128]{2,1,0:T(8,128)(2,1)S(1)}, u32[]{:S(2)}, u32[]{:S(2)}) async-start(bf16[8,224,128]{2,1,0:T(8,128)(2,1)} %get-tuple-element.28), calls=%async_computation | async-start | bytes 917504 | tf_op jit(solution)/shard_map/all_to_all | solution.py:444
  48.6 0.0 collective-permute-done.5.b
  48.6 0.0 collective-permute-done.6.c
  48.6 0.0 collective-permute-done.7.d
  48.6 2.4 %collective-permute-start.8 = (bf16[2,144,512]{2,1,0:T(8,128)(2,1)S(1)}, bf16[2,144,512]{2,1,0:T(8,128)(2,1)S(1)}, u32[]{:S(2)}, u32[]{:S(2)}) collective-permute-start(bf16[2,144,512]{2,1,0:T(8,128)(2,1)S(1)} %get-tuple-element.30.low), channel_id=1, source_target_pairs={{0,32},{32,0},{64,96},{96,64},{128,160},{160,128},{192,224},{224,1... | collective-permute-start | bytes 884744 | tf_op jit(solution)/shard_map/ppermute | solution.py:385
  51.1 1.9 %collective-permute-start.9 = (bf16[2,144,512]{2,1,0:T(8,128)(2,1)S(1)}, bf16[2,144,512]{2,1,0:T(8,128)(2,1)S(1)}, u32[]{:S(2)}, u32[]{:S(2)}) collective-permute-start(bf16[2,144,512]{2,1,0:T(8,128)(2,1)S(1)} %get-tuple-element.31.high), channel_id=1, source_target_pairs={{0,32},{32,0},{64,96},{96,64},{128,160},{160,128},{192,224},{224,1... | collective-permute-start | bytes 884744 | tf_op jit(solution)/shard_map/ppermute | solution.py:385
  53.0 0.5 collective-permute-start.4
  53.5 5.5 %collective-permute-done.4.above = bf16[72,512]{1,0:T(8,128)(2,1)S(1)} collective-permute-done((bf16[72,512]{1,0:T(8,128)(2,1)S(1)}, bf16[72,512]{1,0:T(8,128)(2,1)S(1)}, u32[]{:S(2)}, u32[]{:S(2)}) %collective-permute-start.4) | collective-permute-done | bytes 73760 | tf_op jit(solution)/shard_map/ppermute | solution.py:381
  59.0 0.0 collective-permute-done.8.other_low
  59.0 0.0 collective-permute-done.9.other_high
  59.0 0.0 all-to-all-done.blocks
  59.0 1.9 %shard_map.91 = (bf16[32,24,128]{2,1,0:T(8,128)(2,1)}, bf16[72,512]{1,0:T(8,128)(2,1)S(1)}) custom-call(s32[1]{0:T(128)} %bitcast.7.lat_index, bf16[8,224,128]{2,1,0:T(8,128)(2,1)S(1)} %all-to-all-done.blocks, bf16[2,144,512]{2,1,0:T(8,128)(2,1)S(1)} %get-tuple-element.30.low, bf16[2,144,512]{2,1,0:T(8,128)(2,1)S(1)} %get-tuple-element.31.high, ...), custom_call_target="tpu_custom_call" | custom-call | tf_op jit(solution)/shard_map/pallas_call | solution.py:36
  60.9 8.3 %all-to-all-start.1 = ((bf16[32,24,128]{2,1,0:T(8,128)(2,1)}), bf16[32,24,128]{2,1,0:T(8,128)(2,1)S(1)}, u32[]{:S(2)}, u32[]{:S(2)}) async-start(bf16[32,24,128]{2,1,0:T(8,128)(2,1)} %get-tuple-element.33), calls=%async_computation.1 | async-start | bytes 393216 | tf_op jit(solution)/shard_map/all_to_all | solution.py:457
  69.2 3.7 %collective-permute-start.10 = (bf16[72,512]{1,0:T(8,128)(2,1)S(1)}, bf16[72,512]{1,0:T(8,128)(2,1)S(1)}, u32[]{:S(2)}, u32[]{:S(2)}) collective-permute-start(bf16[72,512]{1,0:T(8,128)(2,1)S(1)} %get-tuple-element.32), channel_id=1, source_target_pairs={{0,1},{1,2},{2,3},{3,4},{4,5},{5,6},{6,7},{7,8},{8,9},{9,10},{10,1... | collective-permute-start | bytes 221192 | tf_op jit(solution)/shard_map/ppermute | solution.py:381
  72.9 8.5 %collective-permute-done.10.left = bf16[72,512]{1,0:T(8,128)(2,1)S(1)} collective-permute-done((bf16[72,512]{1,0:T(8,128)(2,1)S(1)}, bf16[72,512]{1,0:T(8,128)(2,1)S(1)}, u32[]{:S(2)}, u32[]{:S(2)}) %collective-permute-start.10) | collective-permute-done | bytes 73760 | tf_op jit(solution)/shard_map/ppermute | solution.py:381
  81.5 0.1 shard_map.92
  81.5 0.8 copy.9
  82.3 0.0 all-to-all-done.1.parts
  82.3 0.7 shard_map.93
  (2 shorter events, 0.0 us)
Async XLA Ops:
  2.5 21.8 %collective-permute-start.2 = (bf16[80,512]{1,0:T(8,128)(2,1)}, bf16[80,512]{1,0:T(8,128)(2,1)S(1)}, u32[]{:S(2)}, u32[]{:S(2)}) collective-permute-start(bf16[80,512]{1,0:T(8,128)(2,1)} %get-tuple-element.21), channel_id=1, source_target_pairs={{0,255},{1,224},{2,225},{3,226},{4,227},{5,228},{6,229},{7,230},{8... | collective-permute-start | bytes 245768 | tf_op jit(solution)/shard_map/ppermute | solution.py:381
  17.9 6.5 %collective-permute-start = (bf16[72,512]{1,0:T(8,128)(2,1)}, bf16[72,512]{1,0:T(8,128)(2,1)S(1)}, u32[]{:S(2)}, u32[]{:S(2)}) collective-permute-start(bf16[72,512]{1,0:T(8,128)(2,1)} %get-tuple-element.19), channel_id=1, source_target_pairs={{0,31},{1,0},{2,1},{3,2},{4,3},{5,4},{6,5},{7,6},{8,7},{9,8},{10,9... | collective-permute-start | bytes 221192 | tf_op jit(solution)/shard_map/ppermute | solution.py:381
  20.4 4.0 %collective-permute-start.1 = (bf16[72,512]{1,0:T(8,128)(2,1)}, bf16[72,512]{1,0:T(8,128)(2,1)S(1)}, u32[]{:S(2)}, u32[]{:S(2)}) collective-permute-start(bf16[72,512]{1,0:T(8,128)(2,1)} %get-tuple-element.20), channel_id=1, source_target_pairs={{0,224},{1,225},{2,226},{3,227},{4,228},{5,229},{6,230},{7,231},{8... | collective-permute-start | bytes 221192 | tf_op jit(solution)/shard_map/ppermute | solution.py:381
  21.7 2.6 %copy-start = (bf16[1,512,512]{2,1,0:T(8,128)(2,1)S(1)}, bf16[1,512,512]{2,1,0:T(8,128)(2,1)}, u32[]{:S(2)}) copy-start(bf16[1,512,512]{2,1,0:T(8,128)(2,1)} %param.10) | copy-start | bytes 1572868
  21.7 2.6 %copy-start.1 = (bf16[80,512]{1,0:T(8,128)(2,1)S(1)}, bf16[80,512]{1,0:T(8,128)(2,1)}, u32[]{:S(2)}) copy-start(bf16[80,512]{1,0:T(8,128)(2,1)} %get-tuple-element.18.own) | copy-start | bytes 245764
  21.7 2.6 %copy-start.2 = (f32[1,512]{1,0:T(1,128)S(1)}, f32[1,512]{1,0:T(1,128)}, u32[]{:S(2)}) copy-start(f32[1,512]{1,0:T(1,128)} %gain.3) | copy-start | bytes 6148
  29.0 12.7 %collective-permute-start.3 = (bf16[192,512]{1,0:T(8,128)(2,1)S(1)}, bf16[192,512]{1,0:T(8,128)(2,1)S(1)}, u32[]{:S(2)}, u32[]{:S(2)}) collective-permute-start(bf16[192,512]{1,0:T(8,128)(2,1)S(1)} %get-tuple-element.22), channel_id=1, source_target_pairs={{256,0},{257,1},{258,2},{259,3},{260,4},{261,5},{262,6},{263,7},{2... | collective-permute-start | bytes 589832 | tf_op jit(solution)/shard_map/ppermute | solution.py:435
  32.5 16.1 %collective-permute-start.5 = (bf16[144,512]{1,0:T(8,128)(2,1)S(1)}, bf16[144,512]{1,0:T(8,128)(2,1)S(1)}, u32[]{:S(2)}, u32[]{:S(2)}) collective-permute-start(bf16[144,512]{1,0:T(8,128)(2,1)S(1)} %get-tuple-element.29.a), channel_id=1, source_target_pairs={{0,192},{1,193},{2,194},{3,195},{4,196},{5,197},{6,198},{7,199},{8... | collective-permute-start | bytes 442376 | tf_op jit(solution)/shard_map/ppermute | solution.py:381
  36.3 12.3 %collective-permute-start.6 = (bf16[144,512]{1,0:T(8,128)(2,1)S(1)}, bf16[144,512]{1,0:T(8,128)(2,1)S(1)}, u32[]{:S(2)}, u32[]{:S(2)}) collective-permute-start(bf16[144,512]{1,0:T(8,128)(2,1)S(1)} %get-tuple-element.29.a), channel_id=1, source_target_pairs={{0,128},{1,129},{2,130},{3,131},{4,132},{5,133},{6,134},{7,135},{8... | collective-permute-start | bytes 442376 | tf_op jit(solution)/shard_map/ppermute | solution.py:381
  38.8 9.8 %collective-permute-start.7 = (bf16[144,512]{1,0:T(8,128)(2,1)S(1)}, bf16[144,512]{1,0:T(8,128)(2,1)S(1)}, u32[]{:S(2)}, u32[]{:S(2)}) collective-permute-start(bf16[144,512]{1,0:T(8,128)(2,1)S(1)} %get-tuple-element.29.a), channel_id=1, source_target_pairs={{0,64},{1,65},{2,66},{3,67},{4,68},{5,69},{6,70},{7,71},{8,72},{9,... | collective-permute-start | bytes 442376 | tf_op jit(solution)/shard_map/ppermute | solution.py:381
  44.5 14.5 %all-to-all-start = ((bf16[8,224,128]{2,1,0:T(8,128)(2,1)}), bf16[8,224,128]{2,1,0:T(8,128)(2,1)S(1)}, u32[]{:S(2)}, u32[]{:S(2)}) async-start(bf16[8,224,128]{2,1,0:T(8,128)(2,1)} %get-tuple-element.28), calls=%async_computation | async-start | bytes 917504 | tf_op jit(solution)/shard_map/all_to_all | solution.py:444
  48.6 10.4 %collective-permute-start.8 = (bf16[2,144,512]{2,1,0:T(8,128)(2,1)S(1)}, bf16[2,144,512]{2,1,0:T(8,128)(2,1)S(1)}, u32[]{:S(2)}, u32[]{:S(2)}) collective-permute-start(bf16[2,144,512]{2,1,0:T(8,128)(2,1)S(1)} %get-tuple-element.30.low), channel_id=1, source_target_pairs={{0,32},{32,0},{64,96},{96,64},{128,160},{160,128},{192,224},{224,1... | collective-permute-start | bytes 884744 | tf_op jit(solution)/shard_map/ppermute | solution.py:385
  51.1 8.0 %collective-permute-start.9 = (bf16[2,144,512]{2,1,0:T(8,128)(2,1)S(1)}, bf16[2,144,512]{2,1,0:T(8,128)(2,1)S(1)}, u32[]{:S(2)}, u32[]{:S(2)}) collective-permute-start(bf16[2,144,512]{2,1,0:T(8,128)(2,1)S(1)} %get-tuple-element.31.high), channel_id=1, source_target_pairs={{0,32},{32,0},{64,96},{96,64},{128,160},{160,128},{192,224},{224,1... | collective-permute-start | bytes 884744 | tf_op jit(solution)/shard_map/ppermute | solution.py:385
  53.0 6.0 %collective-permute-start.4 = (bf16[72,512]{1,0:T(8,128)(2,1)S(1)}, bf16[72,512]{1,0:T(8,128)(2,1)S(1)}, u32[]{:S(2)}, u32[]{:S(2)}) collective-permute-start(bf16[72,512]{1,0:T(8,128)(2,1)S(1)} %get-tuple-element.27), channel_id=1, source_target_pairs={{0,32},{1,33},{2,34},{3,35},{4,36},{5,37},{6,38},{7,39},{8,40},{9,... | collective-permute-start | bytes 221192 | tf_op jit(solution)/shard_map/ppermute | solution.py:381
  60.9 21.5 %all-to-all-start.1 = ((bf16[32,24,128]{2,1,0:T(8,128)(2,1)}), bf16[32,24,128]{2,1,0:T(8,128)(2,1)S(1)}, u32[]{:S(2)}, u32[]{:S(2)}) async-start(bf16[32,24,128]{2,1,0:T(8,128)(2,1)} %get-tuple-element.33), calls=%async_computation.1 | async-start | bytes 393216 | tf_op jit(solution)/shard_map/all_to_all | solution.py:457
  69.2 12.3 %collective-permute-start.10 = (bf16[72,512]{1,0:T(8,128)(2,1)S(1)}, bf16[72,512]{1,0:T(8,128)(2,1)S(1)}, u32[]{:S(2)}, u32[]{:S(2)}) collective-permute-start(bf16[72,512]{1,0:T(8,128)(2,1)S(1)} %get-tuple-element.32), channel_id=1, source_target_pairs={{0,1},{1,2},{2,3},{3,4},{4,5},{5,6},{6,7},{7,8},{8,9},{9,10},{10,1... | collective-permute-start | bytes 221192 | tf_op jit(solution)/shard_map/ppermute | solution.py:381

commit v10 on v9

--- a/solution.py
+++ b/solution.py
@@ -19,6 +19,7 @@
 LEVEL_ROWS = 96
 ROWS = 192
 PACKED_ROWS = 144
+GROUP = 8
 
 
 def call(kernel, out_shape, scratch=(), places=(), out_places=(), cost=None, limit=50 * MIB):
@@ -139,37 +140,55 @@
     return jnp.concatenate(out, axis=0)
 
 
-def per_head(pair):
-    even = row_index(pair.shape, 1) < 64
-    wide = pair.astype(F32)
+def per_head(pair, factor=1.0):
+    even = (row_index(pair.shape, 1) < 64).astype(F32)
     return jnp.concatenate(
-        [jnp.where(even, wide, 0.0).astype(BF16), jnp.where(even, 0.0, wide).astype(BF16)], axis=0
+        [pair * (even * factor).astype(BF16), pair * ((1.0 - even) * factor).astype(BF16)], axis=0
     )
 
 
 def attention_backward(att, d_low, projected, dqkv):
     lane = row_index((LEVEL_ROWS, 128), 1)
-    for level in range(2):
-        rows = slice(level * LEVEL_ROWS, (level + 1) * LEVEL_ROWS)
-        for pair in range(4):
-            cols = slice(pair * 128, (pair + 1) * 128)
-            probs = att(level, pair)
-            probs_low = probs.astype(BF16).reshape(2 * LEVEL_ROWS, LEVEL_ROWS)
-            d_out = d_low[rows, cols]
-            query = projected[rows, cols]
-            keys = per_head(projected[rows, 512 + pair * 128 : 512 + (pair + 1) * 128])
-            values = per_head(projected[rows, 1024 + pair * 128 : 1024 + (pair + 1) * 128])
-            d_probs = dot(values, d_out, ((1,), (1,))).reshape(2, LEVEL_ROWS, LEVEL_ROWS)
-            inner = jnp.sum(probs * d_probs, axis=1, keepdims=True)
-            d_scores = (probs * (d_probs - inner)).astype(BF16).reshape(2 * LEVEL_ROWS, LEVEL_ROWS)
-            d_value = dot(probs_low, d_out)
-            d_key = dot(d_scores, query)
-            d_query = dot(d_scores, keys, ((0,), (0,)))
-            dqkv[rows, pair * 128 : (pair + 1) * 128] = (d_query * SCORE_SCALE).astype(BF16)
-            dqkv[rows, 512 + pair * 128 : 512 + (pair + 1) * 128] = (
-                jnp.where(lane < 64, d_key[:LEVEL_ROWS], d_key[LEVEL_ROWS:]) * SCORE_SCALE
+    units = [(level, pair) for level in range(2) for pair in range(4)]
+    for first in range(0, len(units), GROUP):
+        group = units[first : first + GROUP]
+        places = [
+            (slice(level * LEVEL_ROWS, (level + 1) * LEVEL_ROWS), slice(pair * 128, (pair + 1) * 128))
+            for level, pair in group
+        ]
+        probs = att(group)
+        d_probs = [
+            dot(
+                per_head(projected[rows, 1024 + cols.start : 1024 + cols.stop]),
+                d_low[rows, cols],
+                ((1,), (1,)),
+            ).reshape(2, LEVEL_ROWS, LEVEL_ROWS)
+            for rows, cols in places
+        ]
+        d_values = [
+            dot(p.astype(BF16).reshape(2 * LEVEL_ROWS, LEVEL_ROWS), d_low[rows, cols])
+            for p, (rows, cols) in zip(probs, places)
+        ]
+        inner = [jnp.sum(p * d, axis=1, keepdims=True) for p, d in zip(probs, d_probs)]
+        d_scores = [
+            (p * (d - i)).astype(BF16).reshape(2 * LEVEL_ROWS, LEVEL_ROWS)
+            for p, d, i in zip(probs, d_probs, inner)
+        ]
+        d_keys = [dot(d, projected[rows, cols]) for d, (rows, cols) in zip(d_scores, places)]
+        d_queries = [
+            dot(
+                d,
+                per_head(projected[rows, 512 + cols.start : 512 + cols.stop], SCORE_SCALE),
+                ((0,), (0,)),
+            )
+            for d, (rows, cols) in zip(d_scores, places)
+        ]
+        for (rows, cols), d_query, d_key, d_value in zip(places, d_queries, d_keys, d_values):
+            dqkv[rows, cols] = d_query.astype(BF16)
+            dqkv[rows, 512 + cols.start : 512 + cols.stop] = jnp.where(
+                lane < 64, d_key[:LEVEL_ROWS], d_key[LEVEL_ROWS:]
             ).astype(BF16)
-            dqkv[rows, 1024 + pair * 128 : 1024 + (pair + 1) * 128] = jnp.where(
+            dqkv[rows, 1024 + cols.start : 1024 + cols.stop] = jnp.where(
                 lane < 64, d_value[:LEVEL_ROWS], d_value[LEVEL_ROWS:]
             ).astype(BF16)
 
@@ -226,7 +245,8 @@
     scaled_low = scaled.astype(BF16)
     for copy, third in zip(fetches, thirds):
         copy.wait()
-        projected_out[:, third] = dot(scaled_low, w_qkv[third, :], ((1,), (1,))).astype(BF16)
+        projected = dot(scaled_low, w_qkv[third, :], ((1,), (1,)))
+        projected_out[:, third] = (projected * (SCORE_SCALE if third.start == 0 else 1.0)).astype(BF16)
 
     lane_row = row_index((1, 128), 1) >> 4
     along = labels[0]
@@ -240,16 +260,22 @@
         axis=0,
     )
 
-    def probabilities(level, pair):
-        rows = slice(level * LEVEL_ROWS, (level + 1) * LEVEL_ROWS)
-        cols = slice(pair * 128, (pair + 1) * 128)
-        added = bias[pair * 192 : (pair + 1) * 192, :].reshape(2, LEVEL_ROWS, 128) + allowed[None]
-        keys = per_head(projected_out[rows, 512 + pair * 128 : 512 + (pair + 1) * 128])
-        scores = dot(keys, projected_out[rows, cols], ((1,), (1,))).reshape(2, LEVEL_ROWS, LEVEL_ROWS)
-        scores = scores * SCORE_SCALE + added[:, :, :LEVEL_ROWS]
-        weights = jnp.exp(scores - jnp.max(scores, axis=1, keepdims=True))
-        probs = weights * (1.0 / jnp.sum(weights, axis=1, keepdims=True))
-        att_out[level, pair] = probs.astype(BF16)
+    def probabilities(group):
+        scores = []
+        for level, pair in group:
+            rows = slice(level * LEVEL_ROWS, (level + 1) * LEVEL_ROWS)
+            cols = slice(pair * 128, (pair + 1) * 128)
+            keys = per_head(projected_out[rows, 512 + cols.start : 512 + cols.stop])
+            score = dot(keys, projected_out[rows, cols], ((1,), (1,)))
+            scores.append(score.reshape(2, LEVEL_ROWS, LEVEL_ROWS))
+        probs = []
+        for (level, pair), score in zip(group, scores):
+            added = bias[pair * 192 : (pair + 1) * 192, :].reshape(2, LEVEL_ROWS, 128) + allowed[None]
+            score = score + added[:, :, :LEVEL_ROWS]
+            weights = jnp.exp(score - jnp.max(score, axis=1, keepdims=True))
+            probs.append(weights * (1.0 / jnp.sum(weights, axis=1, keepdims=True)))
+        for (level, pair), prob in zip(group, probs):
+            att_out[level, pair] = prob.astype(BF16)
         return probs
 
     attention_backward(probabilities, d_low, projected_out, dqkv)
@@ -263,7 +289,9 @@
     fetch = pltpu.make_async_copy(w_qkv_ref, w_qkv, sem)
     fetch.start()
     d_low = (dot(fields[1], w_proj[...]) + dot(arrived[...], w_proj[...])).astype(BF16)
-    attention_backward(lambda level, pair: att[level, pair].astype(F32), d_low, projected, dqkv)
+    attention_backward(
+        lambda group: [att[level, pair].astype(F32) for level, pair in group], d_low, projected, dqkv
+    )
     lane = row_index((80, 128), 1)
     for t in range(4):
         whole = [
@@ -297,32 +325,36 @@
 def product_kernel(
     lat_index, blocks, low, high, other_low, other_high, kept, above, out, sideways
 ):
-    whole = jnp.zeros((128, FEATURES), F32)
-    upper = jnp.zeros((128, FEATURES), F32)
-    lower = jnp.zeros((128, FEATURES), F32)
     lats = blocks.shape[0]
-    for x in range(lats // 2):
-        inputs, other_inputs = (low, other_low) if x < 2 else (high, other_high)
-        first = lat_index[0] + 2 * x
-        first = jnp.where(first >= lats, first - lats, first)
-        second = first + 1 - 2 * lax.rem(lat_index[0], 2)
-        for cells, place in ((inputs, first), (other_inputs, second)):
-            whole += dot(blocks[place, :144, :], cells[x % 2], ((0,), (0,)))
-            folded = blocks[place, 144:, :]
-            upper += dot(folded, cells[x % 2, :80, :], ((0,), (0,)))
-            lower += dot(folded[:64], cells[x % 2, 80:, :], ((0,), (0,)))
-    half = upper[:64] + lower[64:]
-    whole_t = whole.T
-    half_t = jnp.concatenate([half, jnp.zeros((64, FEATURES), F32)], axis=0).T
+
+    def columns(place):
+        folded = blocks[place, 144:, :]
+        bottom = pltpu.roll(folded[:64].astype(F32), 64, 1).astype(BF16)
+        return jnp.concatenate(
+            [blocks[place, :144, :], jnp.concatenate([folded, bottom], axis=0)], axis=1
+        )
+
+    gradients, cells = [], []
+    for x in range(0, lats // 2, 2):
+        places = []
+        for step in (x, x + 1):
+            first = lat_index[0] + 2 * step
+            first = jnp.where(first >= lats, first - lats, first)
+            places.append((first, first + 1 - 2 * lax.rem(lat_index[0], 2)))
+        for same, source in enumerate((low, other_low) if x == 0 else (high, other_high)):
+            gradients.extend(columns(place[same]) for place in places)
+            cells.append(source[...].reshape(2 * PACKED_ROWS, FEATURES))
+    product = dot(
+        jnp.concatenate(cells, axis=0), jnp.concatenate(gradients, axis=0), ((0,), (0,))
+    )
     bands = out.shape[0]
     width = FEATURES // bands
-    lane = row_index((width // 2, 128), 1)
-    for band in range(bands):
-        out[band, :width, :] = whole_t[band * width : (band + 1) * width].astype(BF16)
-        part = half_t[band * width : (band + 1) * width]
-        out[band, width:, :] = jnp.where(
-            lane < 64, part[: width // 2], pltpu.roll(part[width // 2 :], 64, 1)
-        ).astype(BF16)
+    whole = product[:, :128].reshape(bands, width, 128)
+    half = product[:, 128:].reshape(bands, width, 128)
+    lane = row_index((bands, width // 2, 128), 2)
+    out[:, :width, :] = whole.astype(BF16)
+    folded = jnp.where(lane < 64, half[:, : width // 2], pltpu.roll(half[:, width // 2 :], 64, 2))
+    out[:, width:, :] = folded.astype(BF16)
     tiles = []
     for part in (above, kept):
         part = part[...].astype(F32)

time: 83.7 us -> 81.6 us (0.975)
  Pallas kernels: 12.4 us -> 10.3 us
    pallas_call x8, Pallas kernels: 12.4 us -> 10.3 us  [run(): pl.pallas_call(kernel, out_shape=out_shape, in_specs=specs, out_specs=out...]
  transfers between devices with their start and end apart: 13 -> 13, of which waited for: 3 -> 4; matrix products, arithmetic and copies ran while one was open for 2% -> 2% of each run, Pallas kernels for 4% -> 4%
where the time goes in v10:
time: 81.6 us; the launch traced here: 80.9 us
  starting transfers between devices  51.9 us (64%)
  waiting for transfers between devices  16.3 us (20%)
  Pallas kernels  10.3 us (13%)
  local copies, waits for them, and re-layouts  1.61 us (2%)
    ppermute x8, starting transfers between devices, passed(): return lax.ppermute(array, ('lat', 'lon'), pairs)  31.6 us
    ppermute x8, waiting for transfers between devices, passed(): return lax.ppermute(array, ('lat', 'lon'), pairs)  16.3 us
    pallas_call x8, Pallas kernels, run(): pl.pallas_call(kernel, out_shape=out_shape, in_specs=specs, out_specs=out...  10.3 us
    all_to_all x1, starting transfers between devices, per_device(): slices = lax.all_to_all(slices, 'lon', 0, 0, tiled=True)  8.31 us
    ppermute x2, starting transfers between devices, other_core(): lax.ppermute(array, 'lat', [(a, a ^ 1) for a in range(lax.axis_size('lat'...  4.33 us
    all_to_all x1, starting transfers between devices, per_device(): blocks = lax.all_to_all(blocks, 'lat', 0, 0, tiled=True)  4.08 us
    ppermute x1, starting transfers between devices, per_device(): arrived = lax.ppermute(skip, 'phase', [(1, 0)])  3.55 us
  transfers between devices with their start and end apart: 13, of which 4 were waited for; matrix products, arithmetic and copies ran while one was open for 2% of the time, Pallas kernels for 4%

profile of v10, /device:TPU:8, one launch (start us, length us, event | category | flops | bytes accessed | tf_op | source)
XLA Modules:
  0.0 80.9 jit_solution(8789521475202881939)
XLA Ops:
  0.6 1.9 %shard_map.86 = (bf16[80,512]{1,0:T(8,128)(2,1)}, bf16[72,512]{1,0:T(8,128)(2,1)}, bf16[72,512]{1,0:T(8,128)(2,1)}, bf16[80,512]{1,0:T(8,128)(2,1)}) custom-call(s32[6]{0:T(128)} %labels_ref.1, bf16[6,12,2,512]{3,2,1,0:T(2,128)(2,1)} %bitcast.16, bf16[6,12,2,512]{3,2,1,0:T(2,128)(2,1)} %bitcast.17), custom_call_target="tpu_custom_call" | custom-call | tf_op jit(solution)/shard_map/pallas_call | solution.py:37
  2.5 15.4 %collective-permute-start.2 = (bf16[80,512]{1,0:T(8,128)(2,1)}, bf16[80,512]{1,0:T(8,128)(2,1)S(1)}, u32[]{:S(2)}, u32[]{:S(2)}) collective-permute-start(bf16[80,512]{1,0:T(8,128)(2,1)} %get-tuple-element.21), channel_id=1, source_target_pairs={{0,255},{1,224},{2,225},{3,226},{4,227},{5,228},{6,229},{7,230},{8... | collective-permute-start | bytes 245768 | tf_op jit(solution)/shard_map/ppermute | solution.py:413
  17.9 2.5 %collective-permute-start = (bf16[72,512]{1,0:T(8,128)(2,1)}, bf16[72,512]{1,0:T(8,128)(2,1)S(1)}, u32[]{:S(2)}, u32[]{:S(2)}) collective-permute-start(bf16[72,512]{1,0:T(8,128)(2,1)} %get-tuple-element.19), channel_id=1, source_target_pairs={{0,31},{1,0},{2,1},{3,2},{4,3},{5,4},{6,5},{7,6},{8,7},{9,8},{10,9... | collective-permute-start | bytes 221192 | tf_op jit(solution)/shard_map/ppermute | solution.py:413
  20.4 0.6 collective-permute-start.1
  20.9 0.8 slice_bitcast_fusion
  21.7 0.0 copy-start
  21.7 0.0 copy-start.1
  21.7 0.0 copy-start.2
  21.8 0.5 shard_map.87.bias
  22.2 2.1 %collective-permute-done.lon = bf16[72,512]{1,0:T(8,128)(2,1)S(1)} collective-permute-done((bf16[72,512]{1,0:T(8,128)(2,1)}, bf16[72,512]{1,0:T(8,128)(2,1)S(1)}, u32[]{:S(2)}, u32[]{:S(2)}) %collective-permute-start) | collective-permute-done | bytes 73760 | tf_op jit(solution)/shard_map/ppermute | solution.py:413
  24.3 0.0 collective-permute-done.1.lat
  24.3 0.0 collective-permute-done.2.cor
  24.3 0.0 copy-done
  24.4 0.0 copy-done.1
  24.4 0.0 copy-done.2
  24.4 3.4 %shard_map.88 = (bf16[192,512]{1,0:T(8,128)(2,1)S(1)}, bf16[144,512]{1,0:T(8,128)(2,1)S(1)}, bf16[2,192,512]{2,1,0:T(8,128)(2,1)S(1)}, bf16[192,1536]{1,0:T(8,128)(2,1)S(1)}, bf16[2,4,2,96,96]{4,3,2,1,0:T(8,128)(2,1)S(1)}) custom-call(bf16[80,512]{1,0:T(8,128)(2,1)S(1)} %copy-done.1, bf16[72,512]{1,0:T(8,128)(2,1)S(1)} %collective-permute-done.lon, ...), custom_call_target="tpu_custom_call" | custom-call | tf_op jit(solution)/shard_map/pallas_call | solution.py:37
  27.8 3.6 %collective-permute-start.3 = (bf16[192,512]{1,0:T(8,128)(2,1)S(1)}, bf16[192,512]{1,0:T(8,128)(2,1)S(1)}, u32[]{:S(2)}, u32[]{:S(2)}) collective-permute-start(bf16[192,512]{1,0:T(8,128)(2,1)S(1)} %get-tuple-element.22), channel_id=1, source_target_pairs={{256,0},{257,1},{258,2},{259,3},{260,4},{261,5},{262,6},{263,7},{2... | collective-permute-start | bytes 589832 | tf_op jit(solution)/shard_map/ppermute | solution.py:467
  31.4 3.8 %collective-permute-start.5 = (bf16[144,512]{1,0:T(8,128)(2,1)S(1)}, bf16[144,512]{1,0:T(8,128)(2,1)S(1)}, u32[]{:S(2)}, u32[]{:S(2)}) collective-permute-start(bf16[144,512]{1,0:T(8,128)(2,1)S(1)} %get-tuple-element.29.a), channel_id=1, source_target_pairs={{0,192},{1,193},{2,194},{3,195},{4,196},{5,197},{6,198},{7,199},{8... | collective-permute-start | bytes 442376 | tf_op jit(solution)/shard_map/ppermute | solution.py:413
  35.2 2.5 %collective-permute-start.6 = (bf16[144,512]{1,0:T(8,128)(2,1)S(1)}, bf16[144,512]{1,0:T(8,128)(2,1)S(1)}, u32[]{:S(2)}, u32[]{:S(2)}) collective-permute-start(bf16[144,512]{1,0:T(8,128)(2,1)S(1)} %get-tuple-element.29.a), channel_id=1, source_target_pairs={{0,128},{1,129},{2,130},{3,131},{4,132},{5,133},{6,134},{7,135},{8... | collective-permute-start | bytes 442376 | tf_op jit(solution)/shard_map/ppermute | solution.py:413
  37.7 2.8 %collective-permute-start.7 = (bf16[144,512]{1,0:T(8,128)(2,1)S(1)}, bf16[144,512]{1,0:T(8,128)(2,1)S(1)}, u32[]{:S(2)}, u32[]{:S(2)}) collective-permute-start(bf16[144,512]{1,0:T(8,128)(2,1)S(1)} %get-tuple-element.29.a), channel_id=1, source_target_pairs={{0,64},{1,65},{2,66},{3,67},{4,68},{5,69},{6,70},{7,71},{8,72},{9,... | collective-permute-start | bytes 442376 | tf_op jit(solution)/shard_map/ppermute | solution.py:413
  40.5 0.0 collective-permute-done.3.arrived
  40.5 2.3 %shard_map.89 = (bf16[8,224,128]{2,1,0:T(8,128)(2,1)}, bf16[72,512]{1,0:T(8,128)(2,1)S(1)}, bf16[72,512]{1,0:T(8,128)(2,1)S(1)}) custom-call(bf16[192,512]{1,0:T(8,128)(2,1)S(1)} %collective-permute-done.3.arrived, bf16[2,192,512]{2,1,0:T(8,128)(2,1)S(1)} %get-tuple-element.23.fields, bf16[192,1536]{1,0:T(8,128)(2,1)S(1)} %get-tuple-element.24.projected, ...), custom_call_target="tpu_custom_call" | custom-call | flops 4000000000 | bytes 20000000 | tf_op jit(solution)/shard_map/pallas_call | solution.py:37
  42.9 4.1 %all-to-all-start = ((bf16[8,224,128]{2,1,0:T(8,128)(2,1)}), bf16[8,224,128]{2,1,0:T(8,128)(2,1)S(1)}, u32[]{:S(2)}, u32[]{:S(2)}) async-start(bf16[8,224,128]{2,1,0:T(8,128)(2,1)} %get-tuple-element.28), calls=%async_computation | async-start | bytes 917504 | tf_op jit(solution)/shard_map/all_to_all | solution.py:476
  46.9 0.0 collective-permute-done.5.b
  46.9 0.0 collective-permute-done.6.c
  47.0 0.1 collective-permute-done.7.d
  47.1 2.3 %collective-permute-start.8 = (bf16[2,144,512]{2,1,0:T(8,128)(2,1)S(1)}, bf16[2,144,512]{2,1,0:T(8,128)(2,1)S(1)}, u32[]{:S(2)}, u32[]{:S(2)}) collective-permute-start(bf16[2,144,512]{2,1,0:T(8,128)(2,1)S(1)} %get-tuple-element.30.low), channel_id=1, source_target_pairs={{0,32},{32,0},{64,96},{96,64},{128,160},{160,128},{192,224},{224,1... | collective-permute-start | bytes 884744 | tf_op jit(solution)/shard_map/ppermute | solution.py:417
  49.4 2.0 %collective-permute-start.9 = (bf16[2,144,512]{2,1,0:T(8,128)(2,1)S(1)}, bf16[2,144,512]{2,1,0:T(8,128)(2,1)S(1)}, u32[]{:S(2)}, u32[]{:S(2)}) collective-permute-start(bf16[2,144,512]{2,1,0:T(8,128)(2,1)S(1)} %get-tuple-element.31.high), channel_id=1, source_target_pairs={{0,32},{32,0},{64,96},{96,64},{128,160},{160,128},{192,224},{224,1... | collective-permute-start | bytes 884744 | tf_op jit(solution)/shard_map/ppermute | solution.py:417
  51.5 0.4 collective-permute-start.4
  51.9 5.5 %collective-permute-done.4.above = bf16[72,512]{1,0:T(8,128)(2,1)S(1)} collective-permute-done((bf16[72,512]{1,0:T(8,128)(2,1)S(1)}, bf16[72,512]{1,0:T(8,128)(2,1)S(1)}, u32[]{:S(2)}, u32[]{:S(2)}) %collective-permute-start.4) | collective-permute-done | bytes 73760 | tf_op jit(solution)/shard_map/ppermute | solution.py:413
  57.4 0.0 collective-permute-done.8.other_low
  57.4 0.0 collective-permute-done.9.other_high
  57.4 0.0 all-to-all-done.blocks
  57.4 1.4 %shard_map.91 = (bf16[32,24,128]{2,1,0:T(8,128)(2,1)}, bf16[72,512]{1,0:T(8,128)(2,1)S(1)}) custom-call(s32[1]{0:T(128)} %bitcast.7.lat_index, bf16[8,224,128]{2,1,0:T(8,128)(2,1)S(1)} %all-to-all-done.blocks, bf16[2,144,512]{2,1,0:T(8,128)(2,1)S(1)} %get-tuple-element.30.low, bf16[2,144,512]{2,1,0:T(8,128)(2,1)S(1)} %get-tuple-element.31.high, ...), custom_call_target="tpu_custom_call" | custom-call | tf_op jit(solution)/shard_map/pallas_call | solution.py:37
  58.8 8.3 %all-to-all-start.1 = ((bf16[32,24,128]{2,1,0:T(8,128)(2,1)}), bf16[32,24,128]{2,1,0:T(8,128)(2,1)S(1)}, u32[]{:S(2)}, u32[]{:S(2)}) async-start(bf16[32,24,128]{2,1,0:T(8,128)(2,1)} %get-tuple-element.33), calls=%async_computation.1 | async-start | bytes 393216 | tf_op jit(solution)/shard_map/all_to_all | solution.py:489
  67.1 3.7 %collective-permute-start.10 = (bf16[72,512]{1,0:T(8,128)(2,1)S(1)}, bf16[72,512]{1,0:T(8,128)(2,1)S(1)}, u32[]{:S(2)}, u32[]{:S(2)}) collective-permute-start(bf16[72,512]{1,0:T(8,128)(2,1)S(1)} %get-tuple-element.32), channel_id=1, source_target_pairs={{0,1},{1,2},{2,3},{3,4},{4,5},{5,6},{6,7},{7,8},{8,9},{9,10},{10,1... | collective-permute-start | bytes 221192 | tf_op jit(solution)/shard_map/ppermute | solution.py:413
  70.8 8.5 %collective-permute-done.10.left = bf16[72,512]{1,0:T(8,128)(2,1)S(1)} collective-permute-done((bf16[72,512]{1,0:T(8,128)(2,1)S(1)}, bf16[72,512]{1,0:T(8,128)(2,1)S(1)}, u32[]{:S(2)}, u32[]{:S(2)}) %collective-permute-start.10) | collective-permute-done | bytes 73760 | tf_op jit(solution)/shard_map/ppermute | solution.py:413
  79.3 0.1 shard_map.92
  79.4 0.8 %copy.9 = bf16[1,2,6,12,512]{4,1,3,2,0:T(2,128)(2,1)} copy(bf16[1,2,6,12,512]{4,3,2,1,0:T(8,128)(2,1)S(1)} %shard_map.92) | data formatting | bytes 294912
  80.2 0.0 all-to-all-done.1.parts
  80.2 0.7 shard_map.93
  (2 shorter events, 0.0 us)
Async XLA Ops:
  2.5 21.8 %collective-permute-start.2 = (bf16[80,512]{1,0:T(8,128)(2,1)}, bf16[80,512]{1,0:T(8,128)(2,1)S(1)}, u32[]{:S(2)}, u32[]{:S(2)}) collective-permute-start(bf16[80,512]{1,0:T(8,128)(2,1)} %get-tuple-element.21), channel_id=1, source_target_pairs={{0,255},{1,224},{2,225},{3,226},{4,227},{5,228},{6,229},{7,230},{8... | collective-permute-start | bytes 245768 | tf_op jit(solution)/shard_map/ppermute | solution.py:413
  17.9 6.5 %collective-permute-start = (bf16[72,512]{1,0:T(8,128)(2,1)}, bf16[72,512]{1,0:T(8,128)(2,1)S(1)}, u32[]{:S(2)}, u32[]{:S(2)}) collective-permute-start(bf16[72,512]{1,0:T(8,128)(2,1)} %get-tuple-element.19), channel_id=1, source_target_pairs={{0,31},{1,0},{2,1},{3,2},{4,3},{5,4},{6,5},{7,6},{8,7},{9,8},{10,9... | collective-permute-start | bytes 221192 | tf_op jit(solution)/shard_map/ppermute | solution.py:413
  20.4 4.0 %collective-permute-start.1 = (bf16[72,512]{1,0:T(8,128)(2,1)}, bf16[72,512]{1,0:T(8,128)(2,1)S(1)}, u32[]{:S(2)}, u32[]{:S(2)}) collective-permute-start(bf16[72,512]{1,0:T(8,128)(2,1)} %get-tuple-element.20), channel_id=1, source_target_pairs={{0,224},{1,225},{2,226},{3,227},{4,228},{5,229},{6,230},{7,231},{8... | collective-permute-start | bytes 221192 | tf_op jit(solution)/shard_map/ppermute | solution.py:413
  21.7 2.6 %copy-start = (bf16[1,512,512]{2,1,0:T(8,128)(2,1)S(1)}, bf16[1,512,512]{2,1,0:T(8,128)(2,1)}, u32[]{:S(2)}) copy-start(bf16[1,512,512]{2,1,0:T(8,128)(2,1)} %param.10) | copy-start | bytes 1572868
  21.7 2.6 %copy-start.1 = (bf16[80,512]{1,0:T(8,128)(2,1)S(1)}, bf16[80,512]{1,0:T(8,128)(2,1)}, u32[]{:S(2)}) copy-start(bf16[80,512]{1,0:T(8,128)(2,1)} %get-tuple-element.18.own) | copy-start | bytes 245764
  21.7 2.6 %copy-start.2 = (f32[1,512]{1,0:T(1,128)S(1)}, f32[1,512]{1,0:T(1,128)}, u32[]{:S(2)}) copy-start(f32[1,512]{1,0:T(1,128)} %gain.3) | copy-start | bytes 6148
  27.8 12.7 %collective-permute-start.3 = (bf16[192,512]{1,0:T(8,128)(2,1)S(1)}, bf16[192,512]{1,0:T(8,128)(2,1)S(1)}, u32[]{:S(2)}, u32[]{:S(2)}) collective-permute-start(bf16[192,512]{1,0:T(8,128)(2,1)S(1)} %get-tuple-element.22), channel_id=1, source_target_pairs={{256,0},{257,1},{258,2},{259,3},{260,4},{261,5},{262,6},{263,7},{2... | collective-permute-start | bytes 589832 | tf_op jit(solution)/shard_map/ppermute | solution.py:467
  31.4 15.6 %collective-permute-start.5 = (bf16[144,512]{1,0:T(8,128)(2,1)S(1)}, bf16[144,512]{1,0:T(8,128)(2,1)S(1)}, u32[]{:S(2)}, u32[]{:S(2)}) collective-permute-start(bf16[144,512]{1,0:T(8,128)(2,1)S(1)} %get-tuple-element.29.a), channel_id=1, source_target_pairs={{0,192},{1,193},{2,194},{3,195},{4,196},{5,197},{6,198},{7,199},{8... | collective-permute-start | bytes 442376 | tf_op jit(solution)/shard_map/ppermute | solution.py:413
  35.2 11.8 %collective-permute-start.6 = (bf16[144,512]{1,0:T(8,128)(2,1)S(1)}, bf16[144,512]{1,0:T(8,128)(2,1)S(1)}, u32[]{:S(2)}, u32[]{:S(2)}) collective-permute-start(bf16[144,512]{1,0:T(8,128)(2,1)S(1)} %get-tuple-element.29.a), channel_id=1, source_target_pairs={{0,128},{1,129},{2,130},{3,131},{4,132},{5,133},{6,134},{7,135},{8... | collective-permute-start | bytes 442376 | tf_op jit(solution)/shard_map/ppermute | solution.py:413
  37.7 9.4 %collective-permute-start.7 = (bf16[144,512]{1,0:T(8,128)(2,1)S(1)}, bf16[144,512]{1,0:T(8,128)(2,1)S(1)}, u32[]{:S(2)}, u32[]{:S(2)}) collective-permute-start(bf16[144,512]{1,0:T(8,128)(2,1)S(1)} %get-tuple-element.29.a), channel_id=1, source_target_pairs={{0,64},{1,65},{2,66},{3,67},{4,68},{5,69},{6,70},{7,71},{8,72},{9,... | collective-permute-start | bytes 442376 | tf_op jit(solution)/shard_map/ppermute | solution.py:413
  42.9 14.5 %all-to-all-start = ((bf16[8,224,128]{2,1,0:T(8,128)(2,1)}), bf16[8,224,128]{2,1,0:T(8,128)(2,1)S(1)}, u32[]{:S(2)}, u32[]{:S(2)}) async-start(bf16[8,224,128]{2,1,0:T(8,128)(2,1)} %get-tuple-element.28), calls=%async_computation | async-start | bytes 917504 | tf_op jit(solution)/shard_map/all_to_all | solution.py:476
  47.1 10.3 %collective-permute-start.8 = (bf16[2,144,512]{2,1,0:T(8,128)(2,1)S(1)}, bf16[2,144,512]{2,1,0:T(8,128)(2,1)S(1)}, u32[]{:S(2)}, u32[]{:S(2)}) collective-permute-start(bf16[2,144,512]{2,1,0:T(8,128)(2,1)S(1)} %get-tuple-element.30.low), channel_id=1, source_target_pairs={{0,32},{32,0},{64,96},{96,64},{128,160},{160,128},{192,224},{224,1... | collective-permute-start | bytes 884744 | tf_op jit(solution)/shard_map/ppermute | solution.py:417
  49.4 8.0 %collective-permute-start.9 = (bf16[2,144,512]{2,1,0:T(8,128)(2,1)S(1)}, bf16[2,144,512]{2,1,0:T(8,128)(2,1)S(1)}, u32[]{:S(2)}, u32[]{:S(2)}) collective-permute-start(bf16[2,144,512]{2,1,0:T(8,128)(2,1)S(1)} %get-tuple-element.31.high), channel_id=1, source_target_pairs={{0,32},{32,0},{64,96},{96,64},{128,160},{160,128},{192,224},{224,1... | collective-permute-start | bytes 884744 | tf_op jit(solution)/shard_map/ppermute | solution.py:417
  51.5 5.9 %collective-permute-start.4 = (bf16[72,512]{1,0:T(8,128)(2,1)S(1)}, bf16[72,512]{1,0:T(8,128)(2,1)S(1)}, u32[]{:S(2)}, u32[]{:S(2)}) collective-permute-start(bf16[72,512]{1,0:T(8,128)(2,1)S(1)} %get-tuple-element.27), channel_id=1, source_target_pairs={{0,32},{1,33},{2,34},{3,35},{4,36},{5,37},{6,38},{7,39},{8,40},{9,... | collective-permute-start | bytes 221192 | tf_op jit(solution)/shard_map/ppermute | solution.py:413
  58.8 21.4 %all-to-all-start.1 = ((bf16[32,24,128]{2,1,0:T(8,128)(2,1)}), bf16[32,24,128]{2,1,0:T(8,128)(2,1)S(1)}, u32[]{:S(2)}, u32[]{:S(2)}) async-start(bf16[32,24,128]{2,1,0:T(8,128)(2,1)} %get-tuple-element.33), calls=%async_computation.1 | async-start | bytes 393216 | tf_op jit(solution)/shard_map/all_to_all | solution.py:489
  67.1 12.2 %collective-permute-start.10 = (bf16[72,512]{1,0:T(8,128)(2,1)S(1)}, bf16[72,512]{1,0:T(8,128)(2,1)S(1)}, u32[]{:S(2)}, u32[]{:S(2)}) collective-permute-start(bf16[72,512]{1,0:T(8,128)(2,1)S(1)} %get-tuple-element.32), channel_id=1, source_target_pairs={{0,1},{1,2},{2,3},{3,4},{4,5},{5,6},{6,7},{7,8},{8,9},{9,10},{10,1... | collective-permute-start | bytes 221192 | tf_op jit(solution)/shard_map/ppermute | solution.py:413

commit v11 on v10

--- a/solution.py
+++ b/solution.py
@@ -15,6 +15,7 @@
 MASKED = -1e30
 SCORE_SCALE = 0.125
 MIB = 1024 * 1024
+HIDING = pl.CostEstimate(flops=4_000_000_000, bytes_accessed=20_000_000, transcendentals=0)
 
 LEVEL_ROWS = 96
 ROWS = 192
@@ -323,7 +324,7 @@
 
 
 def product_kernel(
-    lat_index, blocks, low, high, other_low, other_high, kept, above, out, sideways
+    lat_index, blocks, low, high, other_low, other_high, out
 ):
     lats = blocks.shape[0]
 
@@ -355,6 +356,9 @@
     out[:, :width, :] = whole.astype(BF16)
     folded = jnp.where(lane < 64, half[:, : width // 2], pltpu.roll(half[:, width // 2 :], 64, 2))
     out[:, width:, :] = folded.astype(BF16)
+
+
+def sideways_kernel(kept, above, sideways):
     tiles = []
     for part in (above, kept):
         part = part[...].astype(F32)
@@ -442,7 +446,7 @@
     bias = call(
         bias_kernel,
         struct((HEADS * LEVEL_ROWS, 128), F32),
-        cost=pl.CostEstimate(flops=4_000_000_000, bytes_accessed=20_000_000, transcendentals=0),
+        cost=HIDING,
     )(table)
 
     scratch = [
@@ -471,7 +475,7 @@
         (struct((lats, 224, 128), BF16), part, part),
         scratch,
         places={5: pl.ANY},
-        cost=pl.CostEstimate(flops=4_000_000_000, bytes_accessed=20_000_000, transcendentals=0),
+        cost=HIDING,
     )(arrived, fields, projected, att, w_proj, w_qkv, norm_gain)
     blocks = lax.all_to_all(blocks, "lat", 0, 0, tiled=True)
     two = struct((2, PACKED_ROWS, FEATURES), BF16)
@@ -479,11 +483,10 @@
     other_low, other_high = other_core(low), other_core(high)
     above = passed(up, 1, 0)
     rows = FEATURES * 3 // 2 // lons
-    slices, sideways = call(
-        product_kernel,
-        (struct((lons, rows, 128), BF16), part),
-        places={0: pltpu.SMEM},
-    )(lat_index, blocks, low, high, other_low, other_high, kept, above)
+    slices = call(product_kernel, struct((lons, rows, 128), BF16), places={0: pltpu.SMEM})(
+        lat_index, blocks, low, high, other_low, other_high
+    )
+    sideways = call(sideways_kernel, part, cost=HIDING)(kept, above)
     left = passed(sideways, 0, 1)
     grad_input = call(join_kernel, struct((1, 2, 6, 12, FEATURES), BF16))(kept, above, left)
     slices = lax.all_to_all(slices, "lon", 0, 0, tiled=True)

time: 81.6 us -> 81.1 us (level)
    ppermute x8, waiting for transfers between devices: 16.3 us -> 11 us  [passed(): return lax.ppermute(array, ('lat', 'lon'), pairs)]
    all_to_all x1, waiting for transfers between devices: 0.01 us -> 3.78 us  [per_device(): blocks = lax.all_to_all(blocks, 'lat', 0, 0, tiled=True)]
    ppermute x2, waiting for transfers between devices: 0.01 us -> 1.04 us  [other_core(): lax.ppermute(array, 'lat', [(a, a ^ 1) for a in range(lax.axis_size('lat'...]
    pallas_call x8 -> x9, Pallas kernels: 10.3 us -> 10.3 us  [run(): pl.pallas_call(kernel, out_shape=out_shape, in_specs=specs, out_specs=out...]
  transfers between devices with their start and end apart: 13 -> 13, of which waited for: 4 -> 5; matrix products, arithmetic and copies ran while one was open for 2% -> 2% of each run, Pallas kernels for 4% -> 5%
where the time goes in v11:
time: 81.1 us; the launch traced here: 80.4 us
  starting transfers between devices  51.9 us (64%)
  waiting for transfers between devices  15.8 us (19%)
  Pallas kernels  10.3 us (13%)
  local copies, waits for them, and re-layouts  1.61 us (2%)
  between operations  0.82 us (1%)
    ppermute x8, starting transfers between devices, passed(): return lax.ppermute(array, ('lat', 'lon'), pairs)  31.6 us
    ppermute x8, waiting for transfers between devices, passed(): return lax.ppermute(array, ('lat', 'lon'), pairs)  11 us
    pallas_call x9, Pallas kernels, run(): pl.pallas_call(kernel, out_shape=out_shape, in_specs=specs, out_specs=out...  10.3 us
    all_to_all x1, starting transfers between devices, per_device(): slices = lax.all_to_all(slices, 'lon', 0, 0, tiled=True)  8.28 us
    ppermute x2, starting transfers between devices, other_core(): lax.ppermute(array, 'lat', [(a, a ^ 1) for a in range(lax.axis_size('lat'...  4.33 us
    all_to_all x1, starting transfers between devices, per_device(): blocks = lax.all_to_all(blocks, 'lat', 0, 0, tiled=True)  4.08 us
    all_to_all x1, waiting for transfers between devices, per_device(): blocks = lax.all_to_all(blocks, 'lat', 0, 0, tiled=True)  3.78 us
    ppermute x1, starting transfers between devices, per_device(): arrived = lax.ppermute(skip, 'phase', [(1, 0)])  3.55 us
  transfers between devices with their start and end apart: 13, of which 5 were waited for; matrix products, arithmetic and copies ran while one was open for 2% of the time, Pallas kernels for 5%

profile of v11, /device:TPU:8, one launch (start us, length us, event | category | flops | bytes accessed | tf_op | source)
XLA Modules:
  0.0 80.4 jit_solution(3336042759410141590)
XLA Ops:
  0.6 1.9 %shard_map.86 = (bf16[80,512]{1,0:T(8,128)(2,1)}, bf16[72,512]{1,0:T(8,128)(2,1)}, bf16[72,512]{1,0:T(8,128)(2,1)}, bf16[80,512]{1,0:T(8,128)(2,1)}) custom-call(s32[6]{0:T(128)} %labels_ref.1, bf16[6,12,2,512]{3,2,1,0:T(2,128)(2,1)} %bitcast.16, bf16[6,12,2,512]{3,2,1,0:T(2,128)(2,1)} %bitcast.17), custom_call_target="tpu_custom_call" | custom-call | tf_op jit(solution)/shard_map/pallas_call | solution.py:38
  2.5 15.4 %collective-permute-start.2 = (bf16[80,512]{1,0:T(8,128)(2,1)}, bf16[80,512]{1,0:T(8,128)(2,1)S(1)}, u32[]{:S(2)}, u32[]{:S(2)}) collective-permute-start(bf16[80,512]{1,0:T(8,128)(2,1)} %get-tuple-element.19), channel_id=1, source_target_pairs={{0,255},{1,224},{2,225},{3,226},{4,227},{5,228},{6,229},{7,230},{8... | collective-permute-start | bytes 245768 | tf_op jit(solution)/shard_map/ppermute | solution.py:417
  17.9 2.5 %collective-permute-start = (bf16[72,512]{1,0:T(8,128)(2,1)}, bf16[72,512]{1,0:T(8,128)(2,1)S(1)}, u32[]{:S(2)}, u32[]{:S(2)}) collective-permute-start(bf16[72,512]{1,0:T(8,128)(2,1)} %get-tuple-element.17), channel_id=1, source_target_pairs={{0,31},{1,0},{2,1},{3,2},{4,3},{5,4},{6,5},{7,6},{8,7},{9,8},{10,9... | collective-permute-start | bytes 221192 | tf_op jit(solution)/shard_map/ppermute | solution.py:417
  20.4 0.6 collective-permute-start.1
  20.9 0.8 slice_bitcast_fusion
  21.7 0.0 copy-start
  21.7 0.0 copy-start.1
  21.7 0.0 copy-start.2
  21.8 0.5 shard_map.87.bias
  22.2 2.1 %collective-permute-done.lon = bf16[72,512]{1,0:T(8,128)(2,1)S(1)} collective-permute-done((bf16[72,512]{1,0:T(8,128)(2,1)}, bf16[72,512]{1,0:T(8,128)(2,1)S(1)}, u32[]{:S(2)}, u32[]{:S(2)}) %collective-permute-start) | collective-permute-done | bytes 73760 | tf_op jit(solution)/shard_map/ppermute | solution.py:417
  24.3 0.0 collective-permute-done.1.lat
  24.3 0.0 collective-permute-done.2.cor
  24.3 0.0 copy-done
  24.4 0.0 copy-done.1
  24.4 0.0 copy-done.2
  24.4 3.4 %shard_map.88 = (bf16[192,512]{1,0:T(8,128)(2,1)S(1)}, bf16[144,512]{1,0:T(8,128)(2,1)S(1)}, bf16[2,192,512]{2,1,0:T(8,128)(2,1)S(1)}, bf16[192,1536]{1,0:T(8,128)(2,1)S(1)}, bf16[2,4,2,96,96]{4,3,2,1,0:T(8,128)(2,1)S(1)}) custom-call(bf16[80,512]{1,0:T(8,128)(2,1)S(1)} %copy-done.1, bf16[72,512]{1,0:T(8,128)(2,1)S(1)} %collective-permute-done.lon, ...), custom_call_target="tpu_custom_call" | custom-call | tf_op jit(solution)/shard_map/pallas_call | solution.py:38
  27.8 3.6 %collective-permute-start.3 = (bf16[192,512]{1,0:T(8,128)(2,1)S(1)}, bf16[192,512]{1,0:T(8,128)(2,1)S(1)}, u32[]{:S(2)}, u32[]{:S(2)}) collective-permute-start(bf16[192,512]{1,0:T(8,128)(2,1)S(1)} %get-tuple-element.20), channel_id=1, source_target_pairs={{256,0},{257,1},{258,2},{259,3},{260,4},{261,5},{262,6},{263,7},{2... | collective-permute-start | bytes 589832 | tf_op jit(solution)/shard_map/ppermute | solution.py:471
  31.4 3.8 %collective-permute-start.6 = (bf16[144,512]{1,0:T(8,128)(2,1)S(1)}, bf16[144,512]{1,0:T(8,128)(2,1)S(1)}, u32[]{:S(2)}, u32[]{:S(2)}) collective-permute-start(bf16[144,512]{1,0:T(8,128)(2,1)S(1)} %get-tuple-element.27.a), channel_id=1, source_target_pairs={{0,192},{1,193},{2,194},{3,195},{4,196},{5,197},{6,198},{7,199},{8... | collective-permute-start | bytes 442376 | tf_op jit(solution)/shard_map/ppermute | solution.py:417
  35.2 2.5 %collective-permute-start.7 = (bf16[144,512]{1,0:T(8,128)(2,1)S(1)}, bf16[144,512]{1,0:T(8,128)(2,1)S(1)}, u32[]{:S(2)}, u32[]{:S(2)}) collective-permute-start(bf16[144,512]{1,0:T(8,128)(2,1)S(1)} %get-tuple-element.27.a), channel_id=1, source_target_pairs={{0,128},{1,129},{2,130},{3,131},{4,132},{5,133},{6,134},{7,135},{8... | collective-permute-start | bytes 442376 | tf_op jit(solution)/shard_map/ppermute | solution.py:417
  37.7 2.8 %collective-permute-start.8 = (bf16[144,512]{1,0:T(8,128)(2,1)S(1)}, bf16[144,512]{1,0:T(8,128)(2,1)S(1)}, u32[]{:S(2)}, u32[]{:S(2)}) collective-permute-start(bf16[144,512]{1,0:T(8,128)(2,1)S(1)} %get-tuple-element.27.a), channel_id=1, source_target_pairs={{0,64},{1,65},{2,66},{3,67},{4,68},{5,69},{6,70},{7,71},{8,72},{9,... | collective-permute-start | bytes 442376 | tf_op jit(solution)/shard_map/ppermute | solution.py:417
  40.5 0.0 collective-permute-done.3.arrived
  40.5 2.3 %shard_map.89 = (bf16[8,224,128]{2,1,0:T(8,128)(2,1)}, bf16[72,512]{1,0:T(8,128)(2,1)S(1)}, bf16[72,512]{1,0:T(8,128)(2,1)S(1)}) custom-call(bf16[192,512]{1,0:T(8,128)(2,1)S(1)} %collective-permute-done.3.arrived, bf16[2,192,512]{2,1,0:T(8,128)(2,1)S(1)} %get-tuple-element.21.fields, bf16[192,1536]{1,0:T(8,128)(2,1)S(1)} %get-tuple-element.22.projected, ...), custom_call_target="tpu_custom_call" | custom-call | flops 4000000000 | bytes 20000000 | tf_op jit(solution)/shard_map/pallas_call | solution.py:38
  42.8 4.1 %all-to-all-start = ((bf16[8,224,128]{2,1,0:T(8,128)(2,1)}), bf16[8,224,128]{2,1,0:T(8,128)(2,1)S(1)}, u32[]{:S(2)}, u32[]{:S(2)}) async-start(bf16[8,224,128]{2,1,0:T(8,128)(2,1)} %get-tuple-element.26), calls=%async_computation | async-start | bytes 917504 | tf_op jit(solution)/shard_map/all_to_all | solution.py:480
  46.9 0.0 collective-permute-done.6.b
  46.9 0.0 collective-permute-done.7.c
  47.0 0.1 collective-permute-done.8.d
  47.1 2.3 %collective-permute-start.10 = (bf16[2,144,512]{2,1,0:T(8,128)(2,1)S(1)}, bf16[2,144,512]{2,1,0:T(8,128)(2,1)S(1)}, u32[]{:S(2)}, u32[]{:S(2)}) collective-permute-start(bf16[2,144,512]{2,1,0:T(8,128)(2,1)S(1)} %get-tuple-element.29.high), channel_id=1, source_target_pairs={{0,32},{32,0},{64,96},{96,64},{128,160},{160,128},{192,224},{224,1... | collective-permute-start | bytes 884744 | tf_op jit(solution)/shard_map/ppermute | solution.py:421
  49.4 2.0 %collective-permute-start.9 = (bf16[2,144,512]{2,1,0:T(8,128)(2,1)S(1)}, bf16[2,144,512]{2,1,0:T(8,128)(2,1)S(1)}, u32[]{:S(2)}, u32[]{:S(2)}) collective-permute-start(bf16[2,144,512]{2,1,0:T(8,128)(2,1)S(1)} %get-tuple-element.28.low), channel_id=1, source_target_pairs={{0,32},{32,0},{64,96},{96,64},{128,160},{160,128},{192,224},{224,1... | collective-permute-start | bytes 884744 | tf_op jit(solution)/shard_map/ppermute | solution.py:421
  51.5 0.4 collective-permute-start.4
  51.9 0.0 collective-permute-done.10.other_high
  51.9 1.0 %collective-permute-done.9.other_low = bf16[2,144,512]{2,1,0:T(8,128)(2,1)S(1)} collective-permute-done((bf16[2,144,512]{2,1,0:T(8,128)(2,1)S(1)}, bf16[2,144,512]{2,1,0:T(8,128)(2,1)S(1)}, u32[]{:S(2)}, u32[]{:S(2)}) %collective-permute-start.9) | collective-permute-done | bytes 294944 | tf_op jit(solution)/shard_map/ppermute | solution.py:421
  52.9 3.8 %all-to-all-done.blocks = bf16[8,224,128]{2,1,0:T(8,128)(2,1)S(1)} async-done(((bf16[8,224,128]{2,1,0:T(8,128)(2,1)}), bf16[8,224,128]{2,1,0:T(8,128)(2,1)S(1)}, u32[]{:S(2)}, u32[]{:S(2)}) %all-to-all-start) | async-done | bytes 458784 | tf_op jit(solution)/shard_map/all_to_all | solution.py:480
  56.7 1.4 %shard_map.93 = bf16[32,24,128]{2,1,0:T(8,128)(2,1)} custom-call(s32[1]{0:T(128)} %bitcast.7.lat_index, bf16[8,224,128]{2,1,0:T(8,128)(2,1)S(1)} %all-to-all-done.blocks, bf16[2,144,512]{2,1,0:T(8,128)(2,1)S(1)} %get-tuple-element.28.low, bf16[2,144,512]{2,1,0:T(8,128)(2,1)S(1)} %get-tuple-element.29.high, ...), custom_call_target="tpu_custom_call" | custom-call | tf_op jit(solution)/shard_map/pallas_call | solution.py:38
  58.0 8.3 %all-to-all-start.1 = ((bf16[32,24,128]{2,1,0:T(8,128)(2,1)}), bf16[32,24,128]{2,1,0:T(8,128)(2,1)S(1)}, u32[]{:S(2)}, u32[]{:S(2)}) async-start(bf16[32,24,128]{2,1,0:T(8,128)(2,1)} %shard_map.93), calls=%async_computation.1 | async-start | bytes 393216 | tf_op jit(solution)/shard_map/all_to_all | solution.py:492
  66.3 0.0 collective-permute-done.4.above
  66.4 3.7 %collective-permute-start.5 = (bf16[72,512]{1,0:T(8,128)(2,1)S(1)}, bf16[72,512]{1,0:T(8,128)(2,1)S(1)}, u32[]{:S(2)}, u32[]{:S(2)}) collective-permute-start(bf16[72,512]{1,0:T(8,128)(2,1)S(1)} %shard_map.90), channel_id=1, source_target_pairs={{0,1},{1,2},{2,3},{3,4},{4,5},{5,6},{6,7},{7,8},{8,9},{9,10},{10,1... | collective-permute-start | bytes 221192 | tf_op jit(solution)/shard_map/ppermute | solution.py:417
  70.1 8.7 %collective-permute-done.5.left = bf16[72,512]{1,0:T(8,128)(2,1)S(1)} collective-permute-done((bf16[72,512]{1,0:T(8,128)(2,1)S(1)}, bf16[72,512]{1,0:T(8,128)(2,1)S(1)}, u32[]{:S(2)}, u32[]{:S(2)}) %collective-permute-start.5) | collective-permute-done | bytes 73760 | tf_op jit(solution)/shard_map/ppermute | solution.py:417
  78.8 0.1 shard_map.91
  78.9 0.8 %copy.9 = bf16[1,2,6,12,512]{4,1,3,2,0:T(2,128)(2,1)} copy(bf16[1,2,6,12,512]{4,3,2,1,0:T(8,128)(2,1)S(1)} %shard_map.91) | data formatting | bytes 294912
  79.7 0.0 all-to-all-done.1.parts
  79.7 0.7 shard_map.94
  (3 shorter events, 0.1 us)
Async XLA Ops:
  2.5 21.8 %collective-permute-start.2 = (bf16[80,512]{1,0:T(8,128)(2,1)}, bf16[80,512]{1,0:T(8,128)(2,1)S(1)}, u32[]{:S(2)}, u32[]{:S(2)}) collective-permute-start(bf16[80,512]{1,0:T(8,128)(2,1)} %get-tuple-element.19), channel_id=1, source_target_pairs={{0,255},{1,224},{2,225},{3,226},{4,227},{5,228},{6,229},{7,230},{8... | collective-permute-start | bytes 245768 | tf_op jit(solution)/shard_map/ppermute | solution.py:417
  17.9 6.5 %collective-permute-start = (bf16[72,512]{1,0:T(8,128)(2,1)}, bf16[72,512]{1,0:T(8,128)(2,1)S(1)}, u32[]{:S(2)}, u32[]{:S(2)}) collective-permute-start(bf16[72,512]{1,0:T(8,128)(2,1)} %get-tuple-element.17), channel_id=1, source_target_pairs={{0,31},{1,0},{2,1},{3,2},{4,3},{5,4},{6,5},{7,6},{8,7},{9,8},{10,9... | collective-permute-start | bytes 221192 | tf_op jit(solution)/shard_map/ppermute | solution.py:417
  20.4 4.0 %collective-permute-start.1 = (bf16[72,512]{1,0:T(8,128)(2,1)}, bf16[72,512]{1,0:T(8,128)(2,1)S(1)}, u32[]{:S(2)}, u32[]{:S(2)}) collective-permute-start(bf16[72,512]{1,0:T(8,128)(2,1)} %get-tuple-element.18), channel_id=1, source_target_pairs={{0,224},{1,225},{2,226},{3,227},{4,228},{5,229},{6,230},{7,231},{8... | collective-permute-start | bytes 221192 | tf_op jit(solution)/shard_map/ppermute | solution.py:417
  21.7 2.6 %copy-start = (bf16[1,512,512]{2,1,0:T(8,128)(2,1)S(1)}, bf16[1,512,512]{2,1,0:T(8,128)(2,1)}, u32[]{:S(2)}) copy-start(bf16[1,512,512]{2,1,0:T(8,128)(2,1)} %param.10) | copy-start | bytes 1572868
  21.7 2.6 %copy-start.1 = (bf16[80,512]{1,0:T(8,128)(2,1)S(1)}, bf16[80,512]{1,0:T(8,128)(2,1)}, u32[]{:S(2)}) copy-start(bf16[80,512]{1,0:T(8,128)(2,1)} %get-tuple-element.16.own) | copy-start | bytes 245764
  21.7 2.6 %copy-start.2 = (f32[1,512]{1,0:T(1,128)S(1)}, f32[1,512]{1,0:T(1,128)}, u32[]{:S(2)}) copy-start(f32[1,512]{1,0:T(1,128)} %gain.3) | copy-start | bytes 6148
  27.8 12.7 %collective-permute-start.3 = (bf16[192,512]{1,0:T(8,128)(2,1)S(1)}, bf16[192,512]{1,0:T(8,128)(2,1)S(1)}, u32[]{:S(2)}, u32[]{:S(2)}) collective-permute-start(bf16[192,512]{1,0:T(8,128)(2,1)S(1)} %get-tuple-element.20), channel_id=1, source_target_pairs={{256,0},{257,1},{258,2},{259,3},{260,4},{261,5},{262,6},{263,7},{2... | collective-permute-start | bytes 589832 | tf_op jit(solution)/shard_map/ppermute | solution.py:471
  31.4 15.5 %collective-permute-start.6 = (bf16[144,512]{1,0:T(8,128)(2,1)S(1)}, bf16[144,512]{1,0:T(8,128)(2,1)S(1)}, u32[]{:S(2)}, u32[]{:S(2)}) collective-permute-start(bf16[144,512]{1,0:T(8,128)(2,1)S(1)} %get-tuple-element.27.a), channel_id=1, source_target_pairs={{0,192},{1,193},{2,194},{3,195},{4,196},{5,197},{6,198},{7,199},{8... | collective-permute-start | bytes 442376 | tf_op jit(solution)/shard_map/ppermute | solution.py:417
  35.2 11.8 %collective-permute-start.7 = (bf16[144,512]{1,0:T(8,128)(2,1)S(1)}, bf16[144,512]{1,0:T(8,128)(2,1)S(1)}, u32[]{:S(2)}, u32[]{:S(2)}) collective-permute-start(bf16[144,512]{1,0:T(8,128)(2,1)S(1)} %get-tuple-element.27.a), channel_id=1, source_target_pairs={{0,128},{1,129},{2,130},{3,131},{4,132},{5,133},{6,134},{7,135},{8... | collective-permute-start | bytes 442376 | tf_op jit(solution)/shard_map/ppermute | solution.py:417
  37.7 9.4 %collective-permute-start.8 = (bf16[144,512]{1,0:T(8,128)(2,1)S(1)}, bf16[144,512]{1,0:T(8,128)(2,1)S(1)}, u32[]{:S(2)}, u32[]{:S(2)}) collective-permute-start(bf16[144,512]{1,0:T(8,128)(2,1)S(1)} %get-tuple-element.27.a), channel_id=1, source_target_pairs={{0,64},{1,65},{2,66},{3,67},{4,68},{5,69},{6,70},{7,71},{8,72},{9,... | collective-permute-start | bytes 442376 | tf_op jit(solution)/shard_map/ppermute | solution.py:417
  42.8 13.8 %all-to-all-start = ((bf16[8,224,128]{2,1,0:T(8,128)(2,1)}), bf16[8,224,128]{2,1,0:T(8,128)(2,1)S(1)}, u32[]{:S(2)}, u32[]{:S(2)}) async-start(bf16[8,224,128]{2,1,0:T(8,128)(2,1)} %get-tuple-element.26), calls=%async_computation | async-start | bytes 917504 | tf_op jit(solution)/shard_map/all_to_all | solution.py:480
  47.1 4.8 %collective-permute-start.10 = (bf16[2,144,512]{2,1,0:T(8,128)(2,1)S(1)}, bf16[2,144,512]{2,1,0:T(8,128)(2,1)S(1)}, u32[]{:S(2)}, u32[]{:S(2)}) collective-permute-start(bf16[2,144,512]{2,1,0:T(8,128)(2,1)S(1)} %get-tuple-element.29.high), channel_id=1, source_target_pairs={{0,32},{32,0},{64,96},{96,64},{128,160},{160,128},{192,224},{224,1... | collective-permute-start | bytes 884744 | tf_op jit(solution)/shard_map/ppermute | solution.py:421
  49.4 3.5 %collective-permute-start.9 = (bf16[2,144,512]{2,1,0:T(8,128)(2,1)S(1)}, bf16[2,144,512]{2,1,0:T(8,128)(2,1)S(1)}, u32[]{:S(2)}, u32[]{:S(2)}) collective-permute-start(bf16[2,144,512]{2,1,0:T(8,128)(2,1)S(1)} %get-tuple-element.28.low), channel_id=1, source_target_pairs={{0,32},{32,0},{64,96},{96,64},{128,160},{160,128},{192,224},{224,1... | collective-permute-start | bytes 884744 | tf_op jit(solution)/shard_map/ppermute | solution.py:421
  51.5 14.9 %collective-permute-start.4 = (bf16[72,512]{1,0:T(8,128)(2,1)S(1)}, bf16[72,512]{1,0:T(8,128)(2,1)S(1)}, u32[]{:S(2)}, u32[]{:S(2)}) collective-permute-start(bf16[72,512]{1,0:T(8,128)(2,1)S(1)} %get-tuple-element.25), channel_id=1, source_target_pairs={{0,32},{1,33},{2,34},{3,35},{4,36},{5,37},{6,38},{7,39},{8,40},{9,... | collective-permute-start | bytes 221192 | tf_op jit(solution)/shard_map/ppermute | solution.py:417
  58.0 21.7 %all-to-all-start.1 = ((bf16[32,24,128]{2,1,0:T(8,128)(2,1)}), bf16[32,24,128]{2,1,0:T(8,128)(2,1)S(1)}, u32[]{:S(2)}, u32[]{:S(2)}) async-start(bf16[32,24,128]{2,1,0:T(8,128)(2,1)} %shard_map.93), calls=%async_computation.1 | async-start | bytes 393216 | tf_op jit(solution)/shard_map/all_to_all | solution.py:492
  66.4 12.4 %collective-permute-start.5 = (bf16[72,512]{1,0:T(8,128)(2,1)S(1)}, bf16[72,512]{1,0:T(8,128)(2,1)S(1)}, u32[]{:S(2)}, u32[]{:S(2)}) collective-permute-start(bf16[72,512]{1,0:T(8,128)(2,1)S(1)} %shard_map.90), channel_id=1, source_target_pairs={{0,1},{1,2},{2,3},{3,4},{4,5},{5,6},{6,7},{7,8},{8,9},{9,10},{10,1... | collective-permute-start | bytes 221192 | tf_op jit(solution)/shard_map/ppermute | solution.py:417

commit v12 on v11

--- a/solution.py
+++ b/solution.py
@@ -319,12 +319,12 @@
         target[...] = jnp.concatenate(parts, axis=0).astype(BF16)
 
 
-def stack_kernel(a, b, c, d, kept, low, high):
-    low[0], low[1], high[0], high[1] = a[...], b[...], c[...], d[...]
+def stack_kernel(a, b, kept, out):
+    out[0], out[1] = a[...], b[...]
 
 
 def product_kernel(
-    lat_index, blocks, low, high, other_low, other_high, out
+    lat_index, blocks, stack, other_stack, far, other_far, last, other_last, out
 ):
     lats = blocks.shape[0]
 
@@ -335,16 +335,16 @@
             [blocks[place, :144, :], jnp.concatenate([folded, bottom], axis=0)], axis=1
         )
 
-    gradients, cells = [], []
-    for x in range(0, lats // 2, 2):
-        places = []
-        for step in (x, x + 1):
-            first = lat_index[0] + 2 * step
-            first = jnp.where(first >= lats, first - lats, first)
-            places.append((first, first + 1 - 2 * lax.rem(lat_index[0], 2)))
-        for same, source in enumerate((low, other_low) if x == 0 else (high, other_high)):
-            gradients.extend(columns(place[same]) for place in places)
-            cells.append(source[...].reshape(2 * PACKED_ROWS, FEATURES))
+    def place(step, same):
+        first = lat_index[0] + 2 * step
+        first = jnp.where(first >= lats, first - lats, first)
+        return first if same else first + 1 - 2 * lax.rem(lat_index[0], 2)
+
+    steps = stack.shape[0]
+    gradients = [columns(place(step, same)) for same in (True, False) for step in range(steps)]
+    gradients += [columns(place(step, same)) for step in (2, 3) for same in (True, False)]
+    cells = [part[...].reshape(steps * PACKED_ROWS, FEATURES) for part in (stack, other_stack)]
+    cells += [far[...], other_far[...], last[...], other_last[...]]
     product = dot(
         jnp.concatenate(cells, axis=0), jnp.concatenate(gradients, axis=0), ((0,), (0,))
     )
@@ -469,7 +469,7 @@
 
     lat_index = lax.axis_index("lat").astype(jnp.int32).reshape(1)
     arrived = lax.ppermute(skip, "phase", [(1, 0)])
-    along = [inputs] + [passed(inputs, -2 * x, 0) for x in range(1, lats // 2)]
+    next_inputs, far = passed(inputs, -2, 0), passed(inputs, -4, 0)
     blocks, kept, up = call(
         second_kernel,
         (struct((lats, 224, 128), BF16), part, part),
@@ -478,13 +478,16 @@
         cost=HIDING,
     )(arrived, fields, projected, att, w_proj, w_qkv, norm_gain)
     blocks = lax.all_to_all(blocks, "lat", 0, 0, tiled=True)
-    two = struct((2, PACKED_ROWS, FEATURES), BF16)
-    low, high = call(stack_kernel, (two, two), places={4: pl.ANY})(*along, kept)
-    other_low, other_high = other_core(low), other_core(high)
+    inputs, far, kept = lax.optimization_barrier((inputs, far, kept))
+    last = passed(inputs, 2, 0)
+    stack = call(
+        stack_kernel, struct((2, PACKED_ROWS, FEATURES), BF16), places={2: pl.ANY}
+    )(inputs, next_inputs, kept)
+    other_stack, other_far, other_last = other_core(stack), other_core(far), other_core(last)
     above = passed(up, 1, 0)
     rows = FEATURES * 3 // 2 // lons
     slices = call(product_kernel, struct((lons, rows, 128), BF16), places={0: pltpu.SMEM})(
-        lat_index, blocks, low, high, other_low, other_high
+        lat_index, blocks, stack, other_stack, far, other_far, last, other_last
     )
     sideways = call(sideways_kernel, part, cost=HIDING)(kept, above)
     left = passed(sideways, 0, 1)

time: 81.1 us -> 85.7 us (1.057)
  starting transfers between devices: 51.9 us -> 55.4 us
  waiting for transfers between devices: 15.8 us -> 16.8 us
    ppermute x8, waiting for transfers between devices: 11 us -> 16 us  [passed(): return lax.ppermute(array, ('lat', 'lon'), pairs)]
    all_to_all x1, waiting for transfers between devices: 3.78 us -> 0.01 us  [per_device(): blocks = lax.all_to_all(blocks, 'lat', 0, 0, tiled=True)]
    ppermute x2 -> x3, starting transfers between devices: 4.33 us -> 6.24 us  [other_core(): lax.ppermute(array, 'lat', [(a, a ^ 1) for a in range(lax.axis_size('lat'...]
    ppermute x8, starting transfers between devices: 31.6 us -> 33.4 us  [passed(): return lax.ppermute(array, ('lat', 'lon'), pairs)]
  transfers between devices with their start and end apart: 13 -> 14, of which waited for: 5 -> 4; matrix products, arithmetic and copies ran while one was open for 2% -> 2% of each run, Pallas kernels for 5% -> 5%
where the time goes in v12:
time: 85.7 us; the launch traced here: 84.9 us
  starting transfers between devices  55.4 us (65%)
  waiting for transfers between devices  16.8 us (20%)
  Pallas kernels  10.3 us (12%)
  local copies, waits for them, and re-layouts  1.61 us (2%)
    ppermute x8, starting transfers between devices, passed(): return lax.ppermute(array, ('lat', 'lon'), pairs)  33.4 us
    ppermute x8, waiting for transfers between devices, passed(): return lax.ppermute(array, ('lat', 'lon'), pairs)  16 us
    pallas_call x9, Pallas kernels, run(): pl.pallas_call(kernel, out_shape=out_shape, in_specs=specs, out_specs=out...  10.3 us
    all_to_all x1, starting transfers between devices, per_device(): slices = lax.all_to_all(slices, 'lon', 0, 0, tiled=True)  8.76 us
    ppermute x3, starting transfers between devices, other_core(): lax.ppermute(array, 'lat', [(a, a ^ 1) for a in range(lax.axis_size('lat'...  6.24 us
    ppermute x1, starting transfers between devices, per_device(): arrived = lax.ppermute(skip, 'phase', [(1, 0)])  3.55 us
    all_to_all x1, starting transfers between devices, per_device(): blocks = lax.all_to_all(blocks, 'lat', 0, 0, tiled=True)  3.48 us
  transfers between devices with their start and end apart: 14, of which 4 were waited for; matrix products, arithmetic and copies ran while one was open for 2% of the time, Pallas kernels for 5%

profile of v12, /device:TPU:8, one launch (start us, length us, event | category | flops | bytes accessed | tf_op | source)
XLA Modules:
  0.0 84.9 jit_solution(3975797694894335855)
XLA Ops:
  0.6 1.9 %shard_map.86 = (bf16[80,512]{1,0:T(8,128)(2,1)}, bf16[72,512]{1,0:T(8,128)(2,1)}, bf16[72,512]{1,0:T(8,128)(2,1)}, bf16[80,512]{1,0:T(8,128)(2,1)}) custom-call(s32[6]{0:T(128)} %labels_ref.1, bf16[6,12,2,512]{3,2,1,0:T(2,128)(2,1)} %bitcast.16, bf16[6,12,2,512]{3,2,1,0:T(2,128)(2,1)} %bitcast.17), custom_call_target="tpu_custom_call" | custom-call | tf_op jit(solution)/shard_map/pallas_call | solution.py:38
  2.5 15.4 %collective-permute-start.2 = (bf16[80,512]{1,0:T(8,128)(2,1)}, bf16[80,512]{1,0:T(8,128)(2,1)S(1)}, u32[]{:S(2)}, u32[]{:S(2)}) collective-permute-start(bf16[80,512]{1,0:T(8,128)(2,1)} %get-tuple-element.20), channel_id=1, source_target_pairs={{0,255},{1,224},{2,225},{3,226},{4,227},{5,228},{6,229},{7,230},{8... | collective-permute-start | bytes 245768 | tf_op jit(solution)/shard_map/ppermute | solution.py:417
  17.9 2.5 %collective-permute-start = (bf16[72,512]{1,0:T(8,128)(2,1)}, bf16[72,512]{1,0:T(8,128)(2,1)S(1)}, u32[]{:S(2)}, u32[]{:S(2)}) collective-permute-start(bf16[72,512]{1,0:T(8,128)(2,1)} %get-tuple-element.18), channel_id=1, source_target_pairs={{0,31},{1,0},{2,1},{3,2},{4,3},{5,4},{6,5},{7,6},{8,7},{9,8},{10,9... | collective-permute-start | bytes 221192 | tf_op jit(solution)/shard_map/ppermute | solution.py:417
  20.4 0.6 collective-permute-start.1
  20.9 0.8 slice_bitcast_fusion
  21.7 0.0 copy-start
  21.7 0.0 copy-start.1
  21.7 0.0 copy-start.2
  21.8 0.5 shard_map.87.bias
  22.2 2.1 %collective-permute-done.lon = bf16[72,512]{1,0:T(8,128)(2,1)S(1)} collective-permute-done((bf16[72,512]{1,0:T(8,128)(2,1)}, bf16[72,512]{1,0:T(8,128)(2,1)S(1)}, u32[]{:S(2)}, u32[]{:S(2)}) %collective-permute-start) | collective-permute-done | bytes 73760 | tf_op jit(solution)/shard_map/ppermute | solution.py:417
  24.3 0.0 collective-permute-done.1.lat
  24.3 0.0 collective-permute-done.2.cor
  24.3 0.0 copy-done
  24.4 0.0 copy-done.1
  24.4 0.0 copy-done.2
  24.4 3.4 %shard_map.88 = (bf16[192,512]{1,0:T(8,128)(2,1)S(1)}, bf16[144,512]{1,0:T(8,128)(2,1)S(1)}, bf16[2,192,512]{2,1,0:T(8,128)(2,1)S(1)}, bf16[192,1536]{1,0:T(8,128)(2,1)S(1)}, bf16[2,4,2,96,96]{4,3,2,1,0:T(8,128)(2,1)S(1)}) custom-call(bf16[80,512]{1,0:T(8,128)(2,1)S(1)} %copy-done.1, bf16[72,512]{1,0:T(8,128)(2,1)S(1)} %collective-permute-done.lon, ...), custom_call_target="tpu_custom_call" | custom-call | tf_op jit(solution)/shard_map/pallas_call | solution.py:38
  27.8 3.6 %collective-permute-start.4 = (bf16[192,512]{1,0:T(8,128)(2,1)S(1)}, bf16[192,512]{1,0:T(8,128)(2,1)S(1)}, u32[]{:S(2)}, u32[]{:S(2)}) collective-permute-start(bf16[192,512]{1,0:T(8,128)(2,1)S(1)} %get-tuple-element.22), channel_id=1, source_target_pairs={{256,0},{257,1},{258,2},{259,3},{260,4},{261,5},{262,6},{263,7},{2... | collective-permute-start | bytes 589832 | tf_op jit(solution)/shard_map/ppermute | solution.py:471
  31.4 3.9 %collective-permute-start.3 = (bf16[144,512]{1,0:T(8,128)(2,1)S(1)}, bf16[144,512]{1,0:T(8,128)(2,1)S(1)}, u32[]{:S(2)}, u32[]{:S(2)}) collective-permute-start(bf16[144,512]{1,0:T(8,128)(2,1)S(1)} %get-tuple-element.30.a), channel_id=1, source_target_pairs={{0,128},{1,129},{2,130},{3,131},{4,132},{5,133},{6,134},{7,135},{8... | collective-permute-start | bytes 442376 | tf_op jit(solution)/shard_map/ppermute | solution.py:417
  35.3 3.0 %collective-permute-start.7 = (bf16[144,512]{1,0:T(8,128)(2,1)S(1)}, bf16[144,512]{1,0:T(8,128)(2,1)S(1)}, u32[]{:S(2)}, u32[]{:S(2)}) collective-permute-start(bf16[144,512]{1,0:T(8,128)(2,1)S(1)} %get-tuple-element.30.a), channel_id=1, source_target_pairs={{0,192},{1,193},{2,194},{3,195},{4,196},{5,197},{6,198},{7,199},{8... | collective-permute-start | bytes 442376 | tf_op jit(solution)/shard_map/ppermute | solution.py:417
  38.3 0.0 collective-permute-done.4.arrived
  38.3 2.3 %shard_map.89 = (bf16[8,224,128]{2,1,0:T(8,128)(2,1)}, bf16[72,512]{1,0:T(8,128)(2,1)S(1)}, bf16[72,512]{1,0:T(8,128)(2,1)S(1)}) custom-call(bf16[192,512]{1,0:T(8,128)(2,1)S(1)} %collective-permute-done.4.arrived, bf16[2,192,512]{2,1,0:T(8,128)(2,1)S(1)} %get-tuple-element.23.fields, bf16[192,1536]{1,0:T(8,128)(2,1)S(1)} %get-tuple-element.24.projected, ...), custom_call_target="tpu_custom_call" | custom-call | flops 4000000000 | bytes 20000000 | tf_op jit(solution)/shard_map/pallas_call | solution.py:38
  40.7 3.5 %all-to-all-start = ((bf16[8,224,128]{2,1,0:T(8,128)(2,1)}), bf16[8,224,128]{2,1,0:T(8,128)(2,1)S(1)}, u32[]{:S(2)}, u32[]{:S(2)}) async-start(bf16[8,224,128]{2,1,0:T(8,128)(2,1)} %get-tuple-element.29), calls=%async_computation | async-start | bytes 917504 | tf_op jit(solution)/shard_map/all_to_all | solution.py:480
  44.1 0.0 collective-permute-done.3.far
  44.2 3.8 %collective-permute-start.10 = (bf16[144,512]{1,0:T(8,128)(2,1)S(1)}, bf16[144,512]{1,0:T(8,128)(2,1)S(1)}, u32[]{:S(2)}, u32[]{:S(2)}) collective-permute-start(bf16[144,512]{1,0:T(8,128)(2,1)S(1)} %get-tuple-element.30.a), channel_id=1, source_target_pairs={{0,64},{1,65},{2,66},{3,67},{4,68},{5,69},{6,70},{7,71},{8,72},{9,... | collective-permute-start | bytes 442376 | tf_op jit(solution)/shard_map/ppermute | solution.py:417
  48.0 0.0 collective-permute-done.7.b
  48.0 1.9 %collective-permute-start.8 = (bf16[2,144,512]{2,1,0:T(8,128)(2,1)S(1)}, bf16[2,144,512]{2,1,0:T(8,128)(2,1)S(1)}, u32[]{:S(2)}, u32[]{:S(2)}) collective-permute-start(bf16[2,144,512]{2,1,0:T(8,128)(2,1)S(1)} %shard_map.92.stack), channel_id=1, source_target_pairs={{0,32},{32,0},{64,96},{96,64},{128,160},{160,128},{192,224},{224,1... | collective-permute-start | bytes 884744 | tf_op jit(solution)/shard_map/ppermute | solution.py:421
  49.9 2.4 %collective-permute-start.9 = (bf16[144,512]{1,0:T(8,128)(2,1)S(1)}, bf16[144,512]{1,0:T(8,128)(2,1)S(1)}, u32[]{:S(2)}, u32[]{:S(2)}) collective-permute-start(bf16[144,512]{1,0:T(8,128)(2,1)S(1)} %collective-permute-done.3.far), channel_id=1, source_target_pairs={{0,32},{32,0},{64,96},{96,64},{128,160},{160,128},{192,224},{224,1... | collective-permute-start | bytes 442376 | tf_op jit(solution)/shard_map/ppermute | solution.py:421
  52.4 4.2 %collective-permute-done.10.last = bf16[144,512]{1,0:T(8,128)(2,1)S(1)} collective-permute-done((bf16[144,512]{1,0:T(8,128)(2,1)S(1)}, bf16[144,512]{1,0:T(8,128)(2,1)S(1)}, u32[]{:S(2)}, u32[]{:S(2)}) %collective-permute-start.10) | collective-permute-done | bytes 147488 | tf_op jit(solution)/shard_map/ppermute | solution.py:417
  56.6 1.9 %collective-permute-start.11 = (bf16[144,512]{1,0:T(8,128)(2,1)S(1)}, bf16[144,512]{1,0:T(8,128)(2,1)S(1)}, u32[]{:S(2)}, u32[]{:S(2)}) collective-permute-start(bf16[144,512]{1,0:T(8,128)(2,1)S(1)} %collective-permute-done.10.last), channel_id=1, source_target_pairs={{0,32},{32,0},{64,96},{96,64},{128,160},{160,128},{192,224},{224,1... | collective-permute-start | bytes 442376 | tf_op jit(solution)/shard_map/ppermute | solution.py:421
  58.5 0.5 collective-permute-start.5
  59.0 0.0 collective-permute-done.9.other_far
  59.0 0.0 collective-permute-done.8.other_stack
  59.0 0.8 collective-permute-done.11.other_last
  59.8 0.0 all-to-all-done.blocks
  59.8 1.4 %shard_map.93 = bf16[32,24,128]{2,1,0:T(8,128)(2,1)} custom-call(s32[1]{0:T(128)} %bitcast.7.lat_index, bf16[8,224,128]{2,1,0:T(8,128)(2,1)S(1)} %all-to-all-done.blocks, bf16[2,144,512]{2,1,0:T(8,128)(2,1)S(1)} %shard_map.92.stack, bf16[2,144,512]{2,1,0:T(8,128)(2,1)S(1)} %collective-permute-done.8.other_stack, ...), custom_call_target="tpu_custom_call" | custom-call | tf_op jit(solution)/shard_map/pallas_call | solution.py:38
  61.2 8.8 %all-to-all-start.1 = ((bf16[32,24,128]{2,1,0:T(8,128)(2,1)}), bf16[32,24,128]{2,1,0:T(8,128)(2,1)S(1)}, u32[]{:S(2)}, u32[]{:S(2)}) async-start(bf16[32,24,128]{2,1,0:T(8,128)(2,1)} %shard_map.93), calls=%async_computation.1 | async-start | bytes 393216 | tf_op jit(solution)/shard_map/all_to_all | solution.py:495
  70.0 0.0 collective-permute-done.5.above
  70.0 3.7 %collective-permute-start.6 = (bf16[72,512]{1,0:T(8,128)(2,1)S(1)}, bf16[72,512]{1,0:T(8,128)(2,1)S(1)}, u32[]{:S(2)}, u32[]{:S(2)}) collective-permute-start(bf16[72,512]{1,0:T(8,128)(2,1)S(1)} %shard_map.90), channel_id=1, source_target_pairs={{0,1},{1,2},{2,3},{3,4},{4,5},{5,6},{6,7},{7,8},{8,9},{9,10},{10,1... | collective-permute-start | bytes 221192 | tf_op jit(solution)/shard_map/ppermute | solution.py:417
  73.8 9.6 %collective-permute-done.6.left = bf16[72,512]{1,0:T(8,128)(2,1)S(1)} collective-permute-done((bf16[72,512]{1,0:T(8,128)(2,1)S(1)}, bf16[72,512]{1,0:T(8,128)(2,1)S(1)}, u32[]{:S(2)}, u32[]{:S(2)}) %collective-permute-start.6) | collective-permute-done | bytes 73760 | tf_op jit(solution)/shard_map/ppermute | solution.py:417
  83.4 0.1 shard_map.91
  83.4 0.8 copy.9
  84.2 0.0 all-to-all-done.1.parts
  84.2 0.7 shard_map.94
  (3 shorter events, 0.1 us)
Async XLA Ops:
  2.5 21.8 %collective-permute-start.2 = (bf16[80,512]{1,0:T(8,128)(2,1)}, bf16[80,512]{1,0:T(8,128)(2,1)S(1)}, u32[]{:S(2)}, u32[]{:S(2)}) collective-permute-start(bf16[80,512]{1,0:T(8,128)(2,1)} %get-tuple-element.20), channel_id=1, source_target_pairs={{0,255},{1,224},{2,225},{3,226},{4,227},{5,228},{6,229},{7,230},{8... | collective-permute-start | bytes 245768 | tf_op jit(solution)/shard_map/ppermute | solution.py:417
  17.9 6.5 %collective-permute-start = (bf16[72,512]{1,0:T(8,128)(2,1)}, bf16[72,512]{1,0:T(8,128)(2,1)S(1)}, u32[]{:S(2)}, u32[]{:S(2)}) collective-permute-start(bf16[72,512]{1,0:T(8,128)(2,1)} %get-tuple-element.18), channel_id=1, source_target_pairs={{0,31},{1,0},{2,1},{3,2},{4,3},{5,4},{6,5},{7,6},{8,7},{9,8},{10,9... | collective-permute-start | bytes 221192 | tf_op jit(solution)/shard_map/ppermute | solution.py:417
  20.4 4.0 %collective-permute-start.1 = (bf16[72,512]{1,0:T(8,128)(2,1)}, bf16[72,512]{1,0:T(8,128)(2,1)S(1)}, u32[]{:S(2)}, u32[]{:S(2)}) collective-permute-start(bf16[72,512]{1,0:T(8,128)(2,1)} %get-tuple-element.19), channel_id=1, source_target_pairs={{0,224},{1,225},{2,226},{3,227},{4,228},{5,229},{6,230},{7,231},{8... | collective-permute-start | bytes 221192 | tf_op jit(solution)/shard_map/ppermute | solution.py:417
  21.7 2.6 %copy-start = (bf16[1,512,512]{2,1,0:T(8,128)(2,1)S(1)}, bf16[1,512,512]{2,1,0:T(8,128)(2,1)}, u32[]{:S(2)}) copy-start(bf16[1,512,512]{2,1,0:T(8,128)(2,1)} %param.10) | copy-start | bytes 1572868
  21.7 2.6 %copy-start.1 = (bf16[80,512]{1,0:T(8,128)(2,1)S(1)}, bf16[80,512]{1,0:T(8,128)(2,1)}, u32[]{:S(2)}) copy-start(bf16[80,512]{1,0:T(8,128)(2,1)} %get-tuple-element.17.own) | copy-start | bytes 245764
  21.7 2.6 %copy-start.2 = (f32[1,512]{1,0:T(1,128)S(1)}, f32[1,512]{1,0:T(1,128)}, u32[]{:S(2)}) copy-start(f32[1,512]{1,0:T(1,128)} %gain.3) | copy-start | bytes 6148
  27.8 10.5 %collective-permute-start.4 = (bf16[192,512]{1,0:T(8,128)(2,1)S(1)}, bf16[192,512]{1,0:T(8,128)(2,1)S(1)}, u32[]{:S(2)}, u32[]{:S(2)}) collective-permute-start(bf16[192,512]{1,0:T(8,128)(2,1)S(1)} %get-tuple-element.22), channel_id=1, source_target_pairs={{256,0},{257,1},{258,2},{259,3},{260,4},{261,5},{262,6},{263,7},{2... | collective-permute-start | bytes 589832 | tf_op jit(solution)/shard_map/ppermute | solution.py:471
  31.4 12.8 %collective-permute-start.3 = (bf16[144,512]{1,0:T(8,128)(2,1)S(1)}, bf16[144,512]{1,0:T(8,128)(2,1)S(1)}, u32[]{:S(2)}, u32[]{:S(2)}) collective-permute-start(bf16[144,512]{1,0:T(8,128)(2,1)S(1)} %get-tuple-element.30.a), channel_id=1, source_target_pairs={{0,128},{1,129},{2,130},{3,131},{4,132},{5,133},{6,134},{7,135},{8... | collective-permute-start | bytes 442376 | tf_op jit(solution)/shard_map/ppermute | solution.py:417
  35.3 12.7 %collective-permute-start.7 = (bf16[144,512]{1,0:T(8,128)(2,1)S(1)}, bf16[144,512]{1,0:T(8,128)(2,1)S(1)}, u32[]{:S(2)}, u32[]{:S(2)}) collective-permute-start(bf16[144,512]{1,0:T(8,128)(2,1)S(1)} %get-tuple-element.30.a), channel_id=1, source_target_pairs={{0,192},{1,193},{2,194},{3,195},{4,196},{5,197},{6,198},{7,199},{8... | collective-permute-start | bytes 442376 | tf_op jit(solution)/shard_map/ppermute | solution.py:417
  40.7 19.2 %all-to-all-start = ((bf16[8,224,128]{2,1,0:T(8,128)(2,1)}), bf16[8,224,128]{2,1,0:T(8,128)(2,1)S(1)}, u32[]{:S(2)}, u32[]{:S(2)}) async-start(bf16[8,224,128]{2,1,0:T(8,128)(2,1)} %get-tuple-element.29), calls=%async_computation | async-start | bytes 917504 | tf_op jit(solution)/shard_map/all_to_all | solution.py:480
  44.2 12.4 %collective-permute-start.10 = (bf16[144,512]{1,0:T(8,128)(2,1)S(1)}, bf16[144,512]{1,0:T(8,128)(2,1)S(1)}, u32[]{:S(2)}, u32[]{:S(2)}) collective-permute-start(bf16[144,512]{1,0:T(8,128)(2,1)S(1)} %get-tuple-element.30.a), channel_id=1, source_target_pairs={{0,64},{1,65},{2,66},{3,67},{4,68},{5,69},{6,70},{7,71},{8,72},{9,... | collective-permute-start | bytes 442376 | tf_op jit(solution)/shard_map/ppermute | solution.py:417
  48.0 11.0 %collective-permute-start.8 = (bf16[2,144,512]{2,1,0:T(8,128)(2,1)S(1)}, bf16[2,144,512]{2,1,0:T(8,128)(2,1)S(1)}, u32[]{:S(2)}, u32[]{:S(2)}) collective-permute-start(bf16[2,144,512]{2,1,0:T(8,128)(2,1)S(1)} %shard_map.92.stack), channel_id=1, source_target_pairs={{0,32},{32,0},{64,96},{96,64},{128,160},{160,128},{192,224},{224,1... | collective-permute-start | bytes 884744 | tf_op jit(solution)/shard_map/ppermute | solution.py:421
  49.9 9.1 %collective-permute-start.9 = (bf16[144,512]{1,0:T(8,128)(2,1)S(1)}, bf16[144,512]{1,0:T(8,128)(2,1)S(1)}, u32[]{:S(2)}, u32[]{:S(2)}) collective-permute-start(bf16[144,512]{1,0:T(8,128)(2,1)S(1)} %collective-permute-done.3.far), channel_id=1, source_target_pairs={{0,32},{32,0},{64,96},{96,64},{128,160},{160,128},{192,224},{224,1... | collective-permute-start | bytes 442376 | tf_op jit(solution)/shard_map/ppermute | solution.py:421
  56.6 3.3 %collective-permute-start.11 = (bf16[144,512]{1,0:T(8,128)(2,1)S(1)}, bf16[144,512]{1,0:T(8,128)(2,1)S(1)}, u32[]{:S(2)}, u32[]{:S(2)}) collective-permute-start(bf16[144,512]{1,0:T(8,128)(2,1)S(1)} %collective-permute-done.10.last), channel_id=1, source_target_pairs={{0,32},{32,0},{64,96},{96,64},{128,160},{160,128},{192,224},{224,1... | collective-permute-start | bytes 442376 | tf_op jit(solution)/shard_map/ppermute | solution.py:421
  58.5 11.5 %collective-permute-start.5 = (bf16[72,512]{1,0:T(8,128)(2,1)S(1)}, bf16[72,512]{1,0:T(8,128)(2,1)S(1)}, u32[]{:S(2)}, u32[]{:S(2)}) collective-permute-start(bf16[72,512]{1,0:T(8,128)(2,1)S(1)} %get-tuple-element.28), channel_id=1, source_target_pairs={{0,32},{1,33},{2,34},{3,35},{4,36},{5,37},{6,38},{7,39},{8,40},{9,... | collective-permute-start | bytes 221192 | tf_op jit(solution)/shard_map/ppermute | solution.py:417
  61.2 23.0 %all-to-all-start.1 = ((bf16[32,24,128]{2,1,0:T(8,128)(2,1)}), bf16[32,24,128]{2,1,0:T(8,128)(2,1)S(1)}, u32[]{:S(2)}, u32[]{:S(2)}) async-start(bf16[32,24,128]{2,1,0:T(8,128)(2,1)} %shard_map.93), calls=%async_computation.1 | async-start | bytes 393216 | tf_op jit(solution)/shard_map/all_to_all | solution.py:495
  70.0 13.3 %collective-permute-start.6 = (bf16[72,512]{1,0:T(8,128)(2,1)S(1)}, bf16[72,512]{1,0:T(8,128)(2,1)S(1)}, u32[]{:S(2)}, u32[]{:S(2)}) collective-permute-start(bf16[72,512]{1,0:T(8,128)(2,1)S(1)} %shard_map.90), channel_id=1, source_target_pairs={{0,1},{1,2},{2,3},{3,4},{4,5},{5,6},{6,7},{7,8},{8,9},{9,10},{10,1... | collective-permute-start | bytes 221192 | tf_op jit(solution)/shard_map/ppermute | solution.py:417

commit v13 on v11

--- a/solution.py
+++ b/solution.py
@@ -339,9 +339,8 @@
     for x in range(0, lats // 2, 2):
         places = []
         for step in (x, x + 1):
-            first = lat_index[0] + 2 * step
-            first = jnp.where(first >= lats, first - lats, first)
-            places.append((first, first + 1 - 2 * lax.rem(lat_index[0], 2)))
+            first = jnp.bitwise_xor(lat_index[0], 2 * step)
+            places.append((first, jnp.bitwise_xor(first, 1)))
         for same, source in enumerate((low, other_low) if x == 0 else (high, other_high)):
             gradients.extend(columns(place[same]) for place in places)
             cells.append(source[...].reshape(2 * PACKED_ROWS, FEATURES))
@@ -417,8 +416,8 @@
     return lax.ppermute(array, ("lat", "lon"), pairs)
 
 
-def other_core(array):
-    return lax.ppermute(array, "lat", [(a, a ^ 1) for a in range(lax.axis_size("lat"))])
+def swapped(array, bits):
+    return lax.ppermute(array, "lat", [(a, a ^ bits) for a in range(lax.axis_size("lat"))])
 
 
 def per_device(x_in, out_grad, w_qkv, w_proj, norm_gain, bias_table, lat_labels):
@@ -469,7 +468,7 @@
 
     lat_index = lax.axis_index("lat").astype(jnp.int32).reshape(1)
     arrived = lax.ppermute(skip, "phase", [(1, 0)])
-    along = [inputs] + [passed(inputs, -2 * x, 0) for x in range(1, lats // 2)]
+    along = [inputs] + [swapped(inputs, 2 * x) for x in range(1, lats // 2)]
     blocks, kept, up = call(
         second_kernel,
         (struct((lats, 224, 128), BF16), part, part),
@@ -480,7 +479,7 @@
     blocks = lax.all_to_all(blocks, "lat", 0, 0, tiled=True)
     two = struct((2, PACKED_ROWS, FEATURES), BF16)
     low, high = call(stack_kernel, (two, two), places={4: pl.ANY})(*along, kept)
-    other_low, other_high = other_core(low), other_core(high)
+    other_low, other_high = swapped(low, 1), swapped(high, 1)
     above = passed(up, 1, 0)
     rows = FEATURES * 3 // 2 // lons
     slices = call(product_kernel, struct((lons, rows, 128), BF16), places={0: pltpu.SMEM})(

time: 81.1 us -> 81.8 us (level)
    ppermute x2 -> x5, starting transfers between devices: 4.33 us -> 14.8 us  [swapped(): lax.ppermute(array, 'lat', [(a, a ^ bits) for a in range(lax.axis_size('l...]
    ppermute x8 -> x5, starting transfers between devices: 31.6 us -> 22.5 us  [passed(): return lax.ppermute(array, ('lat', 'lon'), pairs)]
    ppermute x8 -> x5, waiting for transfers between devices: 11 us -> 10.8 us  [passed(): return lax.ppermute(array, ('lat', 'lon'), pairs)]
  transfers between devices with their start and end apart: 13 -> 13, of which waited for: 5 -> 4; matrix products, arithmetic and copies ran while one was open for 2% -> 2% of each run, Pallas kernels for 5% -> 5%
where the time goes in v13:
time: 81.8 us; the launch traced here: 81.1 us
  starting transfers between devices  52.7 us (64%)
  waiting for transfers between devices  15.7 us (19%)
  Pallas kernels  10.3 us (13%)
  local copies, waits for them, and re-layouts  1.61 us (2%)
  between operations  0.84 us (1%)
    ppermute x5, starting transfers between devices, passed(): return lax.ppermute(array, ('lat', 'lon'), pairs)  22.5 us
    ppermute x5, starting transfers between devices, swapped(): lax.ppermute(array, 'lat', [(a, a ^ bits) for a in range(lax.axis_size('l...  14.8 us
    ppermute x5, waiting for transfers between devices, passed(): return lax.ppermute(array, ('lat', 'lon'), pairs)  10.8 us
    pallas_call x9, Pallas kernels, run(): pl.pallas_call(kernel, out_shape=out_shape, in_specs=specs, out_specs=out...  10.3 us
    all_to_all x1, starting transfers between devices, per_device(): slices = lax.all_to_all(slices, 'lon', 0, 0, tiled=True)  8.36 us
    all_to_all x1, waiting for transfers between devices, per_device(): blocks = lax.all_to_all(blocks, 'lat', 0, 0, tiled=True)  3.8 us
    ppermute x1, starting transfers between devices, per_device(): arrived = lax.ppermute(skip, 'phase', [(1, 0)])  3.55 us
    all_to_all x1, starting transfers between devices, per_device(): blocks = lax.all_to_all(blocks, 'lat', 0, 0, tiled=True)  3.48 us
  transfers between devices with their start and end apart: 13, of which 4 were waited for; matrix products, arithmetic and copies ran while one was open for 2% of the time, Pallas kernels for 5%

profile of v13, /device:TPU:8, one launch (start us, length us, event | category | flops | bytes accessed | tf_op | source)
XLA Modules:
  0.0 81.1 jit_solution(8854363511977770224)
XLA Ops:
  0.6 1.9 %shard_map.86 = (bf16[80,512]{1,0:T(8,128)(2,1)}, bf16[72,512]{1,0:T(8,128)(2,1)}, bf16[72,512]{1,0:T(8,128)(2,1)}, bf16[80,512]{1,0:T(8,128)(2,1)}) custom-call(s32[6]{0:T(128)} %labels_ref.1, bf16[6,12,2,512]{3,2,1,0:T(2,128)(2,1)} %bitcast.16, bf16[6,12,2,512]{3,2,1,0:T(2,128)(2,1)} %bitcast.17), custom_call_target="tpu_custom_call" | custom-call | tf_op jit(solution)/shard_map/pallas_call | solution.py:38
  2.5 15.4 %collective-permute-start.2 = (bf16[80,512]{1,0:T(8,128)(2,1)}, bf16[80,512]{1,0:T(8,128)(2,1)S(1)}, u32[]{:S(2)}, u32[]{:S(2)}) collective-permute-start(bf16[80,512]{1,0:T(8,128)(2,1)} %get-tuple-element.19), channel_id=1, source_target_pairs={{0,255},{1,224},{2,225},{3,226},{4,227},{5,228},{6,229},{7,230},{8... | collective-permute-start | bytes 245768 | tf_op jit(solution)/shard_map/ppermute | solution.py:416
  17.9 2.5 %collective-permute-start = (bf16[72,512]{1,0:T(8,128)(2,1)}, bf16[72,512]{1,0:T(8,128)(2,1)S(1)}, u32[]{:S(2)}, u32[]{:S(2)}) collective-permute-start(bf16[72,512]{1,0:T(8,128)(2,1)} %get-tuple-element.17), channel_id=1, source_target_pairs={{0,31},{1,0},{2,1},{3,2},{4,3},{5,4},{6,5},{7,6},{8,7},{9,8},{10,9... | collective-permute-start | bytes 221192 | tf_op jit(solution)/shard_map/ppermute | solution.py:416
  20.4 0.6 collective-permute-start.1
  20.9 0.8 slice_bitcast_fusion
  21.7 0.0 copy-start
  21.7 0.0 copy-start.1
  21.7 0.0 copy-start.2
  21.8 0.5 shard_map.87.bias
  22.2 2.1 %collective-permute-done.lon = bf16[72,512]{1,0:T(8,128)(2,1)S(1)} collective-permute-done((bf16[72,512]{1,0:T(8,128)(2,1)}, bf16[72,512]{1,0:T(8,128)(2,1)S(1)}, u32[]{:S(2)}, u32[]{:S(2)}) %collective-permute-start) | collective-permute-done | bytes 73760 | tf_op jit(solution)/shard_map/ppermute | solution.py:416
  24.3 0.0 collective-permute-done.1.lat
  24.3 0.0 collective-permute-done.2.cor
  24.3 0.0 copy-done
  24.4 0.0 copy-done.1
  24.4 0.0 copy-done.2
  24.4 3.4 %shard_map.88 = (bf16[192,512]{1,0:T(8,128)(2,1)S(1)}, bf16[144,512]{1,0:T(8,128)(2,1)S(1)}, bf16[2,192,512]{2,1,0:T(8,128)(2,1)S(1)}, bf16[192,1536]{1,0:T(8,128)(2,1)S(1)}, bf16[2,4,2,96,96]{4,3,2,1,0:T(8,128)(2,1)S(1)}) custom-call(bf16[80,512]{1,0:T(8,128)(2,1)S(1)} %copy-done.1, bf16[72,512]{1,0:T(8,128)(2,1)S(1)} %collective-permute-done.lon, ...), custom_call_target="tpu_custom_call" | custom-call | tf_op jit(solution)/shard_map/pallas_call | solution.py:38
  27.8 3.6 %collective-permute-start.3 = (bf16[192,512]{1,0:T(8,128)(2,1)S(1)}, bf16[192,512]{1,0:T(8,128)(2,1)S(1)}, u32[]{:S(2)}, u32[]{:S(2)}) collective-permute-start(bf16[192,512]{1,0:T(8,128)(2,1)S(1)} %get-tuple-element.20), channel_id=1, source_target_pairs={{256,0},{257,1},{258,2},{259,3},{260,4},{261,5},{262,6},{263,7},{2... | collective-permute-start | bytes 589832 | tf_op jit(solution)/shard_map/ppermute | solution.py:470
  31.4 2.3 %collective-permute-start.6 = (bf16[144,512]{1,0:T(8,128)(2,1)S(1)}, bf16[144,512]{1,0:T(8,128)(2,1)S(1)}, u32[]{:S(2)}, u32[]{:S(2)}) collective-permute-start(bf16[144,512]{1,0:T(8,128)(2,1)S(1)} %get-tuple-element.27.a), channel_id=1, source_target_pairs={{0,64},{32,96},{64,0},{96,32},{128,192},{160,224},{192,128},{224,1... | collective-permute-start | bytes 442376 | tf_op jit(solution)/shard_map/ppermute | solution.py:420
  33.7 4.8 %collective-permute-start.7 = (bf16[144,512]{1,0:T(8,128)(2,1)S(1)}, bf16[144,512]{1,0:T(8,128)(2,1)S(1)}, u32[]{:S(2)}, u32[]{:S(2)}) collective-permute-start(bf16[144,512]{1,0:T(8,128)(2,1)S(1)} %get-tuple-element.27.a), channel_id=1, source_target_pairs={{0,128},{32,160},{64,192},{96,224},{128,0},{160,32},{192,64},{224,... | collective-permute-start | bytes 442376 | tf_op jit(solution)/shard_map/ppermute | solution.py:420
  38.6 3.3 %collective-permute-start.8 = (bf16[144,512]{1,0:T(8,128)(2,1)S(1)}, bf16[144,512]{1,0:T(8,128)(2,1)S(1)}, u32[]{:S(2)}, u32[]{:S(2)}) collective-permute-start(bf16[144,512]{1,0:T(8,128)(2,1)S(1)} %get-tuple-element.27.a), channel_id=1, source_target_pairs={{0,192},{32,224},{64,128},{96,160},{128,64},{160,96},{192,0},{224,... | collective-permute-start | bytes 442376 | tf_op jit(solution)/shard_map/ppermute | solution.py:420
  41.8 0.0 collective-permute-done.3.arrived
  41.8 2.3 %shard_map.89 = (bf16[8,224,128]{2,1,0:T(8,128)(2,1)}, bf16[72,512]{1,0:T(8,128)(2,1)S(1)}, bf16[72,512]{1,0:T(8,128)(2,1)S(1)}) custom-call(bf16[192,512]{1,0:T(8,128)(2,1)S(1)} %collective-permute-done.3.arrived, bf16[2,192,512]{2,1,0:T(8,128)(2,1)S(1)} %get-tuple-element.21.fields, bf16[192,1536]{1,0:T(8,128)(2,1)S(1)} %get-tuple-element.22.projected, ...), custom_call_target="tpu_custom_call" | custom-call | flops 4000000000 | bytes 20000000 | tf_op jit(solution)/shard_map/pallas_call | solution.py:38
  44.2 3.5 %all-to-all-start = ((bf16[8,224,128]{2,1,0:T(8,128)(2,1)}), bf16[8,224,128]{2,1,0:T(8,128)(2,1)S(1)}, u32[]{:S(2)}, u32[]{:S(2)}) async-start(bf16[8,224,128]{2,1,0:T(8,128)(2,1)} %get-tuple-element.26), calls=%async_computation | async-start | bytes 917504 | tf_op jit(solution)/shard_map/all_to_all | solution.py:479
  47.7 0.0 collective-permute-done.6.b
  47.7 0.0 collective-permute-done.7.c
  47.7 0.0 collective-permute-done.8.d
  47.8 2.3 %collective-permute-start.10 = (bf16[2,144,512]{2,1,0:T(8,128)(2,1)S(1)}, bf16[2,144,512]{2,1,0:T(8,128)(2,1)S(1)}, u32[]{:S(2)}, u32[]{:S(2)}) collective-permute-start(bf16[2,144,512]{2,1,0:T(8,128)(2,1)S(1)} %get-tuple-element.29.high), channel_id=1, source_target_pairs={{0,32},{32,0},{64,96},{96,64},{128,160},{160,128},{192,224},{224,1... | collective-permute-start | bytes 884744 | tf_op jit(solution)/shard_map/ppermute | solution.py:420
  50.1 2.0 %collective-permute-start.9 = (bf16[2,144,512]{2,1,0:T(8,128)(2,1)S(1)}, bf16[2,144,512]{2,1,0:T(8,128)(2,1)S(1)}, u32[]{:S(2)}, u32[]{:S(2)}) collective-permute-start(bf16[2,144,512]{2,1,0:T(8,128)(2,1)S(1)} %get-tuple-element.28.low), channel_id=1, source_target_pairs={{0,32},{32,0},{64,96},{96,64},{128,160},{160,128},{192,224},{224,1... | collective-permute-start | bytes 884744 | tf_op jit(solution)/shard_map/ppermute | solution.py:420
  52.1 0.4 collective-permute-start.4
  52.5 0.0 collective-permute-done.10.other_high
  52.5 1.0 %collective-permute-done.9.other_low = bf16[2,144,512]{2,1,0:T(8,128)(2,1)S(1)} collective-permute-done((bf16[2,144,512]{2,1,0:T(8,128)(2,1)S(1)}, bf16[2,144,512]{2,1,0:T(8,128)(2,1)S(1)}, u32[]{:S(2)}, u32[]{:S(2)}) %collective-permute-start.9) | collective-permute-done | bytes 294944 | tf_op jit(solution)/shard_map/ppermute | solution.py:420
  53.5 3.8 %all-to-all-done.blocks = bf16[8,224,128]{2,1,0:T(8,128)(2,1)S(1)} async-done(((bf16[8,224,128]{2,1,0:T(8,128)(2,1)}), bf16[8,224,128]{2,1,0:T(8,128)(2,1)S(1)}, u32[]{:S(2)}, u32[]{:S(2)}) %all-to-all-start) | async-done | bytes 458784 | tf_op jit(solution)/shard_map/all_to_all | solution.py:479
  57.3 1.4 %shard_map.93 = bf16[32,24,128]{2,1,0:T(8,128)(2,1)} custom-call(s32[1]{0:T(128)} %bitcast.7.lat_index, bf16[8,224,128]{2,1,0:T(8,128)(2,1)S(1)} %all-to-all-done.blocks, bf16[2,144,512]{2,1,0:T(8,128)(2,1)S(1)} %get-tuple-element.28.low, bf16[2,144,512]{2,1,0:T(8,128)(2,1)S(1)} %get-tuple-element.29.high, ...), custom_call_target="tpu_custom_call" | custom-call | tf_op jit(solution)/shard_map/pallas_call | solution.py:38
  58.7 8.4 %all-to-all-start.1 = ((bf16[32,24,128]{2,1,0:T(8,128)(2,1)}), bf16[32,24,128]{2,1,0:T(8,128)(2,1)S(1)}, u32[]{:S(2)}, u32[]{:S(2)}) async-start(bf16[32,24,128]{2,1,0:T(8,128)(2,1)} %shard_map.93), calls=%async_computation.1 | async-start | bytes 393216 | tf_op jit(solution)/shard_map/all_to_all | solution.py:491
  67.1 0.0 collective-permute-done.4.above
  67.1 3.7 %collective-permute-start.5 = (bf16[72,512]{1,0:T(8,128)(2,1)S(1)}, bf16[72,512]{1,0:T(8,128)(2,1)S(1)}, u32[]{:S(2)}, u32[]{:S(2)}) collective-permute-start(bf16[72,512]{1,0:T(8,128)(2,1)S(1)} %shard_map.90), channel_id=1, source_target_pairs={{0,1},{1,2},{2,3},{3,4},{4,5},{5,6},{6,7},{7,8},{8,9},{9,10},{10,1... | collective-permute-start | bytes 221192 | tf_op jit(solution)/shard_map/ppermute | solution.py:416
  70.8 8.7 %collective-permute-done.5.left = bf16[72,512]{1,0:T(8,128)(2,1)S(1)} collective-permute-done((bf16[72,512]{1,0:T(8,128)(2,1)S(1)}, bf16[72,512]{1,0:T(8,128)(2,1)S(1)}, u32[]{:S(2)}, u32[]{:S(2)}) %collective-permute-start.5) | collective-permute-done | bytes 73760 | tf_op jit(solution)/shard_map/ppermute | solution.py:416
  79.5 0.1 shard_map.91
  79.6 0.8 %copy.9 = bf16[1,2,6,12,512]{4,1,3,2,0:T(2,128)(2,1)} copy(bf16[1,2,6,12,512]{4,3,2,1,0:T(8,128)(2,1)S(1)} %shard_map.91) | data formatting | bytes 294912
  80.4 0.0 all-to-all-done.1.parts
  80.4 0.7 shard_map.94
  (3 shorter events, 0.1 us)
Async XLA Ops:
  2.5 21.8 %collective-permute-start.2 = (bf16[80,512]{1,0:T(8,128)(2,1)}, bf16[80,512]{1,0:T(8,128)(2,1)S(1)}, u32[]{:S(2)}, u32[]{:S(2)}) collective-permute-start(bf16[80,512]{1,0:T(8,128)(2,1)} %get-tuple-element.19), channel_id=1, source_target_pairs={{0,255},{1,224},{2,225},{3,226},{4,227},{5,228},{6,229},{7,230},{8... | collective-permute-start | bytes 245768 | tf_op jit(solution)/shard_map/ppermute | solution.py:416
  17.9 6.5 %collective-permute-start = (bf16[72,512]{1,0:T(8,128)(2,1)}, bf16[72,512]{1,0:T(8,128)(2,1)S(1)}, u32[]{:S(2)}, u32[]{:S(2)}) collective-permute-start(bf16[72,512]{1,0:T(8,128)(2,1)} %get-tuple-element.17), channel_id=1, source_target_pairs={{0,31},{1,0},{2,1},{3,2},{4,3},{5,4},{6,5},{7,6},{8,7},{9,8},{10,9... | collective-permute-start | bytes 221192 | tf_op jit(solution)/shard_map/ppermute | solution.py:416
  20.4 4.0 %collective-permute-start.1 = (bf16[72,512]{1,0:T(8,128)(2,1)}, bf16[72,512]{1,0:T(8,128)(2,1)S(1)}, u32[]{:S(2)}, u32[]{:S(2)}) collective-permute-start(bf16[72,512]{1,0:T(8,128)(2,1)} %get-tuple-element.18), channel_id=1, source_target_pairs={{0,224},{1,225},{2,226},{3,227},{4,228},{5,229},{6,230},{7,231},{8... | collective-permute-start | bytes 221192 | tf_op jit(solution)/shard_map/ppermute | solution.py:416
  21.7 2.6 %copy-start = (bf16[1,512,512]{2,1,0:T(8,128)(2,1)S(1)}, bf16[1,512,512]{2,1,0:T(8,128)(2,1)}, u32[]{:S(2)}) copy-start(bf16[1,512,512]{2,1,0:T(8,128)(2,1)} %param.10) | copy-start | bytes 1572868
  21.7 2.6 %copy-start.1 = (bf16[80,512]{1,0:T(8,128)(2,1)S(1)}, bf16[80,512]{1,0:T(8,128)(2,1)}, u32[]{:S(2)}) copy-start(bf16[80,512]{1,0:T(8,128)(2,1)} %get-tuple-element.16.own) | copy-start | bytes 245764
  21.7 2.6 %copy-start.2 = (f32[1,512]{1,0:T(1,128)S(1)}, f32[1,512]{1,0:T(1,128)}, u32[]{:S(2)}) copy-start(f32[1,512]{1,0:T(1,128)} %gain.3) | copy-start | bytes 6148
  27.8 14.0 %collective-permute-start.3 = (bf16[192,512]{1,0:T(8,128)(2,1)S(1)}, bf16[192,512]{1,0:T(8,128)(2,1)S(1)}, u32[]{:S(2)}, u32[]{:S(2)}) collective-permute-start(bf16[192,512]{1,0:T(8,128)(2,1)S(1)} %get-tuple-element.20), channel_id=1, source_target_pairs={{256,0},{257,1},{258,2},{259,3},{260,4},{261,5},{262,6},{263,7},{2... | collective-permute-start | bytes 589832 | tf_op jit(solution)/shard_map/ppermute | solution.py:470
  31.4 16.3 %collective-permute-start.6 = (bf16[144,512]{1,0:T(8,128)(2,1)S(1)}, bf16[144,512]{1,0:T(8,128)(2,1)S(1)}, u32[]{:S(2)}, u32[]{:S(2)}) collective-permute-start(bf16[144,512]{1,0:T(8,128)(2,1)S(1)} %get-tuple-element.27.a), channel_id=1, source_target_pairs={{0,64},{32,96},{64,0},{96,32},{128,192},{160,224},{192,128},{224,1... | collective-permute-start | bytes 442376 | tf_op jit(solution)/shard_map/ppermute | solution.py:420
  33.7 14.0 %collective-permute-start.7 = (bf16[144,512]{1,0:T(8,128)(2,1)S(1)}, bf16[144,512]{1,0:T(8,128)(2,1)S(1)}, u32[]{:S(2)}, u32[]{:S(2)}) collective-permute-start(bf16[144,512]{1,0:T(8,128)(2,1)S(1)} %get-tuple-element.27.a), channel_id=1, source_target_pairs={{0,128},{32,160},{64,192},{96,224},{128,0},{160,32},{192,64},{224,... | collective-permute-start | bytes 442376 | tf_op jit(solution)/shard_map/ppermute | solution.py:420
  38.6 9.1 %collective-permute-start.8 = (bf16[144,512]{1,0:T(8,128)(2,1)S(1)}, bf16[144,512]{1,0:T(8,128)(2,1)S(1)}, u32[]{:S(2)}, u32[]{:S(2)}) collective-permute-start(bf16[144,512]{1,0:T(8,128)(2,1)S(1)} %get-tuple-element.27.a), channel_id=1, source_target_pairs={{0,192},{32,224},{64,128},{96,160},{128,64},{160,96},{192,0},{224,... | collective-permute-start | bytes 442376 | tf_op jit(solution)/shard_map/ppermute | solution.py:420
  44.2 13.2 %all-to-all-start = ((bf16[8,224,128]{2,1,0:T(8,128)(2,1)}), bf16[8,224,128]{2,1,0:T(8,128)(2,1)S(1)}, u32[]{:S(2)}, u32[]{:S(2)}) async-start(bf16[8,224,128]{2,1,0:T(8,128)(2,1)} %get-tuple-element.26), calls=%async_computation | async-start | bytes 917504 | tf_op jit(solution)/shard_map/all_to_all | solution.py:479
  47.8 4.7 %collective-permute-start.10 = (bf16[2,144,512]{2,1,0:T(8,128)(2,1)S(1)}, bf16[2,144,512]{2,1,0:T(8,128)(2,1)S(1)}, u32[]{:S(2)}, u32[]{:S(2)}) collective-permute-start(bf16[2,144,512]{2,1,0:T(8,128)(2,1)S(1)} %get-tuple-element.29.high), channel_id=1, source_target_pairs={{0,32},{32,0},{64,96},{96,64},{128,160},{160,128},{192,224},{224,1... | collective-permute-start | bytes 884744 | tf_op jit(solution)/shard_map/ppermute | solution.py:420
  50.1 3.5 %collective-permute-start.9 = (bf16[2,144,512]{2,1,0:T(8,128)(2,1)S(1)}, bf16[2,144,512]{2,1,0:T(8,128)(2,1)S(1)}, u32[]{:S(2)}, u32[]{:S(2)}) collective-permute-start(bf16[2,144,512]{2,1,0:T(8,128)(2,1)S(1)} %get-tuple-element.28.low), channel_id=1, source_target_pairs={{0,32},{32,0},{64,96},{96,64},{128,160},{160,128},{192,224},{224,1... | collective-permute-start | bytes 884744 | tf_op jit(solution)/shard_map/ppermute | solution.py:420
  52.1 15.0 %collective-permute-start.4 = (bf16[72,512]{1,0:T(8,128)(2,1)S(1)}, bf16[72,512]{1,0:T(8,128)(2,1)S(1)}, u32[]{:S(2)}, u32[]{:S(2)}) collective-permute-start(bf16[72,512]{1,0:T(8,128)(2,1)S(1)} %get-tuple-element.25), channel_id=1, source_target_pairs={{0,32},{1,33},{2,34},{3,35},{4,36},{5,37},{6,38},{7,39},{8,40},{9,... | collective-permute-start | bytes 221192 | tf_op jit(solution)/shard_map/ppermute | solution.py:416
  58.7 21.7 %all-to-all-start.1 = ((bf16[32,24,128]{2,1,0:T(8,128)(2,1)}), bf16[32,24,128]{2,1,0:T(8,128)(2,1)S(1)}, u32[]{:S(2)}, u32[]{:S(2)}) async-start(bf16[32,24,128]{2,1,0:T(8,128)(2,1)} %shard_map.93), calls=%async_computation.1 | async-start | bytes 393216 | tf_op jit(solution)/shard_map/all_to_all | solution.py:491
  67.1 12.4 %collective-permute-start.5 = (bf16[72,512]{1,0:T(8,128)(2,1)S(1)}, bf16[72,512]{1,0:T(8,128)(2,1)S(1)}, u32[]{:S(2)}, u32[]{:S(2)}) collective-permute-start(bf16[72,512]{1,0:T(8,128)(2,1)S(1)} %shard_map.90), channel_id=1, source_target_pairs={{0,1},{1,2},{2,3},{3,4},{4,5},{5,6},{6,7},{7,8},{8,9},{9,10},{10,1... | collective-permute-start | bytes 221192 | tf_op jit(solution)/shard_map/ppermute | solution.py:416

commit v14 on v11

--- a/solution.py
+++ b/solution.py
@@ -78,9 +78,10 @@
     fetch = pltpu.make_async_copy(labels_ref, labels, sem)
     fetch.start()
     fetches = []
-    for i in range(6):
-        fetches.append(pltpu.make_async_copy(x_ref.at[i], x_rows.at[i], sems.at[0, i]))
-        fetches.append(pltpu.make_async_copy(g_ref.at[i], g_rows.at[i], sems.at[1, i]))
+    halves = [pl.ds(3, 3), pl.ds(0, 3)]
+    for j, rows in enumerate(halves):
+        fetches.append(pltpu.make_async_copy(x_ref.at[rows], x_rows.at[rows], sems.at[0, j]))
+        fetches.append(pltpu.make_async_copy(g_ref.at[rows], g_rows.at[rows], sems.at[1, j]))
     for copy in fetches:
         copy.start()
     row = row_index((8, FEATURES), 0)
@@ -88,9 +89,10 @@
     fetch.wait()
     parts = {}
     marks = [jnp.zeros((8, FEATURES), F32)] * 2
-    for i in range(6):
-        fetches[2 * i].wait()
-        fetches[2 * i + 1].wait()
+    for i in (3, 4, 5, 0, 1, 2):
+        if i % 3 == 0:
+            fetches[2 * (i == 0)].wait()
+            fetches[2 * (i == 0) + 1].wait()
         fields = x_rows[i].astype(F32), g_rows[i].astype(F32)
         low = [field[0:8, level, :] for field in fields for level in range(2)]
         high = [pltpu.roll(field[4:12, level, :], 6, 0) for field in fields for level in range(2)]
@@ -434,7 +436,7 @@
             pltpu.VMEM((6, 12, 2, FEATURES), BF16),
             pltpu.VMEM((6, 12, 2, FEATURES), BF16),
             pltpu.SemaphoreType.DMA,
-            pltpu.SemaphoreType.DMA((2, 6)),
+            pltpu.SemaphoreType.DMA((2, 2)),
         ],
         places={0: pl.ANY, 1: pl.ANY, 2: pl.ANY},
         limit=58 * MIB,

time: 81.1 us -> 81.1 us (level)
  no operation moved by 1% of the time
where the time goes in v14:
time: 81.1 us; the launch traced here: 80.4 us
  starting transfers between devices  51.9 us (64%)
  waiting for transfers between devices  15.8 us (19%)
  Pallas kernels  10.3 us (13%)
  local copies, waits for them, and re-layouts  1.61 us (2%)
  between operations  0.82 us (1%)
    ppermute x8, starting transfers between devices, passed(): return lax.ppermute(array, ('lat', 'lon'), pairs)  31.6 us
    ppermute x8, waiting for transfers between devices, passed(): return lax.ppermute(array, ('lat', 'lon'), pairs)  11 us
    pallas_call x9, Pallas kernels, run(): pl.pallas_call(kernel, out_shape=out_shape, in_specs=specs, out_specs=out...  10.3 us
    all_to_all x1, starting transfers between devices, per_device(): slices = lax.all_to_all(slices, 'lon', 0, 0, tiled=True)  8.28 us
    ppermute x2, starting transfers between devices, other_core(): lax.ppermute(array, 'lat', [(a, a ^ 1) for a in range(lax.axis_size('lat'...  4.33 us
    all_to_all x1, starting transfers between devices, per_device(): blocks = lax.all_to_all(blocks, 'lat', 0, 0, tiled=True)  4.08 us
    all_to_all x1, waiting for transfers between devices, per_device(): blocks = lax.all_to_all(blocks, 'lat', 0, 0, tiled=True)  3.78 us
    ppermute x1, starting transfers between devices, per_device(): arrived = lax.ppermute(skip, 'phase', [(1, 0)])  3.55 us
  transfers between devices with their start and end apart: 13, of which 5 were waited for; matrix products, arithmetic and copies ran while one was open for 2% of the time, Pallas kernels for 5%

profile of v14, /device:TPU:8, one launch (start us, length us, event | category | flops | bytes accessed | tf_op | source)
XLA Modules:
  0.0 80.4 jit_solution(12557882752338076620)
XLA Ops:
  0.6 1.9 %shard_map.86 = (bf16[80,512]{1,0:T(8,128)(2,1)}, bf16[72,512]{1,0:T(8,128)(2,1)}, bf16[72,512]{1,0:T(8,128)(2,1)}, bf16[80,512]{1,0:T(8,128)(2,1)}) custom-call(s32[6]{0:T(128)} %labels_ref.1, bf16[6,12,2,512]{3,2,1,0:T(2,128)(2,1)} %bitcast.16, bf16[6,12,2,512]{3,2,1,0:T(2,128)(2,1)} %bitcast.17), custom_call_target="tpu_custom_call" | custom-call | tf_op jit(solution)/shard_map/pallas_call | solution.py:38
  2.5 15.4 %collective-permute-start.2 = (bf16[80,512]{1,0:T(8,128)(2,1)}, bf16[80,512]{1,0:T(8,128)(2,1)S(1)}, u32[]{:S(2)}, u32[]{:S(2)}) collective-permute-start(bf16[80,512]{1,0:T(8,128)(2,1)} %get-tuple-element.19), channel_id=1, source_target_pairs={{0,255},{1,224},{2,225},{3,226},{4,227},{5,228},{6,229},{7,230},{8... | collective-permute-start | bytes 245768 | tf_op jit(solution)/shard_map/ppermute | solution.py:419
  17.9 2.5 %collective-permute-start = (bf16[72,512]{1,0:T(8,128)(2,1)}, bf16[72,512]{1,0:T(8,128)(2,1)S(1)}, u32[]{:S(2)}, u32[]{:S(2)}) collective-permute-start(bf16[72,512]{1,0:T(8,128)(2,1)} %get-tuple-element.17), channel_id=1, source_target_pairs={{0,31},{1,0},{2,1},{3,2},{4,3},{5,4},{6,5},{7,6},{8,7},{9,8},{10,9... | collective-permute-start | bytes 221192 | tf_op jit(solution)/shard_map/ppermute | solution.py:419
  20.4 0.6 collective-permute-start.1
  21.0 0.8 slice_bitcast_fusion
  21.7 0.0 copy-start
  21.7 0.0 copy-start.1
  21.7 0.0 copy-start.2
  21.8 0.5 shard_map.87.bias
  22.2 2.1 %collective-permute-done.lon = bf16[72,512]{1,0:T(8,128)(2,1)S(1)} collective-permute-done((bf16[72,512]{1,0:T(8,128)(2,1)}, bf16[72,512]{1,0:T(8,128)(2,1)S(1)}, u32[]{:S(2)}, u32[]{:S(2)}) %collective-permute-start) | collective-permute-done | bytes 73760 | tf_op jit(solution)/shard_map/ppermute | solution.py:419
  24.4 0.0 collective-permute-done.1.lat
  24.4 0.0 collective-permute-done.2.cor
  24.4 0.0 copy-done
  24.4 0.0 copy-done.1
  24.4 0.0 copy-done.2
  24.4 3.4 %shard_map.88 = (bf16[192,512]{1,0:T(8,128)(2,1)S(1)}, bf16[144,512]{1,0:T(8,128)(2,1)S(1)}, bf16[2,192,512]{2,1,0:T(8,128)(2,1)S(1)}, bf16[192,1536]{1,0:T(8,128)(2,1)S(1)}, bf16[2,4,2,96,96]{4,3,2,1,0:T(8,128)(2,1)S(1)}) custom-call(bf16[80,512]{1,0:T(8,128)(2,1)S(1)} %copy-done.1, bf16[72,512]{1,0:T(8,128)(2,1)S(1)} %collective-permute-done.lon, ...), custom_call_target="tpu_custom_call" | custom-call | tf_op jit(solution)/shard_map/pallas_call | solution.py:38
  27.8 3.6 %collective-permute-start.3 = (bf16[192,512]{1,0:T(8,128)(2,1)S(1)}, bf16[192,512]{1,0:T(8,128)(2,1)S(1)}, u32[]{:S(2)}, u32[]{:S(2)}) collective-permute-start(bf16[192,512]{1,0:T(8,128)(2,1)S(1)} %get-tuple-element.20), channel_id=1, source_target_pairs={{256,0},{257,1},{258,2},{259,3},{260,4},{261,5},{262,6},{263,7},{2... | collective-permute-start | bytes 589832 | tf_op jit(solution)/shard_map/ppermute | solution.py:473
  31.4 3.8 %collective-permute-start.6 = (bf16[144,512]{1,0:T(8,128)(2,1)S(1)}, bf16[144,512]{1,0:T(8,128)(2,1)S(1)}, u32[]{:S(2)}, u32[]{:S(2)}) collective-permute-start(bf16[144,512]{1,0:T(8,128)(2,1)S(1)} %get-tuple-element.27.a), channel_id=1, source_target_pairs={{0,192},{1,193},{2,194},{3,195},{4,196},{5,197},{6,198},{7,199},{8... | collective-permute-start | bytes 442376 | tf_op jit(solution)/shard_map/ppermute | solution.py:419
  35.2 2.5 %collective-permute-start.7 = (bf16[144,512]{1,0:T(8,128)(2,1)S(1)}, bf16[144,512]{1,0:T(8,128)(2,1)S(1)}, u32[]{:S(2)}, u32[]{:S(2)}) collective-permute-start(bf16[144,512]{1,0:T(8,128)(2,1)S(1)} %get-tuple-element.27.a), channel_id=1, source_target_pairs={{0,128},{1,129},{2,130},{3,131},{4,132},{5,133},{6,134},{7,135},{8... | collective-permute-start | bytes 442376 | tf_op jit(solution)/shard_map/ppermute | solution.py:419
  37.7 2.8 %collective-permute-start.8 = (bf16[144,512]{1,0:T(8,128)(2,1)S(1)}, bf16[144,512]{1,0:T(8,128)(2,1)S(1)}, u32[]{:S(2)}, u32[]{:S(2)}) collective-permute-start(bf16[144,512]{1,0:T(8,128)(2,1)S(1)} %get-tuple-element.27.a), channel_id=1, source_target_pairs={{0,64},{1,65},{2,66},{3,67},{4,68},{5,69},{6,70},{7,71},{8,72},{9,... | collective-permute-start | bytes 442376 | tf_op jit(solution)/shard_map/ppermute | solution.py:419
  40.5 0.0 collective-permute-done.3.arrived
  40.5 2.3 %shard_map.89 = (bf16[8,224,128]{2,1,0:T(8,128)(2,1)}, bf16[72,512]{1,0:T(8,128)(2,1)S(1)}, bf16[72,512]{1,0:T(8,128)(2,1)S(1)}) custom-call(bf16[192,512]{1,0:T(8,128)(2,1)S(1)} %collective-permute-done.3.arrived, bf16[2,192,512]{2,1,0:T(8,128)(2,1)S(1)} %get-tuple-element.21.fields, bf16[192,1536]{1,0:T(8,128)(2,1)S(1)} %get-tuple-element.22.projected, ...), custom_call_target="tpu_custom_call" | custom-call | flops 4000000000 | bytes 20000000 | tf_op jit(solution)/shard_map/pallas_call | solution.py:38
  42.9 4.1 %all-to-all-start = ((bf16[8,224,128]{2,1,0:T(8,128)(2,1)}), bf16[8,224,128]{2,1,0:T(8,128)(2,1)S(1)}, u32[]{:S(2)}, u32[]{:S(2)}) async-start(bf16[8,224,128]{2,1,0:T(8,128)(2,1)} %get-tuple-element.26), calls=%async_computation | async-start | bytes 917504 | tf_op jit(solution)/shard_map/all_to_all | solution.py:482
  46.9 0.0 collective-permute-done.6.b
  46.9 0.0 collective-permute-done.7.c
  47.0 0.1 collective-permute-done.8.d
  47.1 2.3 %collective-permute-start.10 = (bf16[2,144,512]{2,1,0:T(8,128)(2,1)S(1)}, bf16[2,144,512]{2,1,0:T(8,128)(2,1)S(1)}, u32[]{:S(2)}, u32[]{:S(2)}) collective-permute-start(bf16[2,144,512]{2,1,0:T(8,128)(2,1)S(1)} %get-tuple-element.29.high), channel_id=1, source_target_pairs={{0,32},{32,0},{64,96},{96,64},{128,160},{160,128},{192,224},{224,1... | collective-permute-start | bytes 884744 | tf_op jit(solution)/shard_map/ppermute | solution.py:423
  49.4 2.0 %collective-permute-start.9 = (bf16[2,144,512]{2,1,0:T(8,128)(2,1)S(1)}, bf16[2,144,512]{2,1,0:T(8,128)(2,1)S(1)}, u32[]{:S(2)}, u32[]{:S(2)}) collective-permute-start(bf16[2,144,512]{2,1,0:T(8,128)(2,1)S(1)} %get-tuple-element.28.low), channel_id=1, source_target_pairs={{0,32},{32,0},{64,96},{96,64},{128,160},{160,128},{192,224},{224,1... | collective-permute-start | bytes 884744 | tf_op jit(solution)/shard_map/ppermute | solution.py:423
  51.5 0.4 collective-permute-start.4
  51.9 0.0 collective-permute-done.10.other_high
  51.9 1.0 %collective-permute-done.9.other_low = bf16[2,144,512]{2,1,0:T(8,128)(2,1)S(1)} collective-permute-done((bf16[2,144,512]{2,1,0:T(8,128)(2,1)S(1)}, bf16[2,144,512]{2,1,0:T(8,128)(2,1)S(1)}, u32[]{:S(2)}, u32[]{:S(2)}) %collective-permute-start.9) | collective-permute-done | bytes 294944 | tf_op jit(solution)/shard_map/ppermute | solution.py:423
  52.9 3.8 %all-to-all-done.blocks = bf16[8,224,128]{2,1,0:T(8,128)(2,1)S(1)} async-done(((bf16[8,224,128]{2,1,0:T(8,128)(2,1)}), bf16[8,224,128]{2,1,0:T(8,128)(2,1)S(1)}, u32[]{:S(2)}, u32[]{:S(2)}) %all-to-all-start) | async-done | bytes 458784 | tf_op jit(solution)/shard_map/all_to_all | solution.py:482
  56.7 1.4 %shard_map.93 = bf16[32,24,128]{2,1,0:T(8,128)(2,1)} custom-call(s32[1]{0:T(128)} %bitcast.7.lat_index, bf16[8,224,128]{2,1,0:T(8,128)(2,1)S(1)} %all-to-all-done.blocks, bf16[2,144,512]{2,1,0:T(8,128)(2,1)S(1)} %get-tuple-element.28.low, bf16[2,144,512]{2,1,0:T(8,128)(2,1)S(1)} %get-tuple-element.29.high, ...), custom_call_target="tpu_custom_call" | custom-call | tf_op jit(solution)/shard_map/pallas_call | solution.py:38
  58.1 8.3 %all-to-all-start.1 = ((bf16[32,24,128]{2,1,0:T(8,128)(2,1)}), bf16[32,24,128]{2,1,0:T(8,128)(2,1)S(1)}, u32[]{:S(2)}, u32[]{:S(2)}) async-start(bf16[32,24,128]{2,1,0:T(8,128)(2,1)} %shard_map.93), calls=%async_computation.1 | async-start | bytes 393216 | tf_op jit(solution)/shard_map/all_to_all | solution.py:494
  66.3 0.0 collective-permute-done.4.above
  66.4 3.7 %collective-permute-start.5 = (bf16[72,512]{1,0:T(8,128)(2,1)S(1)}, bf16[72,512]{1,0:T(8,128)(2,1)S(1)}, u32[]{:S(2)}, u32[]{:S(2)}) collective-permute-start(bf16[72,512]{1,0:T(8,128)(2,1)S(1)} %shard_map.90), channel_id=1, source_target_pairs={{0,1},{1,2},{2,3},{3,4},{4,5},{5,6},{6,7},{7,8},{8,9},{9,10},{10,1... | collective-permute-start | bytes 221192 | tf_op jit(solution)/shard_map/ppermute | solution.py:419
  70.1 8.7 %collective-permute-done.5.left = bf16[72,512]{1,0:T(8,128)(2,1)S(1)} collective-permute-done((bf16[72,512]{1,0:T(8,128)(2,1)S(1)}, bf16[72,512]{1,0:T(8,128)(2,1)S(1)}, u32[]{:S(2)}, u32[]{:S(2)}) %collective-permute-start.5) | collective-permute-done | bytes 73760 | tf_op jit(solution)/shard_map/ppermute | solution.py:419
  78.9 0.1 shard_map.91
  78.9 0.8 %copy.9 = bf16[1,2,6,12,512]{4,1,3,2,0:T(2,128)(2,1)} copy(bf16[1,2,6,12,512]{4,3,2,1,0:T(8,128)(2,1)S(1)} %shard_map.91) | data formatting | bytes 294912
  79.7 0.0 all-to-all-done.1.parts
  79.7 0.7 shard_map.94
  (3 shorter events, 0.1 us)
Async XLA Ops:
  2.5 21.8 %collective-permute-start.2 = (bf16[80,512]{1,0:T(8,128)(2,1)}, bf16[80,512]{1,0:T(8,128)(2,1)S(1)}, u32[]{:S(2)}, u32[]{:S(2)}) collective-permute-start(bf16[80,512]{1,0:T(8,128)(2,1)} %get-tuple-element.19), channel_id=1, source_target_pairs={{0,255},{1,224},{2,225},{3,226},{4,227},{5,228},{6,229},{7,230},{8... | collective-permute-start | bytes 245768 | tf_op jit(solution)/shard_map/ppermute | solution.py:419
  17.9 6.5 %collective-permute-start = (bf16[72,512]{1,0:T(8,128)(2,1)}, bf16[72,512]{1,0:T(8,128)(2,1)S(1)}, u32[]{:S(2)}, u32[]{:S(2)}) collective-permute-start(bf16[72,512]{1,0:T(8,128)(2,1)} %get-tuple-element.17), channel_id=1, source_target_pairs={{0,31},{1,0},{2,1},{3,2},{4,3},{5,4},{6,5},{7,6},{8,7},{9,8},{10,9... | collective-permute-start | bytes 221192 | tf_op jit(solution)/shard_map/ppermute | solution.py:419
  20.4 4.0 %collective-permute-start.1 = (bf16[72,512]{1,0:T(8,128)(2,1)}, bf16[72,512]{1,0:T(8,128)(2,1)S(1)}, u32[]{:S(2)}, u32[]{:S(2)}) collective-permute-start(bf16[72,512]{1,0:T(8,128)(2,1)} %get-tuple-element.18), channel_id=1, source_target_pairs={{0,224},{1,225},{2,226},{3,227},{4,228},{5,229},{6,230},{7,231},{8... | collective-permute-start | bytes 221192 | tf_op jit(solution)/shard_map/ppermute | solution.py:419
  21.7 2.6 %copy-start = (bf16[1,512,512]{2,1,0:T(8,128)(2,1)S(1)}, bf16[1,512,512]{2,1,0:T(8,128)(2,1)}, u32[]{:S(2)}) copy-start(bf16[1,512,512]{2,1,0:T(8,128)(2,1)} %param.10) | copy-start | bytes 1572868
  21.7 2.6 %copy-start.1 = (bf16[80,512]{1,0:T(8,128)(2,1)S(1)}, bf16[80,512]{1,0:T(8,128)(2,1)}, u32[]{:S(2)}) copy-start(bf16[80,512]{1,0:T(8,128)(2,1)} %get-tuple-element.16.own) | copy-start | bytes 245764
  21.7 2.6 %copy-start.2 = (f32[1,512]{1,0:T(1,128)S(1)}, f32[1,512]{1,0:T(1,128)}, u32[]{:S(2)}) copy-start(f32[1,512]{1,0:T(1,128)} %gain.3) | copy-start | bytes 6148
  27.8 12.7 %collective-permute-start.3 = (bf16[192,512]{1,0:T(8,128)(2,1)S(1)}, bf16[192,512]{1,0:T(8,128)(2,1)S(1)}, u32[]{:S(2)}, u32[]{:S(2)}) collective-permute-start(bf16[192,512]{1,0:T(8,128)(2,1)S(1)} %get-tuple-element.20), channel_id=1, source_target_pairs={{256,0},{257,1},{258,2},{259,3},{260,4},{261,5},{262,6},{263,7},{2... | collective-permute-start | bytes 589832 | tf_op jit(solution)/shard_map/ppermute | solution.py:473
  31.4 15.5 %collective-permute-start.6 = (bf16[144,512]{1,0:T(8,128)(2,1)S(1)}, bf16[144,512]{1,0:T(8,128)(2,1)S(1)}, u32[]{:S(2)}, u32[]{:S(2)}) collective-permute-start(bf16[144,512]{1,0:T(8,128)(2,1)S(1)} %get-tuple-element.27.a), channel_id=1, source_target_pairs={{0,192},{1,193},{2,194},{3,195},{4,196},{5,197},{6,198},{7,199},{8... | collective-permute-start | bytes 442376 | tf_op jit(solution)/shard_map/ppermute | solution.py:419
  35.2 11.8 %collective-permute-start.7 = (bf16[144,512]{1,0:T(8,128)(2,1)S(1)}, bf16[144,512]{1,0:T(8,128)(2,1)S(1)}, u32[]{:S(2)}, u32[]{:S(2)}) collective-permute-start(bf16[144,512]{1,0:T(8,128)(2,1)S(1)} %get-tuple-element.27.a), channel_id=1, source_target_pairs={{0,128},{1,129},{2,130},{3,131},{4,132},{5,133},{6,134},{7,135},{8... | collective-permute-start | bytes 442376 | tf_op jit(solution)/shard_map/ppermute | solution.py:419
  37.7 9.4 %collective-permute-start.8 = (bf16[144,512]{1,0:T(8,128)(2,1)S(1)}, bf16[144,512]{1,0:T(8,128)(2,1)S(1)}, u32[]{:S(2)}, u32[]{:S(2)}) collective-permute-start(bf16[144,512]{1,0:T(8,128)(2,1)S(1)} %get-tuple-element.27.a), channel_id=1, source_target_pairs={{0,64},{1,65},{2,66},{3,67},{4,68},{5,69},{6,70},{7,71},{8,72},{9,... | collective-permute-start | bytes 442376 | tf_op jit(solution)/shard_map/ppermute | solution.py:419
  42.9 13.8 %all-to-all-start = ((bf16[8,224,128]{2,1,0:T(8,128)(2,1)}), bf16[8,224,128]{2,1,0:T(8,128)(2,1)S(1)}, u32[]{:S(2)}, u32[]{:S(2)}) async-start(bf16[8,224,128]{2,1,0:T(8,128)(2,1)} %get-tuple-element.26), calls=%async_computation | async-start | bytes 917504 | tf_op jit(solution)/shard_map/all_to_all | solution.py:482
  47.1 4.8 %collective-permute-start.10 = (bf16[2,144,512]{2,1,0:T(8,128)(2,1)S(1)}, bf16[2,144,512]{2,1,0:T(8,128)(2,1)S(1)}, u32[]{:S(2)}, u32[]{:S(2)}) collective-permute-start(bf16[2,144,512]{2,1,0:T(8,128)(2,1)S(1)} %get-tuple-element.29.high), channel_id=1, source_target_pairs={{0,32},{32,0},{64,96},{96,64},{128,160},{160,128},{192,224},{224,1... | collective-permute-start | bytes 884744 | tf_op jit(solution)/shard_map/ppermute | solution.py:423
  49.4 3.5 %collective-permute-start.9 = (bf16[2,144,512]{2,1,0:T(8,128)(2,1)S(1)}, bf16[2,144,512]{2,1,0:T(8,128)(2,1)S(1)}, u32[]{:S(2)}, u32[]{:S(2)}) collective-permute-start(bf16[2,144,512]{2,1,0:T(8,128)(2,1)S(1)} %get-tuple-element.28.low), channel_id=1, source_target_pairs={{0,32},{32,0},{64,96},{96,64},{128,160},{160,128},{192,224},{224,1... | collective-permute-start | bytes 884744 | tf_op jit(solution)/shard_map/ppermute | solution.py:423
  51.5 14.9 %collective-permute-start.4 = (bf16[72,512]{1,0:T(8,128)(2,1)S(1)}, bf16[72,512]{1,0:T(8,128)(2,1)S(1)}, u32[]{:S(2)}, u32[]{:S(2)}) collective-permute-start(bf16[72,512]{1,0:T(8,128)(2,1)S(1)} %get-tuple-element.25), channel_id=1, source_target_pairs={{0,32},{1,33},{2,34},{3,35},{4,36},{5,37},{6,38},{7,39},{8,40},{9,... | collective-permute-start | bytes 221192 | tf_op jit(solution)/shard_map/ppermute | solution.py:419
  58.1 21.7 %all-to-all-start.1 = ((bf16[32,24,128]{2,1,0:T(8,128)(2,1)}), bf16[32,24,128]{2,1,0:T(8,128)(2,1)S(1)}, u32[]{:S(2)}, u32[]{:S(2)}) async-start(bf16[32,24,128]{2,1,0:T(8,128)(2,1)} %shard_map.93), calls=%async_computation.1 | async-start | bytes 393216 | tf_op jit(solution)/shard_map/all_to_all | solution.py:494
  66.4 12.4 %collective-permute-start.5 = (bf16[72,512]{1,0:T(8,128)(2,1)S(1)}, bf16[72,512]{1,0:T(8,128)(2,1)S(1)}, u32[]{:S(2)}, u32[]{:S(2)}) collective-permute-start(bf16[72,512]{1,0:T(8,128)(2,1)S(1)} %shard_map.90), channel_id=1, source_target_pairs={{0,1},{1,2},{2,3},{3,4},{4,5},{5,6},{6,7},{7,8},{8,9},{9,10},{10,1... | collective-permute-start | bytes 221192 | tf_op jit(solution)/shard_map/ppermute | solution.py:419
